TPU v7x, 128 devices: a whole 4x4x4 slice. The times are simulated.
128 devices in a mesh: seq: 8 (over y, core), exp: 16 (over z, x).
Axes of the slice: x: 4, y: 4, z: 4, core: 2. Of those that a mesh axis runs over, the one named last changes fastest.
Arguments:
- stream_in: bfloat16 [16, 1024, 2048], P('exp', 'seq'), may hold values from -20 to 20
- qkv_heads: bfloat16 [16, 1024, 3, 2048], P('exp', 'seq'), may hold values from -16 to 16
- expert_ids: int32 [16, 1024, 2], P('exp', 'seq'), may hold values from 0 to 15, all different within a row; in each aligned block of 128 rows (0 to 127, 128 to 255, ..., all dimensions but the last counted through in order) at most 24 rows name the same one
- gate_weights: float32 [16, 1024, 2], P('exp', 'seq'), may hold values from 0.25 to 1
- w_out: bfloat16 [2048, 2048], replicated, may hold values from -0.125 to 0.125
- w_gate: bfloat16 [16, 2048, 4096], P('exp', None, 'seq'), may hold values from -0.125 to 0.125
- w_up: bfloat16 [16, 2048, 4096], P('exp', None, 'seq'), may hold values from -0.125 to 0.125
- w_down: bfloat16 [16, 4096, 2048], P('exp', 'seq'), may hold values from -0.09375 to 0.09375
Outputs:
- block_out: bfloat16 [16, 1024, 2048], P('exp', 'seq')
Inputs may be any that keep to these rules, and one draw needn't show every extreme that they name: `expert_ids`: the 2 experts of a token differ. Among the 128 tokens of one device (aligned blocks of 128 tokens along the flattened image and token dimensions) no expert is named more than 24 times, a bound that some block reaches.
All inputs are finite; a program needn't handle non-finite values.
Results may differ from a plain program's by a relative error of at most 0.01.
Values may be sent and summed in bfloat16 or wider, within the bound.
No kernel may reach another device: no remote copies, remote signals or barrier semaphores. Data moves between devices by JAX's collectives and lax.ppermute only.
A program may use at most 128 MiB of HBM per device.

v0:
```python
import jax
import jax.numpy as jnp
from jax import lax
from jax.sharding import PartitionSpec as P

HD = 64
TOP = 2


def attend_block(query, keys, values):
    scale = float(HD) ** (-0.5)
    scores = jnp.einsum("qhd,khd->hqk", query, keys, preferred_element_type=jnp.float32) * scale
    top = jnp.max(scores, axis=2, keepdims=True)
    weights = jnp.exp(scores - top)
    probs = (weights / jnp.sum(weights, axis=2, keepdims=True)).astype(jnp.bfloat16)
    return jnp.einsum("hqk,khd->qhd", probs, values, preferred_element_type=jnp.float32).astype(
        jnp.bfloat16
    )


def expert_term(rows, gate_mat, up_mat, down_mat):
    gate = jnp.dot(rows, gate_mat, preferred_element_type=jnp.float32)
    up_value = jnp.dot(rows, up_mat, preferred_element_type=jnp.float32)
    hidden = (jax.nn.silu(gate) * up_value).astype(jnp.bfloat16)
    return jnp.dot(hidden, down_mat, preferred_element_type=jnp.float32)


def per_device(stream_in, qkv_heads, expert_ids, gate_weights, w_out, w_gate, w_up, w_down):
    tok_rows = stream_in.shape[1]
    width = stream_in.shape[2]
    n_seq = lax.axis_size("seq")
    n_exp = lax.axis_size("exp")
    local_width = width // n_seq
    local_heads = local_width // HD
    spread = lax.all_to_all(qkv_heads[0], "seq", split_axis=2, concat_axis=0, tiled=True)
    length = spread.shape[0]
    query = spread[:, 0].reshape(length, local_heads, HD)
    keys = spread[:, 1].reshape(length, local_heads, HD)
    values = spread[:, 2].reshape(length, local_heads, HD)
    block_rows = min(length, 512)
    query_blocks = query.reshape(length // block_rows, block_rows, local_heads, HD)
    context = lax.map(lambda piece: attend_block(piece, keys, values), query_blocks)
    context = context.reshape(length, local_width)
    merged = lax.all_to_all(context, "seq", split_axis=0, concat_axis=1, tiled=True)
    mid = stream_in[0].astype(jnp.float32) + jnp.dot(
        merged, w_out, preferred_element_type=jnp.float32
    )
    normed = (mid * lax.rsqrt(jnp.mean(mid * mid, axis=1, keepdims=True) + 1e-06)).astype(
        jnp.bfloat16
    )
    capacity = 3 * TOP * tok_rows // (2 * n_exp)
    flat_ids = expert_ids[0].reshape(-1)
    onehot = (flat_ids[:, None] == jnp.arange(n_exp, dtype=jnp.int32)[None, :]).astype(jnp.int32)
    rank = jnp.cumsum(onehot, axis=0) - onehot
    slot = jnp.sum(rank * onehot, axis=1)
    destination = flat_ids * capacity + slot
    sources = jnp.repeat(normed, TOP, axis=0)
    buffer = jnp.zeros((n_exp * capacity, width), jnp.bfloat16).at[destination].set(sources)
    gate_mat = w_gate[0]
    up_mat = w_up[0]
    down_mat = w_down[0]
    outgoing = jnp.broadcast_to(buffer[None], (n_seq, n_exp * capacity, width)).reshape(
        n_seq * n_exp * capacity, width
    )
    arrived = lax.all_to_all(outgoing, ("seq", "exp"), split_axis=0, concat_axis=0, tiled=True)
    shares = expert_term(arrived, gate_mat, up_mat, down_mat).astype(jnp.bfloat16)
    returned = lax.all_to_all(shares, ("seq", "exp"), split_axis=0, concat_axis=0, tiled=True)
    expert_rows = jnp.sum(
        returned.reshape(n_seq, n_exp * capacity, width).astype(jnp.float32), axis=0
    )
    picked = jnp.take(expert_rows, destination, axis=0)
    moe = jnp.sum(picked.reshape(tok_rows, TOP, width) * gate_weights[0][:, :, None], axis=1)
    return (mid + moe).astype(jnp.bfloat16)[None]


def solution(mesh):
    in_specs = (
        P("exp", "seq", None),
        P("exp", "seq", None, None),
        P("exp", "seq", None),
        P("exp", "seq", None),
        P(),
        P("exp", None, "seq"),
        P("exp", None, "seq"),
        P("exp", "seq", None),
    )
    out_specs = P("exp", "seq", None)
    return jax.shard_map(
        per_device, mesh=mesh, in_specs=in_specs, out_specs=out_specs, check_vma=False
    )
```

profile of v0, /device:TPU:2, one launch (start us, length us, event | category | flops | bytes accessed | tf_op | source)
XLA Modules:
  0.0 499.3 jit_solution(10187894833985626529)
XLA Ops:
  0.0 0.0 copy-start
  0.0 0.0 copy-start.6
  0.0 4.3 copy.31
  4.3 4.5 all-to-all-start
  8.8 0.0 copy-done.6
  8.8 0.1 copy.36
  8.9 0.1 eq.26
  9.1 0.1 reshape_squeeze.11
  9.2 0.6 reduce-window.6
  9.8 0.2 slice_reduce_fusion
  10.0 26.1 %all-to-all-done = bf16[128,3,2048]{0,1,2:T(4,128)(2,1)} async-done(((bf16[128,3,2048]{0,1,2:T(4,128)(2,1)}), bf16[128,3,2048]{0,1,2:T(4,128)(2,1)}, u32[]{:S(2)}, u32[]{:S(2)}) %all-to-all-start) | async-done | bytes 1572896 | tf_op jit(solution)/shard_map/all_to_all | solution.py:35
  36.1 4.0 copy.32
  40.1 3.7 all_to_all.44
  43.8 2.5 fusion.45
  46.4 0.4 reshape_reshape_squeeze.3
  46.8 0.9 copy.33
  47.6 25.0 %while.10 = (s32[]{:T(128)}, bf16[2,512,4,64]{1,3,2,0:T(8,128)(2,1)}, bf16[2,512,4,64]{1,3,2,0:T(8,128)(2,1)}, bf16[1024,4,64]{0,2,1:T(8,128)(2,1)}, bf16[1024,4,64]{0,2,1:T(8,128)(2,1)}, /*index=5*/s32[]{:T(128)}) while((s32[]{:T(128)}, bf16[2,512,4,64]{1,3,2,0:T(8,128)(2,1)}, bf16[2,512,4,64]{1,3,2,0:T(8,128)(2,1)}, ...), condition=%wide.region_3.4_spmd, body=%wide.region_0.3_spmd.sunk | while | flops 547488768 | bytes 24658588 | solution.py:42
  47.6 0.0 copy-start.3
  47.6 0.0 copy-start.5
  47.6 6.9 %fusion.61 = (f32[4,512]{1,0:T(4,128)S(1)}, f32[4,512,1024]{2,1,0:T(8,128)}) fusion(bf16[1024,4,64]{0,2,1:T(8,128)(2,1)} %get-tuple-element.115, bf16[2,512,4,64]{1,3,2,0:T(8,128)(2,1)} %get-tuple-element.114, s32[]{:T(128)} %get-tuple-element.106), kind=kOutput, calls=%fused_computation.53.clone.1 | convolution fusion | flops 274727936 | bytes 9183744 | tf_op jit(solution)/shard_map/while/body/eval_jaxpr/sub | solution.py:14
  54.5 0.0 copy-done.3
  54.5 0.0 copy-done.5
  54.5 4.8 fusion.62
  59.3 0.0 copy-start.4
  59.4 0.8 copy-done.4
  60.1 6.9 %fusion.61 = (f32[4,512]{1,0:T(4,128)S(1)}, f32[4,512,1024]{2,1,0:T(8,128)}) fusion(bf16[1024,4,64]{0,2,1:T(8,128)(2,1)} %get-tuple-element.115, bf16[2,512,4,64]{1,3,2,0:T(8,128)(2,1)} %get-tuple-element.114, s32[]{:T(128)} %get-tuple-element.106), kind=kOutput, calls=%fused_computation.53.clone.1 | convolution fusion | flops 274727936 | bytes 9183744 | tf_op jit(solution)/shard_map/while/body/eval_jaxpr/sub | solution.py:14
  67.0 0.0 copy-done.3
  67.0 0.0 copy-done.5
  67.0 4.8 fusion.62
  71.9 0.0 copy-start.4
  71.9 0.8 copy-done.4
  72.7 1.6 copy.34
  74.2 0.3 all_to_all.45
  74.6 0.9 copy.35
  75.5 3.7 all-to-all-start.1
  79.2 0.1 copy.41
  79.3 0.1 mul.60
  79.4 0.1 fusion.37
  79.5 9.7 %all-to-all-done.1 = bf16[8,128,256]{1,2,0:T(8,128)(2,1)S(1)} async-done(((bf16[8,128,256]{1,2,0:T(8,128)(2,1)}), bf16[8,128,256]{1,2,0:T(8,128)(2,1)S(1)}, u32[]{:S(2)}, u32[]{:S(2)}) %all-to-all-start.1) | async-done | bytes 524320 | tf_op jit(solution)/shard_map/all_to_all | solution.py:44
  89.2 0.8 copy-done.2
  90.0 4.9 multiply_reduce_fusion.2
  95.0 0.1 multiply_convert_fusion.1
  95.1 1.7 broadcast_in_dim.40
  96.8 2.3 reshape.110
  99.0 4.2 scatter_custom_fusion
  103.2 7.6 %broadcast_in_dim.41 = bf16[8,384,2048]{2,1,0:T(8,128)(2,1)} broadcast(bf16[384,2048]{1,0:T(8,128)(2,1)} %scatter_custom_fusion), dimensions={1,2} | broadcast | bytes 14155776 | tf_op jit(solution)/shard_map/broadcast_in_dim | solution.py:62
  110.8 149.8 %all_to_all.58 = bf16[128,24,2048]{2,1,0:T(8,128)(2,1)S(1)} all-to-all(bf16[128,24,2048]{2,1,0:T(8,128)(2,1)} %bitcast.99), channel_id=1, replica_groups=mesh['seq'=8,'exp'=16] {'seq','exp'}, dimensions={0} | all-to-all | bytes 25165824 | tf_op jit(solution)/shard_map/all_to_all | solution.py:65
  260.6 4.5 copy-done.1
  265.1 0.0 copy-done.8
  265.1 8.7 %fusion.30 = f32[3072,512]{1,0:T(8,128)} fusion(bf16[3072,2048]{1,0:T(8,128)(2,1)S(1)} %bitcast.101, bf16[1,2048,512]{2,1,0:T(8,128)(2,1)S(1)} %copy-done.8), kind=kOutput, calls=%fused_computation.27 | convolution fusion | flops 6442450944 | bytes 20971520 | tf_op jit(solution)/shard_map/dot_general | solution.py:22
  273.9 0.0 copy-done
  273.9 21.0 %convolution_convert_fusion = bf16[3072,2048]{1,0:T(8,128)(2,1)} fusion(bf16[1,512,2048]{2,1,0:T(8,128)(2,1)S(1)} %copy-done, f32[3072,512]{1,0:T(8,128)} %fusion.30, bf16[3072,2048]{1,0:T(8,128)(2,1)} %bitcast.102, bf16[1,2048,512]{2,1,0:T(8,128)(2,1)} %param.16), kind=kOutput, calls=%fused_computation.22 | convolution fusion | flops 12900630528 | bytes 35651584 | tf_op jit(solution)/shard_map/dot_general | solution.py:25
  294.9 6.5 %all-to-all-start.3 = ((bf16[128,24,2048]{2,1,0:T(8,128)(2,1)}), bf16[128,24,2048]{2,1,0:T(8,128)(2,1)}, u32[]{:S(2)}, u32[]{:S(2)}) async-start(bf16[128,24,2048]{2,1,0:T(8,128)(2,1)} %bitcast.100), calls=%async_computation.3 | async-start | bytes 25165824 | tf_op jit(solution)/shard_map/all_to_all | solution.py:67
  301.4 0.1 reduce_sum.50
  301.6 0.1 copy.39
  301.7 0.1 copy.40
  301.8 0.0 copy-done.7
  301.8 0.1 copy.42
  301.9 172.3 %all-to-all-done.3 = bf16[128,24,2048]{2,1,0:T(8,128)(2,1)} async-done(((bf16[128,24,2048]{2,1,0:T(8,128)(2,1)}), bf16[128,24,2048]{2,1,0:T(8,128)(2,1)}, u32[]{:S(2)}, u32[]{:S(2)}) %all-to-all-start.3) | async-done | bytes 12582944 | tf_op jit(solution)/shard_map/all_to_all | solution.py:67
  474.2 9.4 %convert_reduce_fusion = f32[384,2048]{1,0:T(8,128)} fusion(bf16[8,384,2048]{2,1,0:T(8,128)(2,1)} %bitcast.90), kind=kLoop, calls=%fused_computation.21 | loop fusion | flops 11796480 | bytes 15728640 | tf_op jit(solution)/shard_map/reduce_sum | solution.py:68
  483.7 5.5 %gather_fusion = f32[256,2048]{1,0:T(8,128)} fusion(f32[384,2048]{1,0:T(8,128)} %convert_reduce_fusion, s32[1024]{0:T(1024)S(1)} %pad_clamp_fusion), kind=kCustom, calls=%fused_computation | custom fusion | bytes 4195328 | tf_op jit(solution)/shard_map/jit(_take)/gather | solution.py:71
  489.2 3.5 gather.7
  492.7 5.7 %multiply_reduce_fusion.1 = f32[128,2048]{1,0:T(8,128)S(1)} fusion(f32[128,2,2048]{2,1,0:T(2,128)} %gather.7, pred[128,2]{1,0:T(8,128)(4,1)S(1)} %copy.40, f32[128,2]{1,0:T(8,128)S(1)} %copy.42), kind=kLoop, calls=%fused_computation.29 | loop fusion | flops 1310720 | bytes 3147008 | tf_op jit(solution)/shard_map/reduce_sum | solution.py:72
  498.4 0.9 fusion.34
  (15 shorter events, 0.1 us)
Async XLA Ops:
  0.0 273.9 %copy-start = (bf16[1,512,2048]{2,1,0:T(8,128)(2,1)S(1)}, bf16[1,512,2048]{2,1,0:T(8,128)(2,1)}, u32[]{:S(2)}) copy-start(bf16[1,512,2048]{2,1,0:T(8,128)(2,1)} %param.17) | copy-start | bytes 6291460
  0.0 8.8 %copy-start.6 = (s32[1,128,2]{1,2,0:T(2,128)S(1)}, s32[1,128,2]{1,2,0:T(2,128)}, u32[]{:S(2)}) copy-start(s32[1,128,2]{1,2,0:T(2,128)} %param.12) | copy-start | bytes 3076
  4.3 31.8 %all-to-all-start = ((bf16[128,3,2048]{0,1,2:T(4,128)(2,1)}), bf16[128,3,2048]{0,1,2:T(4,128)(2,1)}, u32[]{:S(2)}, u32[]{:S(2)}) async-start(bf16[128,3,2048]{0,1,2:T(4,128)(2,1)} %bitcast.103), calls=%async_computation | async-start | bytes 4194304 | tf_op jit(solution)/shard_map/all_to_all | solution.py:35
  47.6 6.9 %copy-start.3 = (bf16[2,512,4,64]{1,3,2,0:T(8,128)(2,1)S(1)}, bf16[2,512,4,64]{1,3,2,0:T(8,128)(2,1)}, u32[]{:S(2)}) copy-start(bf16[2,512,4,64]{1,3,2,0:T(8,128)(2,1)} %get-tuple-element.107) | copy-start | bytes 1572868 | tf_op jit(solution)/shard_map/while
  47.6 6.9 %copy-start.5 = (bf16[1024,4,64]{0,2,1:T(8,128)(2,1)S(1)}, bf16[1024,4,64]{0,2,1:T(8,128)(2,1)}, u32[]{:S(2)}) copy-start(bf16[1024,4,64]{0,2,1:T(8,128)(2,1)} %get-tuple-element.116) | copy-start | bytes 1572868 | tf_op jit(solution)/shard_map/while
  59.3 0.8 copy-start.4
  60.1 6.9 %copy-start.3 = (bf16[2,512,4,64]{1,3,2,0:T(8,128)(2,1)S(1)}, bf16[2,512,4,64]{1,3,2,0:T(8,128)(2,1)}, u32[]{:S(2)}) copy-start(bf16[2,512,4,64]{1,3,2,0:T(8,128)(2,1)} %get-tuple-element.107) | copy-start | bytes 1572868 | tf_op jit(solution)/shard_map/while
  60.1 6.9 %copy-start.5 = (bf16[1024,4,64]{0,2,1:T(8,128)(2,1)S(1)}, bf16[1024,4,64]{0,2,1:T(8,128)(2,1)}, u32[]{:S(2)}) copy-start(bf16[1024,4,64]{0,2,1:T(8,128)(2,1)} %get-tuple-element.116) | copy-start | bytes 1572868 | tf_op jit(solution)/shard_map/while
  71.9 0.8 copy-start.4
  75.5 13.8 %all-to-all-start.1 = ((bf16[8,128,256]{1,2,0:T(8,128)(2,1)}), bf16[8,128,256]{1,2,0:T(8,128)(2,1)S(1)}, u32[]{:S(2)}, u32[]{:S(2)}) async-start(bf16[8,128,256]{1,2,0:T(8,128)(2,1)} %copy.35), calls=%async_computation.1 | async-start | bytes 1048576 | tf_op jit(solution)/shard_map/all_to_all | solution.py:44
  89.2 0.8 copy-start.2
  110.8 154.3 %copy-start.8 = (bf16[1,2048,512]{2,1,0:T(8,128)(2,1)S(1)}, bf16[1,2048,512]{2,1,0:T(8,128)(2,1)}, u32[]{:S(2)}) copy-start(bf16[1,2048,512]{2,1,0:T(8,128)(2,1)} %param.15) | copy-start | bytes 6291460
  260.6 4.5 copy-start.1
  294.9 6.9 %copy-start.7 = (f32[1,128,2]{1,2,0:T(2,128)S(1)}, f32[1,128,2]{1,2,0:T(2,128)}, u32[]{:S(2)}) copy-start(f32[1,128,2]{1,2,0:T(2,128)} %param.13) | copy-start | bytes 3076
  294.9 179.3 %all-to-all-start.3 = ((bf16[128,24,2048]{2,1,0:T(8,128)(2,1)}), bf16[128,24,2048]{2,1,0:T(8,128)(2,1)}, u32[]{:S(2)}, u32[]{:S(2)}) async-start(bf16[128,24,2048]{2,1,0:T(8,128)(2,1)} %bitcast.100), calls=%async_computation.3 | async-start | bytes 25165824 | tf_op jit(solution)/shard_map/all_to_all | solution.py:67
where the time goes:
time: 509 us; the launch traced here: 499 us
  waiting for transfers between devices  208 us (41%)
  blocking collectives  150 us (29%)
  matrix products  58.1 us (11%)
  local copies, waits for them, and re-layouts  51.5 us (10%)
  other arithmetic  16.9 us (3%)
  starting transfers between devices  14.7 us (3%)
    all_to_all x1, waiting for transfers between devices, per_device(): lax.all_to_all(shares, ('seq', 'exp'), split_axis=0, concat_axis=0, tiled...  172 us
    all_to_all x1, blocking collectives, per_device(): lax.all_to_all(outgoing, ('seq', 'exp'), split_axis=0, concat_axis=0, til...  150 us
    all_to_all x1, waiting for transfers between devices, per_device(): lax.all_to_all(qkv_heads[0], 'seq', split_axis=2, concat_axis=0, tiled=True)  26.1 us
    dot_general x1, matrix products, expert_term(): return jnp.dot(hidden, down_mat, preferred_element_type=jnp.float32)  21 us
    sub x2, matrix products, attend_block(): weights = jnp.exp(scores - top)  13.7 us
  transfers between devices with their start and end apart: 3, of which 3 were waited for; matrix products, arithmetic and copies ran while one was open for 0% of the time, Pallas kernels for 0%

commit v1 on v0

v1 whole, which is shorter than its diff:
```python
import functools

import jax
import jax.numpy as jnp
from jax import lax
from jax.experimental import pallas as pl
from jax.experimental.pallas import tpu as pltpu
from jax.sharding import Mesh
from jax.sharding import PartitionSpec as P

HD = 64
LANES = 128
MIB = 1 << 20
BF16 = jnp.bfloat16
F32 = jnp.float32
LOG2E = 1.4426950408889634
NUM_CHUNKS = 3


def vmem(shape):
    return pl.BlockSpec(shape, lambda *_: (0,) * len(shape))


def attention_kernel(x_ref, out_ref, *, block):
    n_src, _, rows, lanes = x_ref.shape
    length = n_src * rows
    keys = x_ref[:, 1].reshape(length, lanes)
    values = x_ref[:, 2].reshape(length, lanes)
    wide = jnp.concatenate([values, jnp.ones((length, lanes), BF16)], axis=1)
    lane = lax.broadcasted_iota(jnp.int32, (1, lanes), 1)
    first = lane < HD
    scale = float(HD) ** (-0.5) * LOG2E
    per = block // rows
    for i in range(length // block):
        query = x_ref[i * per : (i + 1) * per, 0].reshape(block, lanes)
        parts = []
        for head in range(2):
            mine = jnp.where(first if head == 0 else ~first, query, jnp.zeros_like(query))
            scores = lax.dot_general(
                mine, keys, (((1,), (1,)), ((), ())), preferred_element_type=F32
            )
            top = jnp.max(scores, axis=1, keepdims=True)
            weights = jnp.exp2((scores - top) * scale).astype(BF16)
            both = jnp.dot(weights, wide, preferred_element_type=F32)
            parts.append(both[:, :lanes] / both[:, lanes:])
        context = jnp.where(first, parts[0], parts[1]).astype(BF16)
        out_ref[i * per : (i + 1) * per] = context.reshape(per, rows, lanes)


def attention(arrived):
    n_src, three, rows, width = arrived.shape
    return pl.pallas_call(
        functools.partial(attention_kernel, block=2 * rows),
        grid=(width // LANES,),
        in_specs=[pl.BlockSpec((n_src, three, rows, LANES), lambda i: (0, 0, 0, i))],
        out_specs=pl.BlockSpec((n_src, rows, LANES), lambda i: (0, 0, i)),
        out_shape=jax.ShapeDtypeStruct((n_src, rows, width), BF16),
        compiler_params=pltpu.CompilerParams(vmem_limit_bytes=40 * MIB),
        name="attention",
    )(arrived)


def places(ids, n_exp, piece):
    tokens = ids.shape[1]
    expert = lax.broadcasted_iota(jnp.int32, (n_exp, tokens), 0)
    named = [expert == ids[k : k + 1] for k in range(ids.shape[0])]
    member = sum(n.astype(F32) for n in named)
    before = (
        lax.broadcasted_iota(jnp.int32, (tokens, tokens), 0)
        < lax.broadcasted_iota(jnp.int32, (tokens, tokens), 1)
    ).astype(BF16)
    rank = jnp.dot(member.astype(BF16), before, preferred_element_type=F32)
    rows = []
    for k, n in enumerate(named):
        slot = jnp.sum(jnp.where(n, rank, 0.0), axis=0, keepdims=True).astype(jnp.int32)
        chunk = slot // piece
        rows.append(chunk * (n_exp * piece) + ids[k : k + 1] * piece + (slot - chunk * piece))
    return rows


def project_kernel(ctx_ref, w_ref, stream_ref, ids_ref, mid_ref, *out_refs, n_exp, piece):
    n_src = ctx_ref.shape[0]
    merged = jnp.concatenate([ctx_ref[s] for s in range(n_src)], axis=1)
    step = pl.program_id(0)
    cols = w_ref.shape[1]
    here = pl.ds(pl.multiple_of(step * cols, cols), cols)
    mid_ref[:, here] = stream_ref[...].astype(F32) + jnp.dot(
        merged, w_ref[...], preferred_element_type=F32
    )

    @pl.when(step == pl.num_programs(0) - 1)
    def _():
        mid = mid_ref[...]
        factor = lax.rsqrt(jnp.mean(mid * mid, axis=1, keepdims=True) + 1e-06)
        normed = (mid * factor).astype(BF16)
        rows = places(ids_ref[...], n_exp, piece)
        slots = n_exp * piece
        for c, ref in enumerate(out_refs):
            at = lax.broadcasted_iota(jnp.int32, (slots, normed.shape[0]), 0) + c * slots
            pick = sum((at == r).astype(F32) for r in rows).astype(BF16)
            ref[...] = jnp.dot(pick, normed, preferred_element_type=F32).astype(BF16)


def project(merged, w_out, stream, ids, n_exp, piece, n_chunks):
    n_src, rows, part = merged.shape
    width = w_out.shape[1]
    cols = 512
    slots = n_exp * piece
    return pl.pallas_call(
        functools.partial(project_kernel, n_exp=n_exp, piece=piece),
        grid=(width // cols,),
        in_specs=[
            vmem((n_src, rows, part)),
            pl.BlockSpec((width, cols), lambda i: (0, i)),
            pl.BlockSpec((rows, cols), lambda i: (0, i)),
            vmem(ids.shape),
        ],
        out_specs=[vmem((rows, width))] + [vmem((slots, width))] * n_chunks,
        out_shape=[jax.ShapeDtypeStruct((rows, width), F32)]
        + [jax.ShapeDtypeStruct((slots, width), BF16)] * n_chunks,
        compiler_params=pltpu.CompilerParams(vmem_limit_bytes=40 * MIB),
        name="project",
    )(merged, w_out, stream, ids)


def expert_kernel(x_ref, g0, g1, u0, u1, d0, d1, out_ref):
    rows = x_ref[...]
    total = None
    for gate_ref, up_ref, down_ref in ((g0, u0, d0), (g1, u1, d1)):
        gate = jnp.dot(rows, gate_ref[...], preferred_element_type=F32)
        up = jnp.dot(rows, up_ref[...], preferred_element_type=F32)
        hidden = (gate / (1.0 + jnp.exp(-gate)) * up).astype(BF16)
        term = jnp.dot(hidden, down_ref[...], preferred_element_type=F32)
        total = term if total is None else total + term
    out_ref[...] = total.astype(BF16)


def experts(rows, gates, ups, downs):
    n, width = rows.shape
    block = 256
    full = [vmem(w.shape) for w in (*gates, *ups, *downs)]
    return pl.pallas_call(
        expert_kernel,
        grid=(n // block,),
        in_specs=[pl.BlockSpec((block, width), lambda i: (i, 0))] + full,
        out_specs=pl.BlockSpec((block, width), lambda i: (i, 0)),
        out_shape=jax.ShapeDtypeStruct((n, width), BF16),
        compiler_params=pltpu.CompilerParams(vmem_limit_bytes=56 * MIB),
        name="experts",
    )(rows, *gates, *ups, *downs)


def combine_kernel(mid_ref, ids_ref, weight_ref, *refs, n_exp, piece):
    *back_refs, out_ref = refs
    rows = places(ids_ref[...], n_exp, piece)
    slots = n_exp * piece
    back = jnp.concatenate([r[...] for r in back_refs], axis=0)
    total = mid_ref[...]
    at = lax.broadcasted_iota(jnp.int32, (back.shape[0], rows[0].shape[1]), 0)
    for k, row in enumerate(rows):
        pick = (at == row).astype(F32).astype(BF16)
        term = lax.dot_general(pick, back, (((0,), (0,)), ((), ())), preferred_element_type=F32)
        total = total + term * weight_ref[:, k : k + 1]
    out_ref[...] = total.astype(BF16)


def combine(mid, ids, weights, backs, n_exp, piece):
    rows, width = mid.shape
    cols = 512
    slots = n_exp * piece
    return pl.pallas_call(
        functools.partial(combine_kernel, n_exp=n_exp, piece=piece),
        grid=(width // cols,),
        in_specs=[
            pl.BlockSpec((rows, cols), lambda i: (0, i)),
            vmem(ids.shape),
            vmem(weights.shape),
        ]
        + [pl.BlockSpec((slots, cols), lambda i: (0, i))] * len(backs),
        out_specs=pl.BlockSpec((rows, cols), lambda i: (0, i)),
        out_shape=jax.ShapeDtypeStruct((rows, width), BF16),
        compiler_params=pltpu.CompilerParams(vmem_limit_bytes=40 * MIB),
        name="combine",
    )(mid, ids, weights, *backs)


def per_device(stream_in, qkv_heads, expert_ids, gate_weights, w_out, w_gate, w_up, w_down):
    rows, width = stream_in.shape[1:]
    seq, exp = ("y", "core"), ("z", "x")
    n_seq, n_exp = lax.axis_size(seq), lax.axis_size(exp)
    capacity = 3 * expert_ids.shape[2] * rows // (2 * n_exp)
    piece = capacity // NUM_CHUNKS
    swap = [(0, 1), (1, 0)]
    gates, ups, downs = (
        (w[0], lax.ppermute(w[0], "core", swap)) for w in (w_gate, w_up, w_down)
    )
    ids = expert_ids[0].T
    qkv = qkv_heads[0].transpose(1, 0, 2).reshape(3, rows, n_seq, width // n_seq)
    qkv = qkv.transpose(2, 0, 1, 3)
    arrived = lax.all_to_all(qkv, seq, split_axis=0, concat_axis=0, tiled=True)
    context = attention(arrived)
    merged = lax.all_to_all(context, seq, split_axis=0, concat_axis=0, tiled=True)
    mid, *buffers = project(merged, w_out, stream_in[0], ids, n_exp, piece, NUM_CHUNKS)
    backs = []
    for buffer in buffers:
        sent = lax.all_to_all(buffer, exp, split_axis=0, concat_axis=0, tiled=True)
        gathered = lax.all_gather(sent, "y", tiled=True)
        shares = experts(gathered, gates, ups, downs)
        summed = lax.psum_scatter(shares, "y", scatter_dimension=0, tiled=True)
        backs.append(lax.all_to_all(summed, exp, split_axis=0, concat_axis=0, tiled=True))
    return combine(mid, ids, gate_weights[0], backs, n_exp, piece)[None]


def solution(mesh):
    split = Mesh(mesh.devices.reshape(-1, 2, 4, 4), ("y", "core", "z", "x"))
    seq, exp = ("y", "core"), ("z", "x")
    in_specs = (
        P(exp, seq, None),
        P(exp, seq, None, None),
        P(exp, seq, None),
        P(exp, seq, None),
        P(),
        P(exp, None, seq),
        P(exp, None, seq),
        P(exp, seq, None),
    )
    return jax.shard_map(
        per_device, mesh=split, in_specs=in_specs, out_specs=P(exp, seq, None), check_vma=False
    )
```

time: 509 us -> 298 us (0.59); the launches traced: 499 us -> 296 us
  waiting for transfers between devices: 208 us -> 116 us
  blocking collectives: 150 us -> 83.9 us
  matrix products: 58.1 us -> 0 us
  Pallas kernels: 0 us -> 51.7 us
  local copies, waits for them, and re-layouts: 51.5 us -> 7.82 us
  other arithmetic: 16.9 us -> 0 us
  between operations: 0.13 us -> 13.5 us
  starting transfers between devices: 14.7 us -> 23.3 us
    all_to_all x3, waiting for transfers between devices: 208 us -> 10.1 us  [per_device(): lax.all_to_all(summed, exp, split_axis=0, concat_axis=0, tiled=True)]
    reduce_scatter x0 -> x3, waiting for transfers between devices: none -> 67.6 us  [per_device(): summed = lax.psum_scatter(shares, 'y', scatter_dimension=0, tiled=True)]
    all_to_all x1 -> x5, blocking collectives: 150 us -> 83.9 us  [the longest x3 45.1 us: per_device(): sent = lax.all_to_all(buffer, exp, split_axis=0, concat_axis=0, tiled=True)]
    pallas_call x0 -> x6, Pallas kernels: none -> 51.7 us  [the longest x3 39.5 us: experts(): pl.pallas_call(expert_kernel, grid=(n // block,), in_specs=[pl.BlockSpec(...]
    dot_general x5 -> x0, matrix products: 44.4 us -> none  [the longest x1 21 us: expert_term(): return jnp.dot(hidden, down_mat, preferred_element_type=jnp.float32)]
    all_gather x0 -> x3, waiting for transfers between devices: none -> 28.1 us  [per_device(): gathered = lax.all_gather(sent, 'y', tiled=True)]
    reduce_sum x3 -> x0, other arithmetic: 15.2 us -> none  [the longest x1 9.45 us: per_device(): jnp.sum(returned.reshape(n_seq, n_exp * capacity, width).astype(jnp.float...]
    sub x2 -> x0, matrix products: 13.7 us -> none  [attend_block(): weights = jnp.exp(scores - top)]
  transfers between devices with their start and end apart: 3 -> 12, of which waited for: 3 -> 9; matrix products, arithmetic and copies ran while one was open for 0% -> 0% of each run, Pallas kernels for 0% -> 13%
where the time goes in v1:
time: 298 us; the launch traced here: 296 us
  waiting for transfers between devices  116 us (39%)
  blocking collectives  83.9 us (28%)
  Pallas kernels  51.7 us (17%)
  starting transfers between devices  23.3 us (8%)
  between operations  13.5 us (5%)
  local copies, waits for them, and re-layouts  7.82 us (3%)
    reduce_scatter x3, waiting for transfers between devices, per_device(): summed = lax.psum_scatter(shares, 'y', scatter_dimension=0, tiled=True)  67.6 us
    all_to_all x3, blocking collectives, per_device(): sent = lax.all_to_all(buffer, exp, split_axis=0, concat_axis=0, tiled=True)  45.1 us
    pallas_call x3, Pallas kernels, experts(): pl.pallas_call(expert_kernel, grid=(n // block,), in_specs=[pl.BlockSpec(...  39.5 us
    all_gather x3, waiting for transfers between devices, per_device(): gathered = lax.all_gather(sent, 'y', tiled=True)  28.1 us
    all_to_all x1, blocking collectives, per_device(): arrived = lax.all_to_all(qkv, seq, split_axis=0, concat_axis=0, tiled=True)  26.1 us
    all_to_all x3, starting transfers between devices, per_device(): lax.all_to_all(summed, exp, split_axis=0, concat_axis=0, tiled=True)  22.2 us
    all_to_all x1, blocking collectives, per_device(): lax.all_to_all(context, seq, split_axis=0, concat_axis=0, tiled=True)  12.8 us
    all_to_all x3, waiting for transfers between devices, per_device(): lax.all_to_all(summed, exp, split_axis=0, concat_axis=0, tiled=True)  10.1 us
  transfers between devices with their start and end apart: 12, of which 9 were waited for; matrix products, arithmetic and copies ran while one was open for 0% of the time, Pallas kernels for 13%

profile of v1, /device:TPU:2, one launch (start us, length us, event | category | flops | bytes accessed | tf_op | source)
XLA Modules:
  0.0 296.1 jit_solution(12028118109175515499)
XLA Ops:
  6.5 0.0 all-gather.4.cloned.1.call-start
  6.5 2.6 copy.10
  9.1 1.7 copy.11
  10.9 26.1 %all_to_all.79.x_ref = bf16[8,3,128,256]{3,2,1,0:T(8,128)(2,1)S(1)} all-to-all(bf16[8,3,128,256]{3,2,1,0:T(8,128)(2,1)S(1)} %bitcast.49), channel_id=1, replica_groups=mesh['y'=4,'core'=2,'z'=4,'x'=4] {'y','core'}, dimensions={0} | all-to-all | bytes 3145728 | tf_op jit(solution)/shard_map/all_to_all | solution.py:200
  36.9 0.0 copy-start.1
  36.9 0.0 copy-start.2
  36.9 6.0 %attention.1 = bf16[8,128,256]{2,1,0:T(8,128)(2,1)S(1)} custom-call(bf16[8,3,128,256]{3,2,1,0:T(8,128)(2,1)S(1)} %all_to_all.79.x_ref), custom_call_target="tpu_custom_call" | custom-call | tf_op jit(solution)/shard_map/attention/pallas_call | solution.py:52
  43.0 12.8 %all_to_all.80.ctx_ref = bf16[8,128,256]{2,1,0:T(8,128)(2,1)S(1)} all-to-all(bf16[8,128,256]{2,1,0:T(8,128)(2,1)S(1)} %attention.1), channel_id=1, replica_groups=mesh['y'=4,'core'=2,'z'=4,'x'=4] {'y','core'}, dimensions={0} | all-to-all | bytes 1048576 | tf_op jit(solution)/shard_map/all_to_all | solution.py:202
  55.8 0.0 copy-done.1
  55.8 0.0 copy-done.2
  55.8 0.0 copy-start
  55.8 3.4 %copy-done = bf16[2048,2048]{1,0:T(8,128)(2,1)S(1)} copy-done((bf16[2048,2048]{1,0:T(8,128)(2,1)S(1)}, bf16[2048,2048]{1,0:T(8,128)(2,1)}, u32[]{:S(2)}) %copy-start) | copy-done | bytes 8388632
  59.2 3.2 %project.1 = (f32[128,2048]{1,0:T(8,128)S(1)}, bf16[128,2048]{1,0:T(8,128)(2,1)S(1)}, bf16[128,2048]{1,0:T(8,128)(2,1)S(1)}, bf16[128,2048]{1,0:T(8,128)(2,1)S(1)}) custom-call(bf16[8,128,256]{2,1,0:T(8,128)(2,1)S(1)} %all_to_all.80.ctx_ref, bf16[2048,2048]{1,0:T(8,128)(2,1)S(1)} %copy-done, bf16[128,2048]{1,0:T(8,128)(2,1)S(1)} %bitcast.30, ...), custom_call_target="tpu_custom_call" | custom-call | tf_op jit(solution)/shard_map/project/pallas_call | solution.py:109
  62.4 18.0 %all_to_all.81 = bf16[16,8,2048]{2,1,0:T(8,128)(2,1)} all-to-all(bf16[16,8,2048]{2,1,0:T(8,128)(2,1)S(1)} %bitcast.33), channel_id=1, replica_groups=mesh['y'=4,'core'=2,'z'=4,'x'=4] {'z','x'}, dimensions={0} | all-to-all | bytes 1048576 | tf_op jit(solution)/shard_map/all_to_all | solution.py:206
  80.4 0.0 all-gather.4.cloned.1.call-update
  80.5 0.0 all-gather.6.cloned.1.call-start
  80.5 13.6 %all_to_all.82 = bf16[16,8,2048]{2,1,0:T(8,128)(2,1)} all-to-all(bf16[16,8,2048]{2,1,0:T(8,128)(2,1)S(1)} %bitcast.32), channel_id=1, replica_groups=mesh['y'=4,'core'=2,'z'=4,'x'=4] {'z','x'}, dimensions={0} | all-to-all | bytes 1048576 | tf_op jit(solution)/shard_map/all_to_all | solution.py:206
  94.1 0.0 all-gather.6.cloned.1.call-update
  94.2 0.0 all-gather.8.cloned.1.call-start
  94.2 13.4 %all_to_all.83 = bf16[16,8,2048]{2,1,0:T(8,128)(2,1)} all-to-all(bf16[16,8,2048]{2,1,0:T(8,128)(2,1)S(1)} %bitcast.31), channel_id=1, replica_groups=mesh['y'=4,'core'=2,'z'=4,'x'=4] {'z','x'}, dimensions={0} | all-to-all | bytes 1048576 | tf_op jit(solution)/shard_map/all_to_all | solution.py:206
  107.6 0.0 all-gather.8.cloned.1.call-update
  107.7 0.0 reduce-scatter.4.cloned.1.call-start
  107.7 0.1 collective-permute-start
  107.8 0.5 collective-permute-start.1
  108.3 0.1 collective-permute-start.2
  108.4 5.8 %collective-permute-done.g1 = bf16[2048,512]{1,0:T(8,128)(2,1)S(1)} collective-permute-done((bf16[2048,512]{1,0:T(8,128)(2,1)}, bf16[2048,512]{1,0:T(8,128)(2,1)S(1)}, u32[]{:S(2)}, u32[]{:S(2)}) %collective-permute-start) | collective-permute-done | bytes 2097184 | tf_op jit(solution)/shard_map/ppermute | solution.py:195
  114.2 0.0 copy-start.3
  114.2 1.1 collective-permute-done.1.u1
  115.3 3.0 %collective-permute-done.2.d1 = bf16[512,2048]{1,0:T(8,128)(2,1)} collective-permute-done((bf16[512,2048]{1,0:T(8,128)(2,1)}, bf16[512,2048]{1,0:T(8,128)(2,1)}, u32[]{:S(2)}, u32[]{:S(2)}) %collective-permute-start.2) | collective-permute-done | bytes 2097184 | tf_op jit(solution)/shard_map/ppermute | solution.py:195
  118.3 0.0 all-gather.4.cloned.1.call-done.x_ref
  118.3 0.0 copy-done.3
  118.3 13.4 %experts.3 = bf16[512,2048]{1,0:T(8,128)(2,1)} custom-call(bf16[512,2048]{1,0:T(8,128)(2,1)} %all-gather.4.cloned.1.call-done.x_ref, bf16[2048,512]{1,0:T(8,128)(2,1)} %bitcast.38, bf16[2048,512]{1,0:T(8,128)(2,1)} %copy-done.3, bf16[2048,512]{1,0:T(8,128)(2,1)} %bitcast.42, bf16[2048,512]{1,0:T(8,128)(2,1)} %collective-permute-done.1.u1, ...), custom_call_target="tpu_custom_call" | custom-call | tf_op jit(solution)/shard_map/experts/pallas_call | solution.py:142
  131.7 0.0 reduce-scatter.4.cloned.1.call-update
  131.7 0.2 reduce-scatter.6.cloned.1.call-start
  132.0 8.6 %all-gather.6.cloned.1.call-done.x_ref = bf16[512,2048]{1,0:T(8,128)(2,1)} async-done(((bf16[128,2048]{1,0:T(8,128)(2,1)}), bf16[512,2048]{1,0:T(8,128)(2,1)}) %all-gather.6.cloned.1.call-update) | async-done | bytes 2097168 | tf_op jit(solution)/shard_map/all_gather | solution.py:207
  140.6 13.0 %experts.4 = bf16[512,2048]{1,0:T(8,128)(2,1)} custom-call(bf16[512,2048]{1,0:T(8,128)(2,1)} %all-gather.6.cloned.1.call-done.x_ref, bf16[2048,512]{1,0:T(8,128)(2,1)} %bitcast.39, bf16[2048,512]{1,0:T(8,128)(2,1)} %copy-done.3, bf16[2048,512]{1,0:T(8,128)(2,1)} %bitcast.43, bf16[2048,512]{1,0:T(8,128)(2,1)} %collective-permute-done.1.u1, ...), custom_call_target="tpu_custom_call" | custom-call | tf_op jit(solution)/shard_map/experts/pallas_call | solution.py:142
  153.6 0.0 reduce-scatter.6.cloned.1.call-update
  153.6 0.0 reduce-scatter.8.cloned.1.call-start
  153.6 19.5 %all-gather.8.cloned.1.call-done.x_ref = bf16[512,2048]{1,0:T(8,128)(2,1)} async-done(((bf16[128,2048]{1,0:T(8,128)(2,1)}), bf16[512,2048]{1,0:T(8,128)(2,1)}) %all-gather.8.cloned.1.call-update) | async-done | bytes 2097168 | tf_op jit(solution)/shard_map/all_gather | solution.py:207
  173.1 13.0 %experts.5 = bf16[512,2048]{1,0:T(8,128)(2,1)} custom-call(bf16[512,2048]{1,0:T(8,128)(2,1)} %all-gather.8.cloned.1.call-done.x_ref, bf16[2048,512]{1,0:T(8,128)(2,1)} %bitcast.40, bf16[2048,512]{1,0:T(8,128)(2,1)} %copy-done.3, bf16[2048,512]{1,0:T(8,128)(2,1)} %bitcast.44, bf16[2048,512]{1,0:T(8,128)(2,1)} %collective-permute-done.1.u1, ...), custom_call_target="tpu_custom_call" | custom-call | tf_op jit(solution)/shard_map/experts/pallas_call | solution.py:142
  186.2 0.0 reduce-scatter.8.cloned.1.call-update
  186.2 0.0 copy-start.4
  186.2 18.9 %reduce-scatter.4.cloned.1.call-done = bf16[128,2048]{1,0:T(8,128)(2,1)} async-done(((bf16[512,2048]{1,0:T(8,128)(2,1)}), bf16[128,2048]{1,0:T(8,128)(2,1)}) %reduce-scatter.4.cloned.1.call-update) | async-done | bytes 524304 | tf_op jit(solution)/shard_map/reduce_scatter | solution.py:209
  205.1 7.4 %all-to-all-start.3 = ((bf16[16,8,2048]{2,1,0:T(8,128)(2,1)}), bf16[16,8,2048]{2,1,0:T(8,128)(2,1)S(1)}, u32[]{:S(2)}, u32[]{:S(2)}) async-start(bf16[16,8,2048]{2,1,0:T(8,128)(2,1)} %bitcast.54), calls=%async_computation.4 | async-start | bytes 1048576 | tf_op jit(solution)/shard_map/all_to_all | solution.py:210
  212.5 24.4 %reduce-scatter.6.cloned.1.call-done = bf16[128,2048]{1,0:T(8,128)(2,1)} async-done(((bf16[512,2048]{1,0:T(8,128)(2,1)}), bf16[128,2048]{1,0:T(8,128)(2,1)}) %reduce-scatter.6.cloned.1.call-update) | async-done | bytes 524304 | tf_op jit(solution)/shard_map/reduce_scatter | solution.py:209
  236.9 0.0 all-to-all-done.3
  236.9 7.4 %all-to-all-start.5 = ((bf16[16,8,2048]{2,1,0:T(8,128)(2,1)}), bf16[16,8,2048]{2,1,0:T(8,128)(2,1)S(1)}, u32[]{:S(2)}, u32[]{:S(2)}) async-start(bf16[16,8,2048]{2,1,0:T(8,128)(2,1)} %bitcast.55), calls=%async_computation.7 | async-start | bytes 1048576 | tf_op jit(solution)/shard_map/all_to_all | solution.py:210
  244.4 24.3 %reduce-scatter.8.cloned.1.call-done = bf16[128,2048]{1,0:T(8,128)(2,1)} async-done(((bf16[512,2048]{1,0:T(8,128)(2,1)}), bf16[128,2048]{1,0:T(8,128)(2,1)}) %reduce-scatter.8.cloned.1.call-update) | async-done | bytes 524304 | tf_op jit(solution)/shard_map/reduce_scatter | solution.py:209
  268.6 0.0 all-to-all-done.5
  268.6 7.4 %all-to-all-start.7 = ((bf16[16,8,2048]{2,1,0:T(8,128)(2,1)}), bf16[16,8,2048]{2,1,0:T(8,128)(2,1)S(1)}, u32[]{:S(2)}, u32[]{:S(2)}) async-start(bf16[16,8,2048]{2,1,0:T(8,128)(2,1)} %bitcast.56), calls=%async_computation.10 | async-start | bytes 1048576 | tf_op jit(solution)/shard_map/all_to_all | solution.py:210
  276.0 0.0 copy-done.4
  276.0 0.1 copy.12
  276.1 10.1 %all-to-all-done.7 = bf16[16,8,2048]{2,1,0:T(8,128)(2,1)S(1)} async-done(((bf16[16,8,2048]{2,1,0:T(8,128)(2,1)}), bf16[16,8,2048]{2,1,0:T(8,128)(2,1)S(1)}, u32[]{:S(2)}, u32[]{:S(2)}) %all-to-all-start.7) | async-done | bytes 524320 | tf_op jit(solution)/shard_map/all_to_all | solution.py:210
  286.2 3.0 %combine.1 = bf16[128,2048]{1,0:T(8,128)(2,1)} custom-call(f32[128,2048]{1,0:T(8,128)S(1)} %get-tuple-element.9.mid_ref, s32[2,128]{1,0:T(2,128)S(1)} %bitcast.36, f32[128,2]{1,0:T(8,128)S(1)} %bitcast.34, bf16[128,2048]{1,0:T(8,128)(2,1)S(1)} %bitcast.27, bf16[128,2048]{1,0:T(8,128)(2,1)S(1)} %bitcast.28, bf16[128,2048]{1,0:T(8,128)(2,1)S(1)} %bitcast.29), custom_call_target="tpu_custom_call" | custom-call | tf_op jit(solution)/shard_map/combine/pallas_call | solution.py:171
Async XLA Ops:
  6.5 111.8 %all-gather.4.cloned.1.call-start = ((), (), s32[]{:S(2)}) async-start(), calls=%async_computation.11 | async-start | bytes 2621440 | tf_op jit(solution)/shard_map/all_gather | solution.py:207
  36.9 18.8 %copy-start.1 = (bf16[1,128,2048]{2,1,0:T(8,128)(2,1)S(1)}, bf16[1,128,2048]{2,1,0:T(8,128)(2,1)}, u32[]{:S(2)}) copy-start(bf16[1,128,2048]{2,1,0:T(8,128)(2,1)} %param.8) | copy-start | bytes 1572868
  36.9 18.8 %copy-start.2 = (s32[1,128,2]{1,2,0:T(2,128)S(1)}, s32[1,128,2]{1,2,0:T(2,128)}, u32[]{:S(2)}) copy-start(s32[1,128,2]{1,2,0:T(2,128)} %param.10) | copy-start | bytes 3076
  55.8 3.4 %copy-start = (bf16[2048,2048]{1,0:T(8,128)(2,1)S(1)}, bf16[2048,2048]{1,0:T(8,128)(2,1)}, u32[]{:S(2)}) copy-start(bf16[2048,2048]{1,0:T(8,128)(2,1)} %w_ref.1) | copy-start | bytes 25165828
  80.5 60.1 %all-gather.6.cloned.1.call-start = ((), (), s32[]{:S(2)}) async-start(), calls=%async_computation.13 | async-start | bytes 2621440 | tf_op jit(solution)/shard_map/all_gather | solution.py:207
  94.2 79.0 %all-gather.8.cloned.1.call-start = ((), (), s32[]{:S(2)}) async-start(), calls=%async_computation.15 | async-start | bytes 2621440 | tf_op jit(solution)/shard_map/all_gather | solution.py:207
  107.7 97.4 %reduce-scatter.4.cloned.1.call-start = ((), (), s32[]{:S(2)}) async-start(), calls=%async_computation.12 | async-start | bytes 2621440 | tf_op jit(solution)/shard_map/reduce_scatter | solution.py:209
  107.7 6.5 %collective-permute-start = (bf16[2048,512]{1,0:T(8,128)(2,1)}, bf16[2048,512]{1,0:T(8,128)(2,1)S(1)}, u32[]{:S(2)}, u32[]{:S(2)}) collective-permute-start(bf16[2048,512]{1,0:T(8,128)(2,1)} %bitcast.37), channel_id=1, source_target_pairs={{0,16},{16,0},{1,17},{17,1},{2,18},{18,2},{3,19},{19,3},{4,20},{20... | collective-permute-start | bytes 6291464 | tf_op jit(solution)/shard_map/ppermute | solution.py:195
  107.8 7.5 %collective-permute-start.1 = (bf16[2048,512]{1,0:T(8,128)(2,1)}, bf16[2048,512]{1,0:T(8,128)(2,1)}, u32[]{:S(2)}, u32[]{:S(2)}) collective-permute-start(bf16[2048,512]{1,0:T(8,128)(2,1)} %bitcast.41), channel_id=1, source_target_pairs={{0,16},{16,0},{1,17},{17,1},{2,18},{18,2},{3,19},{19,3},{4,20},{20... | collective-permute-start | bytes 6291464 | tf_op jit(solution)/shard_map/ppermute | solution.py:195
  108.3 10.0 %collective-permute-start.2 = (bf16[512,2048]{1,0:T(8,128)(2,1)}, bf16[512,2048]{1,0:T(8,128)(2,1)}, u32[]{:S(2)}, u32[]{:S(2)}) collective-permute-start(bf16[512,2048]{1,0:T(8,128)(2,1)} %bitcast.45), channel_id=1, source_target_pairs={{0,16},{16,0},{1,17},{17,1},{2,18},{18,2},{3,19},{19,3},{4,20},{20... | collective-permute-start | bytes 6291464 | tf_op jit(solution)/shard_map/ppermute | solution.py:195
  114.2 4.1 %copy-start.3 = (bf16[2048,512]{1,0:T(8,128)(2,1)}, bf16[2048,512]{1,0:T(8,128)(2,1)S(1)}, u32[]{:S(2)}) copy-start(bf16[2048,512]{1,0:T(8,128)(2,1)S(1)} %collective-permute-done.g1) | copy-start | bytes 6291460
  131.7 105.2 %reduce-scatter.6.cloned.1.call-start = ((), (), s32[]{:S(2)}) async-start(), calls=%async_computation.14 | async-start | bytes 2621440 | tf_op jit(solution)/shard_map/reduce_scatter | solution.py:209
  153.6 115.0 %reduce-scatter.8.cloned.1.call-start = ((), (), s32[]{:S(2)}) async-start(), calls=%async_computation.16 | async-start | bytes 2621440 | tf_op jit(solution)/shard_map/reduce_scatter | solution.py:209
  186.2 89.8 %copy-start.4 = (f32[1,128,2]{1,2,0:T(2,128)S(1)}, f32[1,128,2]{1,2,0:T(2,128)}, u32[]{:S(2)}) copy-start(f32[1,128,2]{1,2,0:T(2,128)} %param.11) | copy-start | bytes 3076
  205.1 31.8 %all-to-all-start.3 = ((bf16[16,8,2048]{2,1,0:T(8,128)(2,1)}), bf16[16,8,2048]{2,1,0:T(8,128)(2,1)S(1)}, u32[]{:S(2)}, u32[]{:S(2)}) async-start(bf16[16,8,2048]{2,1,0:T(8,128)(2,1)} %bitcast.54), calls=%async_computation.4 | async-start | bytes 1048576 | tf_op jit(solution)/shard_map/all_to_all | solution.py:210
  236.9 31.7 %all-to-all-start.5 = ((bf16[16,8,2048]{2,1,0:T(8,128)(2,1)}), bf16[16,8,2048]{2,1,0:T(8,128)(2,1)S(1)}, u32[]{:S(2)}, u32[]{:S(2)}) async-start(bf16[16,8,2048]{2,1,0:T(8,128)(2,1)} %bitcast.55), calls=%async_computation.7 | async-start | bytes 1048576 | tf_op jit(solution)/shard_map/all_to_all | solution.py:210
  268.6 17.6 %all-to-all-start.7 = ((bf16[16,8,2048]{2,1,0:T(8,128)(2,1)}), bf16[16,8,2048]{2,1,0:T(8,128)(2,1)S(1)}, u32[]{:S(2)}, u32[]{:S(2)}) async-start(bf16[16,8,2048]{2,1,0:T(8,128)(2,1)} %bitcast.56), calls=%async_computation.10 | async-start | bytes 1048576 | tf_op jit(solution)/shard_map/all_to_all | solution.py:210
Sparse Core Ops, SparseCore 0:
  80.6 27.3 all-gather.3
  109.7 30.8 all-gather.5
  142.2 30.8 all-gather.7
  175.4 29.6 reduce-scatter.3
  207.5 29.4 reduce-scatter.5
  239.2 29.3 reduce-scatter.7

commit v2 on v1

v2 whole, which is shorter than its diff:
```python
import functools

import jax
import jax.numpy as jnp
from jax import lax
from jax.experimental import pallas as pl
from jax.experimental.pallas import tpu as pltpu
from jax.sharding import Mesh
from jax.sharding import PartitionSpec as P

HD = 64
LANES = 128
MIB = 1 << 20
BF16 = jnp.bfloat16
F32 = jnp.float32
LOG2E = 1.4426950408889634
TOP = 2


def vmem(shape):
    return pl.BlockSpec(shape, lambda *_: (0,) * len(shape))


def attention_kernel(x_ref, out_ref, *, block):
    n_src, _, rows, lanes = x_ref.shape
    length = n_src * rows
    keys = x_ref[:, 1].reshape(length, lanes)
    values = x_ref[:, 2].reshape(length, lanes)
    wide = jnp.concatenate([values, jnp.ones((length, lanes), BF16)], axis=1)
    lane = lax.broadcasted_iota(jnp.int32, (1, lanes), 1)
    first = lane < HD
    scale = float(HD) ** (-0.5) * LOG2E
    per = block // rows
    for i in range(length // block):
        query = x_ref[i * per : (i + 1) * per, 0].reshape(block, lanes)
        parts = []
        for head in range(2):
            mine = jnp.where(first if head == 0 else ~first, query, jnp.zeros_like(query))
            scores = lax.dot_general(
                mine, keys, (((1,), (1,)), ((), ())), preferred_element_type=F32
            )
            top = jnp.max(scores, axis=1, keepdims=True)
            weights = jnp.exp2((scores - top) * scale).astype(BF16)
            both = jnp.dot(weights, wide, preferred_element_type=F32)
            parts.append(both[:, :lanes] / both[:, lanes:])
        context = jnp.where(first, parts[0], parts[1]).astype(BF16)
        out_ref[i * per : (i + 1) * per] = context.reshape(per, rows, lanes)


def attention(arrived):
    n_src, three, rows, width = arrived.shape
    return pl.pallas_call(
        functools.partial(attention_kernel, block=2 * rows),
        grid=(width // LANES,),
        in_specs=[pl.BlockSpec((n_src, three, rows, LANES), lambda i: (0, 0, 0, i))],
        out_specs=pl.BlockSpec((n_src, rows, LANES), lambda i: (0, 0, i)),
        out_shape=jax.ShapeDtypeStruct((n_src, rows, width), BF16),
        compiler_params=pltpu.CompilerParams(vmem_limit_bytes=24 * MIB),
        name="attention",
    )(arrived)


def places(info, n_exp, pieces):
    tokens = info.shape[1]
    ids = info[:TOP].astype(jnp.int32)
    expert = lax.broadcasted_iota(jnp.int32, (n_exp, tokens), 0)
    named = [expert == ids[k : k + 1] for k in range(TOP)]
    member = sum(n.astype(F32) for n in named)
    before = (
        lax.broadcasted_iota(jnp.int32, (tokens, tokens), 0)
        < lax.broadcasted_iota(jnp.int32, (tokens, tokens), 1)
    ).astype(F32)
    rank = jnp.dot(member.astype(BF16), before.astype(BF16), preferred_element_type=F32)
    rows = []
    for k, n in enumerate(named):
        slot = jnp.sum(jnp.where(n, rank, 0.0), axis=0, keepdims=True).astype(jnp.int32)
        row, start = None, 0
        for piece in pieces:
            here = start * n_exp + ids[k : k + 1] * piece + (slot - start)
            row = here if row is None else jnp.where(slot >= start, here, row)
            start += piece
        rows.append(row)
    return rows


def fill(normed, info, out_refs, n_exp, pieces):
    rows = places(info, n_exp, pieces)
    start = 0
    for ref, piece in zip(out_refs, pieces, strict=True):
        slots = n_exp * piece
        at = lax.broadcasted_iota(jnp.int32, (slots, normed.shape[0]), 0) + start
        pick = sum((at == r).astype(F32) for r in rows).astype(BF16)
        ref[...] = jnp.dot(pick, normed, preferred_element_type=F32).astype(BF16)
        start += slots


def project_kernel(ctx_ref, w_ref, stream_ref, info_ref, mid_ref, normed_ref, *out_refs, n_exp, pieces):
    n_src = ctx_ref.shape[0]
    merged = jnp.concatenate([ctx_ref[s] for s in range(n_src)], axis=1)
    step = pl.program_id(0)
    cols = w_ref.shape[1]
    here = pl.ds(pl.multiple_of(step * cols, cols), cols)
    mid_ref[:, here] = stream_ref[...].astype(F32) + jnp.dot(
        merged, w_ref[...], preferred_element_type=F32
    )

    @pl.when(step == pl.num_programs(0) - 1)
    def _():
        mid = mid_ref[...]
        factor = lax.rsqrt(jnp.mean(mid * mid, axis=1, keepdims=True) + 1e-06)
        normed = (mid * factor).astype(BF16)
        normed_ref[...] = normed
        fill(normed, info_ref[...], out_refs, n_exp, pieces)


def project(merged, w_out, stream, info, n_exp, pieces):
    n_src, rows, part = merged.shape
    width = w_out.shape[1]
    cols = 512
    slots = [n_exp * p for p in pieces]
    return pl.pallas_call(
        functools.partial(project_kernel, n_exp=n_exp, pieces=pieces),
        grid=(width // cols,),
        in_specs=[
            vmem((n_src, rows, part)),
            pl.BlockSpec((width, cols), lambda i: (0, i)),
            pl.BlockSpec((rows, cols), lambda i: (0, i)),
            vmem(info.shape),
        ],
        out_specs=[vmem((rows, width))] * 2 + [vmem((s, width)) for s in slots],
        out_shape=[
            jax.ShapeDtypeStruct((rows, width), F32),
            jax.ShapeDtypeStruct((rows, width), BF16),
        ]
        + [jax.ShapeDtypeStruct((s, width), BF16) for s in slots],
        compiler_params=pltpu.CompilerParams(vmem_limit_bytes=32 * MIB),
        name="project",
    )(merged, w_out, stream, info)


def route_kernel(normed_ref, info_ref, *out_refs, n_exp, pieces):
    fill(normed_ref[...], info_ref[...], out_refs, n_exp, pieces)


def route(normed, info, n_exp, pieces):
    rows, width = normed.shape
    slots = [n_exp * p for p in pieces]
    return pl.pallas_call(
        functools.partial(route_kernel, n_exp=n_exp, pieces=pieces),
        grid=(1,),
        in_specs=[vmem(normed.shape), vmem(info.shape)],
        out_specs=[vmem((s, width)) for s in slots],
        out_shape=[jax.ShapeDtypeStruct((s, width), BF16) for s in slots],
        compiler_params=pltpu.CompilerParams(vmem_limit_bytes=24 * MIB),
        name="route",
    )(normed, info)


def expert_kernel(*refs, n_in):
    x_refs, w_refs = refs[:n_in], refs[n_in : n_in + 6]
    out_refs, (rows_ref, total_ref) = refs[n_in + 6 : -2], refs[-2:]
    step, steps = pl.program_id(0), pl.num_programs(0)

    @pl.when(step == 0)
    def _():
        start = 0
        for ref in x_refs:
            rows_ref[start : start + ref.shape[0]] = ref[...]
            start += ref.shape[0]

    def part(gate_ref, up_ref, down_ref):
        rows = rows_ref[...]
        gate = jnp.dot(rows, gate_ref[...], preferred_element_type=F32)
        up = jnp.dot(rows, up_ref[...], preferred_element_type=F32)
        hidden = (gate / (1.0 + jnp.exp(-gate)) * up).astype(BF16)
        return jnp.dot(hidden, down_ref[...], preferred_element_type=F32)

    @pl.when(step == 0)
    def _():
        total_ref[...] = part(*w_refs[:3])

    @pl.when((step > 0) & (step < steps // 2))
    def _():
        total_ref[...] += part(*w_refs[:3])

    @pl.when((step >= steps // 2) & (step < steps - 1))
    def _():
        total_ref[...] += part(*w_refs[3:])

    @pl.when(step == steps - 1)
    def _():
        total = (total_ref[...] + part(*w_refs[3:])).astype(BF16)
        start = 0
        for ref in out_refs:
            ref[...] = total[start : start + ref.shape[0]]
            start += ref.shape[0]


def experts(arrays, mine, other):
    width = arrays[0].shape[1]
    hidden = mine[0].shape[1]
    block = 256
    half = hidden // block
    total = sum(x.shape[0] for x in arrays)

    def specs(at):
        return [
            pl.BlockSpec((width, block), lambda i: (0, at(i))),
            pl.BlockSpec((width, block), lambda i: (0, at(i))),
            pl.BlockSpec((block, width), lambda i: (at(i), 0)),
        ]

    return pl.pallas_call(
        functools.partial(expert_kernel, n_in=len(arrays)),
        grid=(2 * half,),
        in_specs=[vmem(x.shape) for x in arrays]
        + specs(lambda i: jnp.minimum(i, half - 1))
        + specs(lambda i: jnp.maximum(i - half, 0)),
        out_specs=[vmem(x.shape) for x in arrays],
        out_shape=[jax.ShapeDtypeStruct(x.shape, BF16) for x in arrays],
        scratch_shapes=[pltpu.VMEM((total, width), BF16), pltpu.VMEM((total, width), F32)],
        compiler_params=pltpu.CompilerParams(vmem_limit_bytes=48 * MIB),
        cost_estimate=pl.CostEstimate(
            flops=12 * total * width * hidden,
            bytes_accessed=12 * width * hidden + 4 * total * width,
            transcendentals=2 * total * hidden,
        ),
        name="experts",
    )(*arrays, *mine, *other)


def combine_kernel(info_ref, *refs, n_exp, pieces, with_mid):
    *back_refs, out_ref = refs
    info = info_ref[...]
    rows = places(info, n_exp, pieces)
    gates = info.T
    if with_mid:
        mid_ref, far_ref, *back_refs = back_refs
        total = mid_ref[...] + far_ref[...].astype(F32)
    else:
        total = None
    back = jnp.concatenate([r[...] for r in back_refs], axis=0)
    at = lax.broadcasted_iota(jnp.int32, (back.shape[0], rows[0].shape[1]), 0)
    for k, row in enumerate(rows):
        pick = (at == row).astype(F32).astype(BF16)
        term = lax.dot_general(pick, back, (((0,), (0,)), ((), ())), preferred_element_type=F32)
        term = term * gates[:, TOP + k : TOP + k + 1]
        total = term if total is None else total + term
    out_ref[...] = total.astype(BF16)


def combine(info, backs, n_exp, pieces, mid=None, far=None):
    rows, width = info.shape[1], backs[0].shape[1]
    cols = 512
    base = [] if mid is None else [mid, far]
    return pl.pallas_call(
        functools.partial(
            combine_kernel, n_exp=n_exp, pieces=pieces, with_mid=mid is not None
        ),
        grid=(width // cols,),
        in_specs=[vmem(info.shape)]
        + [pl.BlockSpec((x.shape[0], cols), lambda i: (0, i)) for x in (*base, *backs)],
        out_specs=pl.BlockSpec((rows, cols), lambda i: (0, i)),
        out_shape=jax.ShapeDtypeStruct((rows, width), BF16),
        compiler_params=pltpu.CompilerParams(vmem_limit_bytes=24 * MIB),
        name="combine",
    )(info, *base, *backs)


def spread_kernel(x_ref, out_ref):
    out_ref[0] = x_ref[...]


def spread(qkv, n_seq):
    three, rows, width = qkv.shape
    part = width // n_seq
    return pl.pallas_call(
        spread_kernel,
        grid=(n_seq,),
        in_specs=[pl.BlockSpec((three, rows, part), lambda i: (0, 0, i))],
        out_specs=pl.BlockSpec((1, three, rows, part), lambda i: (i, 0, 0, 0)),
        out_shape=jax.ShapeDtypeStruct((n_seq, three, rows, part), BF16),
        compiler_params=pltpu.CompilerParams(vmem_limit_bytes=16 * MIB),
        name="spread",
    )(qkv)


def per_device(stream_in, qkv_heads, expert_ids, gate_weights, w_out, w_gate, w_up, w_down):
    rows, width = stream_in.shape[1:]
    seq, exp = ("y", "core"), ("z", "x")
    n_y, n_seq, n_exp = lax.axis_size("y"), lax.axis_size(seq), lax.axis_size(exp)
    capacity = 3 * TOP * rows // (2 * n_exp)
    pieces = (capacity // 3, capacity - capacity // 3)
    whole = (capacity,)

    def swap(x):
        return lax.ppermute(x, "core", [(0, 1), (1, 0)])

    def shift(x, by):
        return lax.ppermute(x, "y", [(i, (i + by) % n_y) for i in range(n_y)])

    def exchange(x):
        return lax.all_to_all(x, exp, split_axis=0, concat_axis=0, tiled=True)

    mine = [w[0] for w in (w_gate, w_up, w_down)]
    other = [swap(w) for w in mine]
    info = jnp.concatenate(
        [expert_ids[0].T.astype(F32), gate_weights[0].T, jnp.zeros((8 - 2 * TOP, rows), F32)]
    )
    info_far = shift(info, 2)
    qkv = spread(qkv_heads[0].transpose(1, 0, 2), n_seq)
    arrived = lax.all_to_all(qkv, seq, split_axis=0, concat_axis=0, tiled=True)
    context = attention(arrived)
    context, info_far, other = lax.optimization_barrier((context, info_far, other))
    merged = lax.all_to_all(context, seq, split_axis=0, concat_axis=0, tiled=True)
    mid, normed, *buffers = project(merged, w_out, stream_in[0], info, n_exp, pieces)

    [buffer_far] = route(shift(normed, 2), info_far, n_exp, whole)
    own = [exchange(b) for b in buffers]
    far = exchange(buffer_far)
    up, down = [shift(x, 1) for x in own], [shift(x, -1) for x in own]

    own_part = experts(own, mine, other)
    near_part = [experts([u, d], mine, other) for u, d in zip(up, down)]
    [far_part] = experts([far], mine, other)

    far_sum = combine(info_far, [exchange(far_part)], n_exp, whole)
    far_home = shift(far_sum, 2)
    backs = []
    for a, (u, d) in zip(own_part, near_part):
        summed = a.astype(F32) + shift(u, -1).astype(F32) + shift(d, 1).astype(F32)
        backs.append(exchange(summed.astype(BF16)))
    return combine(info, backs, n_exp, pieces, mid, far_home)[None]


def solution(mesh):
    split = Mesh(mesh.devices.reshape(-1, 2, 4, 4), ("y", "core", "z", "x"))
    seq, exp = ("y", "core"), ("z", "x")
    in_specs = (
        P(exp, seq, None),
        P(exp, seq, None, None),
        P(exp, seq, None),
        P(exp, seq, None),
        P(),
        P(exp, None, seq),
        P(exp, None, seq),
        P(exp, seq, None),
    )
    return jax.shard_map(
        per_device, mesh=split, in_specs=in_specs, out_specs=P(exp, seq, None), check_vma=False
    )
```

time: 298 us -> 225 us (0.76)
  waiting for transfers between devices: 116 us -> 61.2 us
  blocking collectives: 83.9 us -> 30.8 us
  starting transfers between devices: 23.3 us -> 56.2 us
  between operations: 13.5 us -> 0.18 us
  Pallas kernels: 51.7 us -> 60.1 us
  other arithmetic: 0 us -> 4.18 us
  local copies, waits for them, and re-layouts: 7.82 us -> 11 us
    reduce_scatter x3 -> x0, waiting for transfers between devices: 67.6 us -> none  [per_device(): summed = lax.psum_scatter(shares, 'y', scatter_dimension=0, tiled=True)]
    all_to_all x4 -> x1, blocking collectives: 71.1 us -> 18 us  [exchange(): return lax.all_to_all(x, exp, split_axis=0, concat_axis=0, tiled=True)]
    all_gather x3 -> x0, waiting for transfers between devices: 28.1 us -> none  [per_device(): gathered = lax.all_gather(sent, 'y', tiled=True)]
    ppermute x3 -> x14, waiting for transfers between devices: 9.89 us -> 30.6 us  [the longest x11 30.6 us: shift(): return lax.ppermute(x, 'y', [(i, (i + by) % n_y) for i in range(n_y)])]
    all_to_all x3 -> x6, waiting for transfers between devices: 10.1 us -> 30.6 us  [the longest x1 17.9 us: per_device(): arrived = lax.all_to_all(qkv, seq, split_axis=0, concat_axis=0, tiled=True)]
    ppermute x3 -> x14, starting transfers between devices: 0.68 us -> 18.2 us  [the longest x11 17.7 us: shift(): return lax.ppermute(x, 'y', [(i, (i + by) % n_y) for i in range(n_y)])]
    all_to_all x3 -> x6, starting transfers between devices: 22.2 us -> 38 us  [the longest x5 33.3 us: exchange(): return lax.all_to_all(x, exp, split_axis=0, concat_axis=0, tiled=True)]
    pallas_call x5 -> x9, Pallas kernels: 45.7 us -> 54.1 us  [the longest x4 39.4 us: experts(): pl.pallas_call(functools.partial(expert_kernel, n_in=len(arrays)), grid=(...]
  transfers between devices with their start and end apart: 12 -> 20, of which waited for: 9 -> 5; matrix products, arithmetic and copies ran while one was open for 0% -> 2% of each run, Pallas kernels for 13% -> 24%
where the time goes in v2:
time: 225 us; the launch traced here: 224 us
  waiting for transfers between devices  61.2 us (27%)
  Pallas kernels  60.1 us (27%)
  starting transfers between devices  56.2 us (25%)
  blocking collectives  30.8 us (14%)
  local copies, waits for them, and re-layouts  11 us (5%)
  other arithmetic  4.18 us (2%)
    pallas_call x4, Pallas kernels, experts(): pl.pallas_call(functools.partial(expert_kernel, n_in=len(arrays)), grid=(...  39.4 us
    all_to_all x5, starting transfers between devices, exchange(): return lax.all_to_all(x, exp, split_axis=0, concat_axis=0, tiled=True)  33.3 us
    ppermute x11, waiting for transfers between devices, shift(): return lax.ppermute(x, 'y', [(i, (i + by) % n_y) for i in range(n_y)])  30.6 us
    all_to_all x1, blocking collectives, exchange(): return lax.all_to_all(x, exp, split_axis=0, concat_axis=0, tiled=True)  18 us
    all_to_all x1, waiting for transfers between devices, per_device(): arrived = lax.all_to_all(qkv, seq, split_axis=0, concat_axis=0, tiled=True)  17.9 us
    ppermute x11, starting transfers between devices, shift(): return lax.ppermute(x, 'y', [(i, (i + by) % n_y) for i in range(n_y)])  17.7 us
    all_to_all x1, blocking collectives, per_device(): lax.all_to_all(context, seq, split_axis=0, concat_axis=0, tiled=True)  12.8 us
    all_to_all x5, waiting for transfers between devices, exchange(): return lax.all_to_all(x, exp, split_axis=0, concat_axis=0, tiled=True)  12.7 us
  transfers between devices with their start and end apart: 20, of which 5 were waited for; matrix products, arithmetic and copies ran while one was open for 2% of the time, Pallas kernels for 24%

profile of v2, /device:TPU:2, one launch (start us, length us, event | category | flops | bytes accessed | tf_op | source)
XLA Modules:
  0.0 223.7 jit_solution(5610881188997834203)
XLA Ops:
  0.0 0.0 collective-permute-start.1
  0.0 0.5 collective-permute-start.2
  0.5 0.0 collective-permute-start.3
  0.5 1.4 copy-done.3
  1.9 3.0 %spread.1 = bf16[8,3,128,256]{3,2,1,0:T(8,128)(2,1)} custom-call(bf16[3,128,2048]{2,1,0:T(8,128)(2,1)S(1)} %bitcast.36), custom_call_target="tpu_custom_call" | custom-call | tf_op jit(solution)/shard_map/spread/pallas_call | solution.py:277
  5.0 4.7 %all-to-all-start = ((bf16[8,3,128,256]{3,2,1,0:T(8,128)(2,1)}), bf16[8,3,128,256]{3,2,1,0:T(8,128)(2,1)S(1)}, u32[]{:S(2)}, u32[]{:S(2)}) async-start(bf16[8,3,128,256]{3,2,1,0:T(8,128)(2,1)} %spread.1), calls=%async_computation | async-start | bytes 3145728 | tf_op jit(solution)/shard_map/all_to_all | solution.py:312
  9.7 0.1 pad.2.clone
  9.8 0.1 maximum_maximum_fusion.info_ref
  9.8 3.5 %collective-permute-start = (f32[8,128]{1,0:T(8,128)S(1)}, f32[8,128]{1,0:T(8,128)S(1)}, u32[]{:S(2)}, u32[]{:S(2)}) collective-permute-start(f32[8,128]{1,0:T(8,128)S(1)} %maximum_maximum_fusion.info_ref), channel_id=1, source_target_pairs={{0,64},{32,96},{64,0},{96,32},{1,65},{33,97},{65,1},{97,33},{2,66}... | collective-permute-start | bytes 12296 | tf_op jit(solution)/shard_map/ppermute | solution.py:300
  13.4 17.9 %all-to-all-done.x_ref = bf16[8,3,128,256]{3,2,1,0:T(8,128)(2,1)S(1)} async-done(((bf16[8,3,128,256]{3,2,1,0:T(8,128)(2,1)}), bf16[8,3,128,256]{3,2,1,0:T(8,128)(2,1)S(1)}, u32[]{:S(2)}, u32[]{:S(2)}) %all-to-all-start) | async-done | bytes 1572896 | tf_op jit(solution)/shard_map/all_to_all | solution.py:312
  31.3 6.0 %attention.1 = bf16[8,128,256]{2,1,0:T(8,128)(2,1)S(1)} custom-call(bf16[8,3,128,256]{3,2,1,0:T(8,128)(2,1)S(1)} %all-to-all-done.x_ref), custom_call_target="tpu_custom_call" | custom-call | tf_op jit(solution)/shard_map/attention/pallas_call | solution.py:52
  37.3 0.0 collective-permute-done.info_ref
  37.3 0.0 collective-permute-done.1.refs_4_.refs_5_
  37.4 0.0 collective-permute-done.2.refs_5_.refs_6_
  37.4 0.0 collective-permute-done.3.refs_6_.refs_7_
  37.4 12.8 %all_to_all.76.ctx_ref = bf16[8,128,256]{2,1,0:T(8,128)(2,1)S(1)} all-to-all(bf16[8,128,256]{2,1,0:T(8,128)(2,1)S(1)} %attention.1), channel_id=1, replica_groups=mesh['y'=4,'core'=2,'z'=4,'x'=4] {'y','core'}, dimensions={0} | all-to-all | bytes 1048576 | tf_op jit(solution)/shard_map/all_to_all | solution.py:315
  50.2 3.4 %copy-done = bf16[2048,2048]{1,0:T(8,128)(2,1)S(1)} copy-done((bf16[2048,2048]{1,0:T(8,128)(2,1)S(1)}, bf16[2048,2048]{1,0:T(8,128)(2,1)}, u32[]{:S(2)}) %copy-start) | copy-done | bytes 8388632
  53.6 4.3 %project.1 = (f32[128,2048]{1,0:T(8,128)S(1)}, bf16[128,2048]{1,0:T(8,128)(2,1)S(1)}, bf16[128,2048]{1,0:T(8,128)(2,1)S(1)}, bf16[256,2048]{1,0:T(8,128)(2,1)}) custom-call(bf16[8,128,256]{2,1,0:T(8,128)(2,1)S(1)} %all_to_all.76.ctx_ref, bf16[2048,2048]{1,0:T(8,128)(2,1)S(1)} %copy-done, bf16[128,2048]{1,0:T(8,128)(2,1)S(1)} %bitcast.41, ...), custom_call_target="tpu_custom_call" | custom-call | tf_op jit(solution)/shard_map/project/pallas_call | solution.py:121
  57.9 1.0 copy-done.5
  58.9 18.0 %all_to_all.77 = bf16[16,8,2048]{2,1,0:T(8,128)(2,1)} all-to-all(bf16[16,8,2048]{2,1,0:T(8,128)(2,1)S(1)} %bitcast.42), channel_id=1, replica_groups=mesh['y'=4,'core'=2,'z'=4,'x'=4] {'z','x'}, dimensions={0} | all-to-all | bytes 1048576 | tf_op jit(solution)/shard_map/all_to_all | solution.py:303
  76.9 4.9 %all-to-all-start.5 = ((bf16[16,16,2048]{2,1,0:T(8,128)(2,1)}), bf16[16,16,2048]{2,1,0:T(8,128)(2,1)S(1)}, u32[]{:S(2)}, u32[]{:S(2)}) async-start(bf16[16,16,2048]{2,1,0:T(8,128)(2,1)} %bitcast.16), calls=%async_computation.5 | async-start | bytes 2097152 | tf_op jit(solution)/shard_map/all_to_all | solution.py:303
  81.8 0.8 collective-permute-start.4
  82.6 1.2 collective-permute-start.6
  83.8 2.0 collective-permute-start.7
  85.8 12.4 %collective-permute-done.4.normed_ref = bf16[128,2048]{1,0:T(8,128)(2,1)S(1)} collective-permute-done((bf16[128,2048]{1,0:T(8,128)(2,1)S(1)}, bf16[128,2048]{1,0:T(8,128)(2,1)S(1)}, u32[]{:S(2)}, u32[]{:S(2)}) %collective-permute-start.4) | collective-permute-done | bytes 524320 | tf_op jit(solution)/shard_map/ppermute | solution.py:300
  98.2 1.9 route.1
  100.1 0.0 all-to-all-done.5
  100.1 7.4 %all-to-all-start.2 = ((bf16[16,24,2048]{2,1,0:T(8,128)(2,1)}), bf16[16,24,2048]{2,1,0:T(8,128)(2,1)}, u32[]{:S(2)}, u32[]{:S(2)}) async-start(bf16[16,24,2048]{2,1,0:T(8,128)(2,1)} %bitcast.10), calls=%async_computation.2 | async-start | bytes 3145728 | tf_op jit(solution)/shard_map/all_to_all | solution.py:303
  107.5 0.6 collective-permute-start.10
  108.1 2.7 %collective-permute-start.11 = (bf16[256,2048]{1,0:T(8,128)(2,1)S(1)}, bf16[256,2048]{1,0:T(8,128)(2,1)}, u32[]{:S(2)}, u32[]{:S(2)}) collective-permute-start(bf16[256,2048]{1,0:T(8,128)(2,1)S(1)} %bitcast.39), channel_id=1, source_target_pairs={{0,96},{32,0},{64,32},{96,64},{1,97},{33,1},{65,33},{97,65},{2,98}... | collective-permute-start | bytes 3145736 | tf_op jit(solution)/shard_map/ppermute | solution.py:300
  110.7 0.0 collective-permute-done.6.refs_0_
  110.7 0.0 collective-permute-done.7.refs_1_
  110.7 8.2 %experts.6 = (bf16[128,2048]{1,0:T(8,128)(2,1)S(1)}, bf16[128,2048]{1,0:T(8,128)(2,1)S(1)}) custom-call(bf16[128,2048]{1,0:T(8,128)(2,1)} %collective-permute-done.6.refs_0_, bf16[128,2048]{1,0:T(8,128)(2,1)} %collective-permute-done.7.refs_1_, bf16[2048,512]{1,0:T(8,128)(2,1)S(1)} %bitcast.33, bf16[2048,512]{1,0:T(8,128)(2,1)} %bitcast.45, ...), custom_call_target="tpu_custom_call" | custom-call | flops 3221225472 | bytes 14680064 | tf_op jit(solution)/shard_map/experts/pallas_call | solution.py:213
  118.9 0.1 collective-permute-start.9
  119.0 3.2 %collective-permute-start.8 = (bf16[128,2048]{1,0:T(8,128)(2,1)S(1)}, bf16[128,2048]{1,0:T(8,128)(2,1)S(1)}, u32[]{:S(2)}, u32[]{:S(2)}) collective-permute-start(bf16[128,2048]{1,0:T(8,128)(2,1)S(1)} %get-tuple-element.30), channel_id=1, source_target_pairs={{0,96},{32,0},{64,32},{96,64},{1,97},{33,1},{65,33},{97,65},{2,98}... | collective-permute-start | bytes 1572872 | tf_op jit(solution)/shard_map/ppermute | solution.py:300
  122.2 9.1 %experts.5 = (bf16[128,2048]{1,0:T(8,128)(2,1)S(1)}, bf16[256,2048]{1,0:T(8,128)(2,1)S(1)}) custom-call(bf16[128,2048]{1,0:T(8,128)(2,1)} %bitcast.15.refs_0_, bf16[256,2048]{1,0:T(8,128)(2,1)S(1)} %bitcast.40, bf16[2048,512]{1,0:T(8,128)(2,1)S(1)} %bitcast.34, bf16[2048,512]{1,0:T(8,128)(2,1)} %bitcast.46, bf16[512,2048]{1,0:T(8,128)(2,1)} %bitcast.51, ...), custom_call_target="tpu_custom_call" | custom-call | flops 4831838208 | bytes 15728640 | tf_op jit(solution)/shard_map/experts/pallas_call | solution.py:213
  131.3 0.9 copy-done.7
  132.3 7.8 %collective-permute-done.9 = bf16[128,2048]{1,0:T(8,128)(2,1)S(1)} collective-permute-done((bf16[128,2048]{1,0:T(8,128)(2,1)S(1)}, bf16[128,2048]{1,0:T(8,128)(2,1)S(1)}, u32[]{:S(2)}, u32[]{:S(2)}) %collective-permute-start.9) | collective-permute-done | bytes 524320 | tf_op jit(solution)/shard_map/ppermute | solution.py:300
  140.1 0.0 collective-permute-done.8
  140.1 1.0 fusion
  141.2 0.0 all-to-all-done.2
  141.2 7.3 %all-to-all-start.6 = ((bf16[16,8,2048]{2,1,0:T(8,128)(2,1)}), bf16[16,8,2048]{2,1,0:T(8,128)(2,1)S(1)}, u32[]{:S(2)}, u32[]{:S(2)}) async-start(bf16[16,8,2048]{2,1,0:T(8,128)(2,1)} %fusion), calls=%async_computation.6 | async-start | bytes 1048576 | tf_op jit(solution)/shard_map/all_to_all | solution.py:303
  148.5 0.0 collective-permute-done.10.refs_0_
  148.5 0.0 collective-permute-done.11.refs_1_
  148.5 12.7 %experts.7 = (bf16[256,2048]{1,0:T(8,128)(2,1)}, bf16[256,2048]{1,0:T(8,128)(2,1)}) custom-call(bf16[256,2048]{1,0:T(8,128)(2,1)} %collective-permute-done.10.refs_0_, bf16[256,2048]{1,0:T(8,128)(2,1)} %collective-permute-done.11.refs_1_, bf16[2048,512]{1,0:T(8,128)(2,1)} %bitcast.32, bf16[2048,512]{1,0:T(8,128)(2,1)} %bitcast.47, ...), custom_call_target="tpu_custom_call" | custom-call | flops 6442450944 | bytes 16777216 | tf_op jit(solution)/shard_map/experts/pallas_call | solution.py:213
  161.2 0.6 collective-permute-start.13
  161.7 2.7 %collective-permute-start.12 = (bf16[256,2048]{1,0:T(8,128)(2,1)}, bf16[256,2048]{1,0:T(8,128)(2,1)}, u32[]{:S(2)}, u32[]{:S(2)}) collective-permute-start(bf16[256,2048]{1,0:T(8,128)(2,1)} %get-tuple-element.33), channel_id=1, source_target_pairs={{0,96},{32,0},{64,32},{96,64},{1,97},{33,1},{65,33},{97,65},{2,98}... | collective-permute-start | bytes 3145736 | tf_op jit(solution)/shard_map/ppermute | solution.py:300
  164.4 9.5 %experts.4 = bf16[384,2048]{1,0:T(8,128)(2,1)S(1)} custom-call(bf16[384,2048]{1,0:T(8,128)(2,1)} %bitcast.11.refs_0_, bf16[2048,512]{1,0:T(8,128)(2,1)S(1)} %bitcast.35, bf16[2048,512]{1,0:T(8,128)(2,1)} %bitcast.48, bf16[512,2048]{1,0:T(8,128)(2,1)} %bitcast.53, bf16[2048,512]{1,0:T(8,128)(2,1)} %collective-permute-done.1.refs_4_.refs_5_, ...), custom_call_target="tpu_custom_call" | custom-call | flops 4831838208 | bytes 15728640 | tf_op jit(solution)/shard_map/experts/pallas_call | solution.py:213
  173.9 1.1 copy-done.4
  175.1 0.0 all-to-all-done.6
  175.1 7.4 %all-to-all-start.3 = ((bf16[16,24,2048]{2,1,0:T(8,128)(2,1)}), bf16[16,24,2048]{2,1,0:T(8,128)(2,1)S(1)}, u32[]{:S(2)}, u32[]{:S(2)}) async-start(bf16[16,24,2048]{2,1,0:T(8,128)(2,1)} %bitcast.37), calls=%async_computation.3 | async-start | bytes 3145728 | tf_op jit(solution)/shard_map/all_to_all | solution.py:303
  182.4 0.0 collective-permute-done.13
  182.4 0.0 collective-permute-done.12
  182.4 3.1 %add_convert_fusion = bf16[256,2048]{1,0:T(8,128)(2,1)} fusion(bf16[256,2048]{1,0:T(8,128)(2,1)} %collective-permute-done.13, bf16[256,2048]{1,0:T(8,128)(2,1)} %collective-permute-done.12, bf16[256,2048]{1,0:T(8,128)(2,1)S(1)} %copy-done.8), kind=kLoop, calls=%fused_computation | loop fusion | flops 3145728 | bytes 4194304 | tf_op jit(solution)/shard_map/convert_element_type | solution.py:332
  185.5 12.7 %all-to-all-done.3 = bf16[16,24,2048]{2,1,0:T(8,128)(2,1)S(1)} async-done(((bf16[16,24,2048]{2,1,0:T(8,128)(2,1)}), bf16[16,24,2048]{2,1,0:T(8,128)(2,1)S(1)}, u32[]{:S(2)}, u32[]{:S(2)}) %all-to-all-start.3) | async-done | bytes 1572896 | tf_op jit(solution)/shard_map/all_to_all | solution.py:303
  198.2 6.3 %all-to-all-start.7 = ((bf16[16,16,2048]{2,1,0:T(8,128)(2,1)}), bf16[16,16,2048]{2,1,0:T(8,128)(2,1)S(1)}, u32[]{:S(2)}, u32[]{:S(2)}) async-start(bf16[16,16,2048]{2,1,0:T(8,128)(2,1)} %bitcast.43), calls=%async_computation.7 | async-start | bytes 2097152 | tf_op jit(solution)/shard_map/all_to_all | solution.py:303
  204.5 2.3 %combine.2 = bf16[128,2048]{1,0:T(8,128)(2,1)S(1)} custom-call(f32[8,128]{1,0:T(8,128)S(1)} %collective-permute-done.info_ref, bf16[384,2048]{1,0:T(8,128)(2,1)S(1)} %bitcast.28), custom_call_target="tpu_custom_call" | custom-call | tf_op jit(solution)/shard_map/combine/pallas_call | solution.py:256
  206.8 0.4 collective-permute-start.5
  207.2 10.4 %collective-permute-done.5.refs_1_ = bf16[128,2048]{1,0:T(8,128)(2,1)S(1)} collective-permute-done((bf16[128,2048]{1,0:T(8,128)(2,1)S(1)}, bf16[128,2048]{1,0:T(8,128)(2,1)S(1)}, u32[]{:S(2)}, u32[]{:S(2)}) %collective-permute-start.5) | collective-permute-done | bytes 524320 | tf_op jit(solution)/shard_map/ppermute | solution.py:300
  217.6 0.8 copy-done.10
  218.4 0.0 all-to-all-done.7
  218.4 1.2 copy-done.6
  219.6 1.0 copy-done.11
  220.6 3.1 %combine.3 = bf16[128,2048]{1,0:T(8,128)(2,1)} custom-call(f32[8,128]{1,0:T(8,128)S(1)} %maximum_maximum_fusion.info_ref, f32[128,2048]{1,0:T(8,128)S(1)} %copy-done.6, bf16[128,2048]{1,0:T(8,128)(2,1)S(1)} %copy-done.11, bf16[128,2048]{1,0:T(8,128)(2,1)S(1)} %bitcast.30, bf16[256,2048]{1,0:T(8,128)(2,1)S(1)} %bitcast.29), custom_call_target="tpu_custom_call" | custom-call | tf_op jit(solution)/shard_map/combine/pallas_call | solution.py:256
  (22 shorter events, 0.0 us)
Async XLA Ops:
  0.0 37.3 %collective-permute-start.1 = (bf16[2048,512]{1,0:T(8,128)(2,1)}, bf16[2048,512]{1,0:T(8,128)(2,1)}, u32[]{:S(2)}, u32[]{:S(2)}) collective-permute-start(bf16[2048,512]{1,0:T(8,128)(2,1)} %bitcast.31), channel_id=1, source_target_pairs={{0,16},{16,0},{1,17},{17,1},{2,18},{18,2},{3,19},{19,3},{4,20},{20... | collective-permute-start | bytes 6291464 | tf_op jit(solution)/shard_map/ppermute | solution.py:297
  0.0 37.4 %collective-permute-start.2 = (bf16[2048,512]{1,0:T(8,128)(2,1)}, bf16[2048,512]{1,0:T(8,128)(2,1)}, u32[]{:S(2)}, u32[]{:S(2)}) collective-permute-start(bf16[2048,512]{1,0:T(8,128)(2,1)} %bitcast.44), channel_id=1, source_target_pairs={{0,16},{16,0},{1,17},{17,1},{2,18},{18,2},{3,19},{19,3},{4,20},{20... | collective-permute-start | bytes 6291464 | tf_op jit(solution)/shard_map/ppermute | solution.py:297
  0.5 36.9 %collective-permute-start.3 = (bf16[512,2048]{1,0:T(8,128)(2,1)}, bf16[512,2048]{1,0:T(8,128)(2,1)}, u32[]{:S(2)}, u32[]{:S(2)}) collective-permute-start(bf16[512,2048]{1,0:T(8,128)(2,1)} %bitcast.49), channel_id=1, source_target_pairs={{0,16},{16,0},{1,17},{17,1},{2,18},{18,2},{3,19},{19,3},{4,20},{20... | collective-permute-start | bytes 6291464 | tf_op jit(solution)/shard_map/ppermute | solution.py:297
  0.5 1.4 copy-start.3
  4.9 4.8 %copy-start.12 = (s32[1,128,2]{1,2,0:T(2,128)S(1)}, s32[1,128,2]{1,2,0:T(2,128)}, u32[]{:S(2)}) copy-start(s32[1,128,2]{1,2,0:T(2,128)} %param.10) | copy-start | bytes 3076
  5.0 4.8 %copy-start.13 = (f32[1,128,2]{1,2,0:T(2,128)S(1)}, f32[1,128,2]{1,2,0:T(2,128)}, u32[]{:S(2)}) copy-start(f32[1,128,2]{1,2,0:T(2,128)} %param.11) | copy-start | bytes 3076
  5.0 26.3 %all-to-all-start = ((bf16[8,3,128,256]{3,2,1,0:T(8,128)(2,1)}), bf16[8,3,128,256]{3,2,1,0:T(8,128)(2,1)S(1)}, u32[]{:S(2)}, u32[]{:S(2)}) async-start(bf16[8,3,128,256]{3,2,1,0:T(8,128)(2,1)} %spread.1), calls=%async_computation | async-start | bytes 3145728 | tf_op jit(solution)/shard_map/all_to_all | solution.py:312
  9.7 40.5 %copy-start.9 = (bf16[1,128,2048]{2,1,0:T(8,128)(2,1)S(1)}, bf16[1,128,2048]{2,1,0:T(8,128)(2,1)}, u32[]{:S(2)}) copy-start(bf16[1,128,2048]{2,1,0:T(8,128)(2,1)} %param.8) | copy-start | bytes 1572868
  9.8 27.5 %collective-permute-start = (f32[8,128]{1,0:T(8,128)S(1)}, f32[8,128]{1,0:T(8,128)S(1)}, u32[]{:S(2)}, u32[]{:S(2)}) collective-permute-start(f32[8,128]{1,0:T(8,128)S(1)} %maximum_maximum_fusion.info_ref), channel_id=1, source_target_pairs={{0,64},{32,96},{64,0},{96,32},{1,65},{33,97},{65,1},{97,33},{2,66}... | collective-permute-start | bytes 12296 | tf_op jit(solution)/shard_map/ppermute | solution.py:300
  50.2 3.4 %copy-start = (bf16[2048,2048]{1,0:T(8,128)(2,1)S(1)}, bf16[2048,2048]{1,0:T(8,128)(2,1)}, u32[]{:S(2)}) copy-start(bf16[2048,2048]{1,0:T(8,128)(2,1)} %w_ref.1) | copy-start | bytes 25165828
  57.9 1.0 copy-start.5
  76.9 23.2 %all-to-all-start.5 = ((bf16[16,16,2048]{2,1,0:T(8,128)(2,1)}), bf16[16,16,2048]{2,1,0:T(8,128)(2,1)S(1)}, u32[]{:S(2)}, u32[]{:S(2)}) async-start(bf16[16,16,2048]{2,1,0:T(8,128)(2,1)} %bitcast.16), calls=%async_computation.5 | async-start | bytes 2097152 | tf_op jit(solution)/shard_map/all_to_all | solution.py:303
  81.8 16.4 %collective-permute-start.4 = (bf16[128,2048]{1,0:T(8,128)(2,1)S(1)}, bf16[128,2048]{1,0:T(8,128)(2,1)S(1)}, u32[]{:S(2)}, u32[]{:S(2)}) collective-permute-start(bf16[128,2048]{1,0:T(8,128)(2,1)S(1)} %get-tuple-element.23), channel_id=1, source_target_pairs={{0,64},{32,96},{64,0},{96,32},{1,65},{33,97},{65,1},{97,33},{2,66}... | collective-permute-start | bytes 1572872 | tf_op jit(solution)/shard_map/ppermute | solution.py:300
  82.6 28.1 %collective-permute-start.6 = (bf16[128,2048]{1,0:T(8,128)(2,1)}, bf16[128,2048]{1,0:T(8,128)(2,1)}, u32[]{:S(2)}, u32[]{:S(2)}) collective-permute-start(bf16[128,2048]{1,0:T(8,128)(2,1)} %bitcast.15.refs_0_), channel_id=1, source_target_pairs={{0,32},{32,64},{64,96},{96,0},{1,33},{33,65},{65,97},{97,1},{2,34}... | collective-permute-start | bytes 1572872 | tf_op jit(solution)/shard_map/ppermute | solution.py:300
  83.8 26.9 %collective-permute-start.7 = (bf16[128,2048]{1,0:T(8,128)(2,1)}, bf16[128,2048]{1,0:T(8,128)(2,1)}, u32[]{:S(2)}, u32[]{:S(2)}) collective-permute-start(bf16[128,2048]{1,0:T(8,128)(2,1)} %bitcast.15.refs_0_), channel_id=1, source_target_pairs={{0,96},{32,0},{64,32},{96,64},{1,97},{33,1},{65,33},{97,65},{2,98}... | collective-permute-start | bytes 1572872 | tf_op jit(solution)/shard_map/ppermute | solution.py:300
  100.1 10.7 %copy-start.1 = (bf16[1,2048,512]{2,1,0:T(8,128)(2,1)S(1)}, bf16[1,2048,512]{2,1,0:T(8,128)(2,1)}, u32[]{:S(2)}) copy-start(bf16[1,2048,512]{2,1,0:T(8,128)(2,1)} %param.13) | copy-start | bytes 6291460
  100.1 41.1 %all-to-all-start.2 = ((bf16[16,24,2048]{2,1,0:T(8,128)(2,1)}), bf16[16,24,2048]{2,1,0:T(8,128)(2,1)}, u32[]{:S(2)}, u32[]{:S(2)}) async-start(bf16[16,24,2048]{2,1,0:T(8,128)(2,1)} %bitcast.10), calls=%async_computation.2 | async-start | bytes 3145728 | tf_op jit(solution)/shard_map/all_to_all | solution.py:303
  107.5 41.0 %collective-permute-start.10 = (bf16[256,2048]{1,0:T(8,128)(2,1)S(1)}, bf16[256,2048]{1,0:T(8,128)(2,1)}, u32[]{:S(2)}, u32[]{:S(2)}) collective-permute-start(bf16[256,2048]{1,0:T(8,128)(2,1)S(1)} %bitcast.38), channel_id=1, source_target_pairs={{0,32},{32,64},{64,96},{96,0},{1,33},{33,65},{65,97},{97,1},{2,34}... | collective-permute-start | bytes 3145736 | tf_op jit(solution)/shard_map/ppermute | solution.py:300
  108.1 40.4 %collective-permute-start.11 = (bf16[256,2048]{1,0:T(8,128)(2,1)S(1)}, bf16[256,2048]{1,0:T(8,128)(2,1)}, u32[]{:S(2)}, u32[]{:S(2)}) collective-permute-start(bf16[256,2048]{1,0:T(8,128)(2,1)S(1)} %bitcast.39), channel_id=1, source_target_pairs={{0,96},{32,0},{64,32},{96,64},{1,97},{33,1},{65,33},{97,65},{2,98}... | collective-permute-start | bytes 3145736 | tf_op jit(solution)/shard_map/ppermute | solution.py:300
  118.9 21.2 %collective-permute-start.9 = (bf16[128,2048]{1,0:T(8,128)(2,1)S(1)}, bf16[128,2048]{1,0:T(8,128)(2,1)S(1)}, u32[]{:S(2)}, u32[]{:S(2)}) collective-permute-start(bf16[128,2048]{1,0:T(8,128)(2,1)S(1)} %get-tuple-element.31), channel_id=1, source_target_pairs={{0,32},{32,64},{64,96},{96,0},{1,33},{33,65},{65,97},{97,1},{2,34}... | collective-permute-start | bytes 1572872 | tf_op jit(solution)/shard_map/ppermute | solution.py:300
  119.0 21.1 %collective-permute-start.8 = (bf16[128,2048]{1,0:T(8,128)(2,1)S(1)}, bf16[128,2048]{1,0:T(8,128)(2,1)S(1)}, u32[]{:S(2)}, u32[]{:S(2)}) collective-permute-start(bf16[128,2048]{1,0:T(8,128)(2,1)S(1)} %get-tuple-element.30), channel_id=1, source_target_pairs={{0,96},{32,0},{64,32},{96,64},{1,97},{33,1},{65,33},{97,65},{2,98}... | collective-permute-start | bytes 1572872 | tf_op jit(solution)/shard_map/ppermute | solution.py:300
  131.3 1.0 copy-start.7
  141.2 33.9 %all-to-all-start.6 = ((bf16[16,8,2048]{2,1,0:T(8,128)(2,1)}), bf16[16,8,2048]{2,1,0:T(8,128)(2,1)S(1)}, u32[]{:S(2)}, u32[]{:S(2)}) async-start(bf16[16,8,2048]{2,1,0:T(8,128)(2,1)} %fusion), calls=%async_computation.6 | async-start | bytes 1048576 | tf_op jit(solution)/shard_map/all_to_all | solution.py:303
  148.5 16.0 %copy-start.2 = (bf16[1,2048,512]{2,1,0:T(8,128)(2,1)S(1)}, bf16[1,2048,512]{2,1,0:T(8,128)(2,1)}, u32[]{:S(2)}) copy-start(bf16[1,2048,512]{2,1,0:T(8,128)(2,1)} %param.13) | copy-start | bytes 6291460
  161.2 21.3 %collective-permute-start.13 = (bf16[256,2048]{1,0:T(8,128)(2,1)}, bf16[256,2048]{1,0:T(8,128)(2,1)}, u32[]{:S(2)}, u32[]{:S(2)}) collective-permute-start(bf16[256,2048]{1,0:T(8,128)(2,1)} %get-tuple-element.34), channel_id=1, source_target_pairs={{0,32},{32,64},{64,96},{96,0},{1,33},{33,65},{65,97},{97,1},{2,34}... | collective-permute-start | bytes 3145736 | tf_op jit(solution)/shard_map/ppermute | solution.py:300
  161.7 20.7 %collective-permute-start.12 = (bf16[256,2048]{1,0:T(8,128)(2,1)}, bf16[256,2048]{1,0:T(8,128)(2,1)}, u32[]{:S(2)}, u32[]{:S(2)}) collective-permute-start(bf16[256,2048]{1,0:T(8,128)(2,1)} %get-tuple-element.33), channel_id=1, source_target_pairs={{0,96},{32,0},{64,32},{96,64},{1,97},{33,1},{65,33},{97,65},{2,98}... | collective-permute-start | bytes 3145736 | tf_op jit(solution)/shard_map/ppermute | solution.py:300
  173.9 1.2 copy-start.4
  175.1 7.4 %copy-start.8 = (bf16[256,2048]{1,0:T(8,128)(2,1)S(1)}, bf16[256,2048]{1,0:T(8,128)(2,1)}, u32[]{:S(2)}) copy-start(bf16[256,2048]{1,0:T(8,128)(2,1)} %copy-done.7) | copy-start | bytes 3145732
  175.1 23.1 %all-to-all-start.3 = ((bf16[16,24,2048]{2,1,0:T(8,128)(2,1)}), bf16[16,24,2048]{2,1,0:T(8,128)(2,1)S(1)}, u32[]{:S(2)}, u32[]{:S(2)}) async-start(bf16[16,24,2048]{2,1,0:T(8,128)(2,1)} %bitcast.37), calls=%async_computation.3 | async-start | bytes 3145728 | tf_op jit(solution)/shard_map/all_to_all | solution.py:303
  198.2 20.2 %all-to-all-start.7 = ((bf16[16,16,2048]{2,1,0:T(8,128)(2,1)}), bf16[16,16,2048]{2,1,0:T(8,128)(2,1)S(1)}, u32[]{:S(2)}, u32[]{:S(2)}) async-start(bf16[16,16,2048]{2,1,0:T(8,128)(2,1)} %bitcast.43), calls=%async_computation.7 | async-start | bytes 2097152 | tf_op jit(solution)/shard_map/all_to_all | solution.py:303
  206.8 10.8 %collective-permute-start.5 = (bf16[128,2048]{1,0:T(8,128)(2,1)S(1)}, bf16[128,2048]{1,0:T(8,128)(2,1)S(1)}, u32[]{:S(2)}, u32[]{:S(2)}) collective-permute-start(bf16[128,2048]{1,0:T(8,128)(2,1)S(1)} %combine.2), channel_id=1, source_target_pairs={{0,64},{32,96},{64,0},{96,32},{1,65},{33,97},{65,1},{97,33},{2,66}... | collective-permute-start | bytes 1572872 | tf_op jit(solution)/shard_map/ppermute | solution.py:300
  217.6 0.8 copy-start.10
  218.4 1.2 copy-start.6
  219.6 1.0 copy-start.11

commit v3 on v2

--- a/solution.py
+++ b/solution.py
@@ -94,48 +94,59 @@
         start += slots
 
 
-def project_kernel(ctx_ref, w_ref, stream_ref, info_ref, mid_ref, normed_ref, *out_refs, n_exp, pieces):
-    n_src = ctx_ref.shape[0]
-    merged = jnp.concatenate([ctx_ref[s] for s in range(n_src)], axis=1)
-    step = pl.program_id(0)
-    cols = w_ref.shape[1]
-    here = pl.ds(pl.multiple_of(step * cols, cols), cols)
-    mid_ref[:, here] = stream_ref[...].astype(F32) + jnp.dot(
-        merged, w_ref[...], preferred_element_type=F32
-    )
-
-    @pl.when(step == pl.num_programs(0) - 1)
-    def _():
-        mid = mid_ref[...]
-        factor = lax.rsqrt(jnp.mean(mid * mid, axis=1, keepdims=True) + 1e-06)
-        normed = (mid * factor).astype(BF16)
-        normed_ref[...] = normed
-        fill(normed, info_ref[...], out_refs, n_exp, pieces)
+def project_kernel(
+    ctx_ref, w_hbm, stream_ref, info_ref, mid_ref, normed_ref, *refs, n_exp, pieces, cuts
+):
+    *out_refs, w_ref, sems = refs
+    cols = w_ref.shape[1] // cuts
+    copies = [
+        pltpu.make_async_copy(
+            w_hbm.at[:, pl.ds(i * cols, cols)], w_ref.at[:, pl.ds(i * cols, cols)], sems.at[i]
+        )
+        for i in range(cuts)
+    ]
+    for copy in copies:
+        copy.start()
+    merged = jnp.concatenate([ctx_ref[s] for s in range(ctx_ref.shape[0])], axis=1)
+    for i, copy in enumerate(copies):
+        copy.wait()
+        here = slice(i * cols, (i + 1) * cols)
+        mid_ref[:, here] = stream_ref[:, here].astype(F32) + jnp.dot(
+            merged, w_ref[:, here], preferred_element_type=F32
+        )
+    mid = mid_ref[...]
+    factor = lax.rsqrt(jnp.mean(mid * mid, axis=1, keepdims=True) + 1e-06)
+    normed = (mid * factor).astype(BF16)
+    normed_ref[...] = normed
+    fill(normed, info_ref[...], out_refs, n_exp, pieces)
 
 
 def project(merged, w_out, stream, info, n_exp, pieces):
-    n_src, rows, part = merged.shape
-    width = w_out.shape[1]
-    cols = 512
+    rows, width = stream.shape
+    cuts = 4
     slots = [n_exp * p for p in pieces]
     return pl.pallas_call(
-        functools.partial(project_kernel, n_exp=n_exp, pieces=pieces),
-        grid=(width // cols,),
+        functools.partial(project_kernel, n_exp=n_exp, pieces=pieces, cuts=cuts),
+        grid=(1,),
         in_specs=[
-            vmem((n_src, rows, part)),
-            pl.BlockSpec((width, cols), lambda i: (0, i)),
-            pl.BlockSpec((rows, cols), lambda i: (0, i)),
+            vmem(merged.shape),
+            pl.BlockSpec(memory_space=pltpu.HBM),
+            vmem(stream.shape),
             vmem(info.shape),
         ],
         out_specs=[vmem((rows, width))] * 2 + [vmem((s, width)) for s in slots],
         out_shape=[
-            jax.ShapeDtypeStruct((rows, width), F32),
+            pltpu.HBM((rows, width), F32),
             jax.ShapeDtypeStruct((rows, width), BF16),
         ]
         + [jax.ShapeDtypeStruct((s, width), BF16) for s in slots],
+        scratch_shapes=[
+            pltpu.VMEM(w_out.shape, BF16),
+            pltpu.SemaphoreType.DMA((cuts,)),
+        ],
         compiler_params=pltpu.CompilerParams(vmem_limit_bytes=32 * MIB),
         name="project",
-    )(merged, w_out, stream, info)
+    )(merged, in_hbm(w_out), stream, info)
 
 
 def route_kernel(normed_ref, info_ref, *out_refs, n_exp, pieces):
@@ -156,77 +167,83 @@
     )(normed, info)
 
 
-def expert_kernel(*refs, n_in):
+def expert_kernel(*refs, n_in, block):
     x_refs, w_refs = refs[:n_in], refs[n_in : n_in + 6]
-    out_refs, (rows_ref, total_ref) = refs[n_in + 6 : -2], refs[-2:]
-    step, steps = pl.program_id(0), pl.num_programs(0)
-
-    @pl.when(step == 0)
-    def _():
-        start = 0
-        for ref in x_refs:
-            rows_ref[start : start + ref.shape[0]] = ref[...]
-            start += ref.shape[0]
-
-    def part(gate_ref, up_ref, down_ref):
-        rows = rows_ref[...]
-        gate = jnp.dot(rows, gate_ref[...], preferred_element_type=F32)
-        up = jnp.dot(rows, up_ref[...], preferred_element_type=F32)
+    *out_refs, rows_ref, gate_ref, up_ref, down_ref, x_sems, w_sems = refs[n_in + 6 :]
+    share = w_refs[0].shape[1]
+    per = share // block
+
+    def weight_copies(i):
+        gate, up, down = w_refs[:3] if i < per else w_refs[3:]
+        there, here = pl.ds(i % per * block, block), pl.ds(i * block, block)
+        return (
+            pltpu.make_async_copy(gate.at[:, there], gate_ref.at[:, here], w_sems.at[i, 0]),
+            pltpu.make_async_copy(up.at[:, there], up_ref.at[:, here], w_sems.at[i, 1]),
+            pltpu.make_async_copy(down.at[there], down_ref.at[here], w_sems.at[i, 2]),
+        )
+
+    row_copies, start = [], 0
+    for i, ref in enumerate(x_refs):
+        here = pl.ds(start, ref.shape[0])
+        row_copies.append(pltpu.make_async_copy(ref, rows_ref.at[here], x_sems.at[i]))
+        start += ref.shape[0]
+    copies = [weight_copies(i) for i in range(2 * per)]
+    for copy in (*row_copies, *copies[0], *copies[1]):
+        copy.start()
+    for copy in row_copies:
+        copy.wait()
+    rows, total = rows_ref[...], None
+    for i in range(2 * per):
+        here = slice(i * block, (i + 1) * block)
+        copies[i][0].wait()
+        copies[i][1].wait()
+        if i + 2 < 2 * per:
+            for copy in copies[i + 2]:
+                copy.start()
+        gate = jnp.dot(rows, gate_ref[:, here], preferred_element_type=F32)
+        up = jnp.dot(rows, up_ref[:, here], preferred_element_type=F32)
         hidden = (gate / (1.0 + jnp.exp(-gate)) * up).astype(BF16)
-        return jnp.dot(hidden, down_ref[...], preferred_element_type=F32)
-
-    @pl.when(step == 0)
-    def _():
-        total_ref[...] = part(*w_refs[:3])
-
-    @pl.when((step > 0) & (step < steps // 2))
-    def _():
-        total_ref[...] += part(*w_refs[:3])
-
-    @pl.when((step >= steps // 2) & (step < steps - 1))
-    def _():
-        total_ref[...] += part(*w_refs[3:])
-
-    @pl.when(step == steps - 1)
-    def _():
-        total = (total_ref[...] + part(*w_refs[3:])).astype(BF16)
-        start = 0
-        for ref in out_refs:
-            ref[...] = total[start : start + ref.shape[0]]
-            start += ref.shape[0]
+        copies[i][2].wait()
+        term = jnp.dot(hidden, down_ref[here], preferred_element_type=F32)
+        total = term if total is None else total + term
+    start = 0
+    for ref in out_refs:
+        ref[...] = total[start : start + ref.shape[0]].astype(BF16)
+        start += ref.shape[0]
+
+
+def in_hbm(x):
+    return pltpu.with_memory_space_constraint(x, pltpu.HBM)
 
 
 def experts(arrays, mine, other):
     width = arrays[0].shape[1]
-    hidden = mine[0].shape[1]
+    hidden = 2 * mine[0].shape[1]
+    total = sum(x.shape[0] for x in arrays)
     block = 256
-    half = hidden // block
-    total = sum(x.shape[0] for x in arrays)
-
-    def specs(at):
-        return [
-            pl.BlockSpec((width, block), lambda i: (0, at(i))),
-            pl.BlockSpec((width, block), lambda i: (0, at(i))),
-            pl.BlockSpec((block, width), lambda i: (at(i), 0)),
-        ]
-
-    return pl.pallas_call(
-        functools.partial(expert_kernel, n_in=len(arrays)),
-        grid=(2 * half,),
-        in_specs=[vmem(x.shape) for x in arrays]
-        + specs(lambda i: jnp.minimum(i, half - 1))
-        + specs(lambda i: jnp.maximum(i - half, 0)),
+    return pl.pallas_call(
+        functools.partial(expert_kernel, n_in=len(arrays), block=block),
+        grid=(1,),
+        in_specs=[pl.BlockSpec(memory_space=pl.ANY)] * len(arrays)
+        + [pl.BlockSpec(memory_space=pltpu.HBM)] * 6,
         out_specs=[vmem(x.shape) for x in arrays],
-        out_shape=[jax.ShapeDtypeStruct(x.shape, BF16) for x in arrays],
-        scratch_shapes=[pltpu.VMEM((total, width), BF16), pltpu.VMEM((total, width), F32)],
-        compiler_params=pltpu.CompilerParams(vmem_limit_bytes=48 * MIB),
+        out_shape=[pltpu.HBM(x.shape, BF16) for x in arrays],
+        scratch_shapes=[
+            pltpu.VMEM((total, width), BF16),
+            pltpu.VMEM((width, hidden), BF16),
+            pltpu.VMEM((width, hidden), BF16),
+            pltpu.VMEM((hidden, width), BF16),
+            pltpu.SemaphoreType.DMA((len(arrays),)),
+            pltpu.SemaphoreType.DMA((hidden // block, 3)),
+        ],
+        compiler_params=pltpu.CompilerParams(vmem_limit_bytes=44 * MIB),
         cost_estimate=pl.CostEstimate(
-            flops=12 * total * width * hidden,
-            bytes_accessed=12 * width * hidden + 4 * total * width,
-            transcendentals=2 * total * hidden,
+            flops=6 * total * width * hidden,
+            bytes_accessed=6 * width * hidden + 4 * total * width,
+            transcendentals=total * hidden,
         ),
         name="experts",
-    )(*arrays, *mine, *other)
+    )(*arrays, *(in_hbm(w) for w in (*mine, *other)))
 
 
 def combine_kernel(info_ref, *refs, n_exp, pieces, with_mid):
@@ -252,7 +269,7 @@
 def combine(info, backs, n_exp, pieces, mid=None, far=None):
     rows, width = info.shape[1], backs[0].shape[1]
     cols = 512
-    base = [] if mid is None else [mid, far]
+    base = [] if mid is None else [in_hbm(mid), far]
     return pl.pallas_call(
         functools.partial(
             combine_kernel, n_exp=n_exp, pieces=pieces, with_mid=mid is not None
@@ -267,22 +284,54 @@
     )(info, *base, *backs)
 
 
-def spread_kernel(x_ref, out_ref):
-    out_ref[0] = x_ref[...]
+def spread_kernel(x_ref, out_ref, sems):
+    part = out_ref.shape[3]
+    copies = [
+        pltpu.make_async_copy(x_ref.at[:, :, pl.ds(i * part, part)], out_ref.at[i], sems.at[i])
+        for i in range(out_ref.shape[0])
+    ]
+    for copy in copies:
+        copy.start()
+    for copy in copies:
+        copy.wait()
 
 
 def spread(qkv, n_seq):
     three, rows, width = qkv.shape
-    part = width // n_seq
     return pl.pallas_call(
         spread_kernel,
-        grid=(n_seq,),
-        in_specs=[pl.BlockSpec((three, rows, part), lambda i: (0, 0, i))],
-        out_specs=pl.BlockSpec((1, three, rows, part), lambda i: (i, 0, 0, 0)),
-        out_shape=jax.ShapeDtypeStruct((n_seq, three, rows, part), BF16),
+        in_specs=[pl.BlockSpec(memory_space=pltpu.HBM)],
+        out_specs=pl.BlockSpec(memory_space=pltpu.HBM),
+        out_shape=jax.ShapeDtypeStruct((n_seq, three, rows, width // n_seq), BF16),
+        scratch_shapes=[pltpu.SemaphoreType.DMA((n_seq,))],
+        compiler_params=pltpu.CompilerParams(vmem_limit_bytes=4 * MIB),
+        name="spread",
+    )(in_hbm(qkv))
+
+
+def total_kernel(own_ref, *refs):
+    *in_refs, out_ref = refs
+    start = 0
+    for up_ref, down_ref in zip(in_refs[::2], in_refs[1::2]):
+        here = slice(start, start + up_ref.shape[0])
+        total = own_ref[here].astype(F32) + up_ref[...].astype(F32) + down_ref[...].astype(F32)
+        out_ref[here] = total.astype(BF16)
+        start += up_ref.shape[0]
+
+
+def add_up(own, pairs):
+    arrays = [own, *(x for pair in pairs for x in pair)]
+    rows, width = own.shape
+    cols = 512
+    return pl.pallas_call(
+        total_kernel,
+        grid=(width // cols,),
+        in_specs=[pl.BlockSpec((x.shape[0], cols), lambda i: (0, i)) for x in arrays],
+        out_specs=pl.BlockSpec((rows, cols), lambda i: (0, i)),
+        out_shape=pltpu.HBM((rows, width), BF16),
         compiler_params=pltpu.CompilerParams(vmem_limit_bytes=16 * MIB),
-        name="spread",
-    )(qkv)
+        name="add_up",
+    )(*arrays)
 
 
 def per_device(stream_in, qkv_heads, expert_ids, gate_weights, w_out, w_gate, w_up, w_down):
@@ -290,8 +339,7 @@
     seq, exp = ("y", "core"), ("z", "x")
     n_y, n_seq, n_exp = lax.axis_size("y"), lax.axis_size(seq), lax.axis_size(exp)
     capacity = 3 * TOP * rows // (2 * n_exp)
-    pieces = (capacity // 3, capacity - capacity // 3)
-    whole = (capacity,)
+    pieces = (capacity,)
 
     def swap(x):
         return lax.ppermute(x, "core", [(0, 1), (1, 0)])
@@ -313,24 +361,35 @@
     context = attention(arrived)
     context, info_far, other = lax.optimization_barrier((context, info_far, other))
     merged = lax.all_to_all(context, seq, split_axis=0, concat_axis=0, tiled=True)
-    mid, normed, *buffers = project(merged, w_out, stream_in[0], info, n_exp, pieces)
-
-    [buffer_far] = route(shift(normed, 2), info_far, n_exp, whole)
-    own = [exchange(b) for b in buffers]
-    far = exchange(buffer_far)
-    up, down = [shift(x, 1) for x in own], [shift(x, -1) for x in own]
-
-    own_part = experts(own, mine, other)
-    near_part = [experts([u, d], mine, other) for u, d in zip(up, down)]
-    [far_part] = experts([far], mine, other)
-
-    far_sum = combine(info_far, [exchange(far_part)], n_exp, whole)
+    mid, normed, buffer = project(merged, w_out, stream_in[0], info, n_exp, pieces)
+
+    tie = lax.optimization_barrier
+    far_tokens = shift(normed, 2)
+    own = exchange(buffer)
+    own, far_tokens = tie((own, far_tokens))
+    [far_buffer] = route(far_tokens, info_far, n_exp, pieces)
+    cut = own.shape[0] // 2
+    low, high = own[:cut], own[cut:]
+    up_low, down_low = shift(low, 1), shift(low, -1)
+    up_high, down_high = shift(high, 1), shift(high, -1)
+    far_rows = exchange(far_buffer)
+
+    [own_part] = experts([own], mine, other)
+    up_low, down_low, own_part = tie((up_low, down_low, own_part))
+    up_low, down_low = experts([up_low, down_low], mine, other)
+    far_rows, up_low, down_low = tie((far_rows, up_low, down_low))
+    [far_part] = experts([far_rows], mine, other)
+    up_high, down_high, far_part = tie((up_high, down_high, far_part))
+    up_high, down_high = experts([up_high, down_high], mine, other)
+    far_back = exchange(far_part)
+    up_low, down_low = shift(up_low, -1), shift(down_low, 1)
+    up_high, down_high = shift(up_high, -1), shift(down_high, 1)
+    far_sum = combine(info_far, [far_back], n_exp, pieces)
+    total = add_up(own_part, [(up_low, down_low), (up_high, down_high)])
+    total, far_back = tie((total, far_back))
+    back = exchange(total)
     far_home = shift(far_sum, 2)
-    backs = []
-    for a, (u, d) in zip(own_part, near_part):
-        summed = a.astype(F32) + shift(u, -1).astype(F32) + shift(d, 1).astype(F32)
-        backs.append(exchange(summed.astype(BF16)))
-    return combine(info, backs, n_exp, pieces, mid, far_home)[None]
+    return combine(info, [back], n_exp, pieces, mid, far_home)[None]
 
 
 def solution(mesh):

time: 225 us -> 255 us (1.13)
  Pallas kernels: 60.1 us -> 110 us
  waiting for transfers between devices: 61.2 us -> 82.4 us
  blocking collectives: 30.8 us -> 12.8 us
  local copies, waits for them, and re-layouts: 11 us -> 1.12 us
  starting transfers between devices: 56.2 us -> 47.5 us
  other arithmetic: 4.18 us -> 0.07 us
    pallas_call x5 -> x6, Pallas kernels: 42.5 us -> 89.2 us  [the longest x1 48.8 us: spread(): pl.pallas_call(spread_kernel, in_specs=[pl.BlockSpec(memory_space=pltpu.H...]
    ppermute x11, waiting for transfers between devices: 30.6 us -> 52 us  [shift(): return lax.ppermute(x, 'y', [(i, (i + by) % n_y) for i in range(n_y)])]
    all_to_all x1 -> x0, blocking collectives: 18 us -> none  [exchange(): return lax.all_to_all(x, exp, split_axis=0, concat_axis=0, tiled=True)]
    unnamed x28 -> x12, local copies, waits for them, and re-layouts: 10.9 us -> 0.03 us
    ppermute x11, starting transfers between devices: 17.7 us -> 13.1 us  [shift(): return lax.ppermute(x, 'y', [(i, (i + by) % n_y) for i in range(n_y)])]
    all_to_all x5 -> x4, starting transfers between devices: 33.3 us -> 29.2 us  [exchange(): return lax.all_to_all(x, exp, split_axis=0, concat_axis=0, tiled=True)]
    convert_element_type x1 -> x0, other arithmetic: 3.07 us -> none  [per_device(): backs.append(exchange(summed.astype(BF16)))]
    all_to_all x5 -> x4, waiting for transfers between devices: 12.7 us -> 12.5 us  [exchange(): return lax.all_to_all(x, exp, split_axis=0, concat_axis=0, tiled=True)]
  transfers between devices with their start and end apart: 20 -> 19, of which waited for: 5 -> 11; matrix products, arithmetic and copies ran while one was open for 2% -> 0% of each run, Pallas kernels for 24% -> 38%
where the time goes in v3:
time: 255 us; the launch traced here: 254 us
  Pallas kernels  110 us (43%)
  waiting for transfers between devices  82.4 us (32%)
  starting transfers between devices  47.5 us (19%)
  blocking collectives  12.8 us (5%)
    ppermute x11, waiting for transfers between devices, shift(): return lax.ppermute(x, 'y', [(i, (i + by) % n_y) for i in range(n_y)])  52 us
    pallas_call x1, Pallas kernels, spread(): pl.pallas_call(spread_kernel, in_specs=[pl.BlockSpec(memory_space=pltpu.H...  48.8 us
    pallas_call x4, Pallas kernels, experts(): pl.pallas_call(functools.partial(expert_kernel, n_in=len(arrays), block=b...  38.1 us
    all_to_all x4, starting transfers between devices, exchange(): return lax.all_to_all(x, exp, split_axis=0, concat_axis=0, tiled=True)  29.2 us
    all_to_all x1, waiting for transfers between devices, per_device(): arrived = lax.all_to_all(qkv, seq, split_axis=0, concat_axis=0, tiled=True)  17.9 us
    ppermute x11, starting transfers between devices, shift(): return lax.ppermute(x, 'y', [(i, (i + by) % n_y) for i in range(n_y)])  13.1 us
    all_to_all x1, blocking collectives, per_device(): lax.all_to_all(context, seq, split_axis=0, concat_axis=0, tiled=True)  12.8 us
    all_to_all x4, waiting for transfers between devices, exchange(): return lax.all_to_all(x, exp, split_axis=0, concat_axis=0, tiled=True)  12.5 us
  transfers between devices with their start and end apart: 19, of which 11 were waited for; matrix products, arithmetic and copies ran while one was open for 0% of the time, Pallas kernels for 38%

profile of v3, /device:TPU:2, one launch (start us, length us, event | category | flops | bytes accessed | tf_op | source)
XLA Modules:
  0.0 253.7 jit_solution(15674208159017879234)
XLA Ops:
  0.0 0.0 collective-permute-start.1
  0.0 0.5 collective-permute-start.2
  0.5 0.0 collective-permute-start.3
  0.5 48.8 %spread.1 = bf16[8,3,128,256]{3,2,1,0:T(8,128)(2,1)} custom-call(bf16[3,128,2048]{2,1,0:T(8,128)(2,1)} %bitcast.30), custom_call_target="tpu_custom_call" | custom-call | tf_op jit(solution)/shard_map/spread/pallas_call | solution.py:301
  49.3 0.0 copy-start.2
  49.4 0.0 copy-start.3
  49.4 4.6 %all-to-all-start = ((bf16[8,3,128,256]{3,2,1,0:T(8,128)(2,1)}), bf16[8,3,128,256]{3,2,1,0:T(8,128)(2,1)S(1)}, u32[]{:S(2)}, u32[]{:S(2)}) async-start(bf16[8,3,128,256]{3,2,1,0:T(8,128)(2,1)} %spread.1), calls=%async_computation | async-start | bytes 3145728 | tf_op jit(solution)/shard_map/all_to_all | solution.py:360
  54.0 0.1 pad.2.clone
  54.0 0.0 copy-done.2
  54.0 0.0 copy-done.3
  54.0 0.1 maximum_maximum_fusion.info_ref
  54.1 3.6 %collective-permute-start = (f32[8,128]{1,0:T(8,128)S(1)}, f32[8,128]{1,0:T(8,128)S(1)}, u32[]{:S(2)}, u32[]{:S(2)}) collective-permute-start(f32[8,128]{1,0:T(8,128)S(1)} %maximum_maximum_fusion.info_ref), channel_id=1, source_target_pairs={{0,64},{32,96},{64,0},{96,32},{1,65},{33,97},{65,1},{97,33},{2,66}... | collective-permute-start | bytes 12296 | tf_op jit(solution)/shard_map/ppermute | solution.py:348
  57.7 17.9 %all-to-all-done.x_ref = bf16[8,3,128,256]{3,2,1,0:T(8,128)(2,1)S(1)} async-done(((bf16[8,3,128,256]{3,2,1,0:T(8,128)(2,1)}), bf16[8,3,128,256]{3,2,1,0:T(8,128)(2,1)S(1)}, u32[]{:S(2)}, u32[]{:S(2)}) %all-to-all-start) | async-done | bytes 1572896 | tf_op jit(solution)/shard_map/all_to_all | solution.py:360
  75.6 6.0 %attention.1 = bf16[8,128,256]{2,1,0:T(8,128)(2,1)S(1)} custom-call(bf16[8,3,128,256]{3,2,1,0:T(8,128)(2,1)S(1)} %all-to-all-done.x_ref), custom_call_target="tpu_custom_call" | custom-call | tf_op jit(solution)/shard_map/attention/pallas_call | solution.py:52
  81.6 0.0 collective-permute-done.info_ref
  81.6 0.0 collective-permute-done.1.refs_4_.refs_5_
  81.6 0.0 collective-permute-done.2.refs_5_.refs_6_
  81.7 0.0 collective-permute-done.3.refs_6_.refs_7_
  81.7 12.8 %all_to_all.56.ctx_ref = bf16[8,128,256]{2,1,0:T(8,128)(2,1)S(1)} all-to-all(bf16[8,128,256]{2,1,0:T(8,128)(2,1)S(1)} %attention.1), channel_id=1, replica_groups=mesh['y'=4,'core'=2,'z'=4,'x'=4] {'y','core'}, dimensions={0} | all-to-all | bytes 1048576 | tf_op jit(solution)/shard_map/all_to_all | solution.py:363
  94.5 0.0 copy-done.1
  94.5 5.8 %project.1 = (f32[128,2048]{1,0:T(8,128)}, bf16[128,2048]{1,0:T(8,128)(2,1)S(1)}, bf16[384,2048]{1,0:T(8,128)(2,1)}) custom-call(bf16[8,128,256]{2,1,0:T(8,128)(2,1)S(1)} %all_to_all.56.ctx_ref, bf16[2048,2048]{1,0:T(8,128)(2,1)} %w_hbm.1, bf16[128,2048]{1,0:T(8,128)(2,1)S(1)} %bitcast.28, f32[8,128]{1,0:T(8,128)S(1)} %maximum_maximum_fusion.info_ref), custom_call_target="tpu_custom_call" | custom-call | tf_op jit(solution)/shard_map/project/pallas_call | solution.py:128
  100.3 8.3 %all-to-all-start.2 = ((bf16[16,24,2048]{2,1,0:T(8,128)(2,1)}), bf16[16,24,2048]{2,1,0:T(8,128)(2,1)S(1)}, u32[]{:S(2)}, u32[]{:S(2)}) async-start(bf16[16,24,2048]{2,1,0:T(8,128)(2,1)} %bitcast.10), calls=%async_computation.2 | async-start | bytes 3145728 | tf_op jit(solution)/shard_map/all_to_all | solution.py:351
  108.6 0.3 collective-permute-start.4
  109.0 13.9 %collective-permute-done.4.normed_ref = bf16[128,2048]{1,0:T(8,128)(2,1)S(1)} collective-permute-done((bf16[128,2048]{1,0:T(8,128)(2,1)S(1)}, bf16[128,2048]{1,0:T(8,128)(2,1)S(1)}, u32[]{:S(2)}, u32[]{:S(2)}) %collective-permute-start.4) | collective-permute-done | bytes 524320 | tf_op jit(solution)/shard_map/ppermute | solution.py:348
  122.9 6.9 %all-to-all-done.2 = bf16[16,24,2048]{2,1,0:T(8,128)(2,1)S(1)} async-done(((bf16[16,24,2048]{2,1,0:T(8,128)(2,1)}), bf16[16,24,2048]{2,1,0:T(8,128)(2,1)S(1)}, u32[]{:S(2)}, u32[]{:S(2)}) %all-to-all-start.2) | async-done | bytes 1572896 | tf_op jit(solution)/shard_map/all_to_all | solution.py:351
  129.8 2.0 route.1
  131.7 6.2 %all-to-all-start.3 = ((bf16[16,24,2048]{2,1,0:T(8,128)(2,1)}), bf16[16,24,2048]{2,1,0:T(8,128)(2,1)S(1)}, u32[]{:S(2)}, u32[]{:S(2)}) async-start(bf16[16,24,2048]{2,1,0:T(8,128)(2,1)} %bitcast.12), calls=%async_computation.3 | async-start | bytes 3145728 | tf_op jit(solution)/shard_map/all_to_all | solution.py:351
  138.0 1.0 fusion
  139.0 1.2 collective-permute-start.8
  140.1 0.9 collective-permute-start.7
  141.0 2.3 collective-permute-start.6
  143.4 0.0 collective-permute-start.5
  143.4 9.1 %experts.4.own_ref = bf16[384,2048]{1,0:T(8,128)(2,1)} custom-call(bf16[384,2048]{1,0:T(8,128)(2,1)S(1)} %bitcast.25, bf16[2048,512]{1,0:T(8,128)(2,1)} %bitcast.34, bf16[2048,512]{1,0:T(8,128)(2,1)} %bitcast.39, bf16[512,2048]{1,0:T(8,128)(2,1)} %bitcast.44, bf16[2048,512]{1,0:T(8,128)(2,1)} %collective-permute-done.1.refs_4_.refs_5_, ...), custom_call_target="tpu_custom_call" | custom-call | flops 4831838208 | bytes 15728640 | tf_op jit(solution)/shard_map/experts/pallas_call | solution.py:224
  152.5 7.0 %collective-permute-done.8.refs_1_ = bf16[192,2048]{1,0:T(8,128)(2,1)S(1)} collective-permute-done((bf16[192,2048]{1,0:T(8,128)(2,1)S(1)}, bf16[192,2048]{1,0:T(8,128)(2,1)S(1)}, u32[]{:S(2)}, u32[]{:S(2)}) %collective-permute-start.8) | collective-permute-done | bytes 786464 | tf_op jit(solution)/shard_map/ppermute | solution.py:348
  159.5 2.3 collective-permute-done.7.refs_0_
  161.8 9.1 %experts.5 = (bf16[192,2048]{1,0:T(8,128)(2,1)}, bf16[192,2048]{1,0:T(8,128)(2,1)}) custom-call(bf16[192,2048]{1,0:T(8,128)(2,1)S(1)} %collective-permute-done.7.refs_0_, bf16[192,2048]{1,0:T(8,128)(2,1)S(1)} %collective-permute-done.8.refs_1_, bf16[2048,512]{1,0:T(8,128)(2,1)} %bitcast.35, bf16[2048,512]{1,0:T(8,128)(2,1)} %bitcast.40, ...), custom_call_target="tpu_custom_call" | custom-call | flops 4831838208 | bytes 15728640 | tf_op jit(solution)/shard_map/experts/pallas_call | solution.py:224
  170.9 0.0 all-to-all-done.3
  170.9 9.4 %experts.6 = bf16[384,2048]{1,0:T(8,128)(2,1)} custom-call(bf16[384,2048]{1,0:T(8,128)(2,1)S(1)} %bitcast.27, bf16[2048,512]{1,0:T(8,128)(2,1)} %bitcast.36, bf16[2048,512]{1,0:T(8,128)(2,1)} %bitcast.41, bf16[512,2048]{1,0:T(8,128)(2,1)} %bitcast.46, bf16[2048,512]{1,0:T(8,128)(2,1)} %collective-permute-done.1.refs_4_.refs_5_, ...), custom_call_target="tpu_custom_call" | custom-call | flops 4831838208 | bytes 15728640 | tf_op jit(solution)/shard_map/experts/pallas_call | solution.py:224
  180.3 0.0 collective-permute-done.6.refs_1_
  180.3 0.0 collective-permute-done.5.refs_0_
  180.4 0.0 copy-start.5
  180.4 0.0 copy-start.4
  180.4 7.4 %all-to-all-start.4 = ((bf16[16,24,2048]{2,1,0:T(8,128)(2,1)}), bf16[16,24,2048]{2,1,0:T(8,128)(2,1)S(1)}, u32[]{:S(2)}, u32[]{:S(2)}) async-start(bf16[16,24,2048]{2,1,0:T(8,128)(2,1)} %bitcast.31), calls=%async_computation.4 | async-start | bytes 3145728 | tf_op jit(solution)/shard_map/all_to_all | solution.py:351
  187.8 0.0 copy-done.5
  187.8 0.0 copy-start
  187.8 0.1 collective-permute-start.10
  187.9 0.0 copy-done.4
  187.9 2.0 collective-permute-start.11
  189.9 10.5 %experts.7 = (bf16[192,2048]{1,0:T(8,128)(2,1)}, bf16[192,2048]{1,0:T(8,128)(2,1)}) custom-call(bf16[192,2048]{1,0:T(8,128)(2,1)} %collective-permute-done.5.refs_0_, bf16[192,2048]{1,0:T(8,128)(2,1)} %collective-permute-done.6.refs_1_, bf16[2048,512]{1,0:T(8,128)(2,1)} %bitcast.37, bf16[2048,512]{1,0:T(8,128)(2,1)} %bitcast.42, bf16[512,2048]{1,0:T(8,128)(2,1)} %bitcast.47, ...), custom_call_target="tpu_custom_call" | custom-call | flops 4831838208 | bytes 15728640 | tf_op jit(solution)/shard_map/experts/pallas_call | solution.py:224
  200.4 1.4 collective-permute-start.12
  201.8 0.7 collective-permute-start.13
  202.5 4.0 %collective-permute-done.10.refs_0_ = bf16[192,2048]{1,0:T(8,128)(2,1)S(1)} collective-permute-done((bf16[192,2048]{1,0:T(8,128)(2,1)S(1)}, bf16[192,2048]{1,0:T(8,128)(2,1)S(1)}, u32[]{:S(2)}, u32[]{:S(2)}) %collective-permute-start.10) | collective-permute-done | bytes 786464 | tf_op jit(solution)/shard_map/ppermute | solution.py:348
  206.5 0.3 collective-permute-done.11.refs_1_
  206.8 12.0 %collective-permute-done.12.refs_2_ = bf16[192,2048]{1,0:T(8,128)(2,1)S(1)} collective-permute-done((bf16[192,2048]{1,0:T(8,128)(2,1)}, bf16[192,2048]{1,0:T(8,128)(2,1)S(1)}, u32[]{:S(2)}, u32[]{:S(2)}) %collective-permute-start.12) | collective-permute-done | bytes 786464 | tf_op jit(solution)/shard_map/ppermute | solution.py:348
  218.8 1.5 collective-permute-done.13.refs_3_
  220.3 0.0 copy-done
  220.3 2.4 add_up.1
  222.7 0.0 all-to-all-done.4
  222.7 7.2 %all-to-all-start.5 = ((bf16[16,24,2048]{2,1,0:T(8,128)(2,1)}), bf16[16,24,2048]{2,1,0:T(8,128)(2,1)S(1)}, u32[]{:S(2)}, u32[]{:S(2)}) async-start(bf16[16,24,2048]{2,1,0:T(8,128)(2,1)} %bitcast.29), calls=%async_computation.5 | async-start | bytes 3145728 | tf_op jit(solution)/shard_map/all_to_all | solution.py:351
  229.9 2.3 combine.2
  232.2 0.7 collective-permute-start.9
  232.9 11.0 %collective-permute-done.9.refs_1_ = bf16[128,2048]{1,0:T(8,128)(2,1)S(1)} collective-permute-done((bf16[128,2048]{1,0:T(8,128)(2,1)S(1)}, bf16[128,2048]{1,0:T(8,128)(2,1)S(1)}, u32[]{:S(2)}, u32[]{:S(2)}) %collective-permute-start.9) | collective-permute-done | bytes 524320 | tf_op jit(solution)/shard_map/ppermute | solution.py:348
  243.9 5.5 %all-to-all-done.5 = bf16[16,24,2048]{2,1,0:T(8,128)(2,1)S(1)} async-done(((bf16[16,24,2048]{2,1,0:T(8,128)(2,1)}), bf16[16,24,2048]{2,1,0:T(8,128)(2,1)S(1)}, u32[]{:S(2)}, u32[]{:S(2)}) %all-to-all-start.5) | async-done | bytes 1572896 | tf_op jit(solution)/shard_map/all_to_all | solution.py:351
  249.4 4.3 %combine.3 = bf16[128,2048]{1,0:T(8,128)(2,1)} custom-call(f32[8,128]{1,0:T(8,128)S(1)} %maximum_maximum_fusion.info_ref, f32[128,2048]{1,0:T(8,128)} %get-tuple-element.30.refs_0_, bf16[128,2048]{1,0:T(8,128)(2,1)S(1)} %collective-permute-done.9.refs_1_, bf16[384,2048]{1,0:T(8,128)(2,1)S(1)} %bitcast.26), custom_call_target="tpu_custom_call" | custom-call | tf_op jit(solution)/shard_map/combine/pallas_call | solution.py:273
  (3 shorter events, 0.0 us)
Async XLA Ops:
  0.0 81.6 %collective-permute-start.1 = (bf16[2048,512]{1,0:T(8,128)(2,1)}, bf16[2048,512]{1,0:T(8,128)(2,1)}, u32[]{:S(2)}, u32[]{:S(2)}) collective-permute-start(bf16[2048,512]{1,0:T(8,128)(2,1)} %bitcast.33), channel_id=1, source_target_pairs={{0,16},{16,0},{1,17},{17,1},{2,18},{18,2},{3,19},{19,3},{4,20},{20... | collective-permute-start | bytes 6291464 | tf_op jit(solution)/shard_map/ppermute | solution.py:345
  0.0 81.6 %collective-permute-start.2 = (bf16[2048,512]{1,0:T(8,128)(2,1)}, bf16[2048,512]{1,0:T(8,128)(2,1)}, u32[]{:S(2)}, u32[]{:S(2)}) collective-permute-start(bf16[2048,512]{1,0:T(8,128)(2,1)} %bitcast.38), channel_id=1, source_target_pairs={{0,16},{16,0},{1,17},{17,1},{2,18},{18,2},{3,19},{19,3},{4,20},{20... | collective-permute-start | bytes 6291464 | tf_op jit(solution)/shard_map/ppermute | solution.py:345
  0.5 81.1 %collective-permute-start.3 = (bf16[512,2048]{1,0:T(8,128)(2,1)}, bf16[512,2048]{1,0:T(8,128)(2,1)}, u32[]{:S(2)}, u32[]{:S(2)}) collective-permute-start(bf16[512,2048]{1,0:T(8,128)(2,1)} %bitcast.43), channel_id=1, source_target_pairs={{0,16},{16,0},{1,17},{17,1},{2,18},{18,2},{3,19},{19,3},{4,20},{20... | collective-permute-start | bytes 6291464 | tf_op jit(solution)/shard_map/ppermute | solution.py:345
  49.3 4.7 %copy-start.2 = (s32[1,128,2]{1,2,0:T(2,128)S(1)}, s32[1,128,2]{1,2,0:T(2,128)}, u32[]{:S(2)}) copy-start(s32[1,128,2]{1,2,0:T(2,128)} %param.10) | copy-start | bytes 3076
  49.4 4.7 %copy-start.3 = (f32[1,128,2]{1,2,0:T(2,128)S(1)}, f32[1,128,2]{1,2,0:T(2,128)}, u32[]{:S(2)}) copy-start(f32[1,128,2]{1,2,0:T(2,128)} %param.11) | copy-start | bytes 3076
  49.4 26.2 %all-to-all-start = ((bf16[8,3,128,256]{3,2,1,0:T(8,128)(2,1)}), bf16[8,3,128,256]{3,2,1,0:T(8,128)(2,1)S(1)}, u32[]{:S(2)}, u32[]{:S(2)}) async-start(bf16[8,3,128,256]{3,2,1,0:T(8,128)(2,1)} %spread.1), calls=%async_computation | async-start | bytes 3145728 | tf_op jit(solution)/shard_map/all_to_all | solution.py:360
  54.1 40.4 %copy-start.1 = (bf16[1,128,2048]{2,1,0:T(8,128)(2,1)S(1)}, bf16[1,128,2048]{2,1,0:T(8,128)(2,1)}, u32[]{:S(2)}) copy-start(bf16[1,128,2048]{2,1,0:T(8,128)(2,1)} %param.8) | copy-start | bytes 1572868
  54.1 27.5 %collective-permute-start = (f32[8,128]{1,0:T(8,128)S(1)}, f32[8,128]{1,0:T(8,128)S(1)}, u32[]{:S(2)}, u32[]{:S(2)}) collective-permute-start(f32[8,128]{1,0:T(8,128)S(1)} %maximum_maximum_fusion.info_ref), channel_id=1, source_target_pairs={{0,64},{32,96},{64,0},{96,32},{1,65},{33,97},{65,1},{97,33},{2,66}... | collective-permute-start | bytes 12296 | tf_op jit(solution)/shard_map/ppermute | solution.py:348
  100.3 29.5 %all-to-all-start.2 = ((bf16[16,24,2048]{2,1,0:T(8,128)(2,1)}), bf16[16,24,2048]{2,1,0:T(8,128)(2,1)S(1)}, u32[]{:S(2)}, u32[]{:S(2)}) async-start(bf16[16,24,2048]{2,1,0:T(8,128)(2,1)} %bitcast.10), calls=%async_computation.2 | async-start | bytes 3145728 | tf_op jit(solution)/shard_map/all_to_all | solution.py:351
  108.6 14.2 %collective-permute-start.4 = (bf16[128,2048]{1,0:T(8,128)(2,1)S(1)}, bf16[128,2048]{1,0:T(8,128)(2,1)S(1)}, u32[]{:S(2)}, u32[]{:S(2)}) collective-permute-start(bf16[128,2048]{1,0:T(8,128)(2,1)S(1)} %get-tuple-element.33), channel_id=1, source_target_pairs={{0,64},{32,96},{64,0},{96,32},{1,65},{33,97},{65,1},{97,33},{2,66}... | collective-permute-start | bytes 1572872 | tf_op jit(solution)/shard_map/ppermute | solution.py:348
  131.7 39.2 %all-to-all-start.3 = ((bf16[16,24,2048]{2,1,0:T(8,128)(2,1)}), bf16[16,24,2048]{2,1,0:T(8,128)(2,1)S(1)}, u32[]{:S(2)}, u32[]{:S(2)}) async-start(bf16[16,24,2048]{2,1,0:T(8,128)(2,1)} %bitcast.12), calls=%async_computation.3 | async-start | bytes 3145728 | tf_op jit(solution)/shard_map/all_to_all | solution.py:351
  139.0 20.5 %collective-permute-start.8 = (bf16[192,2048]{1,0:T(8,128)(2,1)S(1)}, bf16[192,2048]{1,0:T(8,128)(2,1)S(1)}, u32[]{:S(2)}, u32[]{:S(2)}) collective-permute-start(bf16[192,2048]{1,0:T(8,128)(2,1)S(1)} %get-tuple-element.53), channel_id=1, source_target_pairs={{0,96},{32,0},{64,32},{96,64},{1,97},{33,1},{65,33},{97,65},{2,98}... | collective-permute-start | bytes 2359304 | tf_op jit(solution)/shard_map/ppermute | solution.py:348
  140.1 21.7 %collective-permute-start.7 = (bf16[192,2048]{1,0:T(8,128)(2,1)S(1)}, bf16[192,2048]{1,0:T(8,128)(2,1)S(1)}, u32[]{:S(2)}, u32[]{:S(2)}) collective-permute-start(bf16[192,2048]{1,0:T(8,128)(2,1)S(1)} %get-tuple-element.53), channel_id=1, source_target_pairs={{0,32},{32,64},{64,96},{96,0},{1,33},{33,65},{65,97},{97,1},{2,34}... | collective-permute-start | bytes 2359304 | tf_op jit(solution)/shard_map/ppermute | solution.py:348
  141.0 39.3 %collective-permute-start.6 = (bf16[192,2048]{1,0:T(8,128)(2,1)}, bf16[192,2048]{1,0:T(8,128)(2,1)}, u32[]{:S(2)}, u32[]{:S(2)}) collective-permute-start(bf16[192,2048]{1,0:T(8,128)(2,1)} %get-tuple-element.54), channel_id=1, source_target_pairs={{0,96},{32,0},{64,32},{96,64},{1,97},{33,1},{65,33},{97,65},{2,98}... | collective-permute-start | bytes 2359304 | tf_op jit(solution)/shard_map/ppermute | solution.py:348
  143.4 37.0 %collective-permute-start.5 = (bf16[192,2048]{1,0:T(8,128)(2,1)}, bf16[192,2048]{1,0:T(8,128)(2,1)}, u32[]{:S(2)}, u32[]{:S(2)}) collective-permute-start(bf16[192,2048]{1,0:T(8,128)(2,1)} %get-tuple-element.54), channel_id=1, source_target_pairs={{0,32},{32,64},{64,96},{96,0},{1,33},{33,65},{65,97},{97,1},{2,34}... | collective-permute-start | bytes 2359304 | tf_op jit(solution)/shard_map/ppermute | solution.py:348
  180.4 7.5 %copy-start.5 = (bf16[192,2048]{1,0:T(8,128)(2,1)S(1)}, bf16[192,2048]{1,0:T(8,128)(2,1)}, u32[]{:S(2)}) copy-start(bf16[192,2048]{1,0:T(8,128)(2,1)} %get-tuple-element.46) | copy-start | bytes 2359300
  180.4 7.5 %copy-start.4 = (bf16[192,2048]{1,0:T(8,128)(2,1)S(1)}, bf16[192,2048]{1,0:T(8,128)(2,1)}, u32[]{:S(2)}) copy-start(bf16[192,2048]{1,0:T(8,128)(2,1)} %get-tuple-element.47) | copy-start | bytes 2359300
  180.4 42.3 %all-to-all-start.4 = ((bf16[16,24,2048]{2,1,0:T(8,128)(2,1)}), bf16[16,24,2048]{2,1,0:T(8,128)(2,1)S(1)}, u32[]{:S(2)}, u32[]{:S(2)}) async-start(bf16[16,24,2048]{2,1,0:T(8,128)(2,1)} %bitcast.31), calls=%async_computation.4 | async-start | bytes 3145728 | tf_op jit(solution)/shard_map/all_to_all | solution.py:351
  187.8 32.5 %copy-start = (bf16[384,2048]{1,0:T(8,128)(2,1)S(1)}, bf16[384,2048]{1,0:T(8,128)(2,1)}, u32[]{:S(2)}) copy-start(bf16[384,2048]{1,0:T(8,128)(2,1)} %experts.4.own_ref) | copy-start | bytes 4718596
  187.8 18.7 %collective-permute-start.10 = (bf16[192,2048]{1,0:T(8,128)(2,1)S(1)}, bf16[192,2048]{1,0:T(8,128)(2,1)S(1)}, u32[]{:S(2)}, u32[]{:S(2)}) collective-permute-start(bf16[192,2048]{1,0:T(8,128)(2,1)S(1)} %copy-done.5), channel_id=1, source_target_pairs={{0,96},{32,0},{64,32},{96,64},{1,97},{33,1},{65,33},{97,65},{2,98}... | collective-permute-start | bytes 2359304 | tf_op jit(solution)/shard_map/ppermute | solution.py:348
  187.9 18.9 %collective-permute-start.11 = (bf16[192,2048]{1,0:T(8,128)(2,1)S(1)}, bf16[192,2048]{1,0:T(8,128)(2,1)S(1)}, u32[]{:S(2)}, u32[]{:S(2)}) collective-permute-start(bf16[192,2048]{1,0:T(8,128)(2,1)S(1)} %copy-done.4), channel_id=1, source_target_pairs={{0,32},{32,64},{64,96},{96,0},{1,33},{33,65},{65,97},{97,1},{2,34}... | collective-permute-start | bytes 2359304 | tf_op jit(solution)/shard_map/ppermute | solution.py:348
  200.4 18.4 %collective-permute-start.12 = (bf16[192,2048]{1,0:T(8,128)(2,1)}, bf16[192,2048]{1,0:T(8,128)(2,1)S(1)}, u32[]{:S(2)}, u32[]{:S(2)}) collective-permute-start(bf16[192,2048]{1,0:T(8,128)(2,1)} %get-tuple-element.50), channel_id=1, source_target_pairs={{0,96},{32,0},{64,32},{96,64},{1,97},{33,1},{65,33},{97,65},{2,98}... | collective-permute-start | bytes 2359304 | tf_op jit(solution)/shard_map/ppermute | solution.py:348
  201.8 18.5 %collective-permute-start.13 = (bf16[192,2048]{1,0:T(8,128)(2,1)}, bf16[192,2048]{1,0:T(8,128)(2,1)S(1)}, u32[]{:S(2)}, u32[]{:S(2)}) collective-permute-start(bf16[192,2048]{1,0:T(8,128)(2,1)} %get-tuple-element.51), channel_id=1, source_target_pairs={{0,32},{32,64},{64,96},{96,0},{1,33},{33,65},{65,97},{97,1},{2,34}... | collective-permute-start | bytes 2359304 | tf_op jit(solution)/shard_map/ppermute | solution.py:348
  222.7 26.7 %all-to-all-start.5 = ((bf16[16,24,2048]{2,1,0:T(8,128)(2,1)}), bf16[16,24,2048]{2,1,0:T(8,128)(2,1)S(1)}, u32[]{:S(2)}, u32[]{:S(2)}) async-start(bf16[16,24,2048]{2,1,0:T(8,128)(2,1)} %bitcast.29), calls=%async_computation.5 | async-start | bytes 3145728 | tf_op jit(solution)/shard_map/all_to_all | solution.py:351
  232.2 11.7 %collective-permute-start.9 = (bf16[128,2048]{1,0:T(8,128)(2,1)S(1)}, bf16[128,2048]{1,0:T(8,128)(2,1)S(1)}, u32[]{:S(2)}, u32[]{:S(2)}) collective-permute-start(bf16[128,2048]{1,0:T(8,128)(2,1)S(1)} %combine.2), channel_id=1, source_target_pairs={{0,64},{32,96},{64,0},{96,32},{1,65},{33,97},{65,1},{97,33},{2,66}... | collective-permute-start | bytes 1572872 | tf_op jit(solution)/shard_map/ppermute | solution.py:348

commit v4 on v3

v4 whole, which is shorter than its diff:
```python
import functools

import jax
import jax.numpy as jnp
from jax import lax
from jax.experimental import pallas as pl
from jax.experimental.pallas import tpu as pltpu
from jax.sharding import Mesh
from jax.sharding import PartitionSpec as P

HD = 64
LANES = 128
MIB = 1 << 20
BF16 = jnp.bfloat16
F32 = jnp.float32
LOG2E = 1.4426950408889634
TOP = 2


def vmem(shape):
    return pl.BlockSpec(shape, lambda *_: (0,) * len(shape))


def attention_kernel(x_ref, out_ref, *, block):
    n_src, _, rows, lanes = x_ref.shape
    length = n_src * rows
    keys = x_ref[:, 1].reshape(length, lanes)
    values = x_ref[:, 2].reshape(length, lanes)
    wide = jnp.concatenate([values, jnp.ones((length, lanes), BF16)], axis=1)
    lane = lax.broadcasted_iota(jnp.int32, (1, lanes), 1)
    first = lane < HD
    scale = float(HD) ** (-0.5) * LOG2E
    per = block // rows
    for i in range(length // block):
        query = x_ref[i * per : (i + 1) * per, 0].reshape(block, lanes)
        parts = []
        for head in range(2):
            mine = jnp.where(first if head == 0 else ~first, query, jnp.zeros_like(query))
            scores = lax.dot_general(
                mine, keys, (((1,), (1,)), ((), ())), preferred_element_type=F32
            )
            top = jnp.max(scores, axis=1, keepdims=True)
            weights = jnp.exp2((scores - top) * scale).astype(BF16)
            both = jnp.dot(weights, wide, preferred_element_type=F32)
            parts.append(both[:, :lanes] / both[:, lanes:])
        context = jnp.where(first, parts[0], parts[1]).astype(BF16)
        out_ref[i * per : (i + 1) * per] = context.reshape(per, rows, lanes)


def attention(arrived):
    n_src, three, rows, width = arrived.shape
    return pl.pallas_call(
        functools.partial(attention_kernel, block=2 * rows),
        grid=(width // LANES,),
        in_specs=[pl.BlockSpec((n_src, three, rows, LANES), lambda i: (0, 0, 0, i))],
        out_specs=pl.BlockSpec((n_src, rows, LANES), lambda i: (0, 0, i)),
        out_shape=jax.ShapeDtypeStruct((n_src, rows, width), BF16),
        compiler_params=pltpu.CompilerParams(vmem_limit_bytes=24 * MIB),
        name="attention",
    )(arrived)


def plan_kernel(info_ref, out_ref, *, n_exp, capacity):
    info = info_ref[...]
    tokens = info.shape[1]
    ids = info[:TOP].astype(jnp.int32)
    expert = lax.broadcasted_iota(jnp.int32, (n_exp, tokens), 0)
    named = [expert == ids[k : k + 1] for k in range(TOP)]
    member = sum(n.astype(F32) for n in named)
    before = (
        lax.broadcasted_iota(jnp.int32, (tokens, tokens), 0)
        < lax.broadcasted_iota(jnp.int32, (tokens, tokens), 1)
    ).astype(F32)
    rank = jnp.dot(member.astype(BF16), before.astype(BF16), preferred_element_type=F32)
    out_ref[...] = info
    for k, n in enumerate(named):
        slot = jnp.sum(jnp.where(n, rank, 0.0), axis=0, keepdims=True)
        out_ref[2 * TOP + k : 2 * TOP + k + 1] = info[k : k + 1] * capacity + slot


def plan(info, n_exp, capacity):
    return pl.pallas_call(
        functools.partial(plan_kernel, n_exp=n_exp, capacity=capacity),
        grid=(1,),
        in_specs=[vmem(info.shape)],
        out_specs=vmem(info.shape),
        out_shape=jax.ShapeDtypeStruct(info.shape, F32),
        compiler_params=pltpu.CompilerParams(vmem_limit_bytes=4 * MIB),
        name="plan",
    )(info)


def fill(normed, info, out_ref):
    rows = info[2 * TOP : 3 * TOP].astype(jnp.int32)
    at = lax.broadcasted_iota(jnp.int32, (out_ref.shape[0], normed.shape[0]), 0)
    pick = sum((at == rows[k : k + 1]).astype(F32) for k in range(TOP)).astype(BF16)
    out_ref[...] = jnp.dot(pick, normed, preferred_element_type=F32).astype(BF16)


def project_kernel(
    ctx_ref, w_hbm, stream_ref, info_ref, mid_ref, normed_ref, out_ref, w_ref, sems, *, cuts
):
    cols = w_ref.shape[1] // cuts
    copies = [
        pltpu.make_async_copy(
            w_hbm.at[:, pl.ds(i * cols, cols)], w_ref.at[:, pl.ds(i * cols, cols)], sems.at[i]
        )
        for i in range(cuts)
    ]
    for copy in copies:
        copy.start()
    merged = jnp.concatenate([ctx_ref[s] for s in range(ctx_ref.shape[0])], axis=1)
    for i, copy in enumerate(copies):
        copy.wait()
        here = slice(i * cols, (i + 1) * cols)
        mid_ref[:, here] = stream_ref[:, here].astype(F32) + jnp.dot(
            merged, w_ref[:, here], preferred_element_type=F32
        )
    mid = mid_ref[...]
    factor = lax.rsqrt(jnp.mean(mid * mid, axis=1, keepdims=True) + 1e-06)
    normed = (mid * factor).astype(BF16)
    normed_ref[...] = normed
    fill(normed, info_ref[...], out_ref)


def project(merged, w_out, stream, info, slots):
    rows, width = stream.shape
    cuts = 4
    return pl.pallas_call(
        functools.partial(project_kernel, cuts=cuts),
        grid=(1,),
        in_specs=[
            vmem(merged.shape),
            pl.BlockSpec(memory_space=pltpu.HBM),
            vmem(stream.shape),
            vmem(info.shape),
        ],
        out_specs=[vmem((rows, width))] * 2 + [vmem((slots, width))],
        out_shape=[
            pltpu.HBM((rows, width), F32),
            jax.ShapeDtypeStruct((rows, width), BF16),
            jax.ShapeDtypeStruct((slots, width), BF16),
        ],
        scratch_shapes=[
            pltpu.VMEM(w_out.shape, BF16),
            pltpu.SemaphoreType.DMA((cuts,)),
        ],
        compiler_params=pltpu.CompilerParams(vmem_limit_bytes=32 * MIB),
        name="project",
    )(merged, in_hbm(w_out), stream, info)


def route_kernel(normed_ref, info_ref, out_ref):
    fill(normed_ref[...], info_ref[...], out_ref)


def route(normed, info, slots):
    rows, width = normed.shape
    return pl.pallas_call(
        route_kernel,
        grid=(1,),
        in_specs=[vmem(normed.shape), vmem(info.shape)],
        out_specs=vmem((slots, width)),
        out_shape=jax.ShapeDtypeStruct((slots, width), BF16),
        compiler_params=pltpu.CompilerParams(vmem_limit_bytes=16 * MIB),
        name="route",
    )(normed, info)


def expert_kernel(*refs, n_in, block):
    x_refs, w_refs = refs[:n_in], refs[n_in : n_in + 6]
    *out_refs, rows_ref, hidden_ref, gate_ref, up_ref, down_ref, x_sems, w_sems = refs[
        n_in + 6 :
    ]
    share = w_refs[0].shape[1]
    per = share // block

    def weight_copies(i):
        gate, up, down = w_refs[:3] if i < per else w_refs[3:]
        there, here = pl.ds(i % per * block, block), pl.ds(i * block, block)
        return (
            pltpu.make_async_copy(gate.at[:, there], gate_ref.at[:, here], w_sems.at[i, 0]),
            pltpu.make_async_copy(up.at[:, there], up_ref.at[:, here], w_sems.at[i, 1]),
            pltpu.make_async_copy(down.at[there], down_ref.at[here], w_sems.at[i, 2]),
        )

    row_copies, start = [], 0
    for i, ref in enumerate(x_refs):
        here = pl.ds(start, ref.shape[0])
        row_copies.append(pltpu.make_async_copy(ref, rows_ref.at[here], x_sems.at[i]))
        start += ref.shape[0]
    copies = [weight_copies(i) for i in range(2 * per)]
    for copy in (*row_copies, *copies[0], *copies[1]):
        copy.start()
    for copy in row_copies:
        copy.wait()
    rows = rows_ref[...]
    for i in range(2 * per):
        here = slice(i * block, (i + 1) * block)
        copies[i][0].wait()
        copies[i][1].wait()
        if i + 2 < 2 * per:
            for copy in copies[i + 2]:
                copy.start()
        gate = jnp.dot(rows, gate_ref[:, here], preferred_element_type=F32)
        up = jnp.dot(rows, up_ref[:, here], preferred_element_type=F32)
        half = 0.5 * gate
        hidden_ref[:, here] = ((half + half * jnp.tanh(half)) * up).astype(BF16)
    for copy in copies:
        copy[2].wait()
    total = jnp.dot(hidden_ref[...], down_ref[...], preferred_element_type=F32)
    start = 0
    for ref in out_refs:
        ref[...] = total[start : start + ref.shape[0]].astype(BF16)
        start += ref.shape[0]


def in_hbm(x):
    return pltpu.with_memory_space_constraint(x, pltpu.HBM)


def experts(arrays, mine, other):
    width = arrays[0].shape[1]
    hidden = 2 * mine[0].shape[1]
    total = sum(x.shape[0] for x in arrays)
    block = 256
    return pl.pallas_call(
        functools.partial(expert_kernel, n_in=len(arrays), block=block),
        grid=(1,),
        in_specs=[pl.BlockSpec(memory_space=pl.ANY)] * len(arrays)
        + [pl.BlockSpec(memory_space=pltpu.HBM)] * 6,
        out_specs=[vmem(x.shape) for x in arrays],
        out_shape=[pltpu.HBM(x.shape, BF16) for x in arrays],
        scratch_shapes=[
            pltpu.VMEM((total, width), BF16),
            pltpu.VMEM((total, hidden), BF16),
            pltpu.VMEM((width, hidden), BF16),
            pltpu.VMEM((width, hidden), BF16),
            pltpu.VMEM((hidden, width), BF16),
            pltpu.SemaphoreType.DMA((len(arrays),)),
            pltpu.SemaphoreType.DMA((hidden // block, 3)),
        ],
        compiler_params=pltpu.CompilerParams(vmem_limit_bytes=44 * MIB),
        cost_estimate=pl.CostEstimate(
            flops=600 * total * width * hidden,
            bytes_accessed=6 * width * hidden + 4 * total * width,
            transcendentals=total * hidden,
        ),
        name="experts",
    )(*arrays, *(in_hbm(w) for w in (*mine, *other)))


def combine_kernel(info_ref, back_ref, *refs, cuts):
    by_token = info_ref[...].T
    rows = by_token[:, 2 * TOP : 3 * TOP].astype(jnp.int32)
    at = lax.broadcasted_iota(jnp.int32, (rows.shape[0], back_ref.shape[0]), 1)
    picks = [(at == rows[:, k : k + 1]).astype(F32).astype(BF16) for k in range(TOP)]
    gates = [by_token[:, TOP + k : TOP + k + 1] for k in range(TOP)]
    if len(refs) > 1:
        far_ref, mid_hbm, out_ref, mid_ref, sem = refs
        copy = pltpu.make_async_copy(mid_hbm, mid_ref, sem)
        copy.start()
    else:
        [out_ref], copy = refs, None
    cols = out_ref.shape[1] // cuts
    for i in range(cuts):
        here = slice(i * cols, (i + 1) * cols)
        back = back_ref[:, here]
        terms = [
            jnp.dot(pick, back, preferred_element_type=F32) * gate
            for pick, gate in zip(picks, gates, strict=True)
        ]
        total = sum(terms[1:], terms[0])
        if copy is not None:
            if i == 0:
                copy.wait()
            total = mid_ref[:, here] + far_ref[:, here].astype(F32) + total
        out_ref[:, here] = total.astype(BF16)


def combine(info, back, mid=None, far=None):
    rows, width = info.shape[1], back.shape[1]
    held = pl.BlockSpec(memory_space=pltpu.VMEM)
    final = mid is not None
    return pl.pallas_call(
        functools.partial(combine_kernel, cuts=4),
        in_specs=[held] * (3 if final else 2)
        + [pl.BlockSpec(memory_space=pltpu.HBM)] * final,
        out_specs=held,
        out_shape=jax.ShapeDtypeStruct((rows, width), BF16),
        scratch_shapes=[pltpu.VMEM((rows, width), F32), pltpu.SemaphoreType.DMA(())] * final,
        compiler_params=pltpu.CompilerParams(vmem_limit_bytes=16 * MIB),
        name="combine",
    )(info, back, *([far, in_hbm(mid)] if final else []))


def spread_kernel(x_ref, out_ref):
    part = out_ref.shape[3]
    for i in range(out_ref.shape[0]):
        out_ref[i] = x_ref[:, :, i * part : (i + 1) * part]


def spread(qkv, n_seq):
    three, rows, width = qkv.shape
    part = width // n_seq
    return pl.pallas_call(
        spread_kernel,
        grid=(three,),
        in_specs=[pl.BlockSpec((1, rows, width), lambda i: (i, 0, 0))],
        out_specs=pl.BlockSpec((n_seq, 1, rows, part), lambda i: (0, i, 0, 0)),
        out_shape=jax.ShapeDtypeStruct((n_seq, three, rows, part), BF16),
        compiler_params=pltpu.CompilerParams(vmem_limit_bytes=8 * MIB),
        name="spread",
    )(in_hbm(qkv))


def total_kernel(own_ref, *refs):
    *in_refs, out_ref = refs
    start = 0
    for up_ref, down_ref in zip(in_refs[::2], in_refs[1::2]):
        here = slice(start, start + up_ref.shape[0])
        total = own_ref[here].astype(F32) + up_ref[...].astype(F32) + down_ref[...].astype(F32)
        out_ref[here] = total.astype(BF16)
        start = here.stop


def add_up(own, pairs):
    arrays = [own, *(x for pair in pairs for x in pair)]
    rows, width = own.shape
    cols = 512
    return pl.pallas_call(
        total_kernel,
        grid=(width // cols,),
        in_specs=[pl.BlockSpec((x.shape[0], cols), lambda i: (0, i)) for x in arrays],
        out_specs=pl.BlockSpec((rows, cols), lambda i: (0, i)),
        out_shape=pltpu.HBM((rows, width), BF16),
        compiler_params=pltpu.CompilerParams(vmem_limit_bytes=16 * MIB),
        name="add_up",
    )(*arrays)


def per_device(stream_in, qkv_heads, expert_ids, gate_weights, w_out, w_gate, w_up, w_down):
    rows, width = stream_in.shape[1:]
    seq, exp = ("y", "core"), ("z", "x")
    n_y, n_seq, n_exp = lax.axis_size("y"), lax.axis_size(seq), lax.axis_size(exp)
    capacity = 3 * TOP * rows // (2 * n_exp)
    slots = n_exp * capacity

    def swap(x):
        return lax.ppermute(x, "core", [(0, 1), (1, 0)])

    def shift(x, by):
        return lax.ppermute(x, "y", [(i, (i + by) % n_y) for i in range(n_y)])

    def exchange(x):
        return lax.all_to_all(x, exp, split_axis=0, concat_axis=0, tiled=True)

    mine = [w[0] for w in (w_gate, w_up, w_down)]
    other = [swap(w) for w in mine]
    info = jnp.concatenate(
        [expert_ids[0].T.astype(F32), gate_weights[0].T, jnp.zeros((8 - 2 * TOP, rows), F32)]
    )
    info = plan(info, n_exp, capacity)
    info_far = shift(info, 2)
    qkv = spread(qkv_heads[0].transpose(1, 0, 2), n_seq)
    arrived = lax.all_to_all(qkv, seq, split_axis=0, concat_axis=0, tiled=True)
    context = attention(arrived)
    context, info_far, other = lax.optimization_barrier((context, info_far, other))
    merged = lax.all_to_all(context, seq, split_axis=0, concat_axis=0, tiled=True)
    mid, normed, buffer = project(merged, w_out, stream_in[0], info, slots)

    tie = lax.optimization_barrier
    far_tokens = shift(normed, 2)
    far_buffer = route(far_tokens, info_far, slots)
    own = exchange(buffer)
    quarter = own.shape[0] // 4
    bounds = (0, quarter, quarter + 3 * quarter // 2, 4 * quarter)
    parts = [own[i:j] for i, j in zip(bounds[:-1], bounds[1:], strict=True)]
    ups = [shift(x, 1) for x in parts]
    downs = [shift(x, -1) for x in parts]

    def near(i):
        return experts([ups[i], downs[i]], mine, other)

    [own_part] = experts([own], mine, other)
    ups[0], downs[0], own_part, far_buffer = tie((ups[0], downs[0], own_part, far_buffer))
    far_rows = exchange(far_buffer)
    back0 = near(0)
    ups[1], downs[1], back0 = tie((ups[1], downs[1], back0))
    back1 = near(1)
    far_rows, back1 = tie((far_rows, back1))
    [far_part] = experts([far_rows], mine, other)
    ups[2], downs[2], far_part = tie((ups[2], downs[2], far_part))
    back2 = near(2)
    far_back = exchange(far_part)
    far_sum = combine(info_far, far_back)
    total = add_up(own_part, [(shift(u, -1), shift(d, 1)) for u, d in (back0, back1, back2)])
    total, far_back = tie((total, far_back))
    back = exchange(total)
    far_home = shift(far_sum, 2)
    return combine(info, back, mid, far_home)[None]


def solution(mesh):
    split = Mesh(mesh.devices.reshape(-1, 2, 4, 4), ("y", "core", "z", "x"))
    seq, exp = ("y", "core"), ("z", "x")
    in_specs = (
        P(exp, seq, None),
        P(exp, seq, None, None),
        P(exp, seq, None),
        P(exp, seq, None),
        P(),
        P(exp, None, seq),
        P(exp, None, seq),
        P(exp, seq, None),
    )
    return jax.shard_map(
        per_device, mesh=split, in_specs=in_specs, out_specs=P(exp, seq, None), check_vma=False
    )
```

time: 255 us -> 215 us (0.84)
  Pallas kernels: 110 us -> 70.9 us
  waiting for transfers between devices: 82.4 us -> 73.6 us
  starting transfers between devices: 47.5 us -> 52.2 us
    pallas_call x5 -> x6, Pallas kernels: 63.2 us -> 16 us  [the longest x1 5.82 us: project(): pl.pallas_call(functools.partial(project_kernel, cuts=cuts), grid=(1,), i...]
    ppermute x11 -> x15, waiting for transfers between devices: 52 us -> 43.9 us  [shift(): return lax.ppermute(x, 'y', [(i, (i + by) % n_y) for i in range(n_y)])]
    pallas_call x4 -> x5, Pallas kernels: 38.1 us -> 44.8 us  [experts(): pl.pallas_call(functools.partial(expert_kernel, n_in=len(arrays), block=b...]
    ppermute x11 -> x15, starting transfers between devices: 13.1 us -> 18.8 us  [shift(): return lax.ppermute(x, 'y', [(i, (i + by) % n_y) for i in range(n_y)])]
  transfers between devices with their start and end apart: 19 -> 23, of which waited for: 11 -> 7; matrix products, arithmetic and copies ran while one was open for 0% -> 1% of each run, Pallas kernels for 38% -> 29%
where the time goes in v4:
time: 215 us; the launch traced here: 212 us
  waiting for transfers between devices  73.6 us (34%)
  Pallas kernels  70.9 us (33%)
  starting transfers between devices  52.2 us (24%)
  blocking collectives  12.8 us (6%)
    pallas_call x5, Pallas kernels, experts(): pl.pallas_call(functools.partial(expert_kernel, n_in=len(arrays), block=b...  44.8 us
    ppermute x15, waiting for transfers between devices, shift(): return lax.ppermute(x, 'y', [(i, (i + by) % n_y) for i in range(n_y)])  43.9 us
    all_to_all x4, starting transfers between devices, exchange(): return lax.all_to_all(x, exp, split_axis=0, concat_axis=0, tiled=True)  28.2 us
    ppermute x15, starting transfers between devices, shift(): return lax.ppermute(x, 'y', [(i, (i + by) % n_y) for i in range(n_y)])  18.8 us
    all_to_all x1, waiting for transfers between devices, per_device(): arrived = lax.all_to_all(qkv, seq, split_axis=0, concat_axis=0, tiled=True)  17.7 us
    all_to_all x1, blocking collectives, per_device(): lax.all_to_all(context, seq, split_axis=0, concat_axis=0, tiled=True)  12.8 us
    all_to_all x4, waiting for transfers between devices, exchange(): return lax.all_to_all(x, exp, split_axis=0, concat_axis=0, tiled=True)  12 us
    pallas_call x1, Pallas kernels, attention(): pl.pallas_call(functools.partial(attention_kernel, block=2 * rows), grid=...  6.03 us
  transfers between devices with their start and end apart: 23, of which 7 were waited for; matrix products, arithmetic and copies ran while one was open for 1% of the time, Pallas kernels for 29%

profile of v4, /device:TPU:2, one launch (start us, length us, event | category | flops | bytes accessed | tf_op | source)
XLA Modules:
  0.0 212.0 jit_solution(5504422971427395939)
XLA Ops:
  0.0 0.0 collective-permute-start.1
  0.0 0.5 collective-permute-start.2
  0.5 0.0 collective-permute-start.3
  0.5 3.4 %spread.1 = bf16[8,3,128,256]{3,2,1,0:T(8,128)(2,1)} custom-call(bf16[3,128,2048]{2,1,0:T(8,128)(2,1)} %bitcast.30), custom_call_target="tpu_custom_call" | custom-call | tf_op jit(solution)/shard_map/spread/pallas_call | solution.py:306
  3.9 4.7 %all-to-all-start = ((bf16[8,3,128,256]{3,2,1,0:T(8,128)(2,1)}), bf16[8,3,128,256]{3,2,1,0:T(8,128)(2,1)S(1)}, u32[]{:S(2)}, u32[]{:S(2)}) async-start(bf16[8,3,128,256]{3,2,1,0:T(8,128)(2,1)} %spread.1), calls=%async_computation | async-start | bytes 3145728 | tf_op jit(solution)/shard_map/all_to_all | solution.py:366
  8.6 0.1 pad.2.clone
  8.7 0.1 maximum_maximum_fusion.info_ref
  8.8 0.1 plan.1.info_ref
  8.9 3.6 %collective-permute-start = (f32[8,128]{1,0:T(8,128)S(1)}, f32[8,128]{1,0:T(8,128)S(1)}, u32[]{:S(2)}, u32[]{:S(2)}) collective-permute-start(f32[8,128]{1,0:T(8,128)S(1)} %plan.1.info_ref), channel_id=1, source_target_pairs={{0,64},{32,96},{64,0},{96,32},{1,65},{33,97},{65,1},{97,33},{2,66}... | collective-permute-start | bytes 12296 | tf_op jit(solution)/shard_map/ppermute | solution.py:353
  12.5 17.7 %all-to-all-done.x_ref = bf16[8,3,128,256]{3,2,1,0:T(8,128)(2,1)S(1)} async-done(((bf16[8,3,128,256]{3,2,1,0:T(8,128)(2,1)}), bf16[8,3,128,256]{3,2,1,0:T(8,128)(2,1)S(1)}, u32[]{:S(2)}, u32[]{:S(2)}) %all-to-all-start) | async-done | bytes 1572896 | tf_op jit(solution)/shard_map/all_to_all | solution.py:366
  30.2 6.0 %attention.1 = bf16[8,128,256]{2,1,0:T(8,128)(2,1)S(1)} custom-call(bf16[8,3,128,256]{3,2,1,0:T(8,128)(2,1)S(1)} %all-to-all-done.x_ref), custom_call_target="tpu_custom_call" | custom-call | tf_op jit(solution)/shard_map/attention/pallas_call | solution.py:52
  36.3 0.0 collective-permute-done.info_ref
  36.3 0.0 collective-permute-done.1.refs_4_.refs_5_
  36.3 0.0 collective-permute-done.2.refs_5_.refs_6_
  36.3 0.0 collective-permute-done.3.refs_6_.refs_7_
  36.3 12.8 %all_to_all.55.ctx_ref = bf16[8,128,256]{2,1,0:T(8,128)(2,1)S(1)} all-to-all(bf16[8,128,256]{2,1,0:T(8,128)(2,1)S(1)} %attention.1), channel_id=1, replica_groups=mesh['y'=4,'core'=2,'z'=4,'x'=4] {'y','core'}, dimensions={0} | all-to-all | bytes 1048576 | tf_op jit(solution)/shard_map/all_to_all | solution.py:369
  49.1 5.8 %project.1 = (f32[128,2048]{1,0:T(8,128)}, bf16[128,2048]{1,0:T(8,128)(2,1)S(1)}, bf16[384,2048]{1,0:T(8,128)(2,1)}) custom-call(bf16[8,128,256]{2,1,0:T(8,128)(2,1)S(1)} %all_to_all.55.ctx_ref, bf16[2048,2048]{1,0:T(8,128)(2,1)} %w_hbm.1, bf16[128,2048]{1,0:T(8,128)(2,1)S(1)} %bitcast.28, f32[8,128]{1,0:T(8,128)S(1)} %plan.1.info_ref), custom_call_target="tpu_custom_call" | custom-call | tf_op jit(solution)/shard_map/project/pallas_call | solution.py:129
  54.9 8.3 %all-to-all-start.2 = ((bf16[16,24,2048]{2,1,0:T(8,128)(2,1)}), bf16[16,24,2048]{2,1,0:T(8,128)(2,1)S(1)}, u32[]{:S(2)}, u32[]{:S(2)}) async-start(bf16[16,24,2048]{2,1,0:T(8,128)(2,1)} %bitcast.10), calls=%async_computation.2 | async-start | bytes 3145728 | tf_op jit(solution)/shard_map/all_to_all | solution.py:356
  63.3 0.3 collective-permute-start.6
  63.6 13.9 %collective-permute-done.6.normed_ref = bf16[128,2048]{1,0:T(8,128)(2,1)S(1)} collective-permute-done((bf16[128,2048]{1,0:T(8,128)(2,1)S(1)}, bf16[128,2048]{1,0:T(8,128)(2,1)S(1)}, u32[]{:S(2)}, u32[]{:S(2)}) %collective-permute-start.6) | collective-permute-done | bytes 524320 | tf_op jit(solution)/shard_map/ppermute | solution.py:353
  77.5 1.8 route.1
  79.3 5.1 %all-to-all-done.2 = bf16[16,24,2048]{2,1,0:T(8,128)(2,1)S(1)} async-done(((bf16[16,24,2048]{2,1,0:T(8,128)(2,1)}), bf16[16,24,2048]{2,1,0:T(8,128)(2,1)S(1)}, u32[]{:S(2)}, u32[]{:S(2)}) %all-to-all-start.2) | async-done | bytes 1572896 | tf_op jit(solution)/shard_map/all_to_all | solution.py:356
  84.4 0.8 slice.24
  85.2 0.6 collective-permute-start.4
  85.8 2.7 %collective-permute-start.5 = (bf16[96,2048]{1,0:T(8,128)(2,1)}, bf16[96,2048]{1,0:T(8,128)(2,1)}, u32[]{:S(2)}, u32[]{:S(2)}) collective-permute-start(bf16[96,2048]{1,0:T(8,128)(2,1)} %bitcast.11), channel_id=1, source_target_pairs={{0,96},{32,0},{64,32},{96,64},{1,97},{33,1},{65,33},{97,65},{2,98}... | collective-permute-start | bytes 1179656 | tf_op jit(solution)/shard_map/ppermute | solution.py:353
  88.4 1.1 fusion
  89.6 0.0 collective-permute-start.7
  89.6 3.2 %collective-permute-start.8 = (bf16[144,2048]{1,0:T(8,128)(2,1)}, bf16[144,2048]{1,0:T(8,128)(2,1)}, u32[]{:S(2)}, u32[]{:S(2)}) collective-permute-start(bf16[144,2048]{1,0:T(8,128)(2,1)} %bitcast.13), channel_id=1, source_target_pairs={{0,96},{32,0},{64,32},{96,64},{1,97},{33,1},{65,33},{97,65},{2,98}... | collective-permute-start | bytes 1769480 | tf_op jit(solution)/shard_map/ppermute | solution.py:353
  92.8 0.0 collective-permute-start.13
  92.8 8.8 %experts.5.own_ref = bf16[384,2048]{1,0:T(8,128)(2,1)} custom-call(bf16[384,2048]{1,0:T(8,128)(2,1)S(1)} %bitcast.26, bf16[2048,512]{1,0:T(8,128)(2,1)} %bitcast.34, bf16[2048,512]{1,0:T(8,128)(2,1)} %bitcast.40, bf16[512,2048]{1,0:T(8,128)(2,1)} %bitcast.46, bf16[2048,512]{1,0:T(8,128)(2,1)} %collective-permute-done.1.refs_4_.refs_5_, ...), custom_call_target="tpu_custom_call" | custom-call | flops 483183820800 | bytes 15728640 | tf_op jit(solution)/shard_map/experts/pallas_call | solution.py:227
  101.6 0.0 collective-permute-done.4.refs_0_
  101.6 3.3 %collective-permute-start.14 = (bf16[144,2048]{1,0:T(8,128)(2,1)}, bf16[144,2048]{1,0:T(8,128)(2,1)}, u32[]{:S(2)}, u32[]{:S(2)}) collective-permute-start(bf16[144,2048]{1,0:T(8,128)(2,1)} %bitcast.16), channel_id=1, source_target_pairs={{0,96},{32,0},{64,32},{96,64},{1,97},{33,1},{65,33},{97,65},{2,98}... | collective-permute-start | bytes 1769480 | tf_op jit(solution)/shard_map/ppermute | solution.py:353
  104.9 0.0 collective-permute-done.5.refs_1_
  104.9 6.9 %all-to-all-start.3 = ((bf16[16,24,2048]{2,1,0:T(8,128)(2,1)}), bf16[16,24,2048]{2,1,0:T(8,128)(2,1)}, u32[]{:S(2)}, u32[]{:S(2)}) async-start(bf16[16,24,2048]{2,1,0:T(8,128)(2,1)} %bitcast.14), calls=%async_computation.3 | async-start | bytes 3145728 | tf_op jit(solution)/shard_map/all_to_all | solution.py:356
  111.8 7.9 %experts.6 = (bf16[96,2048]{1,0:T(8,128)(2,1)}, bf16[96,2048]{1,0:T(8,128)(2,1)}) custom-call(bf16[96,2048]{1,0:T(8,128)(2,1)} %collective-permute-done.4.refs_0_, bf16[96,2048]{1,0:T(8,128)(2,1)} %collective-permute-done.5.refs_1_, bf16[2048,512]{1,0:T(8,128)(2,1)} %bitcast.35, bf16[2048,512]{1,0:T(8,128)(2,1)} %bitcast.41, bf16[512,2048]{1,0:T(8,128)(2,1)} %bitcast.47, ...), custom_call_target="tpu_custom_call" | custom-call | flops 241591910400 | bytes 14155776 | tf_op jit(solution)/shard_map/experts/pallas_call | solution.py:227
  119.7 0.0 collective-permute-done.7.refs_0_
  119.7 0.0 collective-permute-done.8.refs_1_
  119.8 0.1 collective-permute-start.9
  119.9 8.9 %experts.7 = (bf16[144,2048]{1,0:T(8,128)(2,1)}, bf16[144,2048]{1,0:T(8,128)(2,1)}) custom-call(bf16[144,2048]{1,0:T(8,128)(2,1)} %collective-permute-done.7.refs_0_, bf16[144,2048]{1,0:T(8,128)(2,1)} %collective-permute-done.8.refs_1_, bf16[2048,512]{1,0:T(8,128)(2,1)} %bitcast.36, bf16[2048,512]{1,0:T(8,128)(2,1)} %bitcast.42, bf16[512,2048]{1,0:T(8,128)(2,1)} %bitcast.48, ...), custom_call_target="tpu_custom_call" | custom-call | flops 362387865600 | bytes 14942208 | tf_op jit(solution)/shard_map/experts/pallas_call | solution.py:227
  128.7 3.1 %all-to-all-done.3 = bf16[16,24,2048]{2,1,0:T(8,128)(2,1)} async-done(((bf16[16,24,2048]{2,1,0:T(8,128)(2,1)}), bf16[16,24,2048]{2,1,0:T(8,128)(2,1)}, u32[]{:S(2)}, u32[]{:S(2)}) %all-to-all-start.3) | async-done | bytes 1572896 | tf_op jit(solution)/shard_map/all_to_all | solution.py:356
  131.8 0.1 collective-permute-start.11
  131.9 1.9 collective-permute-start.12
  133.8 10.2 %experts.8 = bf16[384,2048]{1,0:T(8,128)(2,1)} custom-call(bf16[384,2048]{1,0:T(8,128)(2,1)} %bitcast.15.refs_0_, bf16[2048,512]{1,0:T(8,128)(2,1)} %bitcast.37, bf16[2048,512]{1,0:T(8,128)(2,1)} %bitcast.43, bf16[512,2048]{1,0:T(8,128)(2,1)} %bitcast.49, bf16[2048,512]{1,0:T(8,128)(2,1)} %collective-permute-done.1.refs_4_.refs_5_, ...), custom_call_target="tpu_custom_call" | custom-call | flops 483183820800 | bytes 15728640 | tf_op jit(solution)/shard_map/experts/pallas_call | solution.py:227
  144.0 0.0 collective-permute-done.13.refs_0_
  144.0 0.0 collective-permute-done.14.refs_1_
  144.1 5.7 %all-to-all-start.4 = ((bf16[16,24,2048]{2,1,0:T(8,128)(2,1)}), bf16[16,24,2048]{2,1,0:T(8,128)(2,1)}, u32[]{:S(2)}, u32[]{:S(2)}) async-start(bf16[16,24,2048]{2,1,0:T(8,128)(2,1)} %bitcast.31), calls=%async_computation.4 | async-start | bytes 3145728 | tf_op jit(solution)/shard_map/all_to_all | solution.py:356
  149.8 9.0 %experts.9 = (bf16[144,2048]{1,0:T(8,128)(2,1)}, bf16[144,2048]{1,0:T(8,128)(2,1)}) custom-call(bf16[144,2048]{1,0:T(8,128)(2,1)} %collective-permute-done.13.refs_0_, bf16[144,2048]{1,0:T(8,128)(2,1)} %collective-permute-done.14.refs_1_, bf16[2048,512]{1,0:T(8,128)(2,1)} %bitcast.38, bf16[2048,512]{1,0:T(8,128)(2,1)} %bitcast.44, ...), custom_call_target="tpu_custom_call" | custom-call | flops 362387865600 | bytes 14942208 | tf_op jit(solution)/shard_map/experts/pallas_call | solution.py:227
  158.8 1.6 collective-permute-start.15
  160.4 0.5 collective-permute-start.16
  160.9 0.0 collective-permute-done.9.refs_0_
  160.9 0.8 collective-permute-start.10
  161.7 19.3 %collective-permute-done.10.refs_1_ = bf16[96,2048]{1,0:T(8,128)(2,1)S(1)} collective-permute-done((bf16[96,2048]{1,0:T(8,128)(2,1)S(1)}, bf16[96,2048]{1,0:T(8,128)(2,1)S(1)}, u32[]{:S(2)}, u32[]{:S(2)}) %collective-permute-start.10) | collective-permute-done | bytes 393248 | tf_op jit(solution)/shard_map/ppermute | solution.py:353
  181.0 0.0 collective-permute-done.11.refs_2_
  181.0 0.0 collective-permute-done.12.refs_3_
  181.0 0.0 collective-permute-done.15.refs_4_
  181.0 0.0 collective-permute-done.16.refs_5_
  181.0 4.1 %add_up.1 = bf16[384,2048]{1,0:T(8,128)(2,1)} custom-call(bf16[384,2048]{1,0:T(8,128)(2,1)S(1)} %copy-done, bf16[96,2048]{1,0:T(8,128)(2,1)} %collective-permute-done.9.refs_0_, bf16[96,2048]{1,0:T(8,128)(2,1)S(1)} %collective-permute-done.10.refs_1_, bf16[144,2048]{1,0:T(8,128)(2,1)} %collective-permute-done.11.refs_2_, ...), custom_call_target="tpu_custom_call" | custom-call | tf_op jit(solution)/shard_map/add_up/pallas_call | solution.py:331
  185.1 0.0 all-to-all-done.4
  185.1 7.2 %all-to-all-start.5 = ((bf16[16,24,2048]{2,1,0:T(8,128)(2,1)}), bf16[16,24,2048]{2,1,0:T(8,128)(2,1)S(1)}, u32[]{:S(2)}, u32[]{:S(2)}) async-start(bf16[16,24,2048]{2,1,0:T(8,128)(2,1)} %bitcast.29), calls=%async_computation.5 | async-start | bytes 3145728 | tf_op jit(solution)/shard_map/all_to_all | solution.py:356
  192.4 2.2 %combine.2 = bf16[128,2048]{1,0:T(8,128)(2,1)S(1)} custom-call(f32[8,128]{1,0:T(8,128)S(1)} %collective-permute-done.info_ref, bf16[384,2048]{1,0:T(8,128)(2,1)} %bitcast.18.back_ref), custom_call_target="tpu_custom_call" | custom-call | tf_op jit(solution)/shard_map/combine/pallas_call | solution.py:285
  194.6 0.1 collective-permute-start.17
  194.7 10.7 %collective-permute-done.17.refs_0_ = bf16[128,2048]{1,0:T(8,128)(2,1)S(1)} collective-permute-done((bf16[128,2048]{1,0:T(8,128)(2,1)S(1)}, bf16[128,2048]{1,0:T(8,128)(2,1)S(1)}, u32[]{:S(2)}, u32[]{:S(2)}) %collective-permute-start.17) | collective-permute-done | bytes 524320 | tf_op jit(solution)/shard_map/ppermute | solution.py:353
  205.4 3.8 %all-to-all-done.5 = bf16[16,24,2048]{2,1,0:T(8,128)(2,1)S(1)} async-done(((bf16[16,24,2048]{2,1,0:T(8,128)(2,1)}), bf16[16,24,2048]{2,1,0:T(8,128)(2,1)S(1)}, u32[]{:S(2)}, u32[]{:S(2)}) %all-to-all-start.5) | async-done | bytes 1572896 | tf_op jit(solution)/shard_map/all_to_all | solution.py:356
  209.1 2.7 %combine.3 = bf16[128,2048]{1,0:T(8,128)(2,1)} custom-call(f32[8,128]{1,0:T(8,128)S(1)} %plan.1.info_ref, bf16[384,2048]{1,0:T(8,128)(2,1)S(1)} %bitcast.27, bf16[128,2048]{1,0:T(8,128)(2,1)S(1)} %collective-permute-done.17.refs_0_, f32[128,2048]{1,0:T(8,128)} %get-tuple-element.62.refs_1_), custom_call_target="tpu_custom_call" | custom-call | tf_op jit(solution)/shard_map/combine/pallas_call | solution.py:285
  (12 shorter events, 0.0 us)
Async XLA Ops:
  0.0 36.3 %collective-permute-start.1 = (bf16[2048,512]{1,0:T(8,128)(2,1)}, bf16[2048,512]{1,0:T(8,128)(2,1)}, u32[]{:S(2)}, u32[]{:S(2)}) collective-permute-start(bf16[2048,512]{1,0:T(8,128)(2,1)} %bitcast.33), channel_id=1, source_target_pairs={{0,16},{16,0},{1,17},{17,1},{2,18},{18,2},{3,19},{19,3},{4,20},{20... | collective-permute-start | bytes 6291464 | tf_op jit(solution)/shard_map/ppermute | solution.py:350
  0.0 36.3 %collective-permute-start.2 = (bf16[2048,512]{1,0:T(8,128)(2,1)}, bf16[2048,512]{1,0:T(8,128)(2,1)}, u32[]{:S(2)}, u32[]{:S(2)}) collective-permute-start(bf16[2048,512]{1,0:T(8,128)(2,1)} %bitcast.39), channel_id=1, source_target_pairs={{0,16},{16,0},{1,17},{17,1},{2,18},{18,2},{3,19},{19,3},{4,20},{20... | collective-permute-start | bytes 6291464 | tf_op jit(solution)/shard_map/ppermute | solution.py:350
  0.5 35.8 %collective-permute-start.3 = (bf16[512,2048]{1,0:T(8,128)(2,1)}, bf16[512,2048]{1,0:T(8,128)(2,1)}, u32[]{:S(2)}, u32[]{:S(2)}) collective-permute-start(bf16[512,2048]{1,0:T(8,128)(2,1)} %bitcast.45), channel_id=1, source_target_pairs={{0,16},{16,0},{1,17},{17,1},{2,18},{18,2},{3,19},{19,3},{4,20},{20... | collective-permute-start | bytes 6291464 | tf_op jit(solution)/shard_map/ppermute | solution.py:350
  3.9 4.8 %copy-start.2 = (s32[1,128,2]{1,2,0:T(2,128)S(1)}, s32[1,128,2]{1,2,0:T(2,128)}, u32[]{:S(2)}) copy-start(s32[1,128,2]{1,2,0:T(2,128)} %param.10) | copy-start | bytes 3076
  3.9 4.8 %copy-start.3 = (f32[1,128,2]{1,2,0:T(2,128)S(1)}, f32[1,128,2]{1,2,0:T(2,128)}, u32[]{:S(2)}) copy-start(f32[1,128,2]{1,2,0:T(2,128)} %param.11) | copy-start | bytes 3076
  3.9 26.3 %all-to-all-start = ((bf16[8,3,128,256]{3,2,1,0:T(8,128)(2,1)}), bf16[8,3,128,256]{3,2,1,0:T(8,128)(2,1)S(1)}, u32[]{:S(2)}, u32[]{:S(2)}) async-start(bf16[8,3,128,256]{3,2,1,0:T(8,128)(2,1)} %spread.1), calls=%async_computation | async-start | bytes 3145728 | tf_op jit(solution)/shard_map/all_to_all | solution.py:366
  8.9 40.2 %copy-start.1 = (bf16[1,128,2048]{2,1,0:T(8,128)(2,1)S(1)}, bf16[1,128,2048]{2,1,0:T(8,128)(2,1)}, u32[]{:S(2)}) copy-start(bf16[1,128,2048]{2,1,0:T(8,128)(2,1)} %param.8) | copy-start | bytes 1572868
  8.9 27.4 %collective-permute-start = (f32[8,128]{1,0:T(8,128)S(1)}, f32[8,128]{1,0:T(8,128)S(1)}, u32[]{:S(2)}, u32[]{:S(2)}) collective-permute-start(f32[8,128]{1,0:T(8,128)S(1)} %plan.1.info_ref), channel_id=1, source_target_pairs={{0,64},{32,96},{64,0},{96,32},{1,65},{33,97},{65,1},{97,33},{2,66}... | collective-permute-start | bytes 12296 | tf_op jit(solution)/shard_map/ppermute | solution.py:353
  54.9 29.5 %all-to-all-start.2 = ((bf16[16,24,2048]{2,1,0:T(8,128)(2,1)}), bf16[16,24,2048]{2,1,0:T(8,128)(2,1)S(1)}, u32[]{:S(2)}, u32[]{:S(2)}) async-start(bf16[16,24,2048]{2,1,0:T(8,128)(2,1)} %bitcast.10), calls=%async_computation.2 | async-start | bytes 3145728 | tf_op jit(solution)/shard_map/all_to_all | solution.py:356
  63.3 14.2 %collective-permute-start.6 = (bf16[128,2048]{1,0:T(8,128)(2,1)S(1)}, bf16[128,2048]{1,0:T(8,128)(2,1)S(1)}, u32[]{:S(2)}, u32[]{:S(2)}) collective-permute-start(bf16[128,2048]{1,0:T(8,128)(2,1)S(1)} %get-tuple-element.39), channel_id=1, source_target_pairs={{0,64},{32,96},{64,0},{96,32},{1,65},{33,97},{65,1},{97,33},{2,66}... | collective-permute-start | bytes 1572872 | tf_op jit(solution)/shard_map/ppermute | solution.py:353
  85.2 16.4 %collective-permute-start.4 = (bf16[96,2048]{1,0:T(8,128)(2,1)}, bf16[96,2048]{1,0:T(8,128)(2,1)}, u32[]{:S(2)}, u32[]{:S(2)}) collective-permute-start(bf16[96,2048]{1,0:T(8,128)(2,1)} %bitcast.11), channel_id=1, source_target_pairs={{0,32},{32,64},{64,96},{96,0},{1,33},{33,65},{65,97},{97,1},{2,34}... | collective-permute-start | bytes 1179656 | tf_op jit(solution)/shard_map/ppermute | solution.py:353
  85.8 19.2 %collective-permute-start.5 = (bf16[96,2048]{1,0:T(8,128)(2,1)}, bf16[96,2048]{1,0:T(8,128)(2,1)}, u32[]{:S(2)}, u32[]{:S(2)}) collective-permute-start(bf16[96,2048]{1,0:T(8,128)(2,1)} %bitcast.11), channel_id=1, source_target_pairs={{0,96},{32,0},{64,32},{96,64},{1,97},{33,1},{65,33},{97,65},{2,98}... | collective-permute-start | bytes 1179656 | tf_op jit(solution)/shard_map/ppermute | solution.py:353
  89.6 30.2 %collective-permute-start.7 = (bf16[144,2048]{1,0:T(8,128)(2,1)}, bf16[144,2048]{1,0:T(8,128)(2,1)}, u32[]{:S(2)}, u32[]{:S(2)}) collective-permute-start(bf16[144,2048]{1,0:T(8,128)(2,1)} %bitcast.13), channel_id=1, source_target_pairs={{0,32},{32,64},{64,96},{96,0},{1,33},{33,65},{65,97},{97,1},{2,34}... | collective-permute-start | bytes 1769480 | tf_op jit(solution)/shard_map/ppermute | solution.py:353
  89.6 30.2 %collective-permute-start.8 = (bf16[144,2048]{1,0:T(8,128)(2,1)}, bf16[144,2048]{1,0:T(8,128)(2,1)}, u32[]{:S(2)}, u32[]{:S(2)}) collective-permute-start(bf16[144,2048]{1,0:T(8,128)(2,1)} %bitcast.13), channel_id=1, source_target_pairs={{0,96},{32,0},{64,32},{96,64},{1,97},{33,1},{65,33},{97,65},{2,98}... | collective-permute-start | bytes 1769480 | tf_op jit(solution)/shard_map/ppermute | solution.py:353
  92.8 51.2 %collective-permute-start.13 = (bf16[144,2048]{1,0:T(8,128)(2,1)}, bf16[144,2048]{1,0:T(8,128)(2,1)}, u32[]{:S(2)}, u32[]{:S(2)}) collective-permute-start(bf16[144,2048]{1,0:T(8,128)(2,1)} %bitcast.16), channel_id=1, source_target_pairs={{0,32},{32,64},{64,96},{96,0},{1,33},{33,65},{65,97},{97,1},{2,34}... | collective-permute-start | bytes 1769480 | tf_op jit(solution)/shard_map/ppermute | solution.py:353
  101.6 42.4 %collective-permute-start.14 = (bf16[144,2048]{1,0:T(8,128)(2,1)}, bf16[144,2048]{1,0:T(8,128)(2,1)}, u32[]{:S(2)}, u32[]{:S(2)}) collective-permute-start(bf16[144,2048]{1,0:T(8,128)(2,1)} %bitcast.16), channel_id=1, source_target_pairs={{0,96},{32,0},{64,32},{96,64},{1,97},{33,1},{65,33},{97,65},{2,98}... | collective-permute-start | bytes 1769480 | tf_op jit(solution)/shard_map/ppermute | solution.py:353
  104.9 26.9 %all-to-all-start.3 = ((bf16[16,24,2048]{2,1,0:T(8,128)(2,1)}), bf16[16,24,2048]{2,1,0:T(8,128)(2,1)}, u32[]{:S(2)}, u32[]{:S(2)}) async-start(bf16[16,24,2048]{2,1,0:T(8,128)(2,1)} %bitcast.14), calls=%async_computation.3 | async-start | bytes 3145728 | tf_op jit(solution)/shard_map/all_to_all | solution.py:356
  119.8 41.1 %collective-permute-start.9 = (bf16[96,2048]{1,0:T(8,128)(2,1)}, bf16[96,2048]{1,0:T(8,128)(2,1)}, u32[]{:S(2)}, u32[]{:S(2)}) collective-permute-start(bf16[96,2048]{1,0:T(8,128)(2,1)} %get-tuple-element.46), channel_id=1, source_target_pairs={{0,96},{32,0},{64,32},{96,64},{1,97},{33,1},{65,33},{97,65},{2,98}... | collective-permute-start | bytes 1179656 | tf_op jit(solution)/shard_map/ppermute | solution.py:353
  131.8 49.2 %collective-permute-start.11 = (bf16[144,2048]{1,0:T(8,128)(2,1)}, bf16[144,2048]{1,0:T(8,128)(2,1)}, u32[]{:S(2)}, u32[]{:S(2)}) collective-permute-start(bf16[144,2048]{1,0:T(8,128)(2,1)} %get-tuple-element.53), channel_id=1, source_target_pairs={{0,96},{32,0},{64,32},{96,64},{1,97},{33,1},{65,33},{97,65},{2,98}... | collective-permute-start | bytes 1769480 | tf_op jit(solution)/shard_map/ppermute | solution.py:353
  131.9 49.1 %collective-permute-start.12 = (bf16[144,2048]{1,0:T(8,128)(2,1)}, bf16[144,2048]{1,0:T(8,128)(2,1)}, u32[]{:S(2)}, u32[]{:S(2)}) collective-permute-start(bf16[144,2048]{1,0:T(8,128)(2,1)} %get-tuple-element.54), channel_id=1, source_target_pairs={{0,32},{32,64},{64,96},{96,0},{1,33},{33,65},{65,97},{97,1},{2,34}... | collective-permute-start | bytes 1769480 | tf_op jit(solution)/shard_map/ppermute | solution.py:353
  144.1 41.1 %all-to-all-start.4 = ((bf16[16,24,2048]{2,1,0:T(8,128)(2,1)}), bf16[16,24,2048]{2,1,0:T(8,128)(2,1)}, u32[]{:S(2)}, u32[]{:S(2)}) async-start(bf16[16,24,2048]{2,1,0:T(8,128)(2,1)} %bitcast.31), calls=%async_computation.4 | async-start | bytes 3145728 | tf_op jit(solution)/shard_map/all_to_all | solution.py:356
  149.8 11.1 %copy-start.4 = (bf16[96,2048]{1,0:T(8,128)(2,1)S(1)}, bf16[96,2048]{1,0:T(8,128)(2,1)}, u32[]{:S(2)}) copy-start(bf16[96,2048]{1,0:T(8,128)(2,1)} %get-tuple-element.47) | copy-start | bytes 1179652
  149.8 31.3 %copy-start = (bf16[384,2048]{1,0:T(8,128)(2,1)S(1)}, bf16[384,2048]{1,0:T(8,128)(2,1)}, u32[]{:S(2)}) copy-start(bf16[384,2048]{1,0:T(8,128)(2,1)} %experts.5.own_ref) | copy-start | bytes 4718596
  158.8 22.2 %collective-permute-start.15 = (bf16[144,2048]{1,0:T(8,128)(2,1)}, bf16[144,2048]{1,0:T(8,128)(2,1)S(1)}, u32[]{:S(2)}, u32[]{:S(2)}) collective-permute-start(bf16[144,2048]{1,0:T(8,128)(2,1)} %get-tuple-element.58), channel_id=1, source_target_pairs={{0,96},{32,0},{64,32},{96,64},{1,97},{33,1},{65,33},{97,65},{2,98}... | collective-permute-start | bytes 1769480 | tf_op jit(solution)/shard_map/ppermute | solution.py:353
  160.4 20.6 %collective-permute-start.16 = (bf16[144,2048]{1,0:T(8,128)(2,1)}, bf16[144,2048]{1,0:T(8,128)(2,1)S(1)}, u32[]{:S(2)}, u32[]{:S(2)}) collective-permute-start(bf16[144,2048]{1,0:T(8,128)(2,1)} %get-tuple-element.59), channel_id=1, source_target_pairs={{0,32},{32,64},{64,96},{96,0},{1,33},{33,65},{65,97},{97,1},{2,34}... | collective-permute-start | bytes 1769480 | tf_op jit(solution)/shard_map/ppermute | solution.py:353
  160.9 20.1 %collective-permute-start.10 = (bf16[96,2048]{1,0:T(8,128)(2,1)S(1)}, bf16[96,2048]{1,0:T(8,128)(2,1)S(1)}, u32[]{:S(2)}, u32[]{:S(2)}) collective-permute-start(bf16[96,2048]{1,0:T(8,128)(2,1)S(1)} %copy-done.4), channel_id=1, source_target_pairs={{0,32},{32,64},{64,96},{96,0},{1,33},{33,65},{65,97},{97,1},{2,34}... | collective-permute-start | bytes 1179656 | tf_op jit(solution)/shard_map/ppermute | solution.py:353
  185.1 24.0 %all-to-all-start.5 = ((bf16[16,24,2048]{2,1,0:T(8,128)(2,1)}), bf16[16,24,2048]{2,1,0:T(8,128)(2,1)S(1)}, u32[]{:S(2)}, u32[]{:S(2)}) async-start(bf16[16,24,2048]{2,1,0:T(8,128)(2,1)} %bitcast.29), calls=%async_computation.5 | async-start | bytes 3145728 | tf_op jit(solution)/shard_map/all_to_all | solution.py:356
  194.6 10.8 %collective-permute-start.17 = (bf16[128,2048]{1,0:T(8,128)(2,1)S(1)}, bf16[128,2048]{1,0:T(8,128)(2,1)S(1)}, u32[]{:S(2)}, u32[]{:S(2)}) collective-permute-start(bf16[128,2048]{1,0:T(8,128)(2,1)S(1)} %combine.2), channel_id=1, source_target_pairs={{0,64},{32,96},{64,0},{96,32},{1,65},{33,97},{65,1},{97,33},{2,66}... | collective-permute-start | bytes 1572872 | tf_op jit(solution)/shard_map/ppermute | solution.py:353

commit v5 on v4

--- a/solution.py
+++ b/solution.py
@@ -21,7 +21,21 @@
     return pl.BlockSpec(shape, lambda *_: (0,) * len(shape))
 
 
-def attention_kernel(x_ref, out_ref, *, block):
+def attention_kernel(x_ref, w_hbm, out_ref, w_ref, sems, *, block):
+    cuts = sems.shape[0]
+    rows = w_hbm.shape[0] // cuts
+    fetch = [
+        pltpu.make_async_copy(
+            w_hbm.at[pl.ds(i * rows, rows)], w_ref.at[pl.ds(i * rows, rows)], sems.at[i]
+        )
+        for i in range(cuts)
+    ]
+
+    @pl.when(pl.program_id(0) == 0)
+    def _():
+        for copy in fetch:
+            copy.start()
+
     n_src, _, rows, lanes = x_ref.shape
     length = n_src * rows
     keys = x_ref[:, 1].reshape(length, lanes)
@@ -46,18 +60,33 @@
         context = jnp.where(first, parts[0], parts[1]).astype(BF16)
         out_ref[i * per : (i + 1) * per] = context.reshape(per, rows, lanes)
 
-
-def attention(arrived):
+    @pl.when(pl.program_id(0) == pl.num_programs(0) - 1)
+    def _():
+        for copy in fetch:
+            copy.wait()
+
+
+def attention(arrived, w_out):
     n_src, three, rows, width = arrived.shape
     return pl.pallas_call(
         functools.partial(attention_kernel, block=2 * rows),
         grid=(width // LANES,),
-        in_specs=[pl.BlockSpec((n_src, three, rows, LANES), lambda i: (0, 0, 0, i))],
-        out_specs=pl.BlockSpec((n_src, rows, LANES), lambda i: (0, 0, i)),
-        out_shape=jax.ShapeDtypeStruct((n_src, rows, width), BF16),
+        in_specs=[
+            pl.BlockSpec((n_src, three, rows, LANES), lambda i: (0, 0, 0, i)),
+            pl.BlockSpec(memory_space=pltpu.HBM),
+        ],
+        out_specs=[
+            pl.BlockSpec((n_src, rows, LANES), lambda i: (0, 0, i)),
+            pl.BlockSpec(memory_space=pl.ANY),
+        ],
+        out_shape=[
+            jax.ShapeDtypeStruct((n_src, rows, width), BF16),
+            pltpu.VMEM(w_out.shape, BF16),
+        ],
+        scratch_shapes=[pltpu.SemaphoreType.DMA((8,))],
         compiler_params=pltpu.CompilerParams(vmem_limit_bytes=24 * MIB),
         name="attention",
-    )(arrived)
+    )(arrived, in_hbm(w_out))
 
 
 def plan_kernel(info_ref, out_ref, *, n_exp, capacity):
@@ -98,56 +127,38 @@
 
 
 def project_kernel(
-    ctx_ref, w_hbm, stream_ref, info_ref, mid_ref, normed_ref, out_ref, w_ref, sems, *, cuts
+    ctx_ref, w_ref, stream_ref, info_ref, mid_hbm, normed_ref, out_ref, mid_ref, sem
 ):
-    cols = w_ref.shape[1] // cuts
-    copies = [
-        pltpu.make_async_copy(
-            w_hbm.at[:, pl.ds(i * cols, cols)], w_ref.at[:, pl.ds(i * cols, cols)], sems.at[i]
-        )
-        for i in range(cuts)
-    ]
-    for copy in copies:
-        copy.start()
     merged = jnp.concatenate([ctx_ref[s] for s in range(ctx_ref.shape[0])], axis=1)
-    for i, copy in enumerate(copies):
-        copy.wait()
-        here = slice(i * cols, (i + 1) * cols)
-        mid_ref[:, here] = stream_ref[:, here].astype(F32) + jnp.dot(
-            merged, w_ref[:, here], preferred_element_type=F32
-        )
-    mid = mid_ref[...]
+    mid = stream_ref[...].astype(F32) + jnp.dot(
+        merged, w_ref[...], preferred_element_type=F32
+    )
+    mid_ref[...] = mid
+    copy = pltpu.make_async_copy(mid_ref, mid_hbm, sem)
+    copy.start()
     factor = lax.rsqrt(jnp.mean(mid * mid, axis=1, keepdims=True) + 1e-06)
     normed = (mid * factor).astype(BF16)
     normed_ref[...] = normed
     fill(normed, info_ref[...], out_ref)
+    copy.wait()
 
 
 def project(merged, w_out, stream, info, slots):
     rows, width = stream.shape
-    cuts = 4
-    return pl.pallas_call(
-        functools.partial(project_kernel, cuts=cuts),
-        grid=(1,),
-        in_specs=[
-            vmem(merged.shape),
-            pl.BlockSpec(memory_space=pltpu.HBM),
-            vmem(stream.shape),
-            vmem(info.shape),
-        ],
-        out_specs=[vmem((rows, width))] * 2 + [vmem((slots, width))],
+    held = pl.BlockSpec(memory_space=pltpu.VMEM)
+    return pl.pallas_call(
+        project_kernel,
+        in_specs=[held] * 4,
+        out_specs=[pl.BlockSpec(memory_space=pltpu.HBM), held, held],
         out_shape=[
             pltpu.HBM((rows, width), F32),
             jax.ShapeDtypeStruct((rows, width), BF16),
             jax.ShapeDtypeStruct((slots, width), BF16),
         ],
-        scratch_shapes=[
-            pltpu.VMEM(w_out.shape, BF16),
-            pltpu.SemaphoreType.DMA((cuts,)),
-        ],
-        compiler_params=pltpu.CompilerParams(vmem_limit_bytes=32 * MIB),
+        scratch_shapes=[pltpu.VMEM((rows, width), F32), pltpu.SemaphoreType.DMA(())],
+        compiler_params=pltpu.CompilerParams(vmem_limit_bytes=24 * MIB),
         name="project",
-    )(merged, in_hbm(w_out), stream, info)
+    )(merged, pltpu.with_memory_space_constraint(w_out, pltpu.VMEM), stream, info)
 
 
 def route_kernel(normed_ref, info_ref, out_ref):
@@ -294,10 +305,25 @@
     )(info, back, *([far, in_hbm(mid)] if final else []))
 
 
-def spread_kernel(x_ref, out_ref):
-    part = out_ref.shape[3]
-    for i in range(out_ref.shape[0]):
-        out_ref[i] = x_ref[:, :, i * part : (i + 1) * part]
+def spread_kernel(x_hbm, out_hbm, x_ref, in_sems, out_sems):
+    n_seq, three, _, part = out_hbm.shape
+    copies = [
+        pltpu.make_async_copy(x_hbm.at[j], x_ref.at[j], in_sems.at[j]) for j in range(three)
+    ]
+    for copy in copies:
+        copy.start()
+    out = []
+    for j, copy in enumerate(copies):
+        copy.wait()
+        for i in range(n_seq):
+            out.append(
+                pltpu.make_async_copy(
+                    x_ref.at[j, :, pl.ds(i * part, part)], out_hbm.at[i, j], out_sems.at[i, j]
+                )
+            )
+            out[-1].start()
+    for copy in out:
+        copy.wait()
 
 
 def spread(qkv, n_seq):
@@ -305,35 +331,45 @@
     part = width // n_seq
     return pl.pallas_call(
         spread_kernel,
-        grid=(three,),
-        in_specs=[pl.BlockSpec((1, rows, width), lambda i: (i, 0, 0))],
-        out_specs=pl.BlockSpec((n_seq, 1, rows, part), lambda i: (0, i, 0, 0)),
-        out_shape=jax.ShapeDtypeStruct((n_seq, three, rows, part), BF16),
+        in_specs=[pl.BlockSpec(memory_space=pltpu.HBM)],
+        out_specs=pl.BlockSpec(memory_space=pltpu.HBM),
+        out_shape=pltpu.HBM((n_seq, three, rows, part), BF16),
+        scratch_shapes=[
+            pltpu.VMEM(qkv.shape, BF16),
+            pltpu.SemaphoreType.DMA((three,)),
+            pltpu.SemaphoreType.DMA((n_seq, three)),
+        ],
         compiler_params=pltpu.CompilerParams(vmem_limit_bytes=8 * MIB),
         name="spread",
     )(in_hbm(qkv))
 
 
 def total_kernel(own_ref, *refs):
-    *in_refs, out_ref = refs
-    start = 0
-    for up_ref, down_ref in zip(in_refs[::2], in_refs[1::2]):
-        here = slice(start, start + up_ref.shape[0])
-        total = own_ref[here].astype(F32) + up_ref[...].astype(F32) + down_ref[...].astype(F32)
-        out_ref[here] = total.astype(BF16)
-        start = here.stop
+    *in_refs, out_hbm, out_ref, sems = refs
+    start, copies = 0, []
+    for i, (up_ref, down_ref) in enumerate(zip(in_refs[::2], in_refs[1::2], strict=True)):
+        n = up_ref.shape[0]
+        total = own_ref[start : start + n].astype(F32) + up_ref[...].astype(F32)
+        out_ref[start : start + n] = (total + down_ref[...].astype(F32)).astype(BF16)
+        here = pl.ds(start, n)
+        copies.append(pltpu.make_async_copy(out_ref.at[here], out_hbm.at[here], sems.at[i]))
+        copies[-1].start()
+        start += n
+    for copy in copies:
+        copy.wait()
 
 
 def add_up(own, pairs):
     arrays = [own, *(x for pair in pairs for x in pair)]
-    rows, width = own.shape
-    cols = 512
     return pl.pallas_call(
         total_kernel,
-        grid=(width // cols,),
-        in_specs=[pl.BlockSpec((x.shape[0], cols), lambda i: (0, i)) for x in arrays],
-        out_specs=pl.BlockSpec((rows, cols), lambda i: (0, i)),
-        out_shape=pltpu.HBM((rows, width), BF16),
+        in_specs=[pl.BlockSpec(memory_space=pltpu.VMEM)] * len(arrays),
+        out_specs=pl.BlockSpec(memory_space=pltpu.HBM),
+        out_shape=pltpu.HBM(own.shape, BF16),
+        scratch_shapes=[
+            pltpu.VMEM(own.shape, BF16),
+            pltpu.SemaphoreType.DMA((len(pairs),)),
+        ],
         compiler_params=pltpu.CompilerParams(vmem_limit_bytes=16 * MIB),
         name="add_up",
     )(*arrays)
@@ -364,37 +400,43 @@
     info_far = shift(info, 2)
     qkv = spread(qkv_heads[0].transpose(1, 0, 2), n_seq)
     arrived = lax.all_to_all(qkv, seq, split_axis=0, concat_axis=0, tiled=True)
-    context = attention(arrived)
+    context, w_held = attention(arrived, w_out)
     context, info_far, other = lax.optimization_barrier((context, info_far, other))
     merged = lax.all_to_all(context, seq, split_axis=0, concat_axis=0, tiled=True)
-    mid, normed, buffer = project(merged, w_out, stream_in[0], info, slots)
+    mid, normed, buffer = project(merged, w_held, stream_in[0], info, slots)
 
     tie = lax.optimization_barrier
     far_tokens = shift(normed, 2)
+    own = exchange(buffer)
+    eighth = own.shape[0] // 8
+    bounds = (0, 3 * eighth, 6 * eighth, 8 * eighth)
+    parts = [own[i:j] for i, j in zip(bounds[:-1], bounds[1:], strict=True)]
+    far_tokens, parts = tie((far_tokens, parts))
     far_buffer = route(far_tokens, info_far, slots)
-    own = exchange(buffer)
-    quarter = own.shape[0] // 4
-    bounds = (0, quarter, quarter + 3 * quarter // 2, 4 * quarter)
-    parts = [own[i:j] for i, j in zip(bounds[:-1], bounds[1:], strict=True)]
-    ups = [shift(x, 1) for x in parts]
-    downs = [shift(x, -1) for x in parts]
+    ups = [shift(x, 1) for x in parts[:2]]
+    downs = [shift(x, -1) for x in parts[:2]]
+    parts[2], ups[0], downs[0] = tie((parts[2], ups[0], downs[0]))
+    ups.append(shift(parts[2], 1))
+    downs.append(shift(parts[2], -1))
 
     def near(i):
         return experts([ups[i], downs[i]], mine, other)
 
     [own_part] = experts([own], mine, other)
-    ups[0], downs[0], own_part, far_buffer = tie((ups[0], downs[0], own_part, far_buffer))
+    ups[0], downs[0], own_part = tie((ups[0], downs[0], own_part))
     far_rows = exchange(far_buffer)
     back0 = near(0)
     ups[1], downs[1], back0 = tie((ups[1], downs[1], back0))
     back1 = near(1)
     far_rows, back1 = tie((far_rows, back1))
     [far_part] = experts([far_rows], mine, other)
-    ups[2], downs[2], far_part = tie((ups[2], downs[2], far_part))
+    home = [(shift(u, -1), shift(d, 1)) for u, d in (back0, back1)]
+    ups[2], downs[2], far_part, home[0] = tie((ups[2], downs[2], far_part, home[0]))
     back2 = near(2)
+    home.append((shift(back2[0], -1), shift(back2[1], 1)))
     far_back = exchange(far_part)
     far_sum = combine(info_far, far_back)
-    total = add_up(own_part, [(shift(u, -1), shift(d, 1)) for u, d in (back0, back1, back2)])
+    total = add_up(own_part, home)
     total, far_back = tie((total, far_back))
     back = exchange(total)
     far_home = shift(far_sum, 2)

time: 215 us -> 203 us (0.944)
  waiting for transfers between devices: 73.6 us -> 61.3 us
  starting transfers between devices: 52.2 us -> 56.7 us
  Pallas kernels: 70.9 us -> 66.8 us
    ppermute x15, waiting for transfers between devices: 43.9 us -> 19.9 us  [shift(): return lax.ppermute(x, 'y', [(i, (i + by) % n_y) for i in range(n_y)])]
    all_to_all x4, waiting for transfers between devices: 12 us -> 23.7 us  [exchange(): return lax.all_to_all(x, exp, split_axis=0, concat_axis=0, tiled=True)]
    pallas_call x3, Pallas kernels: 13.3 us -> 9.12 us  [the longest x1 3.62 us: project(): pl.pallas_call(project_kernel, in_specs=[held] * 4, out_specs=[pl.BlockSp...]
    ppermute x15, starting transfers between devices: 18.8 us -> 21.9 us  [shift(): return lax.ppermute(x, 'y', [(i, (i + by) % n_y) for i in range(n_y)])]
  transfers between devices with their start and end apart: 23 -> 23, of which waited for: 7 -> 6; matrix products, arithmetic and copies ran while one was open for 1% -> 1% of each run, Pallas kernels for 29% -> 30%
where the time goes in v5:
time: 203 us; the launch traced here: 200 us
  Pallas kernels  66.8 us (33%)
  waiting for transfers between devices  61.3 us (30%)
  starting transfers between devices  56.7 us (28%)
  blocking collectives  12.8 us (6%)
    pallas_call x5, Pallas kernels, experts(): pl.pallas_call(functools.partial(expert_kernel, n_in=len(arrays), block=b...  44.7 us
    all_to_all x4, starting transfers between devices, exchange(): return lax.all_to_all(x, exp, split_axis=0, concat_axis=0, tiled=True)  29.8 us
    all_to_all x4, waiting for transfers between devices, exchange(): return lax.all_to_all(x, exp, split_axis=0, concat_axis=0, tiled=True)  23.7 us
    ppermute x15, starting transfers between devices, shift(): return lax.ppermute(x, 'y', [(i, (i + by) % n_y) for i in range(n_y)])  21.9 us
    ppermute x15, waiting for transfers between devices, shift(): return lax.ppermute(x, 'y', [(i, (i + by) % n_y) for i in range(n_y)])  19.9 us
    all_to_all x1, waiting for transfers between devices, per_device(): arrived = lax.all_to_all(qkv, seq, split_axis=0, concat_axis=0, tiled=True)  17.7 us
    all_to_all x1, blocking collectives, per_device(): lax.all_to_all(context, seq, split_axis=0, concat_axis=0, tiled=True)  12.8 us
    pallas_call x1, Pallas kernels, attention(): pl.pallas_call(functools.partial(attention_kernel, block=2 * rows), grid=...  6.15 us
  transfers between devices with their start and end apart: 23, of which 6 were waited for; matrix products, arithmetic and copies ran while one was open for 1% of the time, Pallas kernels for 30%

profile of v5, /device:TPU:2, one launch (start us, length us, event | category | flops | bytes accessed | tf_op | source)
XLA Modules:
  0.0 200.2 jit_solution(7768413244299881388)
XLA Ops:
  0.0 0.0 collective-permute-start.1
  0.0 0.5 collective-permute-start.2
  0.5 0.0 collective-permute-start.3
  0.5 2.4 %spread.1 = bf16[8,3,128,256]{3,2,1,0:T(8,128)(2,1)} custom-call(bf16[3,128,2048]{2,1,0:T(8,128)(2,1)} %bitcast.30), custom_call_target="tpu_custom_call" | custom-call | tf_op jit(solution)/shard_map/spread/pallas_call | solution.py:332
  3.0 0.0 copy-start.2
  3.0 0.0 copy-start.3
  3.0 4.6 %all-to-all-start = ((bf16[8,3,128,256]{3,2,1,0:T(8,128)(2,1)}), bf16[8,3,128,256]{3,2,1,0:T(8,128)(2,1)S(1)}, u32[]{:S(2)}, u32[]{:S(2)}) async-start(bf16[8,3,128,256]{3,2,1,0:T(8,128)(2,1)} %spread.1), calls=%async_computation | async-start | bytes 3145728 | tf_op jit(solution)/shard_map/all_to_all | solution.py:402
  7.6 0.1 pad.2.clone
  7.7 0.1 maximum_maximum_fusion.info_ref
  7.7 0.1 plan.1.info_ref
  7.9 3.6 %collective-permute-start = (f32[8,128]{1,0:T(8,128)S(1)}, f32[8,128]{1,0:T(8,128)S(1)}, u32[]{:S(2)}, u32[]{:S(2)}) collective-permute-start(f32[8,128]{1,0:T(8,128)S(1)} %plan.1.info_ref), channel_id=1, source_target_pairs={{0,64},{32,96},{64,0},{96,32},{1,65},{33,97},{65,1},{97,33},{2,66}... | collective-permute-start | bytes 12296 | tf_op jit(solution)/shard_map/ppermute | solution.py:389
  11.5 17.7 %all-to-all-done.x_ref = bf16[8,3,128,256]{3,2,1,0:T(8,128)(2,1)S(1)} async-done(((bf16[8,3,128,256]{3,2,1,0:T(8,128)(2,1)}), bf16[8,3,128,256]{3,2,1,0:T(8,128)(2,1)S(1)}, u32[]{:S(2)}, u32[]{:S(2)}) %all-to-all-start) | async-done | bytes 1572896 | tf_op jit(solution)/shard_map/all_to_all | solution.py:402
  29.2 6.2 %attention.1 = (bf16[8,128,256]{2,1,0:T(8,128)(2,1)S(1)}, bf16[2048,2048]{1,0:T(8,128)(2,1)S(1)}) custom-call(bf16[8,3,128,256]{3,2,1,0:T(8,128)(2,1)S(1)} %all-to-all-done.x_ref, bf16[2048,2048]{1,0:T(8,128)(2,1)} %w_hbm.1), custom_call_target="tpu_custom_call" | custom-call | tf_op jit(solution)/shard_map/attention/pallas_call | solution.py:71
  35.4 0.0 collective-permute-done.info_ref
  35.4 0.0 collective-permute-done.1.refs_4_.refs_5_
  35.4 0.0 collective-permute-done.2.refs_5_.refs_6_
  35.4 0.0 collective-permute-done.3.refs_6_.refs_7_
  35.4 12.8 %all_to_all.55.ctx_ref = bf16[8,128,256]{2,1,0:T(8,128)(2,1)S(1)} all-to-all(bf16[8,128,256]{2,1,0:T(8,128)(2,1)S(1)} %get-tuple-element.45), channel_id=1, replica_groups=mesh['y'=4,'core'=2,'z'=4,'x'=4] {'y','core'}, dimensions={0} | all-to-all | bytes 1048576 | tf_op jit(solution)/shard_map/all_to_all | solution.py:405
  48.2 3.6 %project.1 = (f32[128,2048]{1,0:T(8,128)}, bf16[128,2048]{1,0:T(8,128)(2,1)S(1)}, bf16[384,2048]{1,0:T(8,128)(2,1)}) custom-call(bf16[8,128,256]{2,1,0:T(8,128)(2,1)S(1)} %all_to_all.55.ctx_ref, bf16[2048,2048]{1,0:T(8,128)(2,1)S(1)} %get-tuple-element.46.w_ref, bf16[128,2048]{1,0:T(8,128)(2,1)S(1)} %bitcast.28, f32[8,128]{1,0:T(8,128)S(1)} %plan.1.info_ref), custom_call_target="tpu_custom_call" | custom-call | tf_op jit(solution)/shard_map/project/pallas_call | solution.py:149
  51.8 8.3 %all-to-all-start.2 = ((bf16[16,24,2048]{2,1,0:T(8,128)(2,1)}), bf16[16,24,2048]{2,1,0:T(8,128)(2,1)S(1)}, u32[]{:S(2)}, u32[]{:S(2)}) async-start(bf16[16,24,2048]{2,1,0:T(8,128)(2,1)} %bitcast.10), calls=%async_computation.2 | async-start | bytes 3145728 | tf_op jit(solution)/shard_map/all_to_all | solution.py:392
  60.2 0.3 collective-permute-start.4
  60.5 20.8 %all-to-all-done.2 = bf16[16,24,2048]{2,1,0:T(8,128)(2,1)S(1)} async-done(((bf16[16,24,2048]{2,1,0:T(8,128)(2,1)}), bf16[16,24,2048]{2,1,0:T(8,128)(2,1)S(1)}, u32[]{:S(2)}, u32[]{:S(2)}) %all-to-all-start.2) | async-done | bytes 1572896 | tf_op jit(solution)/shard_map/all_to_all | solution.py:392
  81.3 0.8 slice.26
  82.1 1.1 fusion
  83.2 0.0 collective-permute-done.4.normed_ref
  83.2 1.2 collective-permute-start.6
  84.4 0.9 collective-permute-start.5
  85.2 2.4 %collective-permute-start.10 = (bf16[144,2048]{1,0:T(8,128)(2,1)}, bf16[144,2048]{1,0:T(8,128)(2,1)}, u32[]{:S(2)}, u32[]{:S(2)}) collective-permute-start(bf16[144,2048]{1,0:T(8,128)(2,1)} %bitcast.12), channel_id=1, source_target_pairs={{0,96},{32,0},{64,32},{96,64},{1,97},{33,1},{65,33},{97,65},{2,98}... | collective-permute-start | bytes 1769480 | tf_op jit(solution)/shard_map/ppermute | solution.py:389
  87.6 0.0 collective-permute-start.9
  87.6 1.8 route.1
  89.4 6.9 %all-to-all-start.3 = ((bf16[16,24,2048]{2,1,0:T(8,128)(2,1)}), bf16[16,24,2048]{2,1,0:T(8,128)(2,1)}, u32[]{:S(2)}, u32[]{:S(2)}) async-start(bf16[16,24,2048]{2,1,0:T(8,128)(2,1)} %bitcast.15), calls=%async_computation.3 | async-start | bytes 3145728 | tf_op jit(solution)/shard_map/all_to_all | solution.py:392
  96.3 8.8 %experts.5.own_ref = bf16[384,2048]{1,0:T(8,128)(2,1)} custom-call(bf16[384,2048]{1,0:T(8,128)(2,1)S(1)} %bitcast.26, bf16[2048,512]{1,0:T(8,128)(2,1)} %bitcast.34, bf16[2048,512]{1,0:T(8,128)(2,1)} %bitcast.40, bf16[512,2048]{1,0:T(8,128)(2,1)} %bitcast.46, bf16[2048,512]{1,0:T(8,128)(2,1)} %collective-permute-done.1.refs_4_.refs_5_, ...), custom_call_target="tpu_custom_call" | custom-call | flops 483183820800 | bytes 15728640 | tf_op jit(solution)/shard_map/experts/pallas_call | solution.py:238
  105.1 0.0 collective-permute-done.6.refs_1_
  105.1 0.0 collective-permute-done.5.refs_0_
  105.1 3.3 %collective-permute-start.8 = (bf16[96,2048]{1,0:T(8,128)(2,1)}, bf16[96,2048]{1,0:T(8,128)(2,1)}, u32[]{:S(2)}, u32[]{:S(2)}) collective-permute-start(bf16[96,2048]{1,0:T(8,128)(2,1)} %bitcast.13), channel_id=1, source_target_pairs={{0,96},{32,0},{64,32},{96,64},{1,97},{33,1},{65,33},{97,65},{2,98}... | collective-permute-start | bytes 1179656 | tf_op jit(solution)/shard_map/ppermute | solution.py:389
  108.4 0.0 collective-permute-start.7
  108.4 8.8 %experts.6 = (bf16[144,2048]{1,0:T(8,128)(2,1)}, bf16[144,2048]{1,0:T(8,128)(2,1)}) custom-call(bf16[144,2048]{1,0:T(8,128)(2,1)} %collective-permute-done.5.refs_0_, bf16[144,2048]{1,0:T(8,128)(2,1)} %collective-permute-done.6.refs_1_, bf16[2048,512]{1,0:T(8,128)(2,1)} %bitcast.35, bf16[2048,512]{1,0:T(8,128)(2,1)} %bitcast.41, bf16[512,2048]{1,0:T(8,128)(2,1)} %bitcast.47, ...), custom_call_target="tpu_custom_call" | custom-call | flops 362387865600 | bytes 14942208 | tf_op jit(solution)/shard_map/experts/pallas_call | solution.py:238
  117.3 0.0 collective-permute-done.9.refs_0_
  117.3 3.3 %collective-permute-start.11 = (bf16[144,2048]{1,0:T(8,128)(2,1)}, bf16[144,2048]{1,0:T(8,128)(2,1)}, u32[]{:S(2)}, u32[]{:S(2)}) collective-permute-start(bf16[144,2048]{1,0:T(8,128)(2,1)} %get-tuple-element.70), channel_id=1, source_target_pairs={{0,96},{32,0},{64,32},{96,64},{1,97},{33,1},{65,33},{97,65},{2,98}... | collective-permute-start | bytes 1769480 | tf_op jit(solution)/shard_map/ppermute | solution.py:389
  120.6 0.0 collective-permute-start.12
  120.6 8.8 %experts.7 = (bf16[144,2048]{1,0:T(8,128)(2,1)}, bf16[144,2048]{1,0:T(8,128)(2,1)}) custom-call(bf16[144,2048]{1,0:T(8,128)(2,1)} %collective-permute-done.9.refs_0_, bf16[144,2048]{1,0:T(8,128)(2,1)} %collective-permute-done.10.refs_1_, bf16[2048,512]{1,0:T(8,128)(2,1)} %bitcast.36, bf16[2048,512]{1,0:T(8,128)(2,1)} %bitcast.42, ...), custom_call_target="tpu_custom_call" | custom-call | flops 362387865600 | bytes 14942208 | tf_op jit(solution)/shard_map/experts/pallas_call | solution.py:238
  129.4 0.0 all-to-all-done.3
  129.5 10.2 %experts.8 = bf16[384,2048]{1,0:T(8,128)(2,1)} custom-call(bf16[384,2048]{1,0:T(8,128)(2,1)} %bitcast.16.refs_0_, bf16[2048,512]{1,0:T(8,128)(2,1)} %bitcast.37, bf16[2048,512]{1,0:T(8,128)(2,1)} %bitcast.43, bf16[512,2048]{1,0:T(8,128)(2,1)} %bitcast.49, bf16[2048,512]{1,0:T(8,128)(2,1)} %collective-permute-done.1.refs_4_.refs_5_, ...), custom_call_target="tpu_custom_call" | custom-call | flops 483183820800 | bytes 15728640 | tf_op jit(solution)/shard_map/experts/pallas_call | solution.py:238
  139.7 3.3 %collective-permute-start.13 = (bf16[144,2048]{1,0:T(8,128)(2,1)}, bf16[144,2048]{1,0:T(8,128)(2,1)}, u32[]{:S(2)}, u32[]{:S(2)}) collective-permute-start(bf16[144,2048]{1,0:T(8,128)(2,1)} %get-tuple-element.74), channel_id=1, source_target_pairs={{0,96},{32,0},{64,32},{96,64},{1,97},{33,1},{65,33},{97,65},{2,98}... | collective-permute-start | bytes 1769480 | tf_op jit(solution)/shard_map/ppermute | solution.py:389
  143.0 0.0 collective-permute-done.8.refs_1_
  143.0 0.0 collective-permute-start.14
  143.0 0.0 collective-permute-done.7.refs_0_
  143.0 0.0 collective-permute-done.11.refs_0_
  143.0 7.3 %all-to-all-start.4 = ((bf16[16,24,2048]{2,1,0:T(8,128)(2,1)}), bf16[16,24,2048]{2,1,0:T(8,128)(2,1)}, u32[]{:S(2)}, u32[]{:S(2)}) async-start(bf16[16,24,2048]{2,1,0:T(8,128)(2,1)} %bitcast.31), calls=%async_computation.4 | async-start | bytes 3145728 | tf_op jit(solution)/shard_map/all_to_all | solution.py:392
  150.3 8.0 %experts.9 = (bf16[96,2048]{1,0:T(8,128)(2,1)}, bf16[96,2048]{1,0:T(8,128)(2,1)}) custom-call(bf16[96,2048]{1,0:T(8,128)(2,1)} %collective-permute-done.7.refs_0_, bf16[96,2048]{1,0:T(8,128)(2,1)} %collective-permute-done.8.refs_1_, bf16[2048,512]{1,0:T(8,128)(2,1)} %bitcast.38, bf16[2048,512]{1,0:T(8,128)(2,1)} %bitcast.44, bf16[512,2048]{1,0:T(8,128)(2,1)} %bitcast.50, ...), custom_call_target="tpu_custom_call" | custom-call | flops 241591910400 | bytes 14155776 | tf_op jit(solution)/shard_map/experts/pallas_call | solution.py:238
  158.3 3.5 %collective-permute-start.15 = (bf16[96,2048]{1,0:T(8,128)(2,1)}, bf16[96,2048]{1,0:T(8,128)(2,1)S(1)}, u32[]{:S(2)}, u32[]{:S(2)}) collective-permute-start(bf16[96,2048]{1,0:T(8,128)(2,1)} %get-tuple-element.78), channel_id=1, source_target_pairs={{0,96},{32,0},{64,32},{96,64},{1,97},{33,1},{65,33},{97,65},{2,98}... | collective-permute-start | bytes 1179656 | tf_op jit(solution)/shard_map/ppermute | solution.py:389
  161.9 0.0 collective-permute-start.16
  161.9 5.6 %collective-permute-done.15.refs_4_ = bf16[96,2048]{1,0:T(8,128)(2,1)S(1)} collective-permute-done((bf16[96,2048]{1,0:T(8,128)(2,1)}, bf16[96,2048]{1,0:T(8,128)(2,1)S(1)}, u32[]{:S(2)}, u32[]{:S(2)}) %collective-permute-start.15) | collective-permute-done | bytes 393248 | tf_op jit(solution)/shard_map/ppermute | solution.py:389
  167.5 3.6 %collective-permute-done.16.refs_5_ = bf16[96,2048]{1,0:T(8,128)(2,1)S(1)} collective-permute-done((bf16[96,2048]{1,0:T(8,128)(2,1)}, bf16[96,2048]{1,0:T(8,128)(2,1)S(1)}, u32[]{:S(2)}, u32[]{:S(2)}) %collective-permute-start.16) | collective-permute-done | bytes 393248 | tf_op jit(solution)/shard_map/ppermute | solution.py:389
  171.1 0.0 collective-permute-done.13.refs_2_
  171.1 0.0 collective-permute-done.14.refs_3_
  171.1 3.1 %add_up.1 = bf16[384,2048]{1,0:T(8,128)(2,1)} custom-call(bf16[384,2048]{1,0:T(8,128)(2,1)S(1)} %copy-done, bf16[144,2048]{1,0:T(8,128)(2,1)} %collective-permute-done.11.refs_0_, bf16[144,2048]{1,0:T(8,128)(2,1)} %collective-permute-done.12.refs_1_, bf16[144,2048]{1,0:T(8,128)(2,1)} %collective-permute-done.13.refs_2_, ...), custom_call_target="tpu_custom_call" | custom-call | tf_op jit(solution)/shard_map/add_up/pallas_call | solution.py:364
  174.2 0.0 all-to-all-done.4
  174.2 7.2 %all-to-all-start.5 = ((bf16[16,24,2048]{2,1,0:T(8,128)(2,1)}), bf16[16,24,2048]{2,1,0:T(8,128)(2,1)S(1)}, u32[]{:S(2)}, u32[]{:S(2)}) async-start(bf16[16,24,2048]{2,1,0:T(8,128)(2,1)} %bitcast.29), calls=%async_computation.5 | async-start | bytes 3145728 | tf_op jit(solution)/shard_map/all_to_all | solution.py:392
  181.4 2.2 %combine.2 = bf16[128,2048]{1,0:T(8,128)(2,1)S(1)} custom-call(f32[8,128]{1,0:T(8,128)S(1)} %collective-permute-done.info_ref, bf16[384,2048]{1,0:T(8,128)(2,1)} %bitcast.18.back_ref), custom_call_target="tpu_custom_call" | custom-call | tf_op jit(solution)/shard_map/combine/pallas_call | solution.py:296
  183.7 0.1 collective-permute-start.17
  183.7 10.7 %collective-permute-done.17.refs_0_ = bf16[128,2048]{1,0:T(8,128)(2,1)S(1)} collective-permute-done((bf16[128,2048]{1,0:T(8,128)(2,1)S(1)}, bf16[128,2048]{1,0:T(8,128)(2,1)S(1)}, u32[]{:S(2)}, u32[]{:S(2)}) %collective-permute-start.17) | collective-permute-done | bytes 524320 | tf_op jit(solution)/shard_map/ppermute | solution.py:389
  194.4 2.9 %all-to-all-done.5 = bf16[16,24,2048]{2,1,0:T(8,128)(2,1)S(1)} async-done(((bf16[16,24,2048]{2,1,0:T(8,128)(2,1)}), bf16[16,24,2048]{2,1,0:T(8,128)(2,1)S(1)}, u32[]{:S(2)}, u32[]{:S(2)}) %all-to-all-start.5) | async-done | bytes 1572896 | tf_op jit(solution)/shard_map/all_to_all | solution.py:392
  197.3 2.7 %combine.3 = bf16[128,2048]{1,0:T(8,128)(2,1)} custom-call(f32[8,128]{1,0:T(8,128)S(1)} %plan.1.info_ref, bf16[384,2048]{1,0:T(8,128)(2,1)S(1)} %bitcast.27, bf16[128,2048]{1,0:T(8,128)(2,1)S(1)} %collective-permute-done.17.refs_0_, f32[128,2048]{1,0:T(8,128)} %get-tuple-element.82.refs_1_), custom_call_target="tpu_custom_call" | custom-call | tf_op jit(solution)/shard_map/combine/pallas_call | solution.py:296
  (10 shorter events, 0.0 us)
Async XLA Ops:
  0.0 35.4 %collective-permute-start.1 = (bf16[2048,512]{1,0:T(8,128)(2,1)}, bf16[2048,512]{1,0:T(8,128)(2,1)}, u32[]{:S(2)}, u32[]{:S(2)}) collective-permute-start(bf16[2048,512]{1,0:T(8,128)(2,1)} %bitcast.33), channel_id=1, source_target_pairs={{0,16},{16,0},{1,17},{17,1},{2,18},{18,2},{3,19},{19,3},{4,20},{20... | collective-permute-start | bytes 6291464 | tf_op jit(solution)/shard_map/ppermute | solution.py:386
  0.0 35.4 %collective-permute-start.2 = (bf16[2048,512]{1,0:T(8,128)(2,1)}, bf16[2048,512]{1,0:T(8,128)(2,1)}, u32[]{:S(2)}, u32[]{:S(2)}) collective-permute-start(bf16[2048,512]{1,0:T(8,128)(2,1)} %bitcast.39), channel_id=1, source_target_pairs={{0,16},{16,0},{1,17},{17,1},{2,18},{18,2},{3,19},{19,3},{4,20},{20... | collective-permute-start | bytes 6291464 | tf_op jit(solution)/shard_map/ppermute | solution.py:386
  0.5 34.9 %collective-permute-start.3 = (bf16[512,2048]{1,0:T(8,128)(2,1)}, bf16[512,2048]{1,0:T(8,128)(2,1)}, u32[]{:S(2)}, u32[]{:S(2)}) collective-permute-start(bf16[512,2048]{1,0:T(8,128)(2,1)} %bitcast.45), channel_id=1, source_target_pairs={{0,16},{16,0},{1,17},{17,1},{2,18},{18,2},{3,19},{19,3},{4,20},{20... | collective-permute-start | bytes 6291464 | tf_op jit(solution)/shard_map/ppermute | solution.py:386
  3.0 4.7 %copy-start.2 = (s32[1,128,2]{1,2,0:T(2,128)S(1)}, s32[1,128,2]{1,2,0:T(2,128)}, u32[]{:S(2)}) copy-start(s32[1,128,2]{1,2,0:T(2,128)} %param.10) | copy-start | bytes 3076
  3.0 4.7 %copy-start.3 = (f32[1,128,2]{1,2,0:T(2,128)S(1)}, f32[1,128,2]{1,2,0:T(2,128)}, u32[]{:S(2)}) copy-start(f32[1,128,2]{1,2,0:T(2,128)} %param.11) | copy-start | bytes 3076
  3.0 26.2 %all-to-all-start = ((bf16[8,3,128,256]{3,2,1,0:T(8,128)(2,1)}), bf16[8,3,128,256]{3,2,1,0:T(8,128)(2,1)S(1)}, u32[]{:S(2)}, u32[]{:S(2)}) async-start(bf16[8,3,128,256]{3,2,1,0:T(8,128)(2,1)} %spread.1), calls=%async_computation | async-start | bytes 3145728 | tf_op jit(solution)/shard_map/all_to_all | solution.py:402
  7.9 40.3 %copy-start.1 = (bf16[1,128,2048]{2,1,0:T(8,128)(2,1)S(1)}, bf16[1,128,2048]{2,1,0:T(8,128)(2,1)}, u32[]{:S(2)}) copy-start(bf16[1,128,2048]{2,1,0:T(8,128)(2,1)} %param.8) | copy-start | bytes 1572868
  7.9 27.5 %collective-permute-start = (f32[8,128]{1,0:T(8,128)S(1)}, f32[8,128]{1,0:T(8,128)S(1)}, u32[]{:S(2)}, u32[]{:S(2)}) collective-permute-start(f32[8,128]{1,0:T(8,128)S(1)} %plan.1.info_ref), channel_id=1, source_target_pairs={{0,64},{32,96},{64,0},{96,32},{1,65},{33,97},{65,1},{97,33},{2,66}... | collective-permute-start | bytes 12296 | tf_op jit(solution)/shard_map/ppermute | solution.py:389
  51.8 29.5 %all-to-all-start.2 = ((bf16[16,24,2048]{2,1,0:T(8,128)(2,1)}), bf16[16,24,2048]{2,1,0:T(8,128)(2,1)S(1)}, u32[]{:S(2)}, u32[]{:S(2)}) async-start(bf16[16,24,2048]{2,1,0:T(8,128)(2,1)} %bitcast.10), calls=%async_computation.2 | async-start | bytes 3145728 | tf_op jit(solution)/shard_map/all_to_all | solution.py:392
  60.2 23.0 %collective-permute-start.4 = (bf16[128,2048]{1,0:T(8,128)(2,1)S(1)}, bf16[128,2048]{1,0:T(8,128)(2,1)S(1)}, u32[]{:S(2)}, u32[]{:S(2)}) collective-permute-start(bf16[128,2048]{1,0:T(8,128)(2,1)S(1)} %get-tuple-element.47), channel_id=1, source_target_pairs={{0,64},{32,96},{64,0},{96,32},{1,65},{33,97},{65,1},{97,33},{2,66}... | collective-permute-start | bytes 1572872 | tf_op jit(solution)/shard_map/ppermute | solution.py:389
  83.2 21.9 %collective-permute-start.6 = (bf16[144,2048]{1,0:T(8,128)(2,1)}, bf16[144,2048]{1,0:T(8,128)(2,1)}, u32[]{:S(2)}, u32[]{:S(2)}) collective-permute-start(bf16[144,2048]{1,0:T(8,128)(2,1)} %bitcast.11), channel_id=1, source_target_pairs={{0,96},{32,0},{64,32},{96,64},{1,97},{33,1},{65,33},{97,65},{2,98}... | collective-permute-start | bytes 1769480 | tf_op jit(solution)/shard_map/ppermute | solution.py:389
  84.4 20.7 %collective-permute-start.5 = (bf16[144,2048]{1,0:T(8,128)(2,1)}, bf16[144,2048]{1,0:T(8,128)(2,1)}, u32[]{:S(2)}, u32[]{:S(2)}) collective-permute-start(bf16[144,2048]{1,0:T(8,128)(2,1)} %bitcast.11), channel_id=1, source_target_pairs={{0,32},{32,64},{64,96},{96,0},{1,33},{33,65},{65,97},{97,1},{2,34}... | collective-permute-start | bytes 1769480 | tf_op jit(solution)/shard_map/ppermute | solution.py:389
  85.2 32.0 %collective-permute-start.10 = (bf16[144,2048]{1,0:T(8,128)(2,1)}, bf16[144,2048]{1,0:T(8,128)(2,1)}, u32[]{:S(2)}, u32[]{:S(2)}) collective-permute-start(bf16[144,2048]{1,0:T(8,128)(2,1)} %bitcast.12), channel_id=1, source_target_pairs={{0,96},{32,0},{64,32},{96,64},{1,97},{33,1},{65,33},{97,65},{2,98}... | collective-permute-start | bytes 1769480 | tf_op jit(solution)/shard_map/ppermute | solution.py:389
  87.6 29.7 %collective-permute-start.9 = (bf16[144,2048]{1,0:T(8,128)(2,1)}, bf16[144,2048]{1,0:T(8,128)(2,1)}, u32[]{:S(2)}, u32[]{:S(2)}) collective-permute-start(bf16[144,2048]{1,0:T(8,128)(2,1)} %bitcast.12), channel_id=1, source_target_pairs={{0,32},{32,64},{64,96},{96,0},{1,33},{33,65},{65,97},{97,1},{2,34}... | collective-permute-start | bytes 1769480 | tf_op jit(solution)/shard_map/ppermute | solution.py:389
  89.4 40.1 %all-to-all-start.3 = ((bf16[16,24,2048]{2,1,0:T(8,128)(2,1)}), bf16[16,24,2048]{2,1,0:T(8,128)(2,1)}, u32[]{:S(2)}, u32[]{:S(2)}) async-start(bf16[16,24,2048]{2,1,0:T(8,128)(2,1)} %bitcast.15), calls=%async_computation.3 | async-start | bytes 3145728 | tf_op jit(solution)/shard_map/all_to_all | solution.py:392
  105.1 37.9 %collective-permute-start.8 = (bf16[96,2048]{1,0:T(8,128)(2,1)}, bf16[96,2048]{1,0:T(8,128)(2,1)}, u32[]{:S(2)}, u32[]{:S(2)}) collective-permute-start(bf16[96,2048]{1,0:T(8,128)(2,1)} %bitcast.13), channel_id=1, source_target_pairs={{0,96},{32,0},{64,32},{96,64},{1,97},{33,1},{65,33},{97,65},{2,98}... | collective-permute-start | bytes 1179656 | tf_op jit(solution)/shard_map/ppermute | solution.py:389
  108.4 34.6 %collective-permute-start.7 = (bf16[96,2048]{1,0:T(8,128)(2,1)}, bf16[96,2048]{1,0:T(8,128)(2,1)}, u32[]{:S(2)}, u32[]{:S(2)}) collective-permute-start(bf16[96,2048]{1,0:T(8,128)(2,1)} %bitcast.13), channel_id=1, source_target_pairs={{0,32},{32,64},{64,96},{96,0},{1,33},{33,65},{65,97},{97,1},{2,34}... | collective-permute-start | bytes 1179656 | tf_op jit(solution)/shard_map/ppermute | solution.py:389
  117.3 25.7 %collective-permute-start.11 = (bf16[144,2048]{1,0:T(8,128)(2,1)}, bf16[144,2048]{1,0:T(8,128)(2,1)}, u32[]{:S(2)}, u32[]{:S(2)}) collective-permute-start(bf16[144,2048]{1,0:T(8,128)(2,1)} %get-tuple-element.70), channel_id=1, source_target_pairs={{0,96},{32,0},{64,32},{96,64},{1,97},{33,1},{65,33},{97,65},{2,98}... | collective-permute-start | bytes 1769480 | tf_op jit(solution)/shard_map/ppermute | solution.py:389
  120.6 22.4 %collective-permute-start.12 = (bf16[144,2048]{1,0:T(8,128)(2,1)}, bf16[144,2048]{1,0:T(8,128)(2,1)}, u32[]{:S(2)}, u32[]{:S(2)}) collective-permute-start(bf16[144,2048]{1,0:T(8,128)(2,1)} %get-tuple-element.71), channel_id=1, source_target_pairs={{0,32},{32,64},{64,96},{96,0},{1,33},{33,65},{65,97},{97,1},{2,34}... | collective-permute-start | bytes 1769480 | tf_op jit(solution)/shard_map/ppermute | solution.py:389
  139.7 31.4 %collective-permute-start.13 = (bf16[144,2048]{1,0:T(8,128)(2,1)}, bf16[144,2048]{1,0:T(8,128)(2,1)}, u32[]{:S(2)}, u32[]{:S(2)}) collective-permute-start(bf16[144,2048]{1,0:T(8,128)(2,1)} %get-tuple-element.74), channel_id=1, source_target_pairs={{0,96},{32,0},{64,32},{96,64},{1,97},{33,1},{65,33},{97,65},{2,98}... | collective-permute-start | bytes 1769480 | tf_op jit(solution)/shard_map/ppermute | solution.py:389
  143.0 28.1 %collective-permute-start.14 = (bf16[144,2048]{1,0:T(8,128)(2,1)}, bf16[144,2048]{1,0:T(8,128)(2,1)}, u32[]{:S(2)}, u32[]{:S(2)}) collective-permute-start(bf16[144,2048]{1,0:T(8,128)(2,1)} %get-tuple-element.75), channel_id=1, source_target_pairs={{0,32},{32,64},{64,96},{96,0},{1,33},{33,65},{65,97},{97,1},{2,34}... | collective-permute-start | bytes 1769480 | tf_op jit(solution)/shard_map/ppermute | solution.py:389
  143.0 31.1 %all-to-all-start.4 = ((bf16[16,24,2048]{2,1,0:T(8,128)(2,1)}), bf16[16,24,2048]{2,1,0:T(8,128)(2,1)}, u32[]{:S(2)}, u32[]{:S(2)}) async-start(bf16[16,24,2048]{2,1,0:T(8,128)(2,1)} %bitcast.31), calls=%async_computation.4 | async-start | bytes 3145728 | tf_op jit(solution)/shard_map/all_to_all | solution.py:392
  150.3 20.8 %copy-start = (bf16[384,2048]{1,0:T(8,128)(2,1)S(1)}, bf16[384,2048]{1,0:T(8,128)(2,1)}, u32[]{:S(2)}) copy-start(bf16[384,2048]{1,0:T(8,128)(2,1)} %experts.5.own_ref) | copy-start | bytes 4718596
  158.3 9.2 %collective-permute-start.15 = (bf16[96,2048]{1,0:T(8,128)(2,1)}, bf16[96,2048]{1,0:T(8,128)(2,1)S(1)}, u32[]{:S(2)}, u32[]{:S(2)}) collective-permute-start(bf16[96,2048]{1,0:T(8,128)(2,1)} %get-tuple-element.78), channel_id=1, source_target_pairs={{0,96},{32,0},{64,32},{96,64},{1,97},{33,1},{65,33},{97,65},{2,98}... | collective-permute-start | bytes 1179656 | tf_op jit(solution)/shard_map/ppermute | solution.py:389
  161.9 9.2 %collective-permute-start.16 = (bf16[96,2048]{1,0:T(8,128)(2,1)}, bf16[96,2048]{1,0:T(8,128)(2,1)S(1)}, u32[]{:S(2)}, u32[]{:S(2)}) collective-permute-start(bf16[96,2048]{1,0:T(8,128)(2,1)} %get-tuple-element.79), channel_id=1, source_target_pairs={{0,32},{32,64},{64,96},{96,0},{1,33},{33,65},{65,97},{97,1},{2,34}... | collective-permute-start | bytes 1179656 | tf_op jit(solution)/shard_map/ppermute | solution.py:389
  174.2 23.1 %all-to-all-start.5 = ((bf16[16,24,2048]{2,1,0:T(8,128)(2,1)}), bf16[16,24,2048]{2,1,0:T(8,128)(2,1)S(1)}, u32[]{:S(2)}, u32[]{:S(2)}) async-start(bf16[16,24,2048]{2,1,0:T(8,128)(2,1)} %bitcast.29), calls=%async_computation.5 | async-start | bytes 3145728 | tf_op jit(solution)/shard_map/all_to_all | solution.py:392
  183.7 10.8 %collective-permute-start.17 = (bf16[128,2048]{1,0:T(8,128)(2,1)S(1)}, bf16[128,2048]{1,0:T(8,128)(2,1)S(1)}, u32[]{:S(2)}, u32[]{:S(2)}) collective-permute-start(bf16[128,2048]{1,0:T(8,128)(2,1)S(1)} %combine.2), channel_id=1, source_target_pairs={{0,64},{32,96},{64,0},{96,32},{1,65},{33,97},{65,1},{97,33},{2,66}... | collective-permute-start | bytes 1572872 | tf_op jit(solution)/shard_map/ppermute | solution.py:389

commit v6 on v5

--- a/solution.py
+++ b/solution.py
@@ -261,6 +261,23 @@
     )(*arrays, *(in_hbm(w) for w in (*mine, *other)))
 
 
+def keep_kernel(x_ref, out_ref):
+    pass
+
+
+def keep(x):
+    return pl.pallas_call(
+        keep_kernel,
+        in_specs=[pl.BlockSpec(memory_space=pltpu.HBM)],
+        out_specs=pl.BlockSpec(memory_space=pltpu.HBM),
+        out_shape=pltpu.HBM(x.shape, x.dtype),
+        input_output_aliases={0: 0},
+        compiler_params=pltpu.CompilerParams(vmem_limit_bytes=MIB),
+        cost_estimate=pl.CostEstimate(flops=100_000_000_000, bytes_accessed=1, transcendentals=0),
+        name="keep",
+    )(in_hbm(x))
+
+
 def combine_kernel(info_ref, back_ref, *refs, cuts):
     by_token = info_ref[...].T
     rows = by_token[:, 2 * TOP : 3 * TOP].astype(jnp.int32)
@@ -344,35 +361,43 @@
     )(in_hbm(qkv))
 
 
-def total_kernel(own_ref, *refs):
-    *in_refs, out_hbm, out_ref, sems = refs
+def total_kernel(own_ref, *refs, n_in, first):
+    in_refs, (out_hbm, out_ref, sems) = refs[:n_in], refs[-3:]
     start, copies = 0, []
     for i, (up_ref, down_ref) in enumerate(zip(in_refs[::2], in_refs[1::2], strict=True)):
         n = up_ref.shape[0]
-        total = own_ref[start : start + n].astype(F32) + up_ref[...].astype(F32)
+        total = own_ref[first + start : first + start + n].astype(F32) + up_ref[...].astype(F32)
         out_ref[start : start + n] = (total + down_ref[...].astype(F32)).astype(BF16)
-        here = pl.ds(start, n)
-        copies.append(pltpu.make_async_copy(out_ref.at[here], out_hbm.at[here], sems.at[i]))
+        copies.append(
+            pltpu.make_async_copy(
+                out_ref.at[pl.ds(start, n)], out_hbm.at[pl.ds(first + start, n)], sems.at[i]
+            )
+        )
         copies[-1].start()
         start += n
     for copy in copies:
         copy.wait()
 
 
-def add_up(own, pairs):
-    arrays = [own, *(x for pair in pairs for x in pair)]
-    return pl.pallas_call(
-        total_kernel,
-        in_specs=[pl.BlockSpec(memory_space=pltpu.VMEM)] * len(arrays),
-        out_specs=pl.BlockSpec(memory_space=pltpu.HBM),
+def add_up(own, pairs, first=0, into=None):
+    arrays = [x for pair in pairs for x in pair]
+    rows = sum(up.shape[0] for up, _ in pairs)
+    held, far = pl.BlockSpec(memory_space=pltpu.VMEM), pl.BlockSpec(memory_space=pltpu.HBM)
+    more = [] if into is None else [in_hbm(into)]
+    return pl.pallas_call(
+        functools.partial(total_kernel, n_in=len(arrays), first=first),
+        in_specs=[held] * (1 + len(arrays)) + [far] * len(more),
+        out_specs=far,
         out_shape=pltpu.HBM(own.shape, BF16),
+        input_output_aliases={1 + len(arrays): 0} if more else {},
         scratch_shapes=[
-            pltpu.VMEM(own.shape, BF16),
+            pltpu.VMEM((rows, own.shape[1]), BF16),
             pltpu.SemaphoreType.DMA((len(pairs),)),
         ],
         compiler_params=pltpu.CompilerParams(vmem_limit_bytes=16 * MIB),
+        cost_estimate=pl.CostEstimate(flops=1, bytes_accessed=1, transcendentals=0),
         name="add_up",
-    )(*arrays)
+    )(own, *arrays, *more)
 
 
 def per_device(stream_in, qkv_heads, expert_ids, gate_weights, w_out, w_gate, w_up, w_down):
@@ -407,36 +432,36 @@
 
     tie = lax.optimization_barrier
     far_tokens = shift(normed, 2)
-    own = exchange(buffer)
+    far_buffer = route(far_tokens, info_far, slots)
+    own, far_buffer = tie((exchange(buffer), far_buffer))
     eighth = own.shape[0] // 8
-    bounds = (0, 3 * eighth, 6 * eighth, 8 * eighth)
-    parts = [own[i:j] for i, j in zip(bounds[:-1], bounds[1:], strict=True)]
-    far_tokens, parts = tie((far_tokens, parts))
-    far_buffer = route(far_tokens, info_far, slots)
-    ups = [shift(x, 1) for x in parts[:2]]
-    downs = [shift(x, -1) for x in parts[:2]]
-    parts[2], ups[0], downs[0] = tie((parts[2], ups[0], downs[0]))
-    ups.append(shift(parts[2], 1))
-    downs.append(shift(parts[2], -1))
-
-    def near(i):
-        return experts([ups[i], downs[i]], mine, other)
-
-    [own_part] = experts([own], mine, other)
-    ups[0], downs[0], own_part = tie((ups[0], downs[0], own_part))
+    first, second = own[: 3 * eighth], own[3 * eighth : 6 * eighth]
+    rest, first, second = tie((own, first, second))
+    third = rest[6 * eighth :]
+    third, far_buffer = tie((third, far_buffer))
     far_rows = exchange(far_buffer)
-    back0 = near(0)
-    ups[1], downs[1], back0 = tie((ups[1], downs[1], back0))
-    back1 = near(1)
-    far_rows, back1 = tie((far_rows, back1))
-    [far_part] = experts([far_rows], mine, other)
-    home = [(shift(u, -1), shift(d, 1)) for u, d in (back0, back1)]
-    ups[2], downs[2], far_part, home[0] = tie((ups[2], downs[2], far_part, home[0]))
-    back2 = near(2)
-    home.append((shift(back2[0], -1), shift(back2[1], 1)))
-    far_back = exchange(far_part)
+
+    def send(x):
+        return shift(x, 1), shift(x, -1)
+
+    def give_back(pair):
+        return shift(pair[0], -1), shift(pair[1], 1)
+
+    at_first, at_second = send(first), send(second)
+    third, at_first = tie((third, at_first))
+    at_third = send(third)
+    own_part, *back = experts([own, *at_first], mine, other)
+    home = [give_back(back)]
+    far_rows, at_second, own_part = tie((far_rows, at_second, own_part))
+    far_part, *back = experts([far_rows, *at_second], mine, other)
+    home.append(give_back(back))
+    at_third, far_part, home[0] = tie((at_third, far_part, home[0]))
+    far_back = exchange(keep(far_part))
+    back = experts(at_third, mine, other)
+    home.append(give_back(back))
     far_sum = combine(info_far, far_back)
-    total = add_up(own_part, home)
+    total = add_up(own_part, home[:2])
+    total = add_up(own_part, home[2:], 6 * eighth, total)
     total, far_back = tie((total, far_back))
     back = exchange(total)
     far_home = shift(far_sum, 2)

time: 203 us -> 192 us (0.946)
  Pallas kernels: 66.8 us -> 58.1 us
  starting transfers between devices: 56.7 us -> 52.8 us
    ppermute x15, waiting for transfers between devices: 19.9 us -> 37.4 us  [shift(): return lax.ppermute(x, 'y', [(i, (i + by) % n_y) for i in range(n_y)])]
    all_to_all x4, waiting for transfers between devices: 23.7 us -> 8.16 us  [exchange(): return lax.all_to_all(x, exp, split_axis=0, concat_axis=0, tiled=True)]
    pallas_call x5 -> x3, Pallas kernels: 44.7 us -> 35.3 us  [experts(): pl.pallas_call(functools.partial(expert_kernel, n_in=len(arrays), block=b...]
    ppermute x15, starting transfers between devices: 21.9 us -> 18.3 us  [shift(): return lax.ppermute(x, 'y', [(i, (i + by) % n_y) for i in range(n_y)])]
  transfers between devices with their start and end apart: 23 -> 23, of which waited for: 6 -> 9; matrix products, arithmetic and copies ran while one was open for 1% -> 0% of each run, Pallas kernels for 30% -> 27%
where the time goes in v6:
time: 192 us; the launch traced here: 189 us
  waiting for transfers between devices  63.3 us (33%)
  Pallas kernels  58.1 us (30%)
  starting transfers between devices  52.8 us (28%)
  blocking collectives  12.8 us (7%)
    ppermute x15, waiting for transfers between devices, shift(): return lax.ppermute(x, 'y', [(i, (i + by) % n_y) for i in range(n_y)])  37.4 us
    pallas_call x3, Pallas kernels, experts(): pl.pallas_call(functools.partial(expert_kernel, n_in=len(arrays), block=b...  35.3 us
    all_to_all x4, starting transfers between devices, exchange(): return lax.all_to_all(x, exp, split_axis=0, concat_axis=0, tiled=True)  29.4 us
    ppermute x15, starting transfers between devices, shift(): return lax.ppermute(x, 'y', [(i, (i + by) % n_y) for i in range(n_y)])  18.3 us
    all_to_all x1, waiting for transfers between devices, per_device(): arrived = lax.all_to_all(qkv, seq, split_axis=0, concat_axis=0, tiled=True)  17.7 us
    all_to_all x1, blocking collectives, per_device(): lax.all_to_all(context, seq, split_axis=0, concat_axis=0, tiled=True)  12.8 us
    all_to_all x4, waiting for transfers between devices, exchange(): return lax.all_to_all(x, exp, split_axis=0, concat_axis=0, tiled=True)  8.16 us
    pallas_call x1, Pallas kernels, attention(): pl.pallas_call(functools.partial(attention_kernel, block=2 * rows), grid=...  6.15 us
  transfers between devices with their start and end apart: 23, of which 9 were waited for; matrix products, arithmetic and copies ran while one was open for 0% of the time, Pallas kernels for 27%

profile of v6, /device:TPU:2, one launch (start us, length us, event | category | flops | bytes accessed | tf_op | source)
XLA Modules:
  0.0 189.3 jit_solution(11285131427684281533)
XLA Ops:
  0.0 0.0 collective-permute-start.1
  0.0 0.5 collective-permute-start.2
  0.5 0.0 collective-permute-start.3
  0.5 2.4 %spread.1 = bf16[8,3,128,256]{3,2,1,0:T(8,128)(2,1)} custom-call(bf16[3,128,2048]{2,1,0:T(8,128)(2,1)} %bitcast.29), custom_call_target="tpu_custom_call" | custom-call | tf_op jit(solution)/shard_map/spread/pallas_call | solution.py:349
  3.0 0.0 copy-start.2
  3.0 0.0 copy-start.3
  3.0 4.6 %all-to-all-start = ((bf16[8,3,128,256]{3,2,1,0:T(8,128)(2,1)}), bf16[8,3,128,256]{3,2,1,0:T(8,128)(2,1)S(1)}, u32[]{:S(2)}, u32[]{:S(2)}) async-start(bf16[8,3,128,256]{3,2,1,0:T(8,128)(2,1)} %spread.1), calls=%async_computation | async-start | bytes 3145728 | tf_op jit(solution)/shard_map/all_to_all | solution.py:427
  7.6 0.1 pad.2.clone
  7.7 0.1 maximum_maximum_fusion.info_ref
  7.7 0.1 plan.1.info_ref
  7.9 3.6 %collective-permute-start = (f32[8,128]{1,0:T(8,128)S(1)}, f32[8,128]{1,0:T(8,128)S(1)}, u32[]{:S(2)}, u32[]{:S(2)}) collective-permute-start(f32[8,128]{1,0:T(8,128)S(1)} %plan.1.info_ref), channel_id=1, source_target_pairs={{0,64},{32,96},{64,0},{96,32},{1,65},{33,97},{65,1},{97,33},{2,66}... | collective-permute-start | bytes 12296 | tf_op jit(solution)/shard_map/ppermute | solution.py:414
  11.5 17.7 %all-to-all-done.x_ref = bf16[8,3,128,256]{3,2,1,0:T(8,128)(2,1)S(1)} async-done(((bf16[8,3,128,256]{3,2,1,0:T(8,128)(2,1)}), bf16[8,3,128,256]{3,2,1,0:T(8,128)(2,1)S(1)}, u32[]{:S(2)}, u32[]{:S(2)}) %all-to-all-start) | async-done | bytes 1572896 | tf_op jit(solution)/shard_map/all_to_all | solution.py:427
  29.2 6.2 %attention.1 = (bf16[8,128,256]{2,1,0:T(8,128)(2,1)S(1)}, bf16[2048,2048]{1,0:T(8,128)(2,1)S(1)}) custom-call(bf16[8,3,128,256]{3,2,1,0:T(8,128)(2,1)S(1)} %all-to-all-done.x_ref, bf16[2048,2048]{1,0:T(8,128)(2,1)} %w_hbm.1), custom_call_target="tpu_custom_call" | custom-call | tf_op jit(solution)/shard_map/attention/pallas_call | solution.py:71
  35.4 0.0 collective-permute-done.info_ref
  35.4 0.0 collective-permute-done.1.refs_6_.refs_5_
  35.4 0.0 collective-permute-done.2.refs_7_.refs_6_
  35.4 0.0 collective-permute-done.3.refs_8_.refs_7_
  35.4 12.8 %all_to_all.56.ctx_ref = bf16[8,128,256]{2,1,0:T(8,128)(2,1)S(1)} all-to-all(bf16[8,128,256]{2,1,0:T(8,128)(2,1)S(1)} %get-tuple-element.44), channel_id=1, replica_groups=mesh['y'=4,'core'=2,'z'=4,'x'=4] {'y','core'}, dimensions={0} | all-to-all | bytes 1048576 | tf_op jit(solution)/shard_map/all_to_all | solution.py:430
  48.2 3.7 %project.1 = (f32[128,2048]{1,0:T(8,128)}, bf16[128,2048]{1,0:T(8,128)(2,1)S(1)}, bf16[384,2048]{1,0:T(8,128)(2,1)}) custom-call(bf16[8,128,256]{2,1,0:T(8,128)(2,1)S(1)} %all_to_all.56.ctx_ref, bf16[2048,2048]{1,0:T(8,128)(2,1)S(1)} %get-tuple-element.45.w_ref, bf16[128,2048]{1,0:T(8,128)(2,1)S(1)} %bitcast.27, f32[8,128]{1,0:T(8,128)S(1)} %plan.1.info_ref), custom_call_target="tpu_custom_call" | custom-call | tf_op jit(solution)/shard_map/project/pallas_call | solution.py:149
  51.9 8.3 %all-to-all-start.2 = ((bf16[16,24,2048]{2,1,0:T(8,128)(2,1)}), bf16[16,24,2048]{2,1,0:T(8,128)(2,1)S(1)}, u32[]{:S(2)}, u32[]{:S(2)}) async-start(bf16[16,24,2048]{2,1,0:T(8,128)(2,1)} %bitcast.10), calls=%async_computation.2 | async-start | bytes 3145728 | tf_op jit(solution)/shard_map/all_to_all | solution.py:417
  60.2 0.3 collective-permute-start.4
  60.6 13.9 %collective-permute-done.4.normed_ref = bf16[128,2048]{1,0:T(8,128)(2,1)S(1)} collective-permute-done((bf16[128,2048]{1,0:T(8,128)(2,1)S(1)}, bf16[128,2048]{1,0:T(8,128)(2,1)S(1)}, u32[]{:S(2)}, u32[]{:S(2)}) %collective-permute-start.4) | collective-permute-done | bytes 524320 | tf_op jit(solution)/shard_map/ppermute | solution.py:414
  74.5 1.7 route.1
  76.2 5.2 %all-to-all-done.2 = bf16[16,24,2048]{2,1,0:T(8,128)(2,1)S(1)} async-done(((bf16[16,24,2048]{2,1,0:T(8,128)(2,1)}), bf16[16,24,2048]{2,1,0:T(8,128)(2,1)S(1)}, u32[]{:S(2)}, u32[]{:S(2)}) %all-to-all-start.2) | async-done | bytes 1572896 | tf_op jit(solution)/shard_map/all_to_all | solution.py:417
  81.4 0.9 fusion
  82.3 1.2 collective-permute-start.8
  83.4 0.9 collective-permute-start.7
  84.3 2.4 %collective-permute-start.6 = (bf16[144,2048]{1,0:T(8,128)(2,1)}, bf16[144,2048]{1,0:T(8,128)(2,1)}, u32[]{:S(2)}, u32[]{:S(2)}) collective-permute-start(bf16[144,2048]{1,0:T(8,128)(2,1)} %get-tuple-element.53), channel_id=1, source_target_pairs={{0,96},{32,0},{64,32},{96,64},{1,97},{33,1},{65,33},{97,65},{2,98}... | collective-permute-start | bytes 1769480 | tf_op jit(solution)/shard_map/ppermute | solution.py:414
  86.7 0.0 collective-permute-start.5
  86.7 0.8 slice.11
  87.5 6.9 %all-to-all-start.3 = ((bf16[16,24,2048]{2,1,0:T(8,128)(2,1)}), bf16[16,24,2048]{2,1,0:T(8,128)(2,1)}, u32[]{:S(2)}, u32[]{:S(2)}) async-start(bf16[16,24,2048]{2,1,0:T(8,128)(2,1)} %bitcast.12), calls=%async_computation.3 | async-start | bytes 3145728 | tf_op jit(solution)/shard_map/all_to_all | solution.py:417
  94.3 4.2 %collective-permute-done.8.refs_2_ = bf16[144,2048]{1,0:T(8,128)(2,1)S(1)} collective-permute-done((bf16[144,2048]{1,0:T(8,128)(2,1)S(1)}, bf16[144,2048]{1,0:T(8,128)(2,1)S(1)}, u32[]{:S(2)}, u32[]{:S(2)}) %collective-permute-start.8) | collective-permute-done | bytes 589856 | tf_op jit(solution)/shard_map/ppermute | solution.py:414
  98.5 2.4 %collective-permute-done.7.refs_1_ = bf16[144,2048]{1,0:T(8,128)(2,1)S(1)} collective-permute-done((bf16[144,2048]{1,0:T(8,128)(2,1)S(1)}, bf16[144,2048]{1,0:T(8,128)(2,1)S(1)}, u32[]{:S(2)}, u32[]{:S(2)}) %collective-permute-start.7) | collective-permute-done | bytes 589856 | tf_op jit(solution)/shard_map/ppermute | solution.py:414
  100.9 0.0 collective-permute-start.10
  100.9 2.0 %collective-permute-start.9 = (bf16[96,2048]{1,0:T(8,128)(2,1)}, bf16[96,2048]{1,0:T(8,128)(2,1)}, u32[]{:S(2)}, u32[]{:S(2)}) collective-permute-start(bf16[96,2048]{1,0:T(8,128)(2,1)} %slice.11), channel_id=1, source_target_pairs={{0,32},{32,64},{64,96},{96,0},{1,33},{33,65},{65,97},{97,1},{2,34}... | collective-permute-start | bytes 1179656 | tf_op jit(solution)/shard_map/ppermute | solution.py:414
  102.9 12.9 %experts.3 = (bf16[384,2048]{1,0:T(8,128)(2,1)}, bf16[144,2048]{1,0:T(8,128)(2,1)}, bf16[144,2048]{1,0:T(8,128)(2,1)}) custom-call(bf16[384,2048]{1,0:T(8,128)(2,1)S(1)} %bitcast.25, bf16[144,2048]{1,0:T(8,128)(2,1)S(1)} %collective-permute-done.7.refs_1_, bf16[144,2048]{1,0:T(8,128)(2,1)S(1)} %collective-permute-done.8.refs_2_, bf16[2048,512]{1,0:T(8,128)(2,1)} %bitcast.33, ...), custom_call_target="tpu_custom_call" | custom-call | flops 845571686400 | bytes 18087936 | tf_op jit(solution)/shard_map/experts/pallas_call | solution.py:238
  115.8 1.3 collective-permute-start.11
  117.1 0.0 collective-permute-done.6.refs_2_
  117.1 0.8 collective-permute-start.12
  117.9 0.0 collective-permute-done.5.refs_1_
  117.9 0.0 all-to-all-done.3
  117.9 14.4 %experts.4 = (bf16[384,2048]{1,0:T(8,128)(2,1)}, bf16[144,2048]{1,0:T(8,128)(2,1)}, bf16[144,2048]{1,0:T(8,128)(2,1)}) custom-call(bf16[384,2048]{1,0:T(8,128)(2,1)} %bitcast.13.refs_0_, bf16[144,2048]{1,0:T(8,128)(2,1)} %collective-permute-done.5.refs_1_, bf16[144,2048]{1,0:T(8,128)(2,1)} %collective-permute-done.6.refs_2_, bf16[2048,512]{1,0:T(8,128)(2,1)} %bitcast.34, ...), custom_call_target="tpu_custom_call" | custom-call | flops 845571686400 | bytes 18087936 | tf_op jit(solution)/shard_map/experts/pallas_call | solution.py:238
  132.3 2.5 %collective-permute-start.15 = (bf16[144,2048]{1,0:T(8,128)(2,1)}, bf16[144,2048]{1,0:T(8,128)(2,1)}, u32[]{:S(2)}, u32[]{:S(2)}) collective-permute-start(bf16[144,2048]{1,0:T(8,128)(2,1)} %get-tuple-element.76), channel_id=1, source_target_pairs={{0,96},{32,0},{64,32},{96,64},{1,97},{33,1},{65,33},{97,65},{2,98}... | collective-permute-start | bytes 1769480 | tf_op jit(solution)/shard_map/ppermute | solution.py:414
  134.8 0.0 collective-permute-done.10.refs_1_
  134.8 0.0 collective-permute-start.16
  134.8 0.0 collective-permute-done.9.refs_0_
  134.9 0.0 collective-permute-done.11.refs_0_
  134.9 0.0 collective-permute-done.12.refs_1_
  134.9 6.9 %all-to-all-start.4 = ((bf16[16,24,2048]{2,1,0:T(8,128)(2,1)}), bf16[16,24,2048]{2,1,0:T(8,128)(2,1)}, u32[]{:S(2)}, u32[]{:S(2)}) async-start(bf16[16,24,2048]{2,1,0:T(8,128)(2,1)} %bitcast.30), calls=%async_computation.4 | async-start | bytes 3145728 | tf_op jit(solution)/shard_map/all_to_all | solution.py:417
  141.8 8.0 %experts.5 = (bf16[96,2048]{1,0:T(8,128)(2,1)}, bf16[96,2048]{1,0:T(8,128)(2,1)}) custom-call(bf16[96,2048]{1,0:T(8,128)(2,1)} %collective-permute-done.9.refs_0_, bf16[96,2048]{1,0:T(8,128)(2,1)} %collective-permute-done.10.refs_1_, bf16[2048,512]{1,0:T(8,128)(2,1)} %bitcast.35, bf16[2048,512]{1,0:T(8,128)(2,1)} %bitcast.39, bf16[512,2048]{1,0:T(8,128)(2,1)} %bitcast.43, ...), custom_call_target="tpu_custom_call" | custom-call | flops 241591910400 | bytes 14155776 | tf_op jit(solution)/shard_map/experts/pallas_call | solution.py:238
  149.8 3.3 %collective-permute-start.13 = (bf16[96,2048]{1,0:T(8,128)(2,1)}, bf16[96,2048]{1,0:T(8,128)(2,1)S(1)}, u32[]{:S(2)}, u32[]{:S(2)}) collective-permute-start(bf16[96,2048]{1,0:T(8,128)(2,1)} %get-tuple-element.72), channel_id=1, source_target_pairs={{0,96},{32,0},{64,32},{96,64},{1,97},{33,1},{65,33},{97,65},{2,98}... | collective-permute-start | bytes 1179656 | tf_op jit(solution)/shard_map/ppermute | solution.py:414
  153.1 0.0 collective-permute-start.14
  153.1 0.0 collective-permute-done.15.refs_2_
  153.1 0.0 collective-permute-done.16.refs_3_
  153.1 2.9 %add_up.2.refs_2_ = bf16[384,2048]{1,0:T(8,128)(2,1)} custom-call(bf16[384,2048]{1,0:T(8,128)(2,1)S(1)} %copy-done, bf16[144,2048]{1,0:T(8,128)(2,1)} %collective-permute-done.11.refs_0_, bf16[144,2048]{1,0:T(8,128)(2,1)} %collective-permute-done.12.refs_1_, bf16[144,2048]{1,0:T(8,128)(2,1)} %collective-permute-done.15.refs_2_, ...), custom_call_target="tpu_custom_call" | custom-call | flops 1 | bytes 1 | tf_op jit(solution)/shard_map/add_up/pallas_call | solution.py:387
  156.0 2.6 %collective-permute-done.13.refs_0_ = bf16[96,2048]{1,0:T(8,128)(2,1)S(1)} collective-permute-done((bf16[96,2048]{1,0:T(8,128)(2,1)}, bf16[96,2048]{1,0:T(8,128)(2,1)S(1)}, u32[]{:S(2)}, u32[]{:S(2)}) %collective-permute-start.13) | collective-permute-done | bytes 393248 | tf_op jit(solution)/shard_map/ppermute | solution.py:414
  158.7 3.6 %collective-permute-done.14.refs_1_ = bf16[96,2048]{1,0:T(8,128)(2,1)S(1)} collective-permute-done((bf16[96,2048]{1,0:T(8,128)(2,1)}, bf16[96,2048]{1,0:T(8,128)(2,1)S(1)}, u32[]{:S(2)}, u32[]{:S(2)}) %collective-permute-start.14) | collective-permute-done | bytes 393248 | tf_op jit(solution)/shard_map/ppermute | solution.py:414
  162.3 0.9 add_up.3
  163.2 7.3 %all-to-all-start.5 = ((bf16[16,24,2048]{2,1,0:T(8,128)(2,1)}), bf16[16,24,2048]{2,1,0:T(8,128)(2,1)S(1)}, u32[]{:S(2)}, u32[]{:S(2)}) async-start(bf16[16,24,2048]{2,1,0:T(8,128)(2,1)} %bitcast.28), calls=%async_computation.5 | async-start | bytes 3145728 | tf_op jit(solution)/shard_map/all_to_all | solution.py:417
  170.5 2.2 %combine.2 = bf16[128,2048]{1,0:T(8,128)(2,1)S(1)} custom-call(f32[8,128]{1,0:T(8,128)S(1)} %collective-permute-done.info_ref, bf16[384,2048]{1,0:T(8,128)(2,1)} %bitcast.15.back_ref), custom_call_target="tpu_custom_call" | custom-call | tf_op jit(solution)/shard_map/combine/pallas_call | solution.py:313
  172.7 0.1 collective-permute-start.17
  172.8 10.7 %collective-permute-done.17.refs_0_ = bf16[128,2048]{1,0:T(8,128)(2,1)S(1)} collective-permute-done((bf16[128,2048]{1,0:T(8,128)(2,1)S(1)}, bf16[128,2048]{1,0:T(8,128)(2,1)S(1)}, u32[]{:S(2)}, u32[]{:S(2)}) %collective-permute-start.17) | collective-permute-done | bytes 524320 | tf_op jit(solution)/shard_map/ppermute | solution.py:414
  183.5 2.9 %all-to-all-done.5 = bf16[16,24,2048]{2,1,0:T(8,128)(2,1)S(1)} async-done(((bf16[16,24,2048]{2,1,0:T(8,128)(2,1)}), bf16[16,24,2048]{2,1,0:T(8,128)(2,1)S(1)}, u32[]{:S(2)}, u32[]{:S(2)}) %all-to-all-start.5) | async-done | bytes 1572896 | tf_op jit(solution)/shard_map/all_to_all | solution.py:417
  186.4 2.7 %combine.3 = bf16[128,2048]{1,0:T(8,128)(2,1)} custom-call(f32[8,128]{1,0:T(8,128)S(1)} %plan.1.info_ref, bf16[384,2048]{1,0:T(8,128)(2,1)S(1)} %bitcast.26, bf16[128,2048]{1,0:T(8,128)(2,1)S(1)} %collective-permute-done.17.refs_0_, f32[128,2048]{1,0:T(8,128)} %get-tuple-element.80.refs_1_), custom_call_target="tpu_custom_call" | custom-call | tf_op jit(solution)/shard_map/combine/pallas_call | solution.py:313
  (10 shorter events, 0.0 us)
Async XLA Ops:
  0.0 35.4 %collective-permute-start.1 = (bf16[2048,512]{1,0:T(8,128)(2,1)}, bf16[2048,512]{1,0:T(8,128)(2,1)}, u32[]{:S(2)}, u32[]{:S(2)}) collective-permute-start(bf16[2048,512]{1,0:T(8,128)(2,1)} %bitcast.32), channel_id=1, source_target_pairs={{0,16},{16,0},{1,17},{17,1},{2,18},{18,2},{3,19},{19,3},{4,20},{20... | collective-permute-start | bytes 6291464 | tf_op jit(solution)/shard_map/ppermute | solution.py:411
  0.0 35.4 %collective-permute-start.2 = (bf16[2048,512]{1,0:T(8,128)(2,1)}, bf16[2048,512]{1,0:T(8,128)(2,1)}, u32[]{:S(2)}, u32[]{:S(2)}) collective-permute-start(bf16[2048,512]{1,0:T(8,128)(2,1)} %bitcast.36), channel_id=1, source_target_pairs={{0,16},{16,0},{1,17},{17,1},{2,18},{18,2},{3,19},{19,3},{4,20},{20... | collective-permute-start | bytes 6291464 | tf_op jit(solution)/shard_map/ppermute | solution.py:411
  0.5 34.9 %collective-permute-start.3 = (bf16[512,2048]{1,0:T(8,128)(2,1)}, bf16[512,2048]{1,0:T(8,128)(2,1)}, u32[]{:S(2)}, u32[]{:S(2)}) collective-permute-start(bf16[512,2048]{1,0:T(8,128)(2,1)} %bitcast.40), channel_id=1, source_target_pairs={{0,16},{16,0},{1,17},{17,1},{2,18},{18,2},{3,19},{19,3},{4,20},{20... | collective-permute-start | bytes 6291464 | tf_op jit(solution)/shard_map/ppermute | solution.py:411
  3.0 4.7 %copy-start.2 = (s32[1,128,2]{1,2,0:T(2,128)S(1)}, s32[1,128,2]{1,2,0:T(2,128)}, u32[]{:S(2)}) copy-start(s32[1,128,2]{1,2,0:T(2,128)} %param.10) | copy-start | bytes 3076
  3.0 4.7 %copy-start.3 = (f32[1,128,2]{1,2,0:T(2,128)S(1)}, f32[1,128,2]{1,2,0:T(2,128)}, u32[]{:S(2)}) copy-start(f32[1,128,2]{1,2,0:T(2,128)} %param.11) | copy-start | bytes 3076
  3.0 26.2 %all-to-all-start = ((bf16[8,3,128,256]{3,2,1,0:T(8,128)(2,1)}), bf16[8,3,128,256]{3,2,1,0:T(8,128)(2,1)S(1)}, u32[]{:S(2)}, u32[]{:S(2)}) async-start(bf16[8,3,128,256]{3,2,1,0:T(8,128)(2,1)} %spread.1), calls=%async_computation | async-start | bytes 3145728 | tf_op jit(solution)/shard_map/all_to_all | solution.py:427
  7.9 40.3 %copy-start.1 = (bf16[1,128,2048]{2,1,0:T(8,128)(2,1)S(1)}, bf16[1,128,2048]{2,1,0:T(8,128)(2,1)}, u32[]{:S(2)}) copy-start(bf16[1,128,2048]{2,1,0:T(8,128)(2,1)} %param.8) | copy-start | bytes 1572868
  7.9 27.5 %collective-permute-start = (f32[8,128]{1,0:T(8,128)S(1)}, f32[8,128]{1,0:T(8,128)S(1)}, u32[]{:S(2)}, u32[]{:S(2)}) collective-permute-start(f32[8,128]{1,0:T(8,128)S(1)} %plan.1.info_ref), channel_id=1, source_target_pairs={{0,64},{32,96},{64,0},{96,32},{1,65},{33,97},{65,1},{97,33},{2,66}... | collective-permute-start | bytes 12296 | tf_op jit(solution)/shard_map/ppermute | solution.py:414
  51.9 29.5 %all-to-all-start.2 = ((bf16[16,24,2048]{2,1,0:T(8,128)(2,1)}), bf16[16,24,2048]{2,1,0:T(8,128)(2,1)S(1)}, u32[]{:S(2)}, u32[]{:S(2)}) async-start(bf16[16,24,2048]{2,1,0:T(8,128)(2,1)} %bitcast.10), calls=%async_computation.2 | async-start | bytes 3145728 | tf_op jit(solution)/shard_map/all_to_all | solution.py:417
  60.2 14.2 %collective-permute-start.4 = (bf16[128,2048]{1,0:T(8,128)(2,1)S(1)}, bf16[128,2048]{1,0:T(8,128)(2,1)S(1)}, u32[]{:S(2)}, u32[]{:S(2)}) collective-permute-start(bf16[128,2048]{1,0:T(8,128)(2,1)S(1)} %get-tuple-element.47), channel_id=1, source_target_pairs={{0,64},{32,96},{64,0},{96,32},{1,65},{33,97},{65,1},{97,33},{2,66}... | collective-permute-start | bytes 1572872 | tf_op jit(solution)/shard_map/ppermute | solution.py:414
  82.3 16.3 %collective-permute-start.8 = (bf16[144,2048]{1,0:T(8,128)(2,1)S(1)}, bf16[144,2048]{1,0:T(8,128)(2,1)S(1)}, u32[]{:S(2)}, u32[]{:S(2)}) collective-permute-start(bf16[144,2048]{1,0:T(8,128)(2,1)S(1)} %get-tuple-element.55), channel_id=1, source_target_pairs={{0,96},{32,0},{64,32},{96,64},{1,97},{33,1},{65,33},{97,65},{2,98}... | collective-permute-start | bytes 1769480 | tf_op jit(solution)/shard_map/ppermute | solution.py:414
  83.4 17.5 %collective-permute-start.7 = (bf16[144,2048]{1,0:T(8,128)(2,1)S(1)}, bf16[144,2048]{1,0:T(8,128)(2,1)S(1)}, u32[]{:S(2)}, u32[]{:S(2)}) collective-permute-start(bf16[144,2048]{1,0:T(8,128)(2,1)S(1)} %get-tuple-element.55), channel_id=1, source_target_pairs={{0,32},{32,64},{64,96},{96,0},{1,33},{33,65},{65,97},{97,1},{2,34}... | collective-permute-start | bytes 1769480 | tf_op jit(solution)/shard_map/ppermute | solution.py:414
  84.3 32.8 %collective-permute-start.6 = (bf16[144,2048]{1,0:T(8,128)(2,1)}, bf16[144,2048]{1,0:T(8,128)(2,1)}, u32[]{:S(2)}, u32[]{:S(2)}) collective-permute-start(bf16[144,2048]{1,0:T(8,128)(2,1)} %get-tuple-element.53), channel_id=1, source_target_pairs={{0,96},{32,0},{64,32},{96,64},{1,97},{33,1},{65,33},{97,65},{2,98}... | collective-permute-start | bytes 1769480 | tf_op jit(solution)/shard_map/ppermute | solution.py:414
  86.7 31.2 %collective-permute-start.5 = (bf16[144,2048]{1,0:T(8,128)(2,1)}, bf16[144,2048]{1,0:T(8,128)(2,1)}, u32[]{:S(2)}, u32[]{:S(2)}) collective-permute-start(bf16[144,2048]{1,0:T(8,128)(2,1)} %get-tuple-element.53), channel_id=1, source_target_pairs={{0,32},{32,64},{64,96},{96,0},{1,33},{33,65},{65,97},{97,1},{2,34}... | collective-permute-start | bytes 1769480 | tf_op jit(solution)/shard_map/ppermute | solution.py:414
  87.5 30.5 %all-to-all-start.3 = ((bf16[16,24,2048]{2,1,0:T(8,128)(2,1)}), bf16[16,24,2048]{2,1,0:T(8,128)(2,1)}, u32[]{:S(2)}, u32[]{:S(2)}) async-start(bf16[16,24,2048]{2,1,0:T(8,128)(2,1)} %bitcast.12), calls=%async_computation.3 | async-start | bytes 3145728 | tf_op jit(solution)/shard_map/all_to_all | solution.py:417
  100.9 33.9 %collective-permute-start.10 = (bf16[96,2048]{1,0:T(8,128)(2,1)}, bf16[96,2048]{1,0:T(8,128)(2,1)}, u32[]{:S(2)}, u32[]{:S(2)}) collective-permute-start(bf16[96,2048]{1,0:T(8,128)(2,1)} %slice.11), channel_id=1, source_target_pairs={{0,96},{32,0},{64,32},{96,64},{1,97},{33,1},{65,33},{97,65},{2,98}... | collective-permute-start | bytes 1179656 | tf_op jit(solution)/shard_map/ppermute | solution.py:414
  100.9 33.9 %collective-permute-start.9 = (bf16[96,2048]{1,0:T(8,128)(2,1)}, bf16[96,2048]{1,0:T(8,128)(2,1)}, u32[]{:S(2)}, u32[]{:S(2)}) collective-permute-start(bf16[96,2048]{1,0:T(8,128)(2,1)} %slice.11), channel_id=1, source_target_pairs={{0,32},{32,64},{64,96},{96,0},{1,33},{33,65},{65,97},{97,1},{2,34}... | collective-permute-start | bytes 1179656 | tf_op jit(solution)/shard_map/ppermute | solution.py:414
  115.8 19.0 %collective-permute-start.11 = (bf16[144,2048]{1,0:T(8,128)(2,1)}, bf16[144,2048]{1,0:T(8,128)(2,1)}, u32[]{:S(2)}, u32[]{:S(2)}) collective-permute-start(bf16[144,2048]{1,0:T(8,128)(2,1)} %get-tuple-element.68), channel_id=1, source_target_pairs={{0,96},{32,0},{64,32},{96,64},{1,97},{33,1},{65,33},{97,65},{2,98}... | collective-permute-start | bytes 1769480 | tf_op jit(solution)/shard_map/ppermute | solution.py:414
  117.1 17.8 %collective-permute-start.12 = (bf16[144,2048]{1,0:T(8,128)(2,1)}, bf16[144,2048]{1,0:T(8,128)(2,1)}, u32[]{:S(2)}, u32[]{:S(2)}) collective-permute-start(bf16[144,2048]{1,0:T(8,128)(2,1)} %get-tuple-element.69), channel_id=1, source_target_pairs={{0,32},{32,64},{64,96},{96,0},{1,33},{33,65},{65,97},{97,1},{2,34}... | collective-permute-start | bytes 1769480 | tf_op jit(solution)/shard_map/ppermute | solution.py:414
  132.3 20.8 %collective-permute-start.15 = (bf16[144,2048]{1,0:T(8,128)(2,1)}, bf16[144,2048]{1,0:T(8,128)(2,1)}, u32[]{:S(2)}, u32[]{:S(2)}) collective-permute-start(bf16[144,2048]{1,0:T(8,128)(2,1)} %get-tuple-element.76), channel_id=1, source_target_pairs={{0,96},{32,0},{64,32},{96,64},{1,97},{33,1},{65,33},{97,65},{2,98}... | collective-permute-start | bytes 1769480 | tf_op jit(solution)/shard_map/ppermute | solution.py:414
  134.8 18.2 %collective-permute-start.16 = (bf16[144,2048]{1,0:T(8,128)(2,1)}, bf16[144,2048]{1,0:T(8,128)(2,1)}, u32[]{:S(2)}, u32[]{:S(2)}) collective-permute-start(bf16[144,2048]{1,0:T(8,128)(2,1)} %get-tuple-element.77), channel_id=1, source_target_pairs={{0,32},{32,64},{64,96},{96,0},{1,33},{33,65},{65,97},{97,1},{2,34}... | collective-permute-start | bytes 1769480 | tf_op jit(solution)/shard_map/ppermute | solution.py:414
  134.9 28.3 %all-to-all-start.4 = ((bf16[16,24,2048]{2,1,0:T(8,128)(2,1)}), bf16[16,24,2048]{2,1,0:T(8,128)(2,1)}, u32[]{:S(2)}, u32[]{:S(2)}) async-start(bf16[16,24,2048]{2,1,0:T(8,128)(2,1)} %bitcast.30), calls=%async_computation.4 | async-start | bytes 3145728 | tf_op jit(solution)/shard_map/all_to_all | solution.py:417
  141.8 11.3 %copy-start = (bf16[384,2048]{1,0:T(8,128)(2,1)S(1)}, bf16[384,2048]{1,0:T(8,128)(2,1)}, u32[]{:S(2)}) copy-start(bf16[384,2048]{1,0:T(8,128)(2,1)} %get-tuple-element.62.own_ref) | copy-start | bytes 4718596
  149.8 8.9 %collective-permute-start.13 = (bf16[96,2048]{1,0:T(8,128)(2,1)}, bf16[96,2048]{1,0:T(8,128)(2,1)S(1)}, u32[]{:S(2)}, u32[]{:S(2)}) collective-permute-start(bf16[96,2048]{1,0:T(8,128)(2,1)} %get-tuple-element.72), channel_id=1, source_target_pairs={{0,96},{32,0},{64,32},{96,64},{1,97},{33,1},{65,33},{97,65},{2,98}... | collective-permute-start | bytes 1179656 | tf_op jit(solution)/shard_map/ppermute | solution.py:414
  153.1 9.2 %collective-permute-start.14 = (bf16[96,2048]{1,0:T(8,128)(2,1)}, bf16[96,2048]{1,0:T(8,128)(2,1)S(1)}, u32[]{:S(2)}, u32[]{:S(2)}) collective-permute-start(bf16[96,2048]{1,0:T(8,128)(2,1)} %get-tuple-element.73), channel_id=1, source_target_pairs={{0,32},{32,64},{64,96},{96,0},{1,33},{33,65},{65,97},{97,1},{2,34}... | collective-permute-start | bytes 1179656 | tf_op jit(solution)/shard_map/ppermute | solution.py:414
  163.2 23.3 %all-to-all-start.5 = ((bf16[16,24,2048]{2,1,0:T(8,128)(2,1)}), bf16[16,24,2048]{2,1,0:T(8,128)(2,1)S(1)}, u32[]{:S(2)}, u32[]{:S(2)}) async-start(bf16[16,24,2048]{2,1,0:T(8,128)(2,1)} %bitcast.28), calls=%async_computation.5 | async-start | bytes 3145728 | tf_op jit(solution)/shard_map/all_to_all | solution.py:417
  172.7 10.8 %collective-permute-start.17 = (bf16[128,2048]{1,0:T(8,128)(2,1)S(1)}, bf16[128,2048]{1,0:T(8,128)(2,1)S(1)}, u32[]{:S(2)}, u32[]{:S(2)}) collective-permute-start(bf16[128,2048]{1,0:T(8,128)(2,1)S(1)} %combine.2), channel_id=1, source_target_pairs={{0,64},{32,96},{64,0},{96,32},{1,65},{33,97},{65,1},{97,33},{2,66}... | collective-permute-start | bytes 1572872 | tf_op jit(solution)/shard_map/ppermute | solution.py:414

commit v7 on v6

--- a/solution.py
+++ b/solution.py
@@ -450,9 +450,11 @@
     at_first, at_second = send(first), send(second)
     third, at_first = tie((third, at_first))
     at_third = send(third)
-    own_part, *back = experts([own, *at_first], mine, other)
+    [own_part] = experts([own], mine, other)
+    at_first, own_part = tie((at_first, own_part))
+    back = experts(at_first, mine, other)
     home = [give_back(back)]
-    far_rows, at_second, own_part = tie((far_rows, at_second, own_part))
+    far_rows, at_second, back = tie((far_rows, at_second, back))
     far_part, *back = experts([far_rows, *at_second], mine, other)
     home.append(give_back(back))
     at_third, far_part, home[0] = tie((at_third, far_part, home[0]))

time: 192 us -> 194 us (1.010)
  waiting for transfers between devices: 63.3 us -> 56.7 us
  Pallas kernels: 58.1 us -> 63.1 us
  starting transfers between devices: 52.8 us -> 56.5 us
    ppermute x15, waiting for transfers between devices: 37.4 us -> 30.9 us  [shift(): return lax.ppermute(x, 'y', [(i, (i + by) % n_y) for i in range(n_y)])]
    pallas_call x3 -> x4, Pallas kernels: 35.3 us -> 40.2 us  [experts(): pl.pallas_call(functools.partial(expert_kernel, n_in=len(arrays), block=b...]
    ppermute x15, starting transfers between devices: 18.3 us -> 21.6 us  [shift(): return lax.ppermute(x, 'y', [(i, (i + by) % n_y) for i in range(n_y)])]
  transfers between devices with their start and end apart: 23 -> 23, of which waited for: 9 -> 7; matrix products, arithmetic and copies ran while one was open for 0% -> 0% of each run, Pallas kernels for 27% -> 30%
where the time goes in v7:
time: 194 us; the launch traced here: 191 us
  Pallas kernels  63.1 us (33%)
  waiting for transfers between devices  56.7 us (29%)
  starting transfers between devices  56.5 us (29%)
  blocking collectives  12.8 us (7%)
  local copies, waits for them, and re-layouts  1.96 us (1%)
    pallas_call x4, Pallas kernels, experts(): pl.pallas_call(functools.partial(expert_kernel, n_in=len(arrays), block=b...  40.2 us
    ppermute x15, waiting for transfers between devices, shift(): return lax.ppermute(x, 'y', [(i, (i + by) % n_y) for i in range(n_y)])  30.9 us
    all_to_all x4, starting transfers between devices, exchange(): return lax.all_to_all(x, exp, split_axis=0, concat_axis=0, tiled=True)  29.7 us
    ppermute x15, starting transfers between devices, shift(): return lax.ppermute(x, 'y', [(i, (i + by) % n_y) for i in range(n_y)])  21.6 us
    all_to_all x1, waiting for transfers between devices, per_device(): arrived = lax.all_to_all(qkv, seq, split_axis=0, concat_axis=0, tiled=True)  17.7 us
    all_to_all x1, blocking collectives, per_device(): lax.all_to_all(context, seq, split_axis=0, concat_axis=0, tiled=True)  12.8 us
    all_to_all x4, waiting for transfers between devices, exchange(): return lax.all_to_all(x, exp, split_axis=0, concat_axis=0, tiled=True)  8.06 us
    pallas_call x1, Pallas kernels, attention(): pl.pallas_call(functools.partial(attention_kernel, block=2 * rows), grid=...  6.15 us
  transfers between devices with their start and end apart: 23, of which 7 were waited for; matrix products, arithmetic and copies ran while one was open for 0% of the time, Pallas kernels for 30%

profile of v7, /device:TPU:2, one launch (start us, length us, event | category | flops | bytes accessed | tf_op | source)
XLA Modules:
  0.0 191.5 jit_solution(15382569486682088907)
XLA Ops:
  0.0 0.0 collective-permute-start.1
  0.0 0.5 collective-permute-start.2
  0.5 0.0 collective-permute-start.3
  0.5 2.5 %spread.1 = bf16[8,3,128,256]{3,2,1,0:T(8,128)(2,1)} custom-call(bf16[3,128,2048]{2,1,0:T(8,128)(2,1)} %bitcast.29), custom_call_target="tpu_custom_call" | custom-call | tf_op jit(solution)/shard_map/spread/pallas_call | solution.py:349
  3.0 0.0 copy-start.2
  3.0 0.0 copy-start.3
  3.0 4.6 %all-to-all-start = ((bf16[8,3,128,256]{3,2,1,0:T(8,128)(2,1)}), bf16[8,3,128,256]{3,2,1,0:T(8,128)(2,1)S(1)}, u32[]{:S(2)}, u32[]{:S(2)}) async-start(bf16[8,3,128,256]{3,2,1,0:T(8,128)(2,1)} %spread.1), calls=%async_computation | async-start | bytes 3145728 | tf_op jit(solution)/shard_map/all_to_all | solution.py:427
  7.6 0.1 pad.2.clone
  7.7 0.1 maximum_maximum_fusion.info_ref
  7.8 0.1 plan.1.info_ref
  7.9 3.6 %collective-permute-start = (f32[8,128]{1,0:T(8,128)S(1)}, f32[8,128]{1,0:T(8,128)S(1)}, u32[]{:S(2)}, u32[]{:S(2)}) collective-permute-start(f32[8,128]{1,0:T(8,128)S(1)} %plan.1.info_ref), channel_id=1, source_target_pairs={{0,64},{32,96},{64,0},{96,32},{1,65},{33,97},{65,1},{97,33},{2,66}... | collective-permute-start | bytes 12296 | tf_op jit(solution)/shard_map/ppermute | solution.py:414
  11.5 17.7 %all-to-all-done.x_ref = bf16[8,3,128,256]{3,2,1,0:T(8,128)(2,1)S(1)} async-done(((bf16[8,3,128,256]{3,2,1,0:T(8,128)(2,1)}), bf16[8,3,128,256]{3,2,1,0:T(8,128)(2,1)S(1)}, u32[]{:S(2)}, u32[]{:S(2)}) %all-to-all-start) | async-done | bytes 1572896 | tf_op jit(solution)/shard_map/all_to_all | solution.py:427
  29.2 6.2 %attention.1 = (bf16[8,128,256]{2,1,0:T(8,128)(2,1)S(1)}, bf16[2048,2048]{1,0:T(8,128)(2,1)S(1)}) custom-call(bf16[8,3,128,256]{3,2,1,0:T(8,128)(2,1)S(1)} %all-to-all-done.x_ref, bf16[2048,2048]{1,0:T(8,128)(2,1)} %w_hbm.1), custom_call_target="tpu_custom_call" | custom-call | tf_op jit(solution)/shard_map/attention/pallas_call | solution.py:71
  35.4 0.0 collective-permute-done.info_ref
  35.4 0.0 collective-permute-done.1.refs_4_.refs_5_.refs_6_
  35.4 0.0 collective-permute-done.2.refs_5_.refs_6_.refs_7_
  35.4 0.0 collective-permute-done.3.refs_6_.refs_7_.refs_8_
  35.4 12.8 %all_to_all.56.ctx_ref = bf16[8,128,256]{2,1,0:T(8,128)(2,1)S(1)} all-to-all(bf16[8,128,256]{2,1,0:T(8,128)(2,1)S(1)} %get-tuple-element.45), channel_id=1, replica_groups=mesh['y'=4,'core'=2,'z'=4,'x'=4] {'y','core'}, dimensions={0} | all-to-all | bytes 1048576 | tf_op jit(solution)/shard_map/all_to_all | solution.py:430
  48.3 3.7 %project.1 = (f32[128,2048]{1,0:T(8,128)}, bf16[128,2048]{1,0:T(8,128)(2,1)S(1)}, bf16[384,2048]{1,0:T(8,128)(2,1)}) custom-call(bf16[8,128,256]{2,1,0:T(8,128)(2,1)S(1)} %all_to_all.56.ctx_ref, bf16[2048,2048]{1,0:T(8,128)(2,1)S(1)} %get-tuple-element.46.w_ref, bf16[128,2048]{1,0:T(8,128)(2,1)S(1)} %bitcast.27, f32[8,128]{1,0:T(8,128)S(1)} %plan.1.info_ref), custom_call_target="tpu_custom_call" | custom-call | tf_op jit(solution)/shard_map/project/pallas_call | solution.py:149
  52.0 8.3 %all-to-all-start.2 = ((bf16[16,24,2048]{2,1,0:T(8,128)(2,1)}), bf16[16,24,2048]{2,1,0:T(8,128)(2,1)S(1)}, u32[]{:S(2)}, u32[]{:S(2)}) async-start(bf16[16,24,2048]{2,1,0:T(8,128)(2,1)} %bitcast.10), calls=%async_computation.2 | async-start | bytes 3145728 | tf_op jit(solution)/shard_map/all_to_all | solution.py:417
  60.3 0.3 collective-permute-start.4
  60.6 13.9 %collective-permute-done.4.normed_ref = bf16[128,2048]{1,0:T(8,128)(2,1)S(1)} collective-permute-done((bf16[128,2048]{1,0:T(8,128)(2,1)S(1)}, bf16[128,2048]{1,0:T(8,128)(2,1)S(1)}, u32[]{:S(2)}, u32[]{:S(2)}) %collective-permute-start.4) | collective-permute-done | bytes 524320 | tf_op jit(solution)/shard_map/ppermute | solution.py:414
  74.5 1.7 route.1
  76.3 5.2 %all-to-all-done.2 = bf16[16,24,2048]{2,1,0:T(8,128)(2,1)S(1)} async-done(((bf16[16,24,2048]{2,1,0:T(8,128)(2,1)}), bf16[16,24,2048]{2,1,0:T(8,128)(2,1)S(1)}, u32[]{:S(2)}, u32[]{:S(2)}) %all-to-all-start.2) | async-done | bytes 1572896 | tf_op jit(solution)/shard_map/all_to_all | solution.py:417
  81.4 1.1 fusion
  82.5 1.2 collective-permute-start.6
  83.7 0.9 collective-permute-start.5
  84.6 2.4 %collective-permute-start.10 = (bf16[144,2048]{1,0:T(8,128)(2,1)}, bf16[144,2048]{1,0:T(8,128)(2,1)}, u32[]{:S(2)}, u32[]{:S(2)}) collective-permute-start(bf16[144,2048]{1,0:T(8,128)(2,1)} %get-tuple-element.63), channel_id=1, source_target_pairs={{0,96},{32,0},{64,32},{96,64},{1,97},{33,1},{65,33},{97,65},{2,98}... | collective-permute-start | bytes 1769480 | tf_op jit(solution)/shard_map/ppermute | solution.py:414
  86.9 0.0 collective-permute-start.9
  86.9 0.8 slice.11
  87.7 6.9 %all-to-all-start.3 = ((bf16[16,24,2048]{2,1,0:T(8,128)(2,1)}), bf16[16,24,2048]{2,1,0:T(8,128)(2,1)}, u32[]{:S(2)}, u32[]{:S(2)}) async-start(bf16[16,24,2048]{2,1,0:T(8,128)(2,1)} %bitcast.12), calls=%async_computation.3 | async-start | bytes 3145728 | tf_op jit(solution)/shard_map/all_to_all | solution.py:417
  94.6 8.9 %experts.4.own_ref = bf16[384,2048]{1,0:T(8,128)(2,1)} custom-call(bf16[384,2048]{1,0:T(8,128)(2,1)S(1)} %bitcast.25, bf16[2048,512]{1,0:T(8,128)(2,1)} %bitcast.33, bf16[2048,512]{1,0:T(8,128)(2,1)} %bitcast.38, bf16[512,2048]{1,0:T(8,128)(2,1)} %bitcast.43, bf16[2048,512]{1,0:T(8,128)(2,1)} %collective-permute-done.1.refs_4_.refs_5_.refs_6_, ...), custom_call_target="tpu_custom_call" | custom-call | flops 483183820800 | bytes 15728640 | tf_op jit(solution)/shard_map/experts/pallas_call | solution.py:238
  103.5 0.0 collective-permute-done.6.refs_1_
  103.5 0.0 collective-permute-done.5.refs_0_
  103.5 3.3 %collective-permute-start.8 = (bf16[96,2048]{1,0:T(8,128)(2,1)}, bf16[96,2048]{1,0:T(8,128)(2,1)}, u32[]{:S(2)}, u32[]{:S(2)}) collective-permute-start(bf16[96,2048]{1,0:T(8,128)(2,1)} %slice.11), channel_id=1, source_target_pairs={{0,96},{32,0},{64,32},{96,64},{1,97},{33,1},{65,33},{97,65},{2,98}... | collective-permute-start | bytes 1179656 | tf_op jit(solution)/shard_map/ppermute | solution.py:414
  106.8 0.0 collective-permute-start.7
  106.8 8.8 %experts.5 = (bf16[144,2048]{1,0:T(8,128)(2,1)}, bf16[144,2048]{1,0:T(8,128)(2,1)}) custom-call(bf16[144,2048]{1,0:T(8,128)(2,1)} %collective-permute-done.5.refs_0_, bf16[144,2048]{1,0:T(8,128)(2,1)} %collective-permute-done.6.refs_1_, bf16[2048,512]{1,0:T(8,128)(2,1)} %bitcast.34, bf16[2048,512]{1,0:T(8,128)(2,1)} %bitcast.39, bf16[512,2048]{1,0:T(8,128)(2,1)} %bitcast.44, ...), custom_call_target="tpu_custom_call" | custom-call | flops 362387865600 | bytes 14942208 | tf_op jit(solution)/shard_map/experts/pallas_call | solution.py:238
  115.6 3.3 %collective-permute-start.11 = (bf16[144,2048]{1,0:T(8,128)(2,1)}, bf16[144,2048]{1,0:T(8,128)(2,1)}, u32[]{:S(2)}, u32[]{:S(2)}) collective-permute-start(bf16[144,2048]{1,0:T(8,128)(2,1)} %get-tuple-element.66), channel_id=1, source_target_pairs={{0,96},{32,0},{64,32},{96,64},{1,97},{33,1},{65,33},{97,65},{2,98}... | collective-permute-start | bytes 1769480 | tf_op jit(solution)/shard_map/ppermute | solution.py:414
  118.9 0.0 collective-permute-done.10.refs_2_
  118.9 0.0 collective-permute-start.12
  118.9 0.0 collective-permute-done.9.refs_1_
  119.0 0.0 all-to-all-done.3
  119.0 14.4 %experts.6 = (bf16[384,2048]{1,0:T(8,128)(2,1)}, bf16[144,2048]{1,0:T(8,128)(2,1)}, bf16[144,2048]{1,0:T(8,128)(2,1)}) custom-call(bf16[384,2048]{1,0:T(8,128)(2,1)} %bitcast.13.refs_0_, bf16[144,2048]{1,0:T(8,128)(2,1)} %collective-permute-done.9.refs_1_, bf16[144,2048]{1,0:T(8,128)(2,1)} %collective-permute-done.10.refs_2_, bf16[2048,512]{1,0:T(8,128)(2,1)} %bitcast.35, ...), custom_call_target="tpu_custom_call" | custom-call | flops 845571686400 | bytes 18087936 | tf_op jit(solution)/shard_map/experts/pallas_call | solution.py:238
  133.4 3.3 %collective-permute-start.15 = (bf16[144,2048]{1,0:T(8,128)(2,1)}, bf16[144,2048]{1,0:T(8,128)(2,1)}, u32[]{:S(2)}, u32[]{:S(2)}) collective-permute-start(bf16[144,2048]{1,0:T(8,128)(2,1)} %get-tuple-element.78), channel_id=1, source_target_pairs={{0,96},{32,0},{64,32},{96,64},{1,97},{33,1},{65,33},{97,65},{2,98}... | collective-permute-start | bytes 1769480 | tf_op jit(solution)/shard_map/ppermute | solution.py:414
  136.7 0.0 collective-permute-done.8.refs_1_
  136.7 0.0 collective-permute-start.16
  136.7 0.0 collective-permute-done.7.refs_0_
  136.7 0.0 collective-permute-done.11.refs_0_
  136.7 0.0 collective-permute-done.12.refs_1_
  136.7 7.3 %all-to-all-start.4 = ((bf16[16,24,2048]{2,1,0:T(8,128)(2,1)}), bf16[16,24,2048]{2,1,0:T(8,128)(2,1)}, u32[]{:S(2)}, u32[]{:S(2)}) async-start(bf16[16,24,2048]{2,1,0:T(8,128)(2,1)} %bitcast.30), calls=%async_computation.4 | async-start | bytes 3145728 | tf_op jit(solution)/shard_map/all_to_all | solution.py:417
  144.0 8.0 %experts.7 = (bf16[96,2048]{1,0:T(8,128)(2,1)}, bf16[96,2048]{1,0:T(8,128)(2,1)}) custom-call(bf16[96,2048]{1,0:T(8,128)(2,1)} %collective-permute-done.7.refs_0_, bf16[96,2048]{1,0:T(8,128)(2,1)} %collective-permute-done.8.refs_1_, bf16[2048,512]{1,0:T(8,128)(2,1)} %bitcast.36, bf16[2048,512]{1,0:T(8,128)(2,1)} %bitcast.41, bf16[512,2048]{1,0:T(8,128)(2,1)} %bitcast.46, ...), custom_call_target="tpu_custom_call" | custom-call | flops 241591910400 | bytes 14155776 | tf_op jit(solution)/shard_map/experts/pallas_call | solution.py:238
  152.1 3.3 %collective-permute-start.13 = (bf16[96,2048]{1,0:T(8,128)(2,1)}, bf16[96,2048]{1,0:T(8,128)(2,1)S(1)}, u32[]{:S(2)}, u32[]{:S(2)}) collective-permute-start(bf16[96,2048]{1,0:T(8,128)(2,1)} %get-tuple-element.74), channel_id=1, source_target_pairs={{0,96},{32,0},{64,32},{96,64},{1,97},{33,1},{65,33},{97,65},{2,98}... | collective-permute-start | bytes 1179656 | tf_op jit(solution)/shard_map/ppermute | solution.py:414
  155.4 0.0 collective-permute-start.14
  155.4 2.9 %add_up.2.refs_2_ = bf16[384,2048]{1,0:T(8,128)(2,1)} custom-call(bf16[384,2048]{1,0:T(8,128)(2,1)S(1)} %copy-done, bf16[144,2048]{1,0:T(8,128)(2,1)} %collective-permute-done.11.refs_0_, bf16[144,2048]{1,0:T(8,128)(2,1)} %collective-permute-done.12.refs_1_, bf16[144,2048]{1,0:T(8,128)(2,1)} %collective-permute-done.15.refs_2_, ...), custom_call_target="tpu_custom_call" | custom-call | flops 1 | bytes 1 | tf_op jit(solution)/shard_map/add_up/pallas_call | solution.py:387
  158.3 2.7 %collective-permute-done.13.refs_0_ = bf16[96,2048]{1,0:T(8,128)(2,1)S(1)} collective-permute-done((bf16[96,2048]{1,0:T(8,128)(2,1)}, bf16[96,2048]{1,0:T(8,128)(2,1)S(1)}, u32[]{:S(2)}, u32[]{:S(2)}) %collective-permute-start.13) | collective-permute-done | bytes 393248 | tf_op jit(solution)/shard_map/ppermute | solution.py:414
  161.0 3.6 %collective-permute-done.14.refs_1_ = bf16[96,2048]{1,0:T(8,128)(2,1)S(1)} collective-permute-done((bf16[96,2048]{1,0:T(8,128)(2,1)}, bf16[96,2048]{1,0:T(8,128)(2,1)S(1)}, u32[]{:S(2)}, u32[]{:S(2)}) %collective-permute-start.14) | collective-permute-done | bytes 393248 | tf_op jit(solution)/shard_map/ppermute | solution.py:414
  164.6 0.9 add_up.3
  165.5 0.0 all-to-all-done.4
  165.5 7.2 %all-to-all-start.5 = ((bf16[16,24,2048]{2,1,0:T(8,128)(2,1)}), bf16[16,24,2048]{2,1,0:T(8,128)(2,1)S(1)}, u32[]{:S(2)}, u32[]{:S(2)}) async-start(bf16[16,24,2048]{2,1,0:T(8,128)(2,1)} %bitcast.28), calls=%async_computation.5 | async-start | bytes 3145728 | tf_op jit(solution)/shard_map/all_to_all | solution.py:417
  172.7 2.2 %combine.2 = bf16[128,2048]{1,0:T(8,128)(2,1)S(1)} custom-call(f32[8,128]{1,0:T(8,128)S(1)} %collective-permute-done.info_ref, bf16[384,2048]{1,0:T(8,128)(2,1)} %bitcast.15.back_ref), custom_call_target="tpu_custom_call" | custom-call | tf_op jit(solution)/shard_map/combine/pallas_call | solution.py:313
  175.0 0.1 collective-permute-start.17
  175.1 10.7 %collective-permute-done.17.refs_0_ = bf16[128,2048]{1,0:T(8,128)(2,1)S(1)} collective-permute-done((bf16[128,2048]{1,0:T(8,128)(2,1)S(1)}, bf16[128,2048]{1,0:T(8,128)(2,1)S(1)}, u32[]{:S(2)}, u32[]{:S(2)}) %collective-permute-start.17) | collective-permute-done | bytes 524320 | tf_op jit(solution)/shard_map/ppermute | solution.py:414
  185.7 2.9 %all-to-all-done.5 = bf16[16,24,2048]{2,1,0:T(8,128)(2,1)S(1)} async-done(((bf16[16,24,2048]{2,1,0:T(8,128)(2,1)}), bf16[16,24,2048]{2,1,0:T(8,128)(2,1)S(1)}, u32[]{:S(2)}, u32[]{:S(2)}) %all-to-all-start.5) | async-done | bytes 1572896 | tf_op jit(solution)/shard_map/all_to_all | solution.py:417
  188.6 2.7 %combine.3 = bf16[128,2048]{1,0:T(8,128)(2,1)} custom-call(f32[8,128]{1,0:T(8,128)S(1)} %plan.1.info_ref, bf16[384,2048]{1,0:T(8,128)(2,1)S(1)} %bitcast.26, bf16[128,2048]{1,0:T(8,128)(2,1)S(1)} %collective-permute-done.17.refs_0_, f32[128,2048]{1,0:T(8,128)} %get-tuple-element.82.refs_1_), custom_call_target="tpu_custom_call" | custom-call | tf_op jit(solution)/shard_map/combine/pallas_call | solution.py:313
  (11 shorter events, 0.0 us)
Async XLA Ops:
  0.0 35.4 %collective-permute-start.1 = (bf16[2048,512]{1,0:T(8,128)(2,1)}, bf16[2048,512]{1,0:T(8,128)(2,1)}, u32[]{:S(2)}, u32[]{:S(2)}) collective-permute-start(bf16[2048,512]{1,0:T(8,128)(2,1)} %bitcast.32), channel_id=1, source_target_pairs={{0,16},{16,0},{1,17},{17,1},{2,18},{18,2},{3,19},{19,3},{4,20},{20... | collective-permute-start | bytes 6291464 | tf_op jit(solution)/shard_map/ppermute | solution.py:411
  0.0 35.4 %collective-permute-start.2 = (bf16[2048,512]{1,0:T(8,128)(2,1)}, bf16[2048,512]{1,0:T(8,128)(2,1)}, u32[]{:S(2)}, u32[]{:S(2)}) collective-permute-start(bf16[2048,512]{1,0:T(8,128)(2,1)} %bitcast.37), channel_id=1, source_target_pairs={{0,16},{16,0},{1,17},{17,1},{2,18},{18,2},{3,19},{19,3},{4,20},{20... | collective-permute-start | bytes 6291464 | tf_op jit(solution)/shard_map/ppermute | solution.py:411
  0.5 34.9 %collective-permute-start.3 = (bf16[512,2048]{1,0:T(8,128)(2,1)}, bf16[512,2048]{1,0:T(8,128)(2,1)}, u32[]{:S(2)}, u32[]{:S(2)}) collective-permute-start(bf16[512,2048]{1,0:T(8,128)(2,1)} %bitcast.42), channel_id=1, source_target_pairs={{0,16},{16,0},{1,17},{17,1},{2,18},{18,2},{3,19},{19,3},{4,20},{20... | collective-permute-start | bytes 6291464 | tf_op jit(solution)/shard_map/ppermute | solution.py:411
  3.0 4.7 %copy-start.2 = (s32[1,128,2]{1,2,0:T(2,128)S(1)}, s32[1,128,2]{1,2,0:T(2,128)}, u32[]{:S(2)}) copy-start(s32[1,128,2]{1,2,0:T(2,128)} %param.10) | copy-start | bytes 3076
  3.0 4.7 %copy-start.3 = (f32[1,128,2]{1,2,0:T(2,128)S(1)}, f32[1,128,2]{1,2,0:T(2,128)}, u32[]{:S(2)}) copy-start(f32[1,128,2]{1,2,0:T(2,128)} %param.11) | copy-start | bytes 3076
  3.0 26.2 %all-to-all-start = ((bf16[8,3,128,256]{3,2,1,0:T(8,128)(2,1)}), bf16[8,3,128,256]{3,2,1,0:T(8,128)(2,1)S(1)}, u32[]{:S(2)}, u32[]{:S(2)}) async-start(bf16[8,3,128,256]{3,2,1,0:T(8,128)(2,1)} %spread.1), calls=%async_computation | async-start | bytes 3145728 | tf_op jit(solution)/shard_map/all_to_all | solution.py:427
  7.9 40.3 %copy-start.1 = (bf16[1,128,2048]{2,1,0:T(8,128)(2,1)S(1)}, bf16[1,128,2048]{2,1,0:T(8,128)(2,1)}, u32[]{:S(2)}) copy-start(bf16[1,128,2048]{2,1,0:T(8,128)(2,1)} %param.8) | copy-start | bytes 1572868
  7.9 27.5 %collective-permute-start = (f32[8,128]{1,0:T(8,128)S(1)}, f32[8,128]{1,0:T(8,128)S(1)}, u32[]{:S(2)}, u32[]{:S(2)}) collective-permute-start(f32[8,128]{1,0:T(8,128)S(1)} %plan.1.info_ref), channel_id=1, source_target_pairs={{0,64},{32,96},{64,0},{96,32},{1,65},{33,97},{65,1},{97,33},{2,66}... | collective-permute-start | bytes 12296 | tf_op jit(solution)/shard_map/ppermute | solution.py:414
  52.0 29.5 %all-to-all-start.2 = ((bf16[16,24,2048]{2,1,0:T(8,128)(2,1)}), bf16[16,24,2048]{2,1,0:T(8,128)(2,1)S(1)}, u32[]{:S(2)}, u32[]{:S(2)}) async-start(bf16[16,24,2048]{2,1,0:T(8,128)(2,1)} %bitcast.10), calls=%async_computation.2 | async-start | bytes 3145728 | tf_op jit(solution)/shard_map/all_to_all | solution.py:417
  60.3 14.2 %collective-permute-start.4 = (bf16[128,2048]{1,0:T(8,128)(2,1)S(1)}, bf16[128,2048]{1,0:T(8,128)(2,1)S(1)}, u32[]{:S(2)}, u32[]{:S(2)}) collective-permute-start(bf16[128,2048]{1,0:T(8,128)(2,1)S(1)} %get-tuple-element.48), channel_id=1, source_target_pairs={{0,64},{32,96},{64,0},{96,32},{1,65},{33,97},{65,1},{97,33},{2,66}... | collective-permute-start | bytes 1572872 | tf_op jit(solution)/shard_map/ppermute | solution.py:414
  82.5 20.9 %collective-permute-start.6 = (bf16[144,2048]{1,0:T(8,128)(2,1)}, bf16[144,2048]{1,0:T(8,128)(2,1)}, u32[]{:S(2)}, u32[]{:S(2)}) collective-permute-start(bf16[144,2048]{1,0:T(8,128)(2,1)} %get-tuple-element.54), channel_id=1, source_target_pairs={{0,96},{32,0},{64,32},{96,64},{1,97},{33,1},{65,33},{97,65},{2,98}... | collective-permute-start | bytes 1769480 | tf_op jit(solution)/shard_map/ppermute | solution.py:414
  83.7 19.8 %collective-permute-start.5 = (bf16[144,2048]{1,0:T(8,128)(2,1)}, bf16[144,2048]{1,0:T(8,128)(2,1)}, u32[]{:S(2)}, u32[]{:S(2)}) collective-permute-start(bf16[144,2048]{1,0:T(8,128)(2,1)} %get-tuple-element.54), channel_id=1, source_target_pairs={{0,32},{32,64},{64,96},{96,0},{1,33},{33,65},{65,97},{97,1},{2,34}... | collective-permute-start | bytes 1769480 | tf_op jit(solution)/shard_map/ppermute | solution.py:414
  84.6 34.4 %collective-permute-start.10 = (bf16[144,2048]{1,0:T(8,128)(2,1)}, bf16[144,2048]{1,0:T(8,128)(2,1)}, u32[]{:S(2)}, u32[]{:S(2)}) collective-permute-start(bf16[144,2048]{1,0:T(8,128)(2,1)} %get-tuple-element.63), channel_id=1, source_target_pairs={{0,96},{32,0},{64,32},{96,64},{1,97},{33,1},{65,33},{97,65},{2,98}... | collective-permute-start | bytes 1769480 | tf_op jit(solution)/shard_map/ppermute | solution.py:414
  86.9 32.0 %collective-permute-start.9 = (bf16[144,2048]{1,0:T(8,128)(2,1)}, bf16[144,2048]{1,0:T(8,128)(2,1)}, u32[]{:S(2)}, u32[]{:S(2)}) collective-permute-start(bf16[144,2048]{1,0:T(8,128)(2,1)} %get-tuple-element.63), channel_id=1, source_target_pairs={{0,32},{32,64},{64,96},{96,0},{1,33},{33,65},{65,97},{97,1},{2,34}... | collective-permute-start | bytes 1769480 | tf_op jit(solution)/shard_map/ppermute | solution.py:414
  87.7 31.3 %all-to-all-start.3 = ((bf16[16,24,2048]{2,1,0:T(8,128)(2,1)}), bf16[16,24,2048]{2,1,0:T(8,128)(2,1)}, u32[]{:S(2)}, u32[]{:S(2)}) async-start(bf16[16,24,2048]{2,1,0:T(8,128)(2,1)} %bitcast.12), calls=%async_computation.3 | async-start | bytes 3145728 | tf_op jit(solution)/shard_map/all_to_all | solution.py:417
  103.5 33.2 %collective-permute-start.8 = (bf16[96,2048]{1,0:T(8,128)(2,1)}, bf16[96,2048]{1,0:T(8,128)(2,1)}, u32[]{:S(2)}, u32[]{:S(2)}) collective-permute-start(bf16[96,2048]{1,0:T(8,128)(2,1)} %slice.11), channel_id=1, source_target_pairs={{0,96},{32,0},{64,32},{96,64},{1,97},{33,1},{65,33},{97,65},{2,98}... | collective-permute-start | bytes 1179656 | tf_op jit(solution)/shard_map/ppermute | solution.py:414
  106.8 29.9 %collective-permute-start.7 = (bf16[96,2048]{1,0:T(8,128)(2,1)}, bf16[96,2048]{1,0:T(8,128)(2,1)}, u32[]{:S(2)}, u32[]{:S(2)}) collective-permute-start(bf16[96,2048]{1,0:T(8,128)(2,1)} %slice.11), channel_id=1, source_target_pairs={{0,32},{32,64},{64,96},{96,0},{1,33},{33,65},{65,97},{97,1},{2,34}... | collective-permute-start | bytes 1179656 | tf_op jit(solution)/shard_map/ppermute | solution.py:414
  115.6 21.1 %collective-permute-start.11 = (bf16[144,2048]{1,0:T(8,128)(2,1)}, bf16[144,2048]{1,0:T(8,128)(2,1)}, u32[]{:S(2)}, u32[]{:S(2)}) collective-permute-start(bf16[144,2048]{1,0:T(8,128)(2,1)} %get-tuple-element.66), channel_id=1, source_target_pairs={{0,96},{32,0},{64,32},{96,64},{1,97},{33,1},{65,33},{97,65},{2,98}... | collective-permute-start | bytes 1769480 | tf_op jit(solution)/shard_map/ppermute | solution.py:414
  118.9 17.8 %collective-permute-start.12 = (bf16[144,2048]{1,0:T(8,128)(2,1)}, bf16[144,2048]{1,0:T(8,128)(2,1)}, u32[]{:S(2)}, u32[]{:S(2)}) collective-permute-start(bf16[144,2048]{1,0:T(8,128)(2,1)} %get-tuple-element.67), channel_id=1, source_target_pairs={{0,32},{32,64},{64,96},{96,0},{1,33},{33,65},{65,97},{97,1},{2,34}... | collective-permute-start | bytes 1769480 | tf_op jit(solution)/shard_map/ppermute | solution.py:414
  133.4 22.0 %collective-permute-start.15 = (bf16[144,2048]{1,0:T(8,128)(2,1)}, bf16[144,2048]{1,0:T(8,128)(2,1)}, u32[]{:S(2)}, u32[]{:S(2)}) collective-permute-start(bf16[144,2048]{1,0:T(8,128)(2,1)} %get-tuple-element.78), channel_id=1, source_target_pairs={{0,96},{32,0},{64,32},{96,64},{1,97},{33,1},{65,33},{97,65},{2,98}... | collective-permute-start | bytes 1769480 | tf_op jit(solution)/shard_map/ppermute | solution.py:414
  136.7 18.7 %collective-permute-start.16 = (bf16[144,2048]{1,0:T(8,128)(2,1)}, bf16[144,2048]{1,0:T(8,128)(2,1)}, u32[]{:S(2)}, u32[]{:S(2)}) collective-permute-start(bf16[144,2048]{1,0:T(8,128)(2,1)} %get-tuple-element.79), channel_id=1, source_target_pairs={{0,32},{32,64},{64,96},{96,0},{1,33},{33,65},{65,97},{97,1},{2,34}... | collective-permute-start | bytes 1769480 | tf_op jit(solution)/shard_map/ppermute | solution.py:414
  136.7 28.8 %all-to-all-start.4 = ((bf16[16,24,2048]{2,1,0:T(8,128)(2,1)}), bf16[16,24,2048]{2,1,0:T(8,128)(2,1)}, u32[]{:S(2)}, u32[]{:S(2)}) async-start(bf16[16,24,2048]{2,1,0:T(8,128)(2,1)} %bitcast.30), calls=%async_computation.4 | async-start | bytes 3145728 | tf_op jit(solution)/shard_map/all_to_all | solution.py:417
  144.0 11.4 %copy-start = (bf16[384,2048]{1,0:T(8,128)(2,1)S(1)}, bf16[384,2048]{1,0:T(8,128)(2,1)}, u32[]{:S(2)}) copy-start(bf16[384,2048]{1,0:T(8,128)(2,1)} %experts.4.own_ref) | copy-start | bytes 4718596
  152.1 8.9 %collective-permute-start.13 = (bf16[96,2048]{1,0:T(8,128)(2,1)}, bf16[96,2048]{1,0:T(8,128)(2,1)S(1)}, u32[]{:S(2)}, u32[]{:S(2)}) collective-permute-start(bf16[96,2048]{1,0:T(8,128)(2,1)} %get-tuple-element.74), channel_id=1, source_target_pairs={{0,96},{32,0},{64,32},{96,64},{1,97},{33,1},{65,33},{97,65},{2,98}... | collective-permute-start | bytes 1179656 | tf_op jit(solution)/shard_map/ppermute | solution.py:414
  155.4 9.2 %collective-permute-start.14 = (bf16[96,2048]{1,0:T(8,128)(2,1)}, bf16[96,2048]{1,0:T(8,128)(2,1)S(1)}, u32[]{:S(2)}, u32[]{:S(2)}) collective-permute-start(bf16[96,2048]{1,0:T(8,128)(2,1)} %get-tuple-element.75), channel_id=1, source_target_pairs={{0,32},{32,64},{64,96},{96,0},{1,33},{33,65},{65,97},{97,1},{2,34}... | collective-permute-start | bytes 1179656 | tf_op jit(solution)/shard_map/ppermute | solution.py:414
  165.5 23.1 %all-to-all-start.5 = ((bf16[16,24,2048]{2,1,0:T(8,128)(2,1)}), bf16[16,24,2048]{2,1,0:T(8,128)(2,1)S(1)}, u32[]{:S(2)}, u32[]{:S(2)}) async-start(bf16[16,24,2048]{2,1,0:T(8,128)(2,1)} %bitcast.28), calls=%async_computation.5 | async-start | bytes 3145728 | tf_op jit(solution)/shard_map/all_to_all | solution.py:417
  175.0 10.8 %collective-permute-start.17 = (bf16[128,2048]{1,0:T(8,128)(2,1)S(1)}, bf16[128,2048]{1,0:T(8,128)(2,1)S(1)}, u32[]{:S(2)}, u32[]{:S(2)}) collective-permute-start(bf16[128,2048]{1,0:T(8,128)(2,1)S(1)} %combine.2), channel_id=1, source_target_pairs={{0,64},{32,96},{64,0},{96,32},{1,65},{33,97},{65,1},{97,33},{2,66}... | collective-permute-start | bytes 1572872 | tf_op jit(solution)/shard_map/ppermute | solution.py:414

commit v8 on v6

--- a/solution.py
+++ b/solution.py
@@ -180,8 +180,9 @@
 
 def expert_kernel(*refs, n_in, block):
     x_refs, w_refs = refs[:n_in], refs[n_in : n_in + 6]
-    *out_refs, rows_ref, hidden_ref, gate_ref, up_ref, down_ref, x_sems, w_sems = refs[
-        n_in + 6 :
+    out_refs = refs[n_in + 6 : 2 * n_in + 6]
+    rows_ref, total_ref, hidden_ref, gate_ref, up_ref, down_ref, x_sems, w_sems, out_sems = refs[
+        2 * n_in + 6 :
     ]
     share = w_refs[0].shape[1]
     per = share // block
@@ -219,11 +220,25 @@
         hidden_ref[:, here] = ((half + half * jnp.tanh(half)) * up).astype(BF16)
     for copy in copies:
         copy[2].wait()
-    total = jnp.dot(hidden_ref[...], down_ref[...], preferred_element_type=F32)
-    start = 0
-    for ref in out_refs:
-        ref[...] = total[start : start + ref.shape[0]].astype(BF16)
-        start += ref.shape[0]
+    cuts = out_sems.shape[1]
+    cols = out_refs[0].shape[1] // cuts
+    flushes = []
+    for j in range(cuts):
+        here = slice(j * cols, (j + 1) * cols)
+        total = jnp.dot(hidden_ref[...], down_ref[:, here], preferred_element_type=F32)
+        total_ref[:, here] = total.astype(BF16)
+        start = 0
+        for i, ref in enumerate(out_refs):
+            n, lanes = ref.shape[0], pl.ds(j * cols, cols)
+            flushes.append(
+                pltpu.make_async_copy(
+                    total_ref.at[pl.ds(start, n), lanes], ref.at[:, lanes], out_sems.at[i, j]
+                )
+            )
+            flushes[-1].start()
+            start += n
+    for flush in flushes:
+        flush.wait()
 
 
 def in_hbm(x):
@@ -240,9 +255,10 @@
         grid=(1,),
         in_specs=[pl.BlockSpec(memory_space=pl.ANY)] * len(arrays)
         + [pl.BlockSpec(memory_space=pltpu.HBM)] * 6,
-        out_specs=[vmem(x.shape) for x in arrays],
+        out_specs=[pl.BlockSpec(memory_space=pltpu.HBM)] * len(arrays),
         out_shape=[pltpu.HBM(x.shape, BF16) for x in arrays],
         scratch_shapes=[
+            pltpu.VMEM((total, width), BF16),
             pltpu.VMEM((total, width), BF16),
             pltpu.VMEM((total, hidden), BF16),
             pltpu.VMEM((width, hidden), BF16),
@@ -250,6 +266,7 @@
             pltpu.VMEM((hidden, width), BF16),
             pltpu.SemaphoreType.DMA((len(arrays),)),
             pltpu.SemaphoreType.DMA((hidden // block, 3)),
+            pltpu.SemaphoreType.DMA((len(arrays), 4)),
         ],
         compiler_params=pltpu.CompilerParams(vmem_limit_bytes=44 * MIB),
         cost_estimate=pl.CostEstimate(
@@ -278,18 +295,12 @@
     )(in_hbm(x))
 
 
-def combine_kernel(info_ref, back_ref, *refs, cuts):
-    by_token = info_ref[...].T
+def weighted(info, back_ref, out_ref, cuts, base):
+    by_token = info.T
     rows = by_token[:, 2 * TOP : 3 * TOP].astype(jnp.int32)
     at = lax.broadcasted_iota(jnp.int32, (rows.shape[0], back_ref.shape[0]), 1)
     picks = [(at == rows[:, k : k + 1]).astype(F32).astype(BF16) for k in range(TOP)]
     gates = [by_token[:, TOP + k : TOP + k + 1] for k in range(TOP)]
-    if len(refs) > 1:
-        far_ref, mid_hbm, out_ref, mid_ref, sem = refs
-        copy = pltpu.make_async_copy(mid_hbm, mid_ref, sem)
-        copy.start()
-    else:
-        [out_ref], copy = refs, None
     cols = out_ref.shape[1] // cuts
     for i in range(cuts):
         here = slice(i * cols, (i + 1) * cols)
@@ -299,27 +310,52 @@
             for pick, gate in zip(picks, gates, strict=True)
         ]
         total = sum(terms[1:], terms[0])
-        if copy is not None:
-            if i == 0:
-                copy.wait()
-            total = mid_ref[:, here] + far_ref[:, here].astype(F32) + total
+        if base is not None:
+            total = base(here) + total
         out_ref[:, here] = total.astype(BF16)
 
 
-def combine(info, back, mid=None, far=None):
+def combine_far_kernel(info_ref, back_ref, mid_hbm, out_ref, mid_ref, sem, *, cuts):
+    copy = pltpu.make_async_copy(mid_hbm, mid_ref, sem)
+    copy.start()
+    weighted(info_ref[...], back_ref, out_ref, cuts, None)
+    copy.wait()
+
+
+def combine_far(info, back, mid):
     rows, width = info.shape[1], back.shape[1]
     held = pl.BlockSpec(memory_space=pltpu.VMEM)
-    final = mid is not None
+    return pl.pallas_call(
+        functools.partial(combine_far_kernel, cuts=4),
+        in_specs=[held, held, pl.BlockSpec(memory_space=pltpu.HBM)],
+        out_specs=[held, pl.BlockSpec(memory_space=pl.ANY)],
+        out_shape=[
+            jax.ShapeDtypeStruct((rows, width), BF16),
+            pltpu.VMEM((rows, width), F32),
+        ],
+        scratch_shapes=[pltpu.SemaphoreType.DMA(())],
+        compiler_params=pltpu.CompilerParams(vmem_limit_bytes=16 * MIB),
+        name="combine_far",
+    )(info, back, in_hbm(mid))
+
+
+def combine_kernel(info_ref, back_ref, far_ref, mid_ref, out_ref, *, cuts):
+    def base(here):
+        return mid_ref[:, here] + far_ref[:, here].astype(F32)
+
+    weighted(info_ref[...], back_ref, out_ref, cuts, base)
+
+
+def combine(info, back, mid, far):
+    rows, width = mid.shape
     return pl.pallas_call(
         functools.partial(combine_kernel, cuts=4),
-        in_specs=[held] * (3 if final else 2)
-        + [pl.BlockSpec(memory_space=pltpu.HBM)] * final,
-        out_specs=held,
+        in_specs=[pl.BlockSpec(memory_space=pltpu.VMEM)] * 4,
+        out_specs=pl.BlockSpec(memory_space=pltpu.VMEM),
         out_shape=jax.ShapeDtypeStruct((rows, width), BF16),
-        scratch_shapes=[pltpu.VMEM((rows, width), F32), pltpu.SemaphoreType.DMA(())] * final,
         compiler_params=pltpu.CompilerParams(vmem_limit_bytes=16 * MIB),
         name="combine",
-    )(info, back, *([far, in_hbm(mid)] if final else []))
+    )(info, back, far, pltpu.with_memory_space_constraint(mid, pltpu.VMEM))
 
 
 def spread_kernel(x_hbm, out_hbm, x_ref, in_sems, out_sems):
@@ -459,7 +495,7 @@
     far_back = exchange(keep(far_part))
     back = experts(at_third, mine, other)
     home.append(give_back(back))
-    far_sum = combine(info_far, far_back)
+    far_sum, mid = combine_far(info_far, far_back, mid)
     total = add_up(own_part, home[:2])
     total = add_up(own_part, home[2:], 6 * eighth, total)
     total, far_back = tie((total, far_back))

time: 192 us -> 190 us (0.990)
  no operation moved by 1% of the time
where the time goes in v8:
time: 190 us; the launch traced here: 187 us
  waiting for transfers between devices  62.9 us (33%)
  Pallas kernels  56.7 us (30%)
  starting transfers between devices  52.9 us (28%)
  blocking collectives  12.8 us (7%)
    ppermute x15, waiting for transfers between devices, shift(): return lax.ppermute(x, 'y', [(i, (i + by) % n_y) for i in range(n_y)])  37.4 us
    pallas_call x3, Pallas kernels, experts(): pl.pallas_call(functools.partial(expert_kernel, n_in=len(arrays), block=b...  34.4 us
    all_to_all x4, starting transfers between devices, exchange(): return lax.all_to_all(x, exp, split_axis=0, concat_axis=0, tiled=True)  29.5 us
    ppermute x15, starting transfers between devices, shift(): return lax.ppermute(x, 'y', [(i, (i + by) % n_y) for i in range(n_y)])  18.3 us
    all_to_all x1, waiting for transfers between devices, per_device(): arrived = lax.all_to_all(qkv, seq, split_axis=0, concat_axis=0, tiled=True)  17.7 us
    all_to_all x1, blocking collectives, per_device(): lax.all_to_all(context, seq, split_axis=0, concat_axis=0, tiled=True)  12.8 us
    all_to_all x4, waiting for transfers between devices, exchange(): return lax.all_to_all(x, exp, split_axis=0, concat_axis=0, tiled=True)  7.73 us
    pallas_call x1, Pallas kernels, attention(): pl.pallas_call(functools.partial(attention_kernel, block=2 * rows), grid=...  6.15 us
  transfers between devices with their start and end apart: 23, of which 9 were waited for; matrix products, arithmetic and copies ran while one was open for 0% of the time, Pallas kernels for 27%

profile of v8, /device:TPU:2, one launch (start us, length us, event | category | flops | bytes accessed | tf_op | source)
XLA Modules:
  0.0 187.4 jit_solution(85293879223256455)
XLA Ops:
  0.0 0.0 collective-permute-start.1
  0.0 0.5 collective-permute-start.2
  0.5 0.0 collective-permute-start.3
  0.5 2.5 %spread.1 = bf16[8,3,128,256]{3,2,1,0:T(8,128)(2,1)} custom-call(bf16[3,128,2048]{2,1,0:T(8,128)(2,1)} %bitcast.29), custom_call_target="tpu_custom_call" | custom-call | tf_op jit(solution)/shard_map/spread/pallas_call | solution.py:385
  3.0 0.0 copy-start.6
  3.0 0.0 copy-start.7
  3.0 4.6 %all-to-all-start = ((bf16[8,3,128,256]{3,2,1,0:T(8,128)(2,1)}), bf16[8,3,128,256]{3,2,1,0:T(8,128)(2,1)S(1)}, u32[]{:S(2)}, u32[]{:S(2)}) async-start(bf16[8,3,128,256]{3,2,1,0:T(8,128)(2,1)} %spread.1), calls=%async_computation | async-start | bytes 3145728 | tf_op jit(solution)/shard_map/all_to_all | solution.py:463
  7.6 0.1 pad.2.clone
  7.7 0.1 maximum_maximum_fusion.info_ref
  7.8 0.1 plan.1.info_ref
  7.9 3.6 %collective-permute-start = (f32[8,128]{1,0:T(8,128)S(1)}, f32[8,128]{1,0:T(8,128)S(1)}, u32[]{:S(2)}, u32[]{:S(2)}) collective-permute-start(f32[8,128]{1,0:T(8,128)S(1)} %plan.1.info_ref), channel_id=1, source_target_pairs={{0,64},{32,96},{64,0},{96,32},{1,65},{33,97},{65,1},{97,33},{2,66}... | collective-permute-start | bytes 12296 | tf_op jit(solution)/shard_map/ppermute | solution.py:450
  11.5 17.7 %all-to-all-done.x_ref = bf16[8,3,128,256]{3,2,1,0:T(8,128)(2,1)S(1)} async-done(((bf16[8,3,128,256]{3,2,1,0:T(8,128)(2,1)}), bf16[8,3,128,256]{3,2,1,0:T(8,128)(2,1)S(1)}, u32[]{:S(2)}, u32[]{:S(2)}) %all-to-all-start) | async-done | bytes 1572896 | tf_op jit(solution)/shard_map/all_to_all | solution.py:463
  29.2 6.2 %attention.1 = (bf16[8,128,256]{2,1,0:T(8,128)(2,1)S(1)}, bf16[2048,2048]{1,0:T(8,128)(2,1)S(1)}) custom-call(bf16[8,3,128,256]{3,2,1,0:T(8,128)(2,1)S(1)} %all-to-all-done.x_ref, bf16[2048,2048]{1,0:T(8,128)(2,1)} %w_hbm.1), custom_call_target="tpu_custom_call" | custom-call | tf_op jit(solution)/shard_map/attention/pallas_call | solution.py:71
  35.4 0.0 collective-permute-done.info_ref
  35.4 0.0 collective-permute-done.1.refs_6_.refs_5_
  35.4 0.0 collective-permute-done.2.refs_7_.refs_6_
  35.4 0.0 collective-permute-done.3.refs_8_.refs_7_
  35.4 12.8 %all_to_all.56.ctx_ref = bf16[8,128,256]{2,1,0:T(8,128)(2,1)S(1)} all-to-all(bf16[8,128,256]{2,1,0:T(8,128)(2,1)S(1)} %get-tuple-element.46), channel_id=1, replica_groups=mesh['y'=4,'core'=2,'z'=4,'x'=4] {'y','core'}, dimensions={0} | all-to-all | bytes 1048576 | tf_op jit(solution)/shard_map/all_to_all | solution.py:466
  48.2 3.7 %project.1 = (f32[128,2048]{1,0:T(8,128)}, bf16[128,2048]{1,0:T(8,128)(2,1)S(1)}, bf16[384,2048]{1,0:T(8,128)(2,1)}) custom-call(bf16[8,128,256]{2,1,0:T(8,128)(2,1)S(1)} %all_to_all.56.ctx_ref, bf16[2048,2048]{1,0:T(8,128)(2,1)S(1)} %get-tuple-element.47.w_ref, bf16[128,2048]{1,0:T(8,128)(2,1)S(1)} %bitcast.27, f32[8,128]{1,0:T(8,128)S(1)} %plan.1.info_ref), custom_call_target="tpu_custom_call" | custom-call | tf_op jit(solution)/shard_map/project/pallas_call | solution.py:149
  51.9 8.3 %all-to-all-start.2 = ((bf16[16,24,2048]{2,1,0:T(8,128)(2,1)}), bf16[16,24,2048]{2,1,0:T(8,128)(2,1)S(1)}, u32[]{:S(2)}, u32[]{:S(2)}) async-start(bf16[16,24,2048]{2,1,0:T(8,128)(2,1)} %bitcast.10), calls=%async_computation.2 | async-start | bytes 3145728 | tf_op jit(solution)/shard_map/all_to_all | solution.py:453
  60.2 0.4 collective-permute-start.4
  60.6 13.9 %collective-permute-done.4.normed_ref = bf16[128,2048]{1,0:T(8,128)(2,1)S(1)} collective-permute-done((bf16[128,2048]{1,0:T(8,128)(2,1)S(1)}, bf16[128,2048]{1,0:T(8,128)(2,1)S(1)}, u32[]{:S(2)}, u32[]{:S(2)}) %collective-permute-start.4) | collective-permute-done | bytes 524320 | tf_op jit(solution)/shard_map/ppermute | solution.py:450
  74.5 1.7 route.1
  76.2 5.2 %all-to-all-done.2 = bf16[16,24,2048]{2,1,0:T(8,128)(2,1)S(1)} async-done(((bf16[16,24,2048]{2,1,0:T(8,128)(2,1)}), bf16[16,24,2048]{2,1,0:T(8,128)(2,1)S(1)}, u32[]{:S(2)}, u32[]{:S(2)}) %all-to-all-start.2) | async-done | bytes 1572896 | tf_op jit(solution)/shard_map/all_to_all | solution.py:453
  81.4 0.9 fusion
  82.3 1.2 collective-permute-start.8
  83.5 0.9 collective-permute-start.7
  84.4 2.4 %collective-permute-start.6 = (bf16[144,2048]{1,0:T(8,128)(2,1)}, bf16[144,2048]{1,0:T(8,128)(2,1)}, u32[]{:S(2)}, u32[]{:S(2)}) collective-permute-start(bf16[144,2048]{1,0:T(8,128)(2,1)} %get-tuple-element.55), channel_id=1, source_target_pairs={{0,96},{32,0},{64,32},{96,64},{1,97},{33,1},{65,33},{97,65},{2,98}... | collective-permute-start | bytes 1769480 | tf_op jit(solution)/shard_map/ppermute | solution.py:450
  86.7 0.0 collective-permute-start.5
  86.7 0.8 slice.11
  87.5 6.9 %all-to-all-start.3 = ((bf16[16,24,2048]{2,1,0:T(8,128)(2,1)}), bf16[16,24,2048]{2,1,0:T(8,128)(2,1)}, u32[]{:S(2)}, u32[]{:S(2)}) async-start(bf16[16,24,2048]{2,1,0:T(8,128)(2,1)} %bitcast.12), calls=%async_computation.3 | async-start | bytes 3145728 | tf_op jit(solution)/shard_map/all_to_all | solution.py:453
  94.4 4.2 %collective-permute-done.8.refs_2_ = bf16[144,2048]{1,0:T(8,128)(2,1)S(1)} collective-permute-done((bf16[144,2048]{1,0:T(8,128)(2,1)S(1)}, bf16[144,2048]{1,0:T(8,128)(2,1)S(1)}, u32[]{:S(2)}, u32[]{:S(2)}) %collective-permute-start.8) | collective-permute-done | bytes 589856 | tf_op jit(solution)/shard_map/ppermute | solution.py:450
  98.6 2.4 %collective-permute-done.7.refs_1_ = bf16[144,2048]{1,0:T(8,128)(2,1)S(1)} collective-permute-done((bf16[144,2048]{1,0:T(8,128)(2,1)S(1)}, bf16[144,2048]{1,0:T(8,128)(2,1)S(1)}, u32[]{:S(2)}, u32[]{:S(2)}) %collective-permute-start.7) | collective-permute-done | bytes 589856 | tf_op jit(solution)/shard_map/ppermute | solution.py:450
  101.0 0.0 collective-permute-start.10
  101.0 2.0 %collective-permute-start.9 = (bf16[96,2048]{1,0:T(8,128)(2,1)}, bf16[96,2048]{1,0:T(8,128)(2,1)}, u32[]{:S(2)}, u32[]{:S(2)}) collective-permute-start(bf16[96,2048]{1,0:T(8,128)(2,1)} %slice.11), channel_id=1, source_target_pairs={{0,32},{32,64},{64,96},{96,0},{1,33},{33,65},{65,97},{97,1},{2,34}... | collective-permute-start | bytes 1179656 | tf_op jit(solution)/shard_map/ppermute | solution.py:450
  103.0 12.4 %experts.3 = (bf16[384,2048]{1,0:T(8,128)(2,1)}, bf16[144,2048]{1,0:T(8,128)(2,1)}, bf16[144,2048]{1,0:T(8,128)(2,1)}) custom-call(bf16[384,2048]{1,0:T(8,128)(2,1)S(1)} %bitcast.25, bf16[144,2048]{1,0:T(8,128)(2,1)S(1)} %collective-permute-done.7.refs_1_, bf16[144,2048]{1,0:T(8,128)(2,1)S(1)} %collective-permute-done.8.refs_2_, bf16[2048,512]{1,0:T(8,128)(2,1)} %bitcast.33, ...), custom_call_target="tpu_custom_call" | custom-call | flops 845571686400 | bytes 18087936 | tf_op jit(solution)/shard_map/experts/pallas_call | solution.py:253
  115.4 1.3 collective-permute-start.11
  116.7 0.0 collective-permute-done.6.refs_2_
  116.7 0.8 collective-permute-start.12
  117.5 0.0 collective-permute-done.5.refs_1_
  117.5 0.0 all-to-all-done.3
  117.5 14.0 %experts.4 = (bf16[384,2048]{1,0:T(8,128)(2,1)}, bf16[144,2048]{1,0:T(8,128)(2,1)}, bf16[144,2048]{1,0:T(8,128)(2,1)}) custom-call(bf16[384,2048]{1,0:T(8,128)(2,1)} %bitcast.13.refs_0_, bf16[144,2048]{1,0:T(8,128)(2,1)} %collective-permute-done.5.refs_1_, bf16[144,2048]{1,0:T(8,128)(2,1)} %collective-permute-done.6.refs_2_, bf16[2048,512]{1,0:T(8,128)(2,1)} %bitcast.34, ...), custom_call_target="tpu_custom_call" | custom-call | flops 845571686400 | bytes 18087936 | tf_op jit(solution)/shard_map/experts/pallas_call | solution.py:253
  131.6 2.5 %collective-permute-start.15 = (bf16[144,2048]{1,0:T(8,128)(2,1)}, bf16[144,2048]{1,0:T(8,128)(2,1)}, u32[]{:S(2)}, u32[]{:S(2)}) collective-permute-start(bf16[144,2048]{1,0:T(8,128)(2,1)} %get-tuple-element.78), channel_id=1, source_target_pairs={{0,96},{32,0},{64,32},{96,64},{1,97},{33,1},{65,33},{97,65},{2,98}... | collective-permute-start | bytes 1769480 | tf_op jit(solution)/shard_map/ppermute | solution.py:450
  134.1 0.0 collective-permute-done.10.refs_1_
  134.1 0.0 collective-permute-start.16
  134.1 0.0 collective-permute-done.9.refs_0_
  134.1 0.0 collective-permute-done.11.refs_0_
  134.1 0.0 collective-permute-done.12.refs_1_
  134.1 6.9 %all-to-all-start.4 = ((bf16[16,24,2048]{2,1,0:T(8,128)(2,1)}), bf16[16,24,2048]{2,1,0:T(8,128)(2,1)}, u32[]{:S(2)}, u32[]{:S(2)}) async-start(bf16[16,24,2048]{2,1,0:T(8,128)(2,1)} %bitcast.30), calls=%async_computation.4 | async-start | bytes 3145728 | tf_op jit(solution)/shard_map/all_to_all | solution.py:453
  141.0 7.9 %experts.5 = (bf16[96,2048]{1,0:T(8,128)(2,1)}, bf16[96,2048]{1,0:T(8,128)(2,1)}) custom-call(bf16[96,2048]{1,0:T(8,128)(2,1)} %collective-permute-done.9.refs_0_, bf16[96,2048]{1,0:T(8,128)(2,1)} %collective-permute-done.10.refs_1_, bf16[2048,512]{1,0:T(8,128)(2,1)} %bitcast.35, bf16[2048,512]{1,0:T(8,128)(2,1)} %bitcast.39, bf16[512,2048]{1,0:T(8,128)(2,1)} %bitcast.43, ...), custom_call_target="tpu_custom_call" | custom-call | flops 241591910400 | bytes 14155776 | tf_op jit(solution)/shard_map/experts/pallas_call | solution.py:253
  149.0 3.3 %collective-permute-start.13 = (bf16[96,2048]{1,0:T(8,128)(2,1)}, bf16[96,2048]{1,0:T(8,128)(2,1)S(1)}, u32[]{:S(2)}, u32[]{:S(2)}) collective-permute-start(bf16[96,2048]{1,0:T(8,128)(2,1)} %get-tuple-element.74), channel_id=1, source_target_pairs={{0,96},{32,0},{64,32},{96,64},{1,97},{33,1},{65,33},{97,65},{2,98}... | collective-permute-start | bytes 1179656 | tf_op jit(solution)/shard_map/ppermute | solution.py:450
  152.3 0.0 collective-permute-start.14
  152.3 0.0 collective-permute-done.15.refs_2_
  152.3 2.9 %add_up.2.refs_2_ = bf16[384,2048]{1,0:T(8,128)(2,1)} custom-call(bf16[384,2048]{1,0:T(8,128)(2,1)S(1)} %copy-done, bf16[144,2048]{1,0:T(8,128)(2,1)} %collective-permute-done.11.refs_0_, bf16[144,2048]{1,0:T(8,128)(2,1)} %collective-permute-done.12.refs_1_, bf16[144,2048]{1,0:T(8,128)(2,1)} %collective-permute-done.15.refs_2_, ...), custom_call_target="tpu_custom_call" | custom-call | flops 1 | bytes 1 | tf_op jit(solution)/shard_map/add_up/pallas_call | solution.py:423
  155.2 2.7 %collective-permute-done.13.refs_0_ = bf16[96,2048]{1,0:T(8,128)(2,1)S(1)} collective-permute-done((bf16[96,2048]{1,0:T(8,128)(2,1)}, bf16[96,2048]{1,0:T(8,128)(2,1)S(1)}, u32[]{:S(2)}, u32[]{:S(2)}) %collective-permute-start.13) | collective-permute-done | bytes 393248 | tf_op jit(solution)/shard_map/ppermute | solution.py:450
  157.9 3.6 %collective-permute-done.14.refs_1_ = bf16[96,2048]{1,0:T(8,128)(2,1)S(1)} collective-permute-done((bf16[96,2048]{1,0:T(8,128)(2,1)}, bf16[96,2048]{1,0:T(8,128)(2,1)S(1)}, u32[]{:S(2)}, u32[]{:S(2)}) %collective-permute-start.14) | collective-permute-done | bytes 393248 | tf_op jit(solution)/shard_map/ppermute | solution.py:450
  161.5 0.9 add_up.3
  162.4 0.0 all-to-all-done.4
  162.4 7.3 %all-to-all-start.5 = ((bf16[16,24,2048]{2,1,0:T(8,128)(2,1)}), bf16[16,24,2048]{2,1,0:T(8,128)(2,1)S(1)}, u32[]{:S(2)}, u32[]{:S(2)}) async-start(bf16[16,24,2048]{2,1,0:T(8,128)(2,1)} %bitcast.28), calls=%async_computation.5 | async-start | bytes 3145728 | tf_op jit(solution)/shard_map/all_to_all | solution.py:453
  169.7 2.6 %combine_far.1 = (bf16[128,2048]{1,0:T(8,128)(2,1)S(1)}, f32[128,2048]{1,0:T(8,128)S(1)}) custom-call(f32[8,128]{1,0:T(8,128)S(1)} %copy-done.5, bf16[384,2048]{1,0:T(8,128)(2,1)} %bitcast.15.back_ref, f32[128,2048]{1,0:T(8,128)} %get-tuple-element.82.mid_hbm), custom_call_target="tpu_custom_call" | custom-call | tf_op jit(solution)/shard_map/combine_far/pallas_call | solution.py:328
  172.4 0.1 collective-permute-start.17
  172.4 10.7 %collective-permute-done.17.far_ref = bf16[128,2048]{1,0:T(8,128)(2,1)S(1)} collective-permute-done((bf16[128,2048]{1,0:T(8,128)(2,1)S(1)}, bf16[128,2048]{1,0:T(8,128)(2,1)S(1)}, u32[]{:S(2)}, u32[]{:S(2)}) %collective-permute-start.17) | collective-permute-done | bytes 524320 | tf_op jit(solution)/shard_map/ppermute | solution.py:450
  183.1 2.5 %all-to-all-done.5 = bf16[16,24,2048]{2,1,0:T(8,128)(2,1)S(1)} async-done(((bf16[16,24,2048]{2,1,0:T(8,128)(2,1)}), bf16[16,24,2048]{2,1,0:T(8,128)(2,1)S(1)}, u32[]{:S(2)}, u32[]{:S(2)}) %all-to-all-start.5) | async-done | bytes 1572896 | tf_op jit(solution)/shard_map/all_to_all | solution.py:453
  185.7 1.7 combine.1
  (18 shorter events, 0.0 us)
Async XLA Ops:
  0.0 35.4 %collective-permute-start.1 = (bf16[2048,512]{1,0:T(8,128)(2,1)}, bf16[2048,512]{1,0:T(8,128)(2,1)}, u32[]{:S(2)}, u32[]{:S(2)}) collective-permute-start(bf16[2048,512]{1,0:T(8,128)(2,1)} %bitcast.32), channel_id=1, source_target_pairs={{0,16},{16,0},{1,17},{17,1},{2,18},{18,2},{3,19},{19,3},{4,20},{20... | collective-permute-start | bytes 6291464 | tf_op jit(solution)/shard_map/ppermute | solution.py:447
  0.0 35.4 %collective-permute-start.2 = (bf16[2048,512]{1,0:T(8,128)(2,1)}, bf16[2048,512]{1,0:T(8,128)(2,1)}, u32[]{:S(2)}, u32[]{:S(2)}) collective-permute-start(bf16[2048,512]{1,0:T(8,128)(2,1)} %bitcast.36), channel_id=1, source_target_pairs={{0,16},{16,0},{1,17},{17,1},{2,18},{18,2},{3,19},{19,3},{4,20},{20... | collective-permute-start | bytes 6291464 | tf_op jit(solution)/shard_map/ppermute | solution.py:447
  0.5 34.9 %collective-permute-start.3 = (bf16[512,2048]{1,0:T(8,128)(2,1)}, bf16[512,2048]{1,0:T(8,128)(2,1)}, u32[]{:S(2)}, u32[]{:S(2)}) collective-permute-start(bf16[512,2048]{1,0:T(8,128)(2,1)} %bitcast.40), channel_id=1, source_target_pairs={{0,16},{16,0},{1,17},{17,1},{2,18},{18,2},{3,19},{19,3},{4,20},{20... | collective-permute-start | bytes 6291464 | tf_op jit(solution)/shard_map/ppermute | solution.py:447
  3.0 4.7 %copy-start.6 = (s32[1,128,2]{1,2,0:T(2,128)S(1)}, s32[1,128,2]{1,2,0:T(2,128)}, u32[]{:S(2)}) copy-start(s32[1,128,2]{1,2,0:T(2,128)} %param.10) | copy-start | bytes 3076
  3.0 4.7 %copy-start.7 = (f32[1,128,2]{1,2,0:T(2,128)S(1)}, f32[1,128,2]{1,2,0:T(2,128)}, u32[]{:S(2)}) copy-start(f32[1,128,2]{1,2,0:T(2,128)} %param.11) | copy-start | bytes 3076
  3.0 26.2 %all-to-all-start = ((bf16[8,3,128,256]{3,2,1,0:T(8,128)(2,1)}), bf16[8,3,128,256]{3,2,1,0:T(8,128)(2,1)S(1)}, u32[]{:S(2)}, u32[]{:S(2)}) async-start(bf16[8,3,128,256]{3,2,1,0:T(8,128)(2,1)} %spread.1), calls=%async_computation | async-start | bytes 3145728 | tf_op jit(solution)/shard_map/all_to_all | solution.py:463
  7.9 40.3 %copy-start.2 = (f32[8,128]{1,0:T(8,128)}, f32[8,128]{1,0:T(8,128)S(1)}, u32[]{:S(2)}) copy-start(f32[8,128]{1,0:T(8,128)S(1)} %plan.1.info_ref) | copy-start | bytes 12292
  7.9 40.3 %copy-start.1 = (bf16[1,128,2048]{2,1,0:T(8,128)(2,1)S(1)}, bf16[1,128,2048]{2,1,0:T(8,128)(2,1)}, u32[]{:S(2)}) copy-start(bf16[1,128,2048]{2,1,0:T(8,128)(2,1)} %param.8) | copy-start | bytes 1572868
  7.9 27.5 %collective-permute-start = (f32[8,128]{1,0:T(8,128)S(1)}, f32[8,128]{1,0:T(8,128)S(1)}, u32[]{:S(2)}, u32[]{:S(2)}) collective-permute-start(f32[8,128]{1,0:T(8,128)S(1)} %plan.1.info_ref), channel_id=1, source_target_pairs={{0,64},{32,96},{64,0},{96,32},{1,65},{33,97},{65,1},{97,33},{2,66}... | collective-permute-start | bytes 12296 | tf_op jit(solution)/shard_map/ppermute | solution.py:450
  35.4 39.1 %copy-start.4 = (f32[8,128]{1,0:T(8,128)}, f32[8,128]{1,0:T(8,128)S(1)}, u32[]{:S(2)}) copy-start(f32[8,128]{1,0:T(8,128)S(1)} %collective-permute-done.info_ref) | copy-start | bytes 12292
  51.9 29.5 %all-to-all-start.2 = ((bf16[16,24,2048]{2,1,0:T(8,128)(2,1)}), bf16[16,24,2048]{2,1,0:T(8,128)(2,1)S(1)}, u32[]{:S(2)}, u32[]{:S(2)}) async-start(bf16[16,24,2048]{2,1,0:T(8,128)(2,1)} %bitcast.10), calls=%async_computation.2 | async-start | bytes 3145728 | tf_op jit(solution)/shard_map/all_to_all | solution.py:453
  60.2 14.2 %collective-permute-start.4 = (bf16[128,2048]{1,0:T(8,128)(2,1)S(1)}, bf16[128,2048]{1,0:T(8,128)(2,1)S(1)}, u32[]{:S(2)}, u32[]{:S(2)}) collective-permute-start(bf16[128,2048]{1,0:T(8,128)(2,1)S(1)} %get-tuple-element.49), channel_id=1, source_target_pairs={{0,64},{32,96},{64,0},{96,32},{1,65},{33,97},{65,1},{97,33},{2,66}... | collective-permute-start | bytes 1572872 | tf_op jit(solution)/shard_map/ppermute | solution.py:450
  82.3 16.3 %collective-permute-start.8 = (bf16[144,2048]{1,0:T(8,128)(2,1)S(1)}, bf16[144,2048]{1,0:T(8,128)(2,1)S(1)}, u32[]{:S(2)}, u32[]{:S(2)}) collective-permute-start(bf16[144,2048]{1,0:T(8,128)(2,1)S(1)} %get-tuple-element.57), channel_id=1, source_target_pairs={{0,96},{32,0},{64,32},{96,64},{1,97},{33,1},{65,33},{97,65},{2,98}... | collective-permute-start | bytes 1769480 | tf_op jit(solution)/shard_map/ppermute | solution.py:450
  83.5 17.5 %collective-permute-start.7 = (bf16[144,2048]{1,0:T(8,128)(2,1)S(1)}, bf16[144,2048]{1,0:T(8,128)(2,1)S(1)}, u32[]{:S(2)}, u32[]{:S(2)}) collective-permute-start(bf16[144,2048]{1,0:T(8,128)(2,1)S(1)} %get-tuple-element.57), channel_id=1, source_target_pairs={{0,32},{32,64},{64,96},{96,0},{1,33},{33,65},{65,97},{97,1},{2,34}... | collective-permute-start | bytes 1769480 | tf_op jit(solution)/shard_map/ppermute | solution.py:450
  84.4 32.3 %collective-permute-start.6 = (bf16[144,2048]{1,0:T(8,128)(2,1)}, bf16[144,2048]{1,0:T(8,128)(2,1)}, u32[]{:S(2)}, u32[]{:S(2)}) collective-permute-start(bf16[144,2048]{1,0:T(8,128)(2,1)} %get-tuple-element.55), channel_id=1, source_target_pairs={{0,96},{32,0},{64,32},{96,64},{1,97},{33,1},{65,33},{97,65},{2,98}... | collective-permute-start | bytes 1769480 | tf_op jit(solution)/shard_map/ppermute | solution.py:450
  86.7 30.8 %collective-permute-start.5 = (bf16[144,2048]{1,0:T(8,128)(2,1)}, bf16[144,2048]{1,0:T(8,128)(2,1)}, u32[]{:S(2)}, u32[]{:S(2)}) collective-permute-start(bf16[144,2048]{1,0:T(8,128)(2,1)} %get-tuple-element.55), channel_id=1, source_target_pairs={{0,32},{32,64},{64,96},{96,0},{1,33},{33,65},{65,97},{97,1},{2,34}... | collective-permute-start | bytes 1769480 | tf_op jit(solution)/shard_map/ppermute | solution.py:450
  87.5 30.0 %all-to-all-start.3 = ((bf16[16,24,2048]{2,1,0:T(8,128)(2,1)}), bf16[16,24,2048]{2,1,0:T(8,128)(2,1)}, u32[]{:S(2)}, u32[]{:S(2)}) async-start(bf16[16,24,2048]{2,1,0:T(8,128)(2,1)} %bitcast.12), calls=%async_computation.3 | async-start | bytes 3145728 | tf_op jit(solution)/shard_map/all_to_all | solution.py:453
  101.0 33.1 %collective-permute-start.10 = (bf16[96,2048]{1,0:T(8,128)(2,1)}, bf16[96,2048]{1,0:T(8,128)(2,1)}, u32[]{:S(2)}, u32[]{:S(2)}) collective-permute-start(bf16[96,2048]{1,0:T(8,128)(2,1)} %slice.11), channel_id=1, source_target_pairs={{0,96},{32,0},{64,32},{96,64},{1,97},{33,1},{65,33},{97,65},{2,98}... | collective-permute-start | bytes 1179656 | tf_op jit(solution)/shard_map/ppermute | solution.py:450
  101.0 33.1 %collective-permute-start.9 = (bf16[96,2048]{1,0:T(8,128)(2,1)}, bf16[96,2048]{1,0:T(8,128)(2,1)}, u32[]{:S(2)}, u32[]{:S(2)}) collective-permute-start(bf16[96,2048]{1,0:T(8,128)(2,1)} %slice.11), channel_id=1, source_target_pairs={{0,32},{32,64},{64,96},{96,0},{1,33},{33,65},{65,97},{97,1},{2,34}... | collective-permute-start | bytes 1179656 | tf_op jit(solution)/shard_map/ppermute | solution.py:450
  115.4 18.6 %collective-permute-start.11 = (bf16[144,2048]{1,0:T(8,128)(2,1)}, bf16[144,2048]{1,0:T(8,128)(2,1)}, u32[]{:S(2)}, u32[]{:S(2)}) collective-permute-start(bf16[144,2048]{1,0:T(8,128)(2,1)} %get-tuple-element.70), channel_id=1, source_target_pairs={{0,96},{32,0},{64,32},{96,64},{1,97},{33,1},{65,33},{97,65},{2,98}... | collective-permute-start | bytes 1769480 | tf_op jit(solution)/shard_map/ppermute | solution.py:450
  116.7 17.4 %collective-permute-start.12 = (bf16[144,2048]{1,0:T(8,128)(2,1)}, bf16[144,2048]{1,0:T(8,128)(2,1)}, u32[]{:S(2)}, u32[]{:S(2)}) collective-permute-start(bf16[144,2048]{1,0:T(8,128)(2,1)} %get-tuple-element.71), channel_id=1, source_target_pairs={{0,32},{32,64},{64,96},{96,0},{1,33},{33,65},{65,97},{97,1},{2,34}... | collective-permute-start | bytes 1769480 | tf_op jit(solution)/shard_map/ppermute | solution.py:450
  131.6 20.7 %collective-permute-start.15 = (bf16[144,2048]{1,0:T(8,128)(2,1)}, bf16[144,2048]{1,0:T(8,128)(2,1)}, u32[]{:S(2)}, u32[]{:S(2)}) collective-permute-start(bf16[144,2048]{1,0:T(8,128)(2,1)} %get-tuple-element.78), channel_id=1, source_target_pairs={{0,96},{32,0},{64,32},{96,64},{1,97},{33,1},{65,33},{97,65},{2,98}... | collective-permute-start | bytes 1769480 | tf_op jit(solution)/shard_map/ppermute | solution.py:450
  134.1 18.2 %collective-permute-start.16 = (bf16[144,2048]{1,0:T(8,128)(2,1)}, bf16[144,2048]{1,0:T(8,128)(2,1)}, u32[]{:S(2)}, u32[]{:S(2)}) collective-permute-start(bf16[144,2048]{1,0:T(8,128)(2,1)} %get-tuple-element.79), channel_id=1, source_target_pairs={{0,32},{32,64},{64,96},{96,0},{1,33},{33,65},{65,97},{97,1},{2,34}... | collective-permute-start | bytes 1769480 | tf_op jit(solution)/shard_map/ppermute | solution.py:450
  134.1 28.3 %all-to-all-start.4 = ((bf16[16,24,2048]{2,1,0:T(8,128)(2,1)}), bf16[16,24,2048]{2,1,0:T(8,128)(2,1)}, u32[]{:S(2)}, u32[]{:S(2)}) async-start(bf16[16,24,2048]{2,1,0:T(8,128)(2,1)} %bitcast.30), calls=%async_computation.4 | async-start | bytes 3145728 | tf_op jit(solution)/shard_map/all_to_all | solution.py:453
  141.0 11.2 %copy-start = (bf16[384,2048]{1,0:T(8,128)(2,1)S(1)}, bf16[384,2048]{1,0:T(8,128)(2,1)}, u32[]{:S(2)}) copy-start(bf16[384,2048]{1,0:T(8,128)(2,1)} %get-tuple-element.64.own_ref) | copy-start | bytes 4718596
  149.0 8.9 %collective-permute-start.13 = (bf16[96,2048]{1,0:T(8,128)(2,1)}, bf16[96,2048]{1,0:T(8,128)(2,1)S(1)}, u32[]{:S(2)}, u32[]{:S(2)}) collective-permute-start(bf16[96,2048]{1,0:T(8,128)(2,1)} %get-tuple-element.74), channel_id=1, source_target_pairs={{0,96},{32,0},{64,32},{96,64},{1,97},{33,1},{65,33},{97,65},{2,98}... | collective-permute-start | bytes 1179656 | tf_op jit(solution)/shard_map/ppermute | solution.py:450
  152.3 9.2 %collective-permute-start.14 = (bf16[96,2048]{1,0:T(8,128)(2,1)}, bf16[96,2048]{1,0:T(8,128)(2,1)S(1)}, u32[]{:S(2)}, u32[]{:S(2)}) collective-permute-start(bf16[96,2048]{1,0:T(8,128)(2,1)} %get-tuple-element.75), channel_id=1, source_target_pairs={{0,32},{32,64},{64,96},{96,0},{1,33},{33,65},{65,97},{97,1},{2,34}... | collective-permute-start | bytes 1179656 | tf_op jit(solution)/shard_map/ppermute | solution.py:450
  162.4 7.3 %copy-start.5 = (f32[8,128]{1,0:T(8,128)S(1)}, f32[8,128]{1,0:T(8,128)}, u32[]{:S(2)}) copy-start(f32[8,128]{1,0:T(8,128)} %copy-done.4) | copy-start | bytes 12292
  162.4 23.3 %all-to-all-start.5 = ((bf16[16,24,2048]{2,1,0:T(8,128)(2,1)}), bf16[16,24,2048]{2,1,0:T(8,128)(2,1)S(1)}, u32[]{:S(2)}, u32[]{:S(2)}) async-start(bf16[16,24,2048]{2,1,0:T(8,128)(2,1)} %bitcast.28), calls=%async_computation.5 | async-start | bytes 3145728 | tf_op jit(solution)/shard_map/all_to_all | solution.py:453
  169.7 16.0 %copy-start.3 = (f32[8,128]{1,0:T(8,128)S(1)}, f32[8,128]{1,0:T(8,128)}, u32[]{:S(2)}) copy-start(f32[8,128]{1,0:T(8,128)} %copy-done.2) | copy-start | bytes 12292
  172.4 10.8 %collective-permute-start.17 = (bf16[128,2048]{1,0:T(8,128)(2,1)S(1)}, bf16[128,2048]{1,0:T(8,128)(2,1)S(1)}, u32[]{:S(2)}, u32[]{:S(2)}) collective-permute-start(bf16[128,2048]{1,0:T(8,128)(2,1)S(1)} %get-tuple-element.83), channel_id=1, source_target_pairs={{0,64},{32,96},{64,0},{96,32},{1,65},{33,97},{65,1},{97,33},{2,66}... | collective-permute-start | bytes 1572872 | tf_op jit(solution)/shard_map/ppermute | solution.py:450

commit v9 on v8

--- a/solution.py
+++ b/solution.py
@@ -471,9 +471,9 @@
     far_buffer = route(far_tokens, info_far, slots)
     own, far_buffer = tie((exchange(buffer), far_buffer))
     eighth = own.shape[0] // 8
-    first, second = own[: 3 * eighth], own[3 * eighth : 6 * eighth]
+    first, second = own[: 2 * eighth], own[2 * eighth : 5 * eighth]
     rest, first, second = tie((own, first, second))
-    third = rest[6 * eighth :]
+    third = rest[5 * eighth :]
     third, far_buffer = tie((third, far_buffer))
     far_rows = exchange(far_buffer)
 
@@ -497,7 +497,7 @@
     home.append(give_back(back))
     far_sum, mid = combine_far(info_far, far_back, mid)
     total = add_up(own_part, home[:2])
-    total = add_up(own_part, home[2:], 6 * eighth, total)
+    total = add_up(own_part, home[2:], 5 * eighth, total)
     total, far_back = tie((total, far_back))
     back = exchange(total)
     far_home = shift(far_sum, 2)

time: 190 us -> 193 us (1.016)
  waiting for transfers between devices: 62.9 us -> 66.1 us
    all_to_all x4, waiting for transfers between devices: 7.73 us -> 11.6 us  [exchange(): return lax.all_to_all(x, exp, split_axis=0, concat_axis=0, tiled=True)]
  transfers between devices with their start and end apart: 23 -> 23, of which waited for: 9 -> 9; matrix products, arithmetic and copies ran while one was open for 0% -> 1% of each run, Pallas kernels for 27% -> 27%
where the time goes in v9:
time: 193 us; the launch traced here: 191 us
  waiting for transfers between devices  66.1 us (34%)
  Pallas kernels  56.3 us (29%)
  starting transfers between devices  53.1 us (28%)
  blocking collectives  12.8 us (7%)
    ppermute x15, waiting for transfers between devices, shift(): return lax.ppermute(x, 'y', [(i, (i + by) % n_y) for i in range(n_y)])  36.8 us
    pallas_call x3, Pallas kernels, experts(): pl.pallas_call(functools.partial(expert_kernel, n_in=len(arrays), block=b...  34.1 us
    all_to_all x4, starting transfers between devices, exchange(): return lax.all_to_all(x, exp, split_axis=0, concat_axis=0, tiled=True)  28.4 us
    ppermute x15, starting transfers between devices, shift(): return lax.ppermute(x, 'y', [(i, (i + by) % n_y) for i in range(n_y)])  19.7 us
    all_to_all x1, waiting for transfers between devices, per_device(): arrived = lax.all_to_all(qkv, seq, split_axis=0, concat_axis=0, tiled=True)  17.7 us
    all_to_all x1, blocking collectives, per_device(): lax.all_to_all(context, seq, split_axis=0, concat_axis=0, tiled=True)  12.8 us
    all_to_all x4, waiting for transfers between devices, exchange(): return lax.all_to_all(x, exp, split_axis=0, concat_axis=0, tiled=True)  11.6 us
    pallas_call x1, Pallas kernels, attention(): pl.pallas_call(functools.partial(attention_kernel, block=2 * rows), grid=...  6.15 us
  transfers between devices with their start and end apart: 23, of which 9 were waited for; matrix products, arithmetic and copies ran while one was open for 1% of the time, Pallas kernels for 27%

profile of v9, /device:TPU:2, one launch (start us, length us, event | category | flops | bytes accessed | tf_op | source)
XLA Modules:
  0.0 190.6 jit_solution(6819278661303260369)
XLA Ops:
  0.0 0.0 collective-permute-start.1
  0.0 0.5 collective-permute-start.2
  0.5 0.0 collective-permute-start.3
  0.5 2.4 %spread.1 = bf16[8,3,128,256]{3,2,1,0:T(8,128)(2,1)} custom-call(bf16[3,128,2048]{2,1,0:T(8,128)(2,1)} %bitcast.30), custom_call_target="tpu_custom_call" | custom-call | tf_op jit(solution)/shard_map/spread/pallas_call | solution.py:385
  3.0 0.0 copy-start.6
  3.0 0.0 copy-start.7
  3.0 4.6 %all-to-all-start = ((bf16[8,3,128,256]{3,2,1,0:T(8,128)(2,1)}), bf16[8,3,128,256]{3,2,1,0:T(8,128)(2,1)S(1)}, u32[]{:S(2)}, u32[]{:S(2)}) async-start(bf16[8,3,128,256]{3,2,1,0:T(8,128)(2,1)} %spread.1), calls=%async_computation | async-start | bytes 3145728 | tf_op jit(solution)/shard_map/all_to_all | solution.py:463
  7.6 0.1 pad.2.clone
  7.7 0.1 maximum_maximum_fusion.info_ref
  7.7 0.1 plan.1.info_ref
  7.9 3.6 %collective-permute-start = (f32[8,128]{1,0:T(8,128)S(1)}, f32[8,128]{1,0:T(8,128)S(1)}, u32[]{:S(2)}, u32[]{:S(2)}) collective-permute-start(f32[8,128]{1,0:T(8,128)S(1)} %plan.1.info_ref), channel_id=1, source_target_pairs={{0,64},{32,96},{64,0},{96,32},{1,65},{33,97},{65,1},{97,33},{2,66}... | collective-permute-start | bytes 12296 | tf_op jit(solution)/shard_map/ppermute | solution.py:450
  11.5 17.7 %all-to-all-done.x_ref = bf16[8,3,128,256]{3,2,1,0:T(8,128)(2,1)S(1)} async-done(((bf16[8,3,128,256]{3,2,1,0:T(8,128)(2,1)}), bf16[8,3,128,256]{3,2,1,0:T(8,128)(2,1)S(1)}, u32[]{:S(2)}, u32[]{:S(2)}) %all-to-all-start) | async-done | bytes 1572896 | tf_op jit(solution)/shard_map/all_to_all | solution.py:463
  29.2 6.2 %attention.1 = (bf16[8,128,256]{2,1,0:T(8,128)(2,1)S(1)}, bf16[2048,2048]{1,0:T(8,128)(2,1)S(1)}) custom-call(bf16[8,3,128,256]{3,2,1,0:T(8,128)(2,1)S(1)} %all-to-all-done.x_ref, bf16[2048,2048]{1,0:T(8,128)(2,1)} %w_hbm.1), custom_call_target="tpu_custom_call" | custom-call | tf_op jit(solution)/shard_map/attention/pallas_call | solution.py:71
  35.4 0.0 collective-permute-done.info_ref
  35.4 0.0 collective-permute-done.1.refs_6_.refs_5_
  35.4 0.0 collective-permute-done.2.refs_7_.refs_6_
  35.4 0.0 collective-permute-done.3.refs_8_.refs_7_
  35.4 12.8 %all_to_all.56.ctx_ref = bf16[8,128,256]{2,1,0:T(8,128)(2,1)S(1)} all-to-all(bf16[8,128,256]{2,1,0:T(8,128)(2,1)S(1)} %get-tuple-element.46), channel_id=1, replica_groups=mesh['y'=4,'core'=2,'z'=4,'x'=4] {'y','core'}, dimensions={0} | all-to-all | bytes 1048576 | tf_op jit(solution)/shard_map/all_to_all | solution.py:466
  48.2 3.7 %project.1 = (f32[128,2048]{1,0:T(8,128)}, bf16[128,2048]{1,0:T(8,128)(2,1)S(1)}, bf16[384,2048]{1,0:T(8,128)(2,1)}) custom-call(bf16[8,128,256]{2,1,0:T(8,128)(2,1)S(1)} %all_to_all.56.ctx_ref, bf16[2048,2048]{1,0:T(8,128)(2,1)S(1)} %get-tuple-element.47.w_ref, bf16[128,2048]{1,0:T(8,128)(2,1)S(1)} %bitcast.28, f32[8,128]{1,0:T(8,128)S(1)} %plan.1.info_ref), custom_call_target="tpu_custom_call" | custom-call | tf_op jit(solution)/shard_map/project/pallas_call | solution.py:149
  51.9 8.3 %all-to-all-start.2 = ((bf16[16,24,2048]{2,1,0:T(8,128)(2,1)}), bf16[16,24,2048]{2,1,0:T(8,128)(2,1)S(1)}, u32[]{:S(2)}, u32[]{:S(2)}) async-start(bf16[16,24,2048]{2,1,0:T(8,128)(2,1)} %bitcast.10), calls=%async_computation.2 | async-start | bytes 3145728 | tf_op jit(solution)/shard_map/all_to_all | solution.py:453
  60.2 0.4 collective-permute-start.4
  60.6 13.9 %collective-permute-done.4.normed_ref = bf16[128,2048]{1,0:T(8,128)(2,1)S(1)} collective-permute-done((bf16[128,2048]{1,0:T(8,128)(2,1)S(1)}, bf16[128,2048]{1,0:T(8,128)(2,1)S(1)}, u32[]{:S(2)}, u32[]{:S(2)}) %collective-permute-start.4) | collective-permute-done | bytes 524320 | tf_op jit(solution)/shard_map/ppermute | solution.py:450
  74.5 1.7 route.1
  76.2 5.2 %all-to-all-done.2 = bf16[16,24,2048]{2,1,0:T(8,128)(2,1)S(1)} async-done(((bf16[16,24,2048]{2,1,0:T(8,128)(2,1)}), bf16[16,24,2048]{2,1,0:T(8,128)(2,1)S(1)}, u32[]{:S(2)}, u32[]{:S(2)}) %all-to-all-start.2) | async-done | bytes 1572896 | tf_op jit(solution)/shard_map/all_to_all | solution.py:453
  81.4 0.9 slice.10
  82.3 1.2 collective-permute-start.8
  83.4 0.9 collective-permute-start.7
  84.3 2.4 %collective-permute-start.6 = (bf16[144,2048]{1,0:T(8,128)(2,1)}, bf16[144,2048]{1,0:T(8,128)(2,1)}, u32[]{:S(2)}, u32[]{:S(2)}) collective-permute-start(bf16[144,2048]{1,0:T(8,128)(2,1)} %slice.10), channel_id=1, source_target_pairs={{0,96},{32,0},{64,32},{96,64},{1,97},{33,1},{65,33},{97,65},{2,98}... | collective-permute-start | bytes 1769480 | tf_op jit(solution)/shard_map/ppermute | solution.py:450
  86.7 0.0 collective-permute-start.5
  86.7 0.9 slice.11
  87.5 6.9 %all-to-all-start.3 = ((bf16[16,24,2048]{2,1,0:T(8,128)(2,1)}), bf16[16,24,2048]{2,1,0:T(8,128)(2,1)}, u32[]{:S(2)}, u32[]{:S(2)}) async-start(bf16[16,24,2048]{2,1,0:T(8,128)(2,1)} %bitcast.12), calls=%async_computation.3 | async-start | bytes 3145728 | tf_op jit(solution)/shard_map/all_to_all | solution.py:453
  94.4 0.0 collective-permute-done.8.refs_2_
  94.4 2.3 %collective-permute-done.7.refs_1_ = bf16[96,2048]{1,0:T(8,128)(2,1)S(1)} collective-permute-done((bf16[96,2048]{1,0:T(8,128)(2,1)S(1)}, bf16[96,2048]{1,0:T(8,128)(2,1)S(1)}, u32[]{:S(2)}, u32[]{:S(2)}) %collective-permute-start.7) | collective-permute-done | bytes 393248 | tf_op jit(solution)/shard_map/ppermute | solution.py:450
  96.7 1.0 collective-permute-start.10
  97.7 1.0 collective-permute-start.9
  98.7 11.3 %experts.3 = (bf16[384,2048]{1,0:T(8,128)(2,1)}, bf16[96,2048]{1,0:T(8,128)(2,1)}, bf16[96,2048]{1,0:T(8,128)(2,1)}) custom-call(bf16[384,2048]{1,0:T(8,128)(2,1)S(1)} %bitcast.26, bf16[96,2048]{1,0:T(8,128)(2,1)S(1)} %collective-permute-done.7.refs_1_, bf16[96,2048]{1,0:T(8,128)(2,1)S(1)} %collective-permute-done.8.refs_2_, bf16[2048,512]{1,0:T(8,128)(2,1)} %bitcast.34, ...), custom_call_target="tpu_custom_call" | custom-call | flops 724775731200 | bytes 17301504 | tf_op jit(solution)/shard_map/experts/pallas_call | solution.py:253
  110.0 2.3 %collective-permute-start.11 = (bf16[96,2048]{1,0:T(8,128)(2,1)}, bf16[96,2048]{1,0:T(8,128)(2,1)}, u32[]{:S(2)}, u32[]{:S(2)}) collective-permute-start(bf16[96,2048]{1,0:T(8,128)(2,1)} %get-tuple-element.70), channel_id=1, source_target_pairs={{0,96},{32,0},{64,32},{96,64},{1,97},{33,1},{65,33},{97,65},{2,98}... | collective-permute-start | bytes 1179656 | tf_op jit(solution)/shard_map/ppermute | solution.py:450
  112.3 0.0 collective-permute-done.6.refs_2_
  112.3 0.0 collective-permute-start.12
  112.3 0.0 collective-permute-done.5.refs_1_
  112.4 2.2 %all-to-all-done.3 = bf16[16,24,2048]{2,1,0:T(8,128)(2,1)} async-done(((bf16[16,24,2048]{2,1,0:T(8,128)(2,1)}), bf16[16,24,2048]{2,1,0:T(8,128)(2,1)}, u32[]{:S(2)}, u32[]{:S(2)}) %all-to-all-start.3) | async-done | bytes 1572896 | tf_op jit(solution)/shard_map/all_to_all | solution.py:453
  114.6 14.0 %experts.4 = (bf16[384,2048]{1,0:T(8,128)(2,1)}, bf16[144,2048]{1,0:T(8,128)(2,1)}, bf16[144,2048]{1,0:T(8,128)(2,1)}) custom-call(bf16[384,2048]{1,0:T(8,128)(2,1)} %bitcast.13.refs_0_, bf16[144,2048]{1,0:T(8,128)(2,1)} %collective-permute-done.5.refs_1_, bf16[144,2048]{1,0:T(8,128)(2,1)} %collective-permute-done.6.refs_2_, bf16[2048,512]{1,0:T(8,128)(2,1)} %bitcast.35, ...), custom_call_target="tpu_custom_call" | custom-call | flops 845571686400 | bytes 18087936 | tf_op jit(solution)/shard_map/experts/pallas_call | solution.py:253
  128.6 0.0 collective-permute-done.11.refs_0_
  128.6 0.0 collective-permute-done.12.refs_1_
  128.6 0.0 collective-permute-done.10.refs_1_
  128.7 0.0 collective-permute-done.9.refs_0_
  128.7 3.3 %collective-permute-start.15 = (bf16[144,2048]{1,0:T(8,128)(2,1)}, bf16[144,2048]{1,0:T(8,128)(2,1)}, u32[]{:S(2)}, u32[]{:S(2)}) collective-permute-start(bf16[144,2048]{1,0:T(8,128)(2,1)} %get-tuple-element.78), channel_id=1, source_target_pairs={{0,96},{32,0},{64,32},{96,64},{1,97},{33,1},{65,33},{97,65},{2,98}... | collective-permute-start | bytes 1769480 | tf_op jit(solution)/shard_map/ppermute | solution.py:450
  132.0 0.0 collective-permute-start.16
  132.0 5.9 %all-to-all-start.4 = ((bf16[16,24,2048]{2,1,0:T(8,128)(2,1)}), bf16[16,24,2048]{2,1,0:T(8,128)(2,1)}, u32[]{:S(2)}, u32[]{:S(2)}) async-start(bf16[16,24,2048]{2,1,0:T(8,128)(2,1)} %bitcast.31), calls=%async_computation.4 | async-start | bytes 3145728 | tf_op jit(solution)/shard_map/all_to_all | solution.py:453
  137.9 8.8 %experts.5 = (bf16[144,2048]{1,0:T(8,128)(2,1)}, bf16[144,2048]{1,0:T(8,128)(2,1)}) custom-call(bf16[144,2048]{1,0:T(8,128)(2,1)} %collective-permute-done.9.refs_0_, bf16[144,2048]{1,0:T(8,128)(2,1)} %collective-permute-done.10.refs_1_, bf16[2048,512]{1,0:T(8,128)(2,1)} %bitcast.36, bf16[2048,512]{1,0:T(8,128)(2,1)} %bitcast.40, ...), custom_call_target="tpu_custom_call" | custom-call | flops 362387865600 | bytes 14942208 | tf_op jit(solution)/shard_map/experts/pallas_call | solution.py:253
  146.7 3.6 %collective-permute-start.13 = (bf16[144,2048]{1,0:T(8,128)(2,1)}, bf16[144,2048]{1,0:T(8,128)(2,1)S(1)}, u32[]{:S(2)}, u32[]{:S(2)}) collective-permute-start(bf16[144,2048]{1,0:T(8,128)(2,1)} %get-tuple-element.74), channel_id=1, source_target_pairs={{0,96},{32,0},{64,32},{96,64},{1,97},{33,1},{65,33},{97,65},{2,98}... | collective-permute-start | bytes 1769480 | tf_op jit(solution)/shard_map/ppermute | solution.py:450
  150.3 0.0 collective-permute-start.14
  150.3 0.0 collective-permute-done.15.refs_2_
  150.3 2.7 %add_up.2.refs_2_ = bf16[384,2048]{1,0:T(8,128)(2,1)} custom-call(bf16[384,2048]{1,0:T(8,128)(2,1)S(1)} %copy-done, bf16[96,2048]{1,0:T(8,128)(2,1)} %collective-permute-done.11.refs_0_, bf16[96,2048]{1,0:T(8,128)(2,1)} %collective-permute-done.12.refs_1_, bf16[144,2048]{1,0:T(8,128)(2,1)} %collective-permute-done.15.refs_2_, ...), custom_call_target="tpu_custom_call" | custom-call | flops 1 | bytes 1 | tf_op jit(solution)/shard_map/add_up/pallas_call | solution.py:423
  153.0 6.7 %collective-permute-done.13.refs_0_ = bf16[144,2048]{1,0:T(8,128)(2,1)S(1)} collective-permute-done((bf16[144,2048]{1,0:T(8,128)(2,1)}, bf16[144,2048]{1,0:T(8,128)(2,1)S(1)}, u32[]{:S(2)}, u32[]{:S(2)}) %collective-permute-start.13) | collective-permute-done | bytes 589856 | tf_op jit(solution)/shard_map/ppermute | solution.py:450
  159.7 3.3 %collective-permute-done.14.refs_1_ = bf16[144,2048]{1,0:T(8,128)(2,1)S(1)} collective-permute-done((bf16[144,2048]{1,0:T(8,128)(2,1)}, bf16[144,2048]{1,0:T(8,128)(2,1)S(1)}, u32[]{:S(2)}, u32[]{:S(2)}) %collective-permute-start.14) | collective-permute-done | bytes 589856 | tf_op jit(solution)/shard_map/ppermute | solution.py:450
  163.0 1.0 add_up.3
  164.0 0.0 all-to-all-done.4
  164.0 7.2 %all-to-all-start.5 = ((bf16[16,24,2048]{2,1,0:T(8,128)(2,1)}), bf16[16,24,2048]{2,1,0:T(8,128)(2,1)S(1)}, u32[]{:S(2)}, u32[]{:S(2)}) async-start(bf16[16,24,2048]{2,1,0:T(8,128)(2,1)} %bitcast.29), calls=%async_computation.5 | async-start | bytes 3145728 | tf_op jit(solution)/shard_map/all_to_all | solution.py:453
  171.3 2.6 %combine_far.1 = (bf16[128,2048]{1,0:T(8,128)(2,1)S(1)}, f32[128,2048]{1,0:T(8,128)S(1)}) custom-call(f32[8,128]{1,0:T(8,128)S(1)} %copy-done.5, bf16[384,2048]{1,0:T(8,128)(2,1)} %bitcast.15.back_ref, f32[128,2048]{1,0:T(8,128)} %get-tuple-element.82.mid_hbm), custom_call_target="tpu_custom_call" | custom-call | tf_op jit(solution)/shard_map/combine_far/pallas_call | solution.py:328
  174.0 0.1 collective-permute-start.17
  174.0 10.7 %collective-permute-done.17.far_ref = bf16[128,2048]{1,0:T(8,128)(2,1)S(1)} collective-permute-done((bf16[128,2048]{1,0:T(8,128)(2,1)S(1)}, bf16[128,2048]{1,0:T(8,128)(2,1)S(1)}, u32[]{:S(2)}, u32[]{:S(2)}) %collective-permute-start.17) | collective-permute-done | bytes 524320 | tf_op jit(solution)/shard_map/ppermute | solution.py:450
  184.7 4.1 %all-to-all-done.5 = bf16[16,24,2048]{2,1,0:T(8,128)(2,1)S(1)} async-done(((bf16[16,24,2048]{2,1,0:T(8,128)(2,1)}), bf16[16,24,2048]{2,1,0:T(8,128)(2,1)S(1)}, u32[]{:S(2)}, u32[]{:S(2)}) %all-to-all-start.5) | async-done | bytes 1572896 | tf_op jit(solution)/shard_map/all_to_all | solution.py:453
  188.9 1.7 combine.1
  (19 shorter events, 0.1 us)
Async XLA Ops:
  0.0 35.4 %collective-permute-start.1 = (bf16[2048,512]{1,0:T(8,128)(2,1)}, bf16[2048,512]{1,0:T(8,128)(2,1)}, u32[]{:S(2)}, u32[]{:S(2)}) collective-permute-start(bf16[2048,512]{1,0:T(8,128)(2,1)} %bitcast.33), channel_id=1, source_target_pairs={{0,16},{16,0},{1,17},{17,1},{2,18},{18,2},{3,19},{19,3},{4,20},{20... | collective-permute-start | bytes 6291464 | tf_op jit(solution)/shard_map/ppermute | solution.py:447
  0.0 35.4 %collective-permute-start.2 = (bf16[2048,512]{1,0:T(8,128)(2,1)}, bf16[2048,512]{1,0:T(8,128)(2,1)}, u32[]{:S(2)}, u32[]{:S(2)}) collective-permute-start(bf16[2048,512]{1,0:T(8,128)(2,1)} %bitcast.37), channel_id=1, source_target_pairs={{0,16},{16,0},{1,17},{17,1},{2,18},{18,2},{3,19},{19,3},{4,20},{20... | collective-permute-start | bytes 6291464 | tf_op jit(solution)/shard_map/ppermute | solution.py:447
  0.5 34.9 %collective-permute-start.3 = (bf16[512,2048]{1,0:T(8,128)(2,1)}, bf16[512,2048]{1,0:T(8,128)(2,1)}, u32[]{:S(2)}, u32[]{:S(2)}) collective-permute-start(bf16[512,2048]{1,0:T(8,128)(2,1)} %bitcast.41), channel_id=1, source_target_pairs={{0,16},{16,0},{1,17},{17,1},{2,18},{18,2},{3,19},{19,3},{4,20},{20... | collective-permute-start | bytes 6291464 | tf_op jit(solution)/shard_map/ppermute | solution.py:447
  3.0 4.7 %copy-start.6 = (s32[1,128,2]{1,2,0:T(2,128)S(1)}, s32[1,128,2]{1,2,0:T(2,128)}, u32[]{:S(2)}) copy-start(s32[1,128,2]{1,2,0:T(2,128)} %param.10) | copy-start | bytes 3076
  3.0 4.7 %copy-start.7 = (f32[1,128,2]{1,2,0:T(2,128)S(1)}, f32[1,128,2]{1,2,0:T(2,128)}, u32[]{:S(2)}) copy-start(f32[1,128,2]{1,2,0:T(2,128)} %param.11) | copy-start | bytes 3076
  3.0 26.2 %all-to-all-start = ((bf16[8,3,128,256]{3,2,1,0:T(8,128)(2,1)}), bf16[8,3,128,256]{3,2,1,0:T(8,128)(2,1)S(1)}, u32[]{:S(2)}, u32[]{:S(2)}) async-start(bf16[8,3,128,256]{3,2,1,0:T(8,128)(2,1)} %spread.1), calls=%async_computation | async-start | bytes 3145728 | tf_op jit(solution)/shard_map/all_to_all | solution.py:463
  7.9 40.3 %copy-start.2 = (f32[8,128]{1,0:T(8,128)}, f32[8,128]{1,0:T(8,128)S(1)}, u32[]{:S(2)}) copy-start(f32[8,128]{1,0:T(8,128)S(1)} %plan.1.info_ref) | copy-start | bytes 12292
  7.9 40.3 %copy-start.1 = (bf16[1,128,2048]{2,1,0:T(8,128)(2,1)S(1)}, bf16[1,128,2048]{2,1,0:T(8,128)(2,1)}, u32[]{:S(2)}) copy-start(bf16[1,128,2048]{2,1,0:T(8,128)(2,1)} %param.8) | copy-start | bytes 1572868
  7.9 27.5 %collective-permute-start = (f32[8,128]{1,0:T(8,128)S(1)}, f32[8,128]{1,0:T(8,128)S(1)}, u32[]{:S(2)}, u32[]{:S(2)}) collective-permute-start(f32[8,128]{1,0:T(8,128)S(1)} %plan.1.info_ref), channel_id=1, source_target_pairs={{0,64},{32,96},{64,0},{96,32},{1,65},{33,97},{65,1},{97,33},{2,66}... | collective-permute-start | bytes 12296 | tf_op jit(solution)/shard_map/ppermute | solution.py:450
  35.4 39.1 %copy-start.4 = (f32[8,128]{1,0:T(8,128)}, f32[8,128]{1,0:T(8,128)S(1)}, u32[]{:S(2)}) copy-start(f32[8,128]{1,0:T(8,128)S(1)} %collective-permute-done.info_ref) | copy-start | bytes 12292
  51.9 29.5 %all-to-all-start.2 = ((bf16[16,24,2048]{2,1,0:T(8,128)(2,1)}), bf16[16,24,2048]{2,1,0:T(8,128)(2,1)S(1)}, u32[]{:S(2)}, u32[]{:S(2)}) async-start(bf16[16,24,2048]{2,1,0:T(8,128)(2,1)} %bitcast.10), calls=%async_computation.2 | async-start | bytes 3145728 | tf_op jit(solution)/shard_map/all_to_all | solution.py:453
  60.2 14.2 %collective-permute-start.4 = (bf16[128,2048]{1,0:T(8,128)(2,1)S(1)}, bf16[128,2048]{1,0:T(8,128)(2,1)S(1)}, u32[]{:S(2)}, u32[]{:S(2)}) collective-permute-start(bf16[128,2048]{1,0:T(8,128)(2,1)S(1)} %get-tuple-element.49), channel_id=1, source_target_pairs={{0,64},{32,96},{64,0},{96,32},{1,65},{33,97},{65,1},{97,33},{2,66}... | collective-permute-start | bytes 1572872 | tf_op jit(solution)/shard_map/ppermute | solution.py:450
  82.3 12.1 %collective-permute-start.8 = (bf16[96,2048]{1,0:T(8,128)(2,1)S(1)}, bf16[96,2048]{1,0:T(8,128)(2,1)S(1)}, u32[]{:S(2)}, u32[]{:S(2)}) collective-permute-start(bf16[96,2048]{1,0:T(8,128)(2,1)S(1)} %slice.9), channel_id=1, source_target_pairs={{0,96},{32,0},{64,32},{96,64},{1,97},{33,1},{65,33},{97,65},{2,98}... | collective-permute-start | bytes 1179656 | tf_op jit(solution)/shard_map/ppermute | solution.py:450
  83.4 13.3 %collective-permute-start.7 = (bf16[96,2048]{1,0:T(8,128)(2,1)S(1)}, bf16[96,2048]{1,0:T(8,128)(2,1)S(1)}, u32[]{:S(2)}, u32[]{:S(2)}) collective-permute-start(bf16[96,2048]{1,0:T(8,128)(2,1)S(1)} %slice.9), channel_id=1, source_target_pairs={{0,32},{32,64},{64,96},{96,0},{1,33},{33,65},{65,97},{97,1},{2,34}... | collective-permute-start | bytes 1179656 | tf_op jit(solution)/shard_map/ppermute | solution.py:450
  84.3 28.0 %collective-permute-start.6 = (bf16[144,2048]{1,0:T(8,128)(2,1)}, bf16[144,2048]{1,0:T(8,128)(2,1)}, u32[]{:S(2)}, u32[]{:S(2)}) collective-permute-start(bf16[144,2048]{1,0:T(8,128)(2,1)} %slice.10), channel_id=1, source_target_pairs={{0,96},{32,0},{64,32},{96,64},{1,97},{33,1},{65,33},{97,65},{2,98}... | collective-permute-start | bytes 1769480 | tf_op jit(solution)/shard_map/ppermute | solution.py:450
  86.7 25.7 %collective-permute-start.5 = (bf16[144,2048]{1,0:T(8,128)(2,1)}, bf16[144,2048]{1,0:T(8,128)(2,1)}, u32[]{:S(2)}, u32[]{:S(2)}) collective-permute-start(bf16[144,2048]{1,0:T(8,128)(2,1)} %slice.10), channel_id=1, source_target_pairs={{0,32},{32,64},{64,96},{96,0},{1,33},{33,65},{65,97},{97,1},{2,34}... | collective-permute-start | bytes 1769480 | tf_op jit(solution)/shard_map/ppermute | solution.py:450
  87.5 27.0 %all-to-all-start.3 = ((bf16[16,24,2048]{2,1,0:T(8,128)(2,1)}), bf16[16,24,2048]{2,1,0:T(8,128)(2,1)}, u32[]{:S(2)}, u32[]{:S(2)}) async-start(bf16[16,24,2048]{2,1,0:T(8,128)(2,1)} %bitcast.12), calls=%async_computation.3 | async-start | bytes 3145728 | tf_op jit(solution)/shard_map/all_to_all | solution.py:453
  96.7 31.9 %collective-permute-start.10 = (bf16[144,2048]{1,0:T(8,128)(2,1)}, bf16[144,2048]{1,0:T(8,128)(2,1)}, u32[]{:S(2)}, u32[]{:S(2)}) collective-permute-start(bf16[144,2048]{1,0:T(8,128)(2,1)} %slice.11), channel_id=1, source_target_pairs={{0,96},{32,0},{64,32},{96,64},{1,97},{33,1},{65,33},{97,65},{2,98}... | collective-permute-start | bytes 1769480 | tf_op jit(solution)/shard_map/ppermute | solution.py:450
  97.7 30.9 %collective-permute-start.9 = (bf16[144,2048]{1,0:T(8,128)(2,1)}, bf16[144,2048]{1,0:T(8,128)(2,1)}, u32[]{:S(2)}, u32[]{:S(2)}) collective-permute-start(bf16[144,2048]{1,0:T(8,128)(2,1)} %slice.11), channel_id=1, source_target_pairs={{0,32},{32,64},{64,96},{96,0},{1,33},{33,65},{65,97},{97,1},{2,34}... | collective-permute-start | bytes 1769480 | tf_op jit(solution)/shard_map/ppermute | solution.py:450
  110.0 18.6 %collective-permute-start.11 = (bf16[96,2048]{1,0:T(8,128)(2,1)}, bf16[96,2048]{1,0:T(8,128)(2,1)}, u32[]{:S(2)}, u32[]{:S(2)}) collective-permute-start(bf16[96,2048]{1,0:T(8,128)(2,1)} %get-tuple-element.70), channel_id=1, source_target_pairs={{0,96},{32,0},{64,32},{96,64},{1,97},{33,1},{65,33},{97,65},{2,98}... | collective-permute-start | bytes 1179656 | tf_op jit(solution)/shard_map/ppermute | solution.py:450
  112.3 16.3 %collective-permute-start.12 = (bf16[96,2048]{1,0:T(8,128)(2,1)}, bf16[96,2048]{1,0:T(8,128)(2,1)}, u32[]{:S(2)}, u32[]{:S(2)}) collective-permute-start(bf16[96,2048]{1,0:T(8,128)(2,1)} %get-tuple-element.71), channel_id=1, source_target_pairs={{0,32},{32,64},{64,96},{96,0},{1,33},{33,65},{65,97},{97,1},{2,34}... | collective-permute-start | bytes 1179656 | tf_op jit(solution)/shard_map/ppermute | solution.py:450
  128.7 21.6 %collective-permute-start.15 = (bf16[144,2048]{1,0:T(8,128)(2,1)}, bf16[144,2048]{1,0:T(8,128)(2,1)}, u32[]{:S(2)}, u32[]{:S(2)}) collective-permute-start(bf16[144,2048]{1,0:T(8,128)(2,1)} %get-tuple-element.78), channel_id=1, source_target_pairs={{0,96},{32,0},{64,32},{96,64},{1,97},{33,1},{65,33},{97,65},{2,98}... | collective-permute-start | bytes 1769480 | tf_op jit(solution)/shard_map/ppermute | solution.py:450
  132.0 18.3 %collective-permute-start.16 = (bf16[144,2048]{1,0:T(8,128)(2,1)}, bf16[144,2048]{1,0:T(8,128)(2,1)}, u32[]{:S(2)}, u32[]{:S(2)}) collective-permute-start(bf16[144,2048]{1,0:T(8,128)(2,1)} %get-tuple-element.79), channel_id=1, source_target_pairs={{0,32},{32,64},{64,96},{96,0},{1,33},{33,65},{65,97},{97,1},{2,34}... | collective-permute-start | bytes 1769480 | tf_op jit(solution)/shard_map/ppermute | solution.py:450
  132.0 32.0 %all-to-all-start.4 = ((bf16[16,24,2048]{2,1,0:T(8,128)(2,1)}), bf16[16,24,2048]{2,1,0:T(8,128)(2,1)}, u32[]{:S(2)}, u32[]{:S(2)}) async-start(bf16[16,24,2048]{2,1,0:T(8,128)(2,1)} %bitcast.31), calls=%async_computation.4 | async-start | bytes 3145728 | tf_op jit(solution)/shard_map/all_to_all | solution.py:453
  137.9 12.4 %copy-start = (bf16[384,2048]{1,0:T(8,128)(2,1)S(1)}, bf16[384,2048]{1,0:T(8,128)(2,1)}, u32[]{:S(2)}) copy-start(bf16[384,2048]{1,0:T(8,128)(2,1)} %get-tuple-element.64.own_ref) | copy-start | bytes 4718596
  146.7 12.9 %collective-permute-start.13 = (bf16[144,2048]{1,0:T(8,128)(2,1)}, bf16[144,2048]{1,0:T(8,128)(2,1)S(1)}, u32[]{:S(2)}, u32[]{:S(2)}) collective-permute-start(bf16[144,2048]{1,0:T(8,128)(2,1)} %get-tuple-element.74), channel_id=1, source_target_pairs={{0,96},{32,0},{64,32},{96,64},{1,97},{33,1},{65,33},{97,65},{2,98}... | collective-permute-start | bytes 1769480 | tf_op jit(solution)/shard_map/ppermute | solution.py:450
  150.3 12.7 %collective-permute-start.14 = (bf16[144,2048]{1,0:T(8,128)(2,1)}, bf16[144,2048]{1,0:T(8,128)(2,1)S(1)}, u32[]{:S(2)}, u32[]{:S(2)}) collective-permute-start(bf16[144,2048]{1,0:T(8,128)(2,1)} %get-tuple-element.75), channel_id=1, source_target_pairs={{0,32},{32,64},{64,96},{96,0},{1,33},{33,65},{65,97},{97,1},{2,34}... | collective-permute-start | bytes 1769480 | tf_op jit(solution)/shard_map/ppermute | solution.py:450
  164.0 7.3 %copy-start.5 = (f32[8,128]{1,0:T(8,128)S(1)}, f32[8,128]{1,0:T(8,128)}, u32[]{:S(2)}) copy-start(f32[8,128]{1,0:T(8,128)} %copy-done.4) | copy-start | bytes 12292
  164.0 24.8 %all-to-all-start.5 = ((bf16[16,24,2048]{2,1,0:T(8,128)(2,1)}), bf16[16,24,2048]{2,1,0:T(8,128)(2,1)S(1)}, u32[]{:S(2)}, u32[]{:S(2)}) async-start(bf16[16,24,2048]{2,1,0:T(8,128)(2,1)} %bitcast.29), calls=%async_computation.5 | async-start | bytes 3145728 | tf_op jit(solution)/shard_map/all_to_all | solution.py:453
  171.3 17.6 %copy-start.3 = (f32[8,128]{1,0:T(8,128)S(1)}, f32[8,128]{1,0:T(8,128)}, u32[]{:S(2)}) copy-start(f32[8,128]{1,0:T(8,128)} %copy-done.2) | copy-start | bytes 12292
  174.0 10.8 %collective-permute-start.17 = (bf16[128,2048]{1,0:T(8,128)(2,1)S(1)}, bf16[128,2048]{1,0:T(8,128)(2,1)S(1)}, u32[]{:S(2)}, u32[]{:S(2)}) collective-permute-start(bf16[128,2048]{1,0:T(8,128)(2,1)S(1)} %get-tuple-element.83), channel_id=1, source_target_pairs={{0,64},{32,96},{64,0},{96,32},{1,65},{33,97},{65,1},{97,33},{2,66}... | collective-permute-start | bytes 1572872 | tf_op jit(solution)/shard_map/ppermute | solution.py:450

commit v10 on v8

--- a/solution.py
+++ b/solution.py
@@ -471,7 +471,7 @@
     far_buffer = route(far_tokens, info_far, slots)
     own, far_buffer = tie((exchange(buffer), far_buffer))
     eighth = own.shape[0] // 8
-    first, second = own[: 3 * eighth], own[3 * eighth : 6 * eighth]
+    first, second = own[: 2 * eighth], own[2 * eighth : 6 * eighth]
     rest, first, second = tie((own, first, second))
     third = rest[6 * eighth :]
     third, far_buffer = tie((third, far_buffer))

time: 190 us -> 190 us (level)
    ppermute x15, waiting for transfers between devices: 37.4 us -> 34.6 us  [shift(): return lax.ppermute(x, 'y', [(i, (i + by) % n_y) for i in range(n_y)])]
    all_to_all x4, waiting for transfers between devices: 7.73 us -> 10.2 us  [exchange(): return lax.all_to_all(x, exp, split_axis=0, concat_axis=0, tiled=True)]
  transfers between devices with their start and end apart: 23 -> 23, of which waited for: 9 -> 10; matrix products, arithmetic and copies ran while one was open for 0% -> 0% of each run, Pallas kernels for 27% -> 27%
where the time goes in v10:
time: 190 us; the launch traced here: 187 us
  waiting for transfers between devices  62.5 us (33%)
  Pallas kernels  56.9 us (30%)
  starting transfers between devices  53.1 us (28%)
  blocking collectives  12.8 us (7%)
  local copies, waits for them, and re-layouts  1.91 us (1%)
    ppermute x15, waiting for transfers between devices, shift(): return lax.ppermute(x, 'y', [(i, (i + by) % n_y) for i in range(n_y)])  34.6 us
    pallas_call x3, Pallas kernels, experts(): pl.pallas_call(functools.partial(expert_kernel, n_in=len(arrays), block=b...  34.6 us
    all_to_all x4, starting transfers between devices, exchange(): return lax.all_to_all(x, exp, split_axis=0, concat_axis=0, tiled=True)  28.4 us
    ppermute x15, starting transfers between devices, shift(): return lax.ppermute(x, 'y', [(i, (i + by) % n_y) for i in range(n_y)])  19.6 us
    all_to_all x1, waiting for transfers between devices, per_device(): arrived = lax.all_to_all(qkv, seq, split_axis=0, concat_axis=0, tiled=True)  17.7 us
    all_to_all x1, blocking collectives, per_device(): lax.all_to_all(context, seq, split_axis=0, concat_axis=0, tiled=True)  12.8 us
    all_to_all x4, waiting for transfers between devices, exchange(): return lax.all_to_all(x, exp, split_axis=0, concat_axis=0, tiled=True)  10.2 us
    pallas_call x1, Pallas kernels, attention(): pl.pallas_call(functools.partial(attention_kernel, block=2 * rows), grid=...  6.15 us
  transfers between devices with their start and end apart: 23, of which 10 were waited for; matrix products, arithmetic and copies ran while one was open for 0% of the time, Pallas kernels for 27%

profile of v10, /device:TPU:2, one launch (start us, length us, event | category | flops | bytes accessed | tf_op | source)
XLA Modules:
  0.0 187.5 jit_solution(791441165301667669)
XLA Ops:
  0.0 0.0 collective-permute-start.1
  0.0 0.5 collective-permute-start.2
  0.5 0.0 collective-permute-start.3
  0.5 2.4 %spread.1 = bf16[8,3,128,256]{3,2,1,0:T(8,128)(2,1)} custom-call(bf16[3,128,2048]{2,1,0:T(8,128)(2,1)} %bitcast.30), custom_call_target="tpu_custom_call" | custom-call | tf_op jit(solution)/shard_map/spread/pallas_call | solution.py:385
  3.0 0.0 copy-start.6
  3.0 0.0 copy-start.7
  3.0 4.6 %all-to-all-start = ((bf16[8,3,128,256]{3,2,1,0:T(8,128)(2,1)}), bf16[8,3,128,256]{3,2,1,0:T(8,128)(2,1)S(1)}, u32[]{:S(2)}, u32[]{:S(2)}) async-start(bf16[8,3,128,256]{3,2,1,0:T(8,128)(2,1)} %spread.1), calls=%async_computation | async-start | bytes 3145728 | tf_op jit(solution)/shard_map/all_to_all | solution.py:463
  7.6 0.1 pad.2.clone
  7.7 0.1 maximum_maximum_fusion.info_ref
  7.7 0.1 plan.1.info_ref
  7.9 3.6 %collective-permute-start = (f32[8,128]{1,0:T(8,128)S(1)}, f32[8,128]{1,0:T(8,128)S(1)}, u32[]{:S(2)}, u32[]{:S(2)}) collective-permute-start(f32[8,128]{1,0:T(8,128)S(1)} %plan.1.info_ref), channel_id=1, source_target_pairs={{0,64},{32,96},{64,0},{96,32},{1,65},{33,97},{65,1},{97,33},{2,66}... | collective-permute-start | bytes 12296 | tf_op jit(solution)/shard_map/ppermute | solution.py:450
  11.5 17.7 %all-to-all-done.x_ref = bf16[8,3,128,256]{3,2,1,0:T(8,128)(2,1)S(1)} async-done(((bf16[8,3,128,256]{3,2,1,0:T(8,128)(2,1)}), bf16[8,3,128,256]{3,2,1,0:T(8,128)(2,1)S(1)}, u32[]{:S(2)}, u32[]{:S(2)}) %all-to-all-start) | async-done | bytes 1572896 | tf_op jit(solution)/shard_map/all_to_all | solution.py:463
  29.2 6.2 %attention.1 = (bf16[8,128,256]{2,1,0:T(8,128)(2,1)S(1)}, bf16[2048,2048]{1,0:T(8,128)(2,1)S(1)}) custom-call(bf16[8,3,128,256]{3,2,1,0:T(8,128)(2,1)S(1)} %all-to-all-done.x_ref, bf16[2048,2048]{1,0:T(8,128)(2,1)} %w_hbm.1), custom_call_target="tpu_custom_call" | custom-call | tf_op jit(solution)/shard_map/attention/pallas_call | solution.py:71
  35.4 0.0 collective-permute-done.info_ref
  35.4 0.0 collective-permute-done.1.refs_6_.refs_5_
  35.4 0.0 collective-permute-done.2.refs_7_.refs_6_
  35.4 0.0 collective-permute-done.3.refs_8_.refs_7_
  35.4 12.8 %all_to_all.56.ctx_ref = bf16[8,128,256]{2,1,0:T(8,128)(2,1)S(1)} all-to-all(bf16[8,128,256]{2,1,0:T(8,128)(2,1)S(1)} %get-tuple-element.46), channel_id=1, replica_groups=mesh['y'=4,'core'=2,'z'=4,'x'=4] {'y','core'}, dimensions={0} | all-to-all | bytes 1048576 | tf_op jit(solution)/shard_map/all_to_all | solution.py:466
  48.2 3.7 %project.1 = (f32[128,2048]{1,0:T(8,128)}, bf16[128,2048]{1,0:T(8,128)(2,1)S(1)}, bf16[384,2048]{1,0:T(8,128)(2,1)}) custom-call(bf16[8,128,256]{2,1,0:T(8,128)(2,1)S(1)} %all_to_all.56.ctx_ref, bf16[2048,2048]{1,0:T(8,128)(2,1)S(1)} %get-tuple-element.47.w_ref, bf16[128,2048]{1,0:T(8,128)(2,1)S(1)} %bitcast.28, f32[8,128]{1,0:T(8,128)S(1)} %plan.1.info_ref), custom_call_target="tpu_custom_call" | custom-call | tf_op jit(solution)/shard_map/project/pallas_call | solution.py:149
  51.9 8.3 %all-to-all-start.2 = ((bf16[16,24,2048]{2,1,0:T(8,128)(2,1)}), bf16[16,24,2048]{2,1,0:T(8,128)(2,1)S(1)}, u32[]{:S(2)}, u32[]{:S(2)}) async-start(bf16[16,24,2048]{2,1,0:T(8,128)(2,1)} %bitcast.10), calls=%async_computation.2 | async-start | bytes 3145728 | tf_op jit(solution)/shard_map/all_to_all | solution.py:453
  60.2 0.4 collective-permute-start.4
  60.6 13.9 %collective-permute-done.4.normed_ref = bf16[128,2048]{1,0:T(8,128)(2,1)S(1)} collective-permute-done((bf16[128,2048]{1,0:T(8,128)(2,1)S(1)}, bf16[128,2048]{1,0:T(8,128)(2,1)S(1)}, u32[]{:S(2)}, u32[]{:S(2)}) %collective-permute-start.4) | collective-permute-done | bytes 524320 | tf_op jit(solution)/shard_map/ppermute | solution.py:450
  74.5 1.7 route.1
  76.2 5.2 %all-to-all-done.2 = bf16[16,24,2048]{2,1,0:T(8,128)(2,1)S(1)} async-done(((bf16[16,24,2048]{2,1,0:T(8,128)(2,1)}), bf16[16,24,2048]{2,1,0:T(8,128)(2,1)S(1)}, u32[]{:S(2)}, u32[]{:S(2)}) %all-to-all-start.2) | async-done | bytes 1572896 | tf_op jit(solution)/shard_map/all_to_all | solution.py:453
  81.4 1.0 slice.10
  82.4 1.2 collective-permute-start.8
  83.6 0.9 collective-permute-start.7
  84.4 2.4 %collective-permute-start.6 = (bf16[192,2048]{1,0:T(8,128)(2,1)}, bf16[192,2048]{1,0:T(8,128)(2,1)}, u32[]{:S(2)}, u32[]{:S(2)}) collective-permute-start(bf16[192,2048]{1,0:T(8,128)(2,1)} %slice.10), channel_id=1, source_target_pairs={{0,96},{32,0},{64,32},{96,64},{1,97},{33,1},{65,33},{97,65},{2,98}... | collective-permute-start | bytes 2359304 | tf_op jit(solution)/shard_map/ppermute | solution.py:450
  86.8 0.0 collective-permute-start.5
  86.8 0.8 slice.11
  87.6 6.9 %all-to-all-start.3 = ((bf16[16,24,2048]{2,1,0:T(8,128)(2,1)}), bf16[16,24,2048]{2,1,0:T(8,128)(2,1)}, u32[]{:S(2)}, u32[]{:S(2)}) async-start(bf16[16,24,2048]{2,1,0:T(8,128)(2,1)} %bitcast.12), calls=%async_computation.3 | async-start | bytes 3145728 | tf_op jit(solution)/shard_map/all_to_all | solution.py:453
  94.5 0.0 collective-permute-done.8.refs_2_
  94.5 2.4 %collective-permute-done.7.refs_1_ = bf16[96,2048]{1,0:T(8,128)(2,1)S(1)} collective-permute-done((bf16[96,2048]{1,0:T(8,128)(2,1)S(1)}, bf16[96,2048]{1,0:T(8,128)(2,1)S(1)}, u32[]{:S(2)}, u32[]{:S(2)}) %collective-permute-start.7) | collective-permute-done | bytes 393248 | tf_op jit(solution)/shard_map/ppermute | solution.py:450
  96.8 0.9 collective-permute-start.10
  97.8 1.1 collective-permute-start.9
  98.9 11.3 %experts.3 = (bf16[384,2048]{1,0:T(8,128)(2,1)}, bf16[96,2048]{1,0:T(8,128)(2,1)}, bf16[96,2048]{1,0:T(8,128)(2,1)}) custom-call(bf16[384,2048]{1,0:T(8,128)(2,1)S(1)} %bitcast.26, bf16[96,2048]{1,0:T(8,128)(2,1)S(1)} %collective-permute-done.7.refs_1_, bf16[96,2048]{1,0:T(8,128)(2,1)S(1)} %collective-permute-done.8.refs_2_, bf16[2048,512]{1,0:T(8,128)(2,1)} %bitcast.34, ...), custom_call_target="tpu_custom_call" | custom-call | flops 724775731200 | bytes 17301504 | tf_op jit(solution)/shard_map/experts/pallas_call | solution.py:253
  110.1 2.2 %collective-permute-start.11 = (bf16[96,2048]{1,0:T(8,128)(2,1)}, bf16[96,2048]{1,0:T(8,128)(2,1)}, u32[]{:S(2)}, u32[]{:S(2)}) collective-permute-start(bf16[96,2048]{1,0:T(8,128)(2,1)} %get-tuple-element.70), channel_id=1, source_target_pairs={{0,96},{32,0},{64,32},{96,64},{1,97},{33,1},{65,33},{97,65},{2,98}... | collective-permute-start | bytes 1179656 | tf_op jit(solution)/shard_map/ppermute | solution.py:450
  112.4 0.0 collective-permute-done.6.refs_2_
  112.4 0.0 collective-permute-start.12
  112.4 1.4 collective-permute-done.5.refs_1_
  113.8 0.8 all-to-all-done.3
  114.6 15.4 %experts.4 = (bf16[384,2048]{1,0:T(8,128)(2,1)}, bf16[192,2048]{1,0:T(8,128)(2,1)}, bf16[192,2048]{1,0:T(8,128)(2,1)}) custom-call(bf16[384,2048]{1,0:T(8,128)(2,1)} %bitcast.13.refs_0_, bf16[192,2048]{1,0:T(8,128)(2,1)} %collective-permute-done.5.refs_1_, bf16[192,2048]{1,0:T(8,128)(2,1)} %collective-permute-done.6.refs_2_, bf16[2048,512]{1,0:T(8,128)(2,1)} %bitcast.35, ...), custom_call_target="tpu_custom_call" | custom-call | flops 966367641600 | bytes 18874368 | tf_op jit(solution)/shard_map/experts/pallas_call | solution.py:253
  130.0 0.0 collective-permute-done.11.refs_0_
  130.0 0.0 collective-permute-done.12.refs_1_
  130.0 0.0 collective-permute-done.10.refs_1_
  130.0 3.3 %collective-permute-start.15 = (bf16[192,2048]{1,0:T(8,128)(2,1)}, bf16[192,2048]{1,0:T(8,128)(2,1)}, u32[]{:S(2)}, u32[]{:S(2)}) collective-permute-start(bf16[192,2048]{1,0:T(8,128)(2,1)} %get-tuple-element.78), channel_id=1, source_target_pairs={{0,96},{32,0},{64,32},{96,64},{1,97},{33,1},{65,33},{97,65},{2,98}... | collective-permute-start | bytes 2359304 | tf_op jit(solution)/shard_map/ppermute | solution.py:450
  133.3 0.0 collective-permute-start.16
  133.3 5.9 %all-to-all-start.4 = ((bf16[16,24,2048]{2,1,0:T(8,128)(2,1)}), bf16[16,24,2048]{2,1,0:T(8,128)(2,1)}, u32[]{:S(2)}, u32[]{:S(2)}) async-start(bf16[16,24,2048]{2,1,0:T(8,128)(2,1)} %bitcast.31), calls=%async_computation.4 | async-start | bytes 3145728 | tf_op jit(solution)/shard_map/all_to_all | solution.py:453
  139.3 7.9 %experts.5 = (bf16[96,2048]{1,0:T(8,128)(2,1)}, bf16[96,2048]{1,0:T(8,128)(2,1)}) custom-call(bf16[96,2048]{1,0:T(8,128)(2,1)} %collective-permute-done.9.refs_0_, bf16[96,2048]{1,0:T(8,128)(2,1)} %collective-permute-done.10.refs_1_, bf16[2048,512]{1,0:T(8,128)(2,1)} %bitcast.36, bf16[2048,512]{1,0:T(8,128)(2,1)} %bitcast.40, bf16[512,2048]{1,0:T(8,128)(2,1)} %bitcast.44, ...), custom_call_target="tpu_custom_call" | custom-call | flops 241591910400 | bytes 14155776 | tf_op jit(solution)/shard_map/experts/pallas_call | solution.py:253
  147.2 3.6 %collective-permute-start.13 = (bf16[96,2048]{1,0:T(8,128)(2,1)}, bf16[96,2048]{1,0:T(8,128)(2,1)S(1)}, u32[]{:S(2)}, u32[]{:S(2)}) collective-permute-start(bf16[96,2048]{1,0:T(8,128)(2,1)} %get-tuple-element.74), channel_id=1, source_target_pairs={{0,96},{32,0},{64,32},{96,64},{1,97},{33,1},{65,33},{97,65},{2,98}... | collective-permute-start | bytes 1179656 | tf_op jit(solution)/shard_map/ppermute | solution.py:450
  150.8 0.0 collective-permute-start.14
  150.8 0.0 collective-permute-done.15.refs_2_
  150.8 0.0 collective-permute-done.16.refs_3_
  150.8 3.0 %add_up.2.refs_2_ = bf16[384,2048]{1,0:T(8,128)(2,1)} custom-call(bf16[384,2048]{1,0:T(8,128)(2,1)S(1)} %copy-done, bf16[96,2048]{1,0:T(8,128)(2,1)} %collective-permute-done.11.refs_0_, bf16[96,2048]{1,0:T(8,128)(2,1)} %collective-permute-done.12.refs_1_, bf16[192,2048]{1,0:T(8,128)(2,1)} %collective-permute-done.15.refs_2_, ...), custom_call_target="tpu_custom_call" | custom-call | flops 1 | bytes 1 | tf_op jit(solution)/shard_map/add_up/pallas_call | solution.py:423
  153.8 2.6 %collective-permute-done.13.refs_0_ = bf16[96,2048]{1,0:T(8,128)(2,1)S(1)} collective-permute-done((bf16[96,2048]{1,0:T(8,128)(2,1)}, bf16[96,2048]{1,0:T(8,128)(2,1)S(1)}, u32[]{:S(2)}, u32[]{:S(2)}) %collective-permute-start.13) | collective-permute-done | bytes 393248 | tf_op jit(solution)/shard_map/ppermute | solution.py:450
  156.4 3.6 %collective-permute-done.14.refs_1_ = bf16[96,2048]{1,0:T(8,128)(2,1)S(1)} collective-permute-done((bf16[96,2048]{1,0:T(8,128)(2,1)}, bf16[96,2048]{1,0:T(8,128)(2,1)S(1)}, u32[]{:S(2)}, u32[]{:S(2)}) %collective-permute-start.14) | collective-permute-done | bytes 393248 | tf_op jit(solution)/shard_map/ppermute | solution.py:450
  160.0 0.9 add_up.3
  160.9 0.0 all-to-all-done.4
  160.9 7.3 %all-to-all-start.5 = ((bf16[16,24,2048]{2,1,0:T(8,128)(2,1)}), bf16[16,24,2048]{2,1,0:T(8,128)(2,1)S(1)}, u32[]{:S(2)}, u32[]{:S(2)}) async-start(bf16[16,24,2048]{2,1,0:T(8,128)(2,1)} %bitcast.29), calls=%async_computation.5 | async-start | bytes 3145728 | tf_op jit(solution)/shard_map/all_to_all | solution.py:453
  168.2 2.6 %combine_far.1 = (bf16[128,2048]{1,0:T(8,128)(2,1)S(1)}, f32[128,2048]{1,0:T(8,128)S(1)}) custom-call(f32[8,128]{1,0:T(8,128)S(1)} %copy-done.5, bf16[384,2048]{1,0:T(8,128)(2,1)} %bitcast.15.back_ref, f32[128,2048]{1,0:T(8,128)} %get-tuple-element.82.mid_hbm), custom_call_target="tpu_custom_call" | custom-call | tf_op jit(solution)/shard_map/combine_far/pallas_call | solution.py:328
  170.9 0.1 collective-permute-start.17
  171.0 10.7 %collective-permute-done.17.far_ref = bf16[128,2048]{1,0:T(8,128)(2,1)S(1)} collective-permute-done((bf16[128,2048]{1,0:T(8,128)(2,1)S(1)}, bf16[128,2048]{1,0:T(8,128)(2,1)S(1)}, u32[]{:S(2)}, u32[]{:S(2)}) %collective-permute-start.17) | collective-permute-done | bytes 524320 | tf_op jit(solution)/shard_map/ppermute | solution.py:450
  181.6 4.1 %all-to-all-done.5 = bf16[16,24,2048]{2,1,0:T(8,128)(2,1)S(1)} async-done(((bf16[16,24,2048]{2,1,0:T(8,128)(2,1)}), bf16[16,24,2048]{2,1,0:T(8,128)(2,1)S(1)}, u32[]{:S(2)}, u32[]{:S(2)}) %all-to-all-start.5) | async-done | bytes 1572896 | tf_op jit(solution)/shard_map/all_to_all | solution.py:453
  185.8 1.7 combine.1
  (19 shorter events, 0.1 us)
Async XLA Ops:
  0.0 35.4 %collective-permute-start.1 = (bf16[2048,512]{1,0:T(8,128)(2,1)}, bf16[2048,512]{1,0:T(8,128)(2,1)}, u32[]{:S(2)}, u32[]{:S(2)}) collective-permute-start(bf16[2048,512]{1,0:T(8,128)(2,1)} %bitcast.33), channel_id=1, source_target_pairs={{0,16},{16,0},{1,17},{17,1},{2,18},{18,2},{3,19},{19,3},{4,20},{20... | collective-permute-start | bytes 6291464 | tf_op jit(solution)/shard_map/ppermute | solution.py:447
  0.0 35.4 %collective-permute-start.2 = (bf16[2048,512]{1,0:T(8,128)(2,1)}, bf16[2048,512]{1,0:T(8,128)(2,1)}, u32[]{:S(2)}, u32[]{:S(2)}) collective-permute-start(bf16[2048,512]{1,0:T(8,128)(2,1)} %bitcast.37), channel_id=1, source_target_pairs={{0,16},{16,0},{1,17},{17,1},{2,18},{18,2},{3,19},{19,3},{4,20},{20... | collective-permute-start | bytes 6291464 | tf_op jit(solution)/shard_map/ppermute | solution.py:447
  0.5 34.9 %collective-permute-start.3 = (bf16[512,2048]{1,0:T(8,128)(2,1)}, bf16[512,2048]{1,0:T(8,128)(2,1)}, u32[]{:S(2)}, u32[]{:S(2)}) collective-permute-start(bf16[512,2048]{1,0:T(8,128)(2,1)} %bitcast.41), channel_id=1, source_target_pairs={{0,16},{16,0},{1,17},{17,1},{2,18},{18,2},{3,19},{19,3},{4,20},{20... | collective-permute-start | bytes 6291464 | tf_op jit(solution)/shard_map/ppermute | solution.py:447
  3.0 4.7 %copy-start.6 = (s32[1,128,2]{1,2,0:T(2,128)S(1)}, s32[1,128,2]{1,2,0:T(2,128)}, u32[]{:S(2)}) copy-start(s32[1,128,2]{1,2,0:T(2,128)} %param.10) | copy-start | bytes 3076
  3.0 4.7 %copy-start.7 = (f32[1,128,2]{1,2,0:T(2,128)S(1)}, f32[1,128,2]{1,2,0:T(2,128)}, u32[]{:S(2)}) copy-start(f32[1,128,2]{1,2,0:T(2,128)} %param.11) | copy-start | bytes 3076
  3.0 26.2 %all-to-all-start = ((bf16[8,3,128,256]{3,2,1,0:T(8,128)(2,1)}), bf16[8,3,128,256]{3,2,1,0:T(8,128)(2,1)S(1)}, u32[]{:S(2)}, u32[]{:S(2)}) async-start(bf16[8,3,128,256]{3,2,1,0:T(8,128)(2,1)} %spread.1), calls=%async_computation | async-start | bytes 3145728 | tf_op jit(solution)/shard_map/all_to_all | solution.py:463
  7.9 40.3 %copy-start.2 = (f32[8,128]{1,0:T(8,128)}, f32[8,128]{1,0:T(8,128)S(1)}, u32[]{:S(2)}) copy-start(f32[8,128]{1,0:T(8,128)S(1)} %plan.1.info_ref) | copy-start | bytes 12292
  7.9 40.3 %copy-start.1 = (bf16[1,128,2048]{2,1,0:T(8,128)(2,1)S(1)}, bf16[1,128,2048]{2,1,0:T(8,128)(2,1)}, u32[]{:S(2)}) copy-start(bf16[1,128,2048]{2,1,0:T(8,128)(2,1)} %param.8) | copy-start | bytes 1572868
  7.9 27.5 %collective-permute-start = (f32[8,128]{1,0:T(8,128)S(1)}, f32[8,128]{1,0:T(8,128)S(1)}, u32[]{:S(2)}, u32[]{:S(2)}) collective-permute-start(f32[8,128]{1,0:T(8,128)S(1)} %plan.1.info_ref), channel_id=1, source_target_pairs={{0,64},{32,96},{64,0},{96,32},{1,65},{33,97},{65,1},{97,33},{2,66}... | collective-permute-start | bytes 12296 | tf_op jit(solution)/shard_map/ppermute | solution.py:450
  35.4 39.1 %copy-start.4 = (f32[8,128]{1,0:T(8,128)}, f32[8,128]{1,0:T(8,128)S(1)}, u32[]{:S(2)}) copy-start(f32[8,128]{1,0:T(8,128)S(1)} %collective-permute-done.info_ref) | copy-start | bytes 12292
  51.9 29.5 %all-to-all-start.2 = ((bf16[16,24,2048]{2,1,0:T(8,128)(2,1)}), bf16[16,24,2048]{2,1,0:T(8,128)(2,1)S(1)}, u32[]{:S(2)}, u32[]{:S(2)}) async-start(bf16[16,24,2048]{2,1,0:T(8,128)(2,1)} %bitcast.10), calls=%async_computation.2 | async-start | bytes 3145728 | tf_op jit(solution)/shard_map/all_to_all | solution.py:453
  60.2 14.2 %collective-permute-start.4 = (bf16[128,2048]{1,0:T(8,128)(2,1)S(1)}, bf16[128,2048]{1,0:T(8,128)(2,1)S(1)}, u32[]{:S(2)}, u32[]{:S(2)}) collective-permute-start(bf16[128,2048]{1,0:T(8,128)(2,1)S(1)} %get-tuple-element.49), channel_id=1, source_target_pairs={{0,64},{32,96},{64,0},{96,32},{1,65},{33,97},{65,1},{97,33},{2,66}... | collective-permute-start | bytes 1572872 | tf_op jit(solution)/shard_map/ppermute | solution.py:450
  82.4 12.1 %collective-permute-start.8 = (bf16[96,2048]{1,0:T(8,128)(2,1)S(1)}, bf16[96,2048]{1,0:T(8,128)(2,1)S(1)}, u32[]{:S(2)}, u32[]{:S(2)}) collective-permute-start(bf16[96,2048]{1,0:T(8,128)(2,1)S(1)} %slice.9), channel_id=1, source_target_pairs={{0,96},{32,0},{64,32},{96,64},{1,97},{33,1},{65,33},{97,65},{2,98}... | collective-permute-start | bytes 1179656 | tf_op jit(solution)/shard_map/ppermute | solution.py:450
  83.6 13.3 %collective-permute-start.7 = (bf16[96,2048]{1,0:T(8,128)(2,1)S(1)}, bf16[96,2048]{1,0:T(8,128)(2,1)S(1)}, u32[]{:S(2)}, u32[]{:S(2)}) collective-permute-start(bf16[96,2048]{1,0:T(8,128)(2,1)S(1)} %slice.9), channel_id=1, source_target_pairs={{0,32},{32,64},{64,96},{96,0},{1,33},{33,65},{65,97},{97,1},{2,34}... | collective-permute-start | bytes 1179656 | tf_op jit(solution)/shard_map/ppermute | solution.py:450
  84.4 27.9 %collective-permute-start.6 = (bf16[192,2048]{1,0:T(8,128)(2,1)}, bf16[192,2048]{1,0:T(8,128)(2,1)}, u32[]{:S(2)}, u32[]{:S(2)}) collective-permute-start(bf16[192,2048]{1,0:T(8,128)(2,1)} %slice.10), channel_id=1, source_target_pairs={{0,96},{32,0},{64,32},{96,64},{1,97},{33,1},{65,33},{97,65},{2,98}... | collective-permute-start | bytes 2359304 | tf_op jit(solution)/shard_map/ppermute | solution.py:450
  86.8 27.0 %collective-permute-start.5 = (bf16[192,2048]{1,0:T(8,128)(2,1)}, bf16[192,2048]{1,0:T(8,128)(2,1)}, u32[]{:S(2)}, u32[]{:S(2)}) collective-permute-start(bf16[192,2048]{1,0:T(8,128)(2,1)} %slice.10), channel_id=1, source_target_pairs={{0,32},{32,64},{64,96},{96,0},{1,33},{33,65},{65,97},{97,1},{2,34}... | collective-permute-start | bytes 2359304 | tf_op jit(solution)/shard_map/ppermute | solution.py:450
  87.6 27.0 %all-to-all-start.3 = ((bf16[16,24,2048]{2,1,0:T(8,128)(2,1)}), bf16[16,24,2048]{2,1,0:T(8,128)(2,1)}, u32[]{:S(2)}, u32[]{:S(2)}) async-start(bf16[16,24,2048]{2,1,0:T(8,128)(2,1)} %bitcast.12), calls=%async_computation.3 | async-start | bytes 3145728 | tf_op jit(solution)/shard_map/all_to_all | solution.py:453
  96.8 33.2 %collective-permute-start.10 = (bf16[96,2048]{1,0:T(8,128)(2,1)}, bf16[96,2048]{1,0:T(8,128)(2,1)}, u32[]{:S(2)}, u32[]{:S(2)}) collective-permute-start(bf16[96,2048]{1,0:T(8,128)(2,1)} %slice.11), channel_id=1, source_target_pairs={{0,96},{32,0},{64,32},{96,64},{1,97},{33,1},{65,33},{97,65},{2,98}... | collective-permute-start | bytes 1179656 | tf_op jit(solution)/shard_map/ppermute | solution.py:450
  97.8 32.3 %collective-permute-start.9 = (bf16[96,2048]{1,0:T(8,128)(2,1)}, bf16[96,2048]{1,0:T(8,128)(2,1)}, u32[]{:S(2)}, u32[]{:S(2)}) collective-permute-start(bf16[96,2048]{1,0:T(8,128)(2,1)} %slice.11), channel_id=1, source_target_pairs={{0,32},{32,64},{64,96},{96,0},{1,33},{33,65},{65,97},{97,1},{2,34}... | collective-permute-start | bytes 1179656 | tf_op jit(solution)/shard_map/ppermute | solution.py:450
  110.1 19.9 %collective-permute-start.11 = (bf16[96,2048]{1,0:T(8,128)(2,1)}, bf16[96,2048]{1,0:T(8,128)(2,1)}, u32[]{:S(2)}, u32[]{:S(2)}) collective-permute-start(bf16[96,2048]{1,0:T(8,128)(2,1)} %get-tuple-element.70), channel_id=1, source_target_pairs={{0,96},{32,0},{64,32},{96,64},{1,97},{33,1},{65,33},{97,65},{2,98}... | collective-permute-start | bytes 1179656 | tf_op jit(solution)/shard_map/ppermute | solution.py:450
  112.4 17.6 %collective-permute-start.12 = (bf16[96,2048]{1,0:T(8,128)(2,1)}, bf16[96,2048]{1,0:T(8,128)(2,1)}, u32[]{:S(2)}, u32[]{:S(2)}) collective-permute-start(bf16[96,2048]{1,0:T(8,128)(2,1)} %get-tuple-element.71), channel_id=1, source_target_pairs={{0,32},{32,64},{64,96},{96,0},{1,33},{33,65},{65,97},{97,1},{2,34}... | collective-permute-start | bytes 1179656 | tf_op jit(solution)/shard_map/ppermute | solution.py:450
  130.0 20.7 %collective-permute-start.15 = (bf16[192,2048]{1,0:T(8,128)(2,1)}, bf16[192,2048]{1,0:T(8,128)(2,1)}, u32[]{:S(2)}, u32[]{:S(2)}) collective-permute-start(bf16[192,2048]{1,0:T(8,128)(2,1)} %get-tuple-element.78), channel_id=1, source_target_pairs={{0,96},{32,0},{64,32},{96,64},{1,97},{33,1},{65,33},{97,65},{2,98}... | collective-permute-start | bytes 2359304 | tf_op jit(solution)/shard_map/ppermute | solution.py:450
  133.3 17.4 %collective-permute-start.16 = (bf16[192,2048]{1,0:T(8,128)(2,1)}, bf16[192,2048]{1,0:T(8,128)(2,1)}, u32[]{:S(2)}, u32[]{:S(2)}) collective-permute-start(bf16[192,2048]{1,0:T(8,128)(2,1)} %get-tuple-element.79), channel_id=1, source_target_pairs={{0,32},{32,64},{64,96},{96,0},{1,33},{33,65},{65,97},{97,1},{2,34}... | collective-permute-start | bytes 2359304 | tf_op jit(solution)/shard_map/ppermute | solution.py:450
  133.3 27.5 %all-to-all-start.4 = ((bf16[16,24,2048]{2,1,0:T(8,128)(2,1)}), bf16[16,24,2048]{2,1,0:T(8,128)(2,1)}, u32[]{:S(2)}, u32[]{:S(2)}) async-start(bf16[16,24,2048]{2,1,0:T(8,128)(2,1)} %bitcast.31), calls=%async_computation.4 | async-start | bytes 3145728 | tf_op jit(solution)/shard_map/all_to_all | solution.py:453
  139.3 11.5 %copy-start = (bf16[384,2048]{1,0:T(8,128)(2,1)S(1)}, bf16[384,2048]{1,0:T(8,128)(2,1)}, u32[]{:S(2)}) copy-start(bf16[384,2048]{1,0:T(8,128)(2,1)} %get-tuple-element.64.own_ref) | copy-start | bytes 4718596
  147.2 9.2 %collective-permute-start.13 = (bf16[96,2048]{1,0:T(8,128)(2,1)}, bf16[96,2048]{1,0:T(8,128)(2,1)S(1)}, u32[]{:S(2)}, u32[]{:S(2)}) collective-permute-start(bf16[96,2048]{1,0:T(8,128)(2,1)} %get-tuple-element.74), channel_id=1, source_target_pairs={{0,96},{32,0},{64,32},{96,64},{1,97},{33,1},{65,33},{97,65},{2,98}... | collective-permute-start | bytes 1179656 | tf_op jit(solution)/shard_map/ppermute | solution.py:450
  150.8 9.2 %collective-permute-start.14 = (bf16[96,2048]{1,0:T(8,128)(2,1)}, bf16[96,2048]{1,0:T(8,128)(2,1)S(1)}, u32[]{:S(2)}, u32[]{:S(2)}) collective-permute-start(bf16[96,2048]{1,0:T(8,128)(2,1)} %get-tuple-element.75), channel_id=1, source_target_pairs={{0,32},{32,64},{64,96},{96,0},{1,33},{33,65},{65,97},{97,1},{2,34}... | collective-permute-start | bytes 1179656 | tf_op jit(solution)/shard_map/ppermute | solution.py:450
  160.9 7.3 %copy-start.5 = (f32[8,128]{1,0:T(8,128)S(1)}, f32[8,128]{1,0:T(8,128)}, u32[]{:S(2)}) copy-start(f32[8,128]{1,0:T(8,128)} %copy-done.4) | copy-start | bytes 12292
  160.9 24.9 %all-to-all-start.5 = ((bf16[16,24,2048]{2,1,0:T(8,128)(2,1)}), bf16[16,24,2048]{2,1,0:T(8,128)(2,1)S(1)}, u32[]{:S(2)}, u32[]{:S(2)}) async-start(bf16[16,24,2048]{2,1,0:T(8,128)(2,1)} %bitcast.29), calls=%async_computation.5 | async-start | bytes 3145728 | tf_op jit(solution)/shard_map/all_to_all | solution.py:453
  168.2 17.6 %copy-start.3 = (f32[8,128]{1,0:T(8,128)S(1)}, f32[8,128]{1,0:T(8,128)}, u32[]{:S(2)}) copy-start(f32[8,128]{1,0:T(8,128)} %copy-done.2) | copy-start | bytes 12292
  170.9 10.8 %collective-permute-start.17 = (bf16[128,2048]{1,0:T(8,128)(2,1)S(1)}, bf16[128,2048]{1,0:T(8,128)(2,1)S(1)}, u32[]{:S(2)}, u32[]{:S(2)}) collective-permute-start(bf16[128,2048]{1,0:T(8,128)(2,1)S(1)} %get-tuple-element.83), channel_id=1, source_target_pairs={{0,64},{32,96},{64,0},{96,32},{1,65},{33,97},{65,1},{97,33},{2,66}... | collective-permute-start | bytes 1572872 | tf_op jit(solution)/shard_map/ppermute | solution.py:450

commit v11 on v10

--- a/solution.py
+++ b/solution.py
@@ -45,20 +45,26 @@
     first = lane < HD
     scale = float(HD) ** (-0.5) * LOG2E
     per = block // rows
-    for i in range(length // block):
+    steps = [(i, head) for i in range(length // block) for head in range(2)]
+
+    def score(i, head):
         query = x_ref[i * per : (i + 1) * per, 0].reshape(block, lanes)
-        parts = []
-        for head in range(2):
-            mine = jnp.where(first if head == 0 else ~first, query, jnp.zeros_like(query))
-            scores = lax.dot_general(
-                mine, keys, (((1,), (1,)), ((), ())), preferred_element_type=F32
-            )
-            top = jnp.max(scores, axis=1, keepdims=True)
-            weights = jnp.exp2((scores - top) * scale).astype(BF16)
-            both = jnp.dot(weights, wide, preferred_element_type=F32)
-            parts.append(both[:, :lanes] / both[:, lanes:])
-        context = jnp.where(first, parts[0], parts[1]).astype(BF16)
-        out_ref[i * per : (i + 1) * per] = context.reshape(per, rows, lanes)
+        mine = jnp.where(first if head == 0 else ~first, query, jnp.zeros_like(query))
+        return lax.dot_general(mine, keys, (((1,), (1,)), ((), ())), preferred_element_type=F32)
+
+    following, parts = score(*steps[0]), []
+    for step, (i, head) in enumerate(steps):
+        scores = following
+        if step + 1 < len(steps):
+            following = score(*steps[step + 1])
+        top = jnp.max(scores, axis=1, keepdims=True)
+        weights = jnp.exp2((scores - top) * scale).astype(BF16)
+        both = jnp.dot(weights, wide, preferred_element_type=F32)
+        parts.append(both[:, :lanes] / both[:, lanes:])
+        if head == 1:
+            context = jnp.where(first, parts[0], parts[1]).astype(BF16)
+            out_ref[i * per : (i + 1) * per] = context.reshape(per, rows, lanes)
+            parts = []
 
     @pl.when(pl.program_id(0) == pl.num_programs(0) - 1)
     def _():

time: 190 us -> 190 us (level)
  no operation moved by 1% of the time
where the time goes in v11:
time: 190 us; the launch traced here: 187 us
  waiting for transfers between devices  62.5 us (33%)
  Pallas kernels  56.6 us (30%)
  starting transfers between devices  53.1 us (28%)
  blocking collectives  12.8 us (7%)
  local copies, waits for them, and re-layouts  1.91 us (1%)
    pallas_call x3, Pallas kernels, experts(): pl.pallas_call(functools.partial(expert_kernel, n_in=len(arrays), block=b...  34.6 us
    ppermute x15, waiting for transfers between devices, shift(): return lax.ppermute(x, 'y', [(i, (i + by) % n_y) for i in range(n_y)])  34.6 us
    all_to_all x4, starting transfers between devices, exchange(): return lax.all_to_all(x, exp, split_axis=0, concat_axis=0, tiled=True)  28.4 us
    ppermute x15, starting transfers between devices, shift(): return lax.ppermute(x, 'y', [(i, (i + by) % n_y) for i in range(n_y)])  19.6 us
    all_to_all x1, waiting for transfers between devices, per_device(): arrived = lax.all_to_all(qkv, seq, split_axis=0, concat_axis=0, tiled=True)  17.7 us
    all_to_all x1, blocking collectives, per_device(): lax.all_to_all(context, seq, split_axis=0, concat_axis=0, tiled=True)  12.8 us
    all_to_all x4, waiting for transfers between devices, exchange(): return lax.all_to_all(x, exp, split_axis=0, concat_axis=0, tiled=True)  10.2 us
    pallas_call x1, Pallas kernels, attention(): pl.pallas_call(functools.partial(attention_kernel, block=2 * rows), grid=...  5.88 us
  transfers between devices with their start and end apart: 23, of which 10 were waited for; matrix products, arithmetic and copies ran while one was open for 0% of the time, Pallas kernels for 27%

profile of v11, /device:TPU:2, one launch (start us, length us, event | category | flops | bytes accessed | tf_op | source)
XLA Modules:
  0.0 187.2 jit_solution(11771984542425438115)
XLA Ops:
  0.0 0.0 collective-permute-start.1
  0.0 0.5 collective-permute-start.2
  0.5 0.0 collective-permute-start.3
  0.5 2.4 %spread.1 = bf16[8,3,128,256]{3,2,1,0:T(8,128)(2,1)} custom-call(bf16[3,128,2048]{2,1,0:T(8,128)(2,1)} %bitcast.30), custom_call_target="tpu_custom_call" | custom-call | tf_op jit(solution)/shard_map/spread/pallas_call | solution.py:391
  3.0 0.0 copy-start.6
  3.0 0.0 copy-start.7
  3.0 4.6 %all-to-all-start = ((bf16[8,3,128,256]{3,2,1,0:T(8,128)(2,1)}), bf16[8,3,128,256]{3,2,1,0:T(8,128)(2,1)S(1)}, u32[]{:S(2)}, u32[]{:S(2)}) async-start(bf16[8,3,128,256]{3,2,1,0:T(8,128)(2,1)} %spread.1), calls=%async_computation | async-start | bytes 3145728 | tf_op jit(solution)/shard_map/all_to_all | solution.py:469
  7.6 0.1 pad.2.clone
  7.7 0.1 maximum_maximum_fusion.info_ref
  7.7 0.1 plan.1.info_ref
  7.9 3.6 %collective-permute-start = (f32[8,128]{1,0:T(8,128)S(1)}, f32[8,128]{1,0:T(8,128)S(1)}, u32[]{:S(2)}, u32[]{:S(2)}) collective-permute-start(f32[8,128]{1,0:T(8,128)S(1)} %plan.1.info_ref), channel_id=1, source_target_pairs={{0,64},{32,96},{64,0},{96,32},{1,65},{33,97},{65,1},{97,33},{2,66}... | collective-permute-start | bytes 12296 | tf_op jit(solution)/shard_map/ppermute | solution.py:456
  11.5 17.7 %all-to-all-done.x_ref = bf16[8,3,128,256]{3,2,1,0:T(8,128)(2,1)S(1)} async-done(((bf16[8,3,128,256]{3,2,1,0:T(8,128)(2,1)}), bf16[8,3,128,256]{3,2,1,0:T(8,128)(2,1)S(1)}, u32[]{:S(2)}, u32[]{:S(2)}) %all-to-all-start) | async-done | bytes 1572896 | tf_op jit(solution)/shard_map/all_to_all | solution.py:469
  29.2 5.9 %attention.1 = (bf16[8,128,256]{2,1,0:T(8,128)(2,1)S(1)}, bf16[2048,2048]{1,0:T(8,128)(2,1)S(1)}) custom-call(bf16[8,3,128,256]{3,2,1,0:T(8,128)(2,1)S(1)} %all-to-all-done.x_ref, bf16[2048,2048]{1,0:T(8,128)(2,1)} %w_hbm.1), custom_call_target="tpu_custom_call" | custom-call | tf_op jit(solution)/shard_map/attention/pallas_call | solution.py:77
  35.1 0.0 collective-permute-done.info_ref
  35.1 0.0 collective-permute-done.1.refs_6_.refs_5_
  35.1 0.0 collective-permute-done.2.refs_7_.refs_6_
  35.1 0.0 collective-permute-done.3.refs_8_.refs_7_
  35.1 12.8 %all_to_all.56.ctx_ref = bf16[8,128,256]{2,1,0:T(8,128)(2,1)S(1)} all-to-all(bf16[8,128,256]{2,1,0:T(8,128)(2,1)S(1)} %get-tuple-element.46), channel_id=1, replica_groups=mesh['y'=4,'core'=2,'z'=4,'x'=4] {'y','core'}, dimensions={0} | all-to-all | bytes 1048576 | tf_op jit(solution)/shard_map/all_to_all | solution.py:472
  48.0 3.7 %project.1 = (f32[128,2048]{1,0:T(8,128)}, bf16[128,2048]{1,0:T(8,128)(2,1)S(1)}, bf16[384,2048]{1,0:T(8,128)(2,1)}) custom-call(bf16[8,128,256]{2,1,0:T(8,128)(2,1)S(1)} %all_to_all.56.ctx_ref, bf16[2048,2048]{1,0:T(8,128)(2,1)S(1)} %get-tuple-element.47.w_ref, bf16[128,2048]{1,0:T(8,128)(2,1)S(1)} %bitcast.28, f32[8,128]{1,0:T(8,128)S(1)} %plan.1.info_ref), custom_call_target="tpu_custom_call" | custom-call | tf_op jit(solution)/shard_map/project/pallas_call | solution.py:155
  51.6 8.3 %all-to-all-start.2 = ((bf16[16,24,2048]{2,1,0:T(8,128)(2,1)}), bf16[16,24,2048]{2,1,0:T(8,128)(2,1)S(1)}, u32[]{:S(2)}, u32[]{:S(2)}) async-start(bf16[16,24,2048]{2,1,0:T(8,128)(2,1)} %bitcast.10), calls=%async_computation.2 | async-start | bytes 3145728 | tf_op jit(solution)/shard_map/all_to_all | solution.py:459
  60.0 0.3 collective-permute-start.4
  60.3 13.9 %collective-permute-done.4.normed_ref = bf16[128,2048]{1,0:T(8,128)(2,1)S(1)} collective-permute-done((bf16[128,2048]{1,0:T(8,128)(2,1)S(1)}, bf16[128,2048]{1,0:T(8,128)(2,1)S(1)}, u32[]{:S(2)}, u32[]{:S(2)}) %collective-permute-start.4) | collective-permute-done | bytes 524320 | tf_op jit(solution)/shard_map/ppermute | solution.py:456
  74.2 1.7 route.1
  75.9 5.2 %all-to-all-done.2 = bf16[16,24,2048]{2,1,0:T(8,128)(2,1)S(1)} async-done(((bf16[16,24,2048]{2,1,0:T(8,128)(2,1)}), bf16[16,24,2048]{2,1,0:T(8,128)(2,1)S(1)}, u32[]{:S(2)}, u32[]{:S(2)}) %all-to-all-start.2) | async-done | bytes 1572896 | tf_op jit(solution)/shard_map/all_to_all | solution.py:459
  81.1 1.0 slice.10
  82.1 1.2 collective-permute-start.8
  83.3 0.9 collective-permute-start.7
  84.2 2.4 %collective-permute-start.6 = (bf16[192,2048]{1,0:T(8,128)(2,1)}, bf16[192,2048]{1,0:T(8,128)(2,1)}, u32[]{:S(2)}, u32[]{:S(2)}) collective-permute-start(bf16[192,2048]{1,0:T(8,128)(2,1)} %slice.10), channel_id=1, source_target_pairs={{0,96},{32,0},{64,32},{96,64},{1,97},{33,1},{65,33},{97,65},{2,98}... | collective-permute-start | bytes 2359304 | tf_op jit(solution)/shard_map/ppermute | solution.py:456
  86.5 0.0 collective-permute-start.5
  86.5 0.8 slice.11
  87.3 6.9 %all-to-all-start.3 = ((bf16[16,24,2048]{2,1,0:T(8,128)(2,1)}), bf16[16,24,2048]{2,1,0:T(8,128)(2,1)}, u32[]{:S(2)}, u32[]{:S(2)}) async-start(bf16[16,24,2048]{2,1,0:T(8,128)(2,1)} %bitcast.12), calls=%async_computation.3 | async-start | bytes 3145728 | tf_op jit(solution)/shard_map/all_to_all | solution.py:459
  94.2 0.0 collective-permute-done.8.refs_2_
  94.2 2.4 %collective-permute-done.7.refs_1_ = bf16[96,2048]{1,0:T(8,128)(2,1)S(1)} collective-permute-done((bf16[96,2048]{1,0:T(8,128)(2,1)S(1)}, bf16[96,2048]{1,0:T(8,128)(2,1)S(1)}, u32[]{:S(2)}, u32[]{:S(2)}) %collective-permute-start.7) | collective-permute-done | bytes 393248 | tf_op jit(solution)/shard_map/ppermute | solution.py:456
  96.6 1.0 collective-permute-start.10
  97.5 1.1 collective-permute-start.9
  98.6 11.3 %experts.3 = (bf16[384,2048]{1,0:T(8,128)(2,1)}, bf16[96,2048]{1,0:T(8,128)(2,1)}, bf16[96,2048]{1,0:T(8,128)(2,1)}) custom-call(bf16[384,2048]{1,0:T(8,128)(2,1)S(1)} %bitcast.26, bf16[96,2048]{1,0:T(8,128)(2,1)S(1)} %collective-permute-done.7.refs_1_, bf16[96,2048]{1,0:T(8,128)(2,1)S(1)} %collective-permute-done.8.refs_2_, bf16[2048,512]{1,0:T(8,128)(2,1)} %bitcast.34, ...), custom_call_target="tpu_custom_call" | custom-call | flops 724775731200 | bytes 17301504 | tf_op jit(solution)/shard_map/experts/pallas_call | solution.py:259
  109.9 2.2 %collective-permute-start.11 = (bf16[96,2048]{1,0:T(8,128)(2,1)}, bf16[96,2048]{1,0:T(8,128)(2,1)}, u32[]{:S(2)}, u32[]{:S(2)}) collective-permute-start(bf16[96,2048]{1,0:T(8,128)(2,1)} %get-tuple-element.70), channel_id=1, source_target_pairs={{0,96},{32,0},{64,32},{96,64},{1,97},{33,1},{65,33},{97,65},{2,98}... | collective-permute-start | bytes 1179656 | tf_op jit(solution)/shard_map/ppermute | solution.py:456
  112.1 0.0 collective-permute-done.6.refs_2_
  112.1 0.0 collective-permute-start.12
  112.1 1.4 collective-permute-done.5.refs_1_
  113.5 0.8 all-to-all-done.3
  114.4 15.4 %experts.4 = (bf16[384,2048]{1,0:T(8,128)(2,1)}, bf16[192,2048]{1,0:T(8,128)(2,1)}, bf16[192,2048]{1,0:T(8,128)(2,1)}) custom-call(bf16[384,2048]{1,0:T(8,128)(2,1)} %bitcast.13.refs_0_, bf16[192,2048]{1,0:T(8,128)(2,1)} %collective-permute-done.5.refs_1_, bf16[192,2048]{1,0:T(8,128)(2,1)} %collective-permute-done.6.refs_2_, bf16[2048,512]{1,0:T(8,128)(2,1)} %bitcast.35, ...), custom_call_target="tpu_custom_call" | custom-call | flops 966367641600 | bytes 18874368 | tf_op jit(solution)/shard_map/experts/pallas_call | solution.py:259
  129.7 0.0 collective-permute-done.11.refs_0_
  129.7 0.0 collective-permute-done.12.refs_1_
  129.8 0.0 collective-permute-done.10.refs_1_
  129.8 0.0 collective-permute-done.9.refs_0_
  129.8 3.3 %collective-permute-start.15 = (bf16[192,2048]{1,0:T(8,128)(2,1)}, bf16[192,2048]{1,0:T(8,128)(2,1)}, u32[]{:S(2)}, u32[]{:S(2)}) collective-permute-start(bf16[192,2048]{1,0:T(8,128)(2,1)} %get-tuple-element.78), channel_id=1, source_target_pairs={{0,96},{32,0},{64,32},{96,64},{1,97},{33,1},{65,33},{97,65},{2,98}... | collective-permute-start | bytes 2359304 | tf_op jit(solution)/shard_map/ppermute | solution.py:456
  133.1 0.0 collective-permute-start.16
  133.1 5.9 %all-to-all-start.4 = ((bf16[16,24,2048]{2,1,0:T(8,128)(2,1)}), bf16[16,24,2048]{2,1,0:T(8,128)(2,1)}, u32[]{:S(2)}, u32[]{:S(2)}) async-start(bf16[16,24,2048]{2,1,0:T(8,128)(2,1)} %bitcast.31), calls=%async_computation.4 | async-start | bytes 3145728 | tf_op jit(solution)/shard_map/all_to_all | solution.py:459
  139.0 7.9 %experts.5 = (bf16[96,2048]{1,0:T(8,128)(2,1)}, bf16[96,2048]{1,0:T(8,128)(2,1)}) custom-call(bf16[96,2048]{1,0:T(8,128)(2,1)} %collective-permute-done.9.refs_0_, bf16[96,2048]{1,0:T(8,128)(2,1)} %collective-permute-done.10.refs_1_, bf16[2048,512]{1,0:T(8,128)(2,1)} %bitcast.36, bf16[2048,512]{1,0:T(8,128)(2,1)} %bitcast.40, bf16[512,2048]{1,0:T(8,128)(2,1)} %bitcast.44, ...), custom_call_target="tpu_custom_call" | custom-call | flops 241591910400 | bytes 14155776 | tf_op jit(solution)/shard_map/experts/pallas_call | solution.py:259
  146.9 3.6 %collective-permute-start.13 = (bf16[96,2048]{1,0:T(8,128)(2,1)}, bf16[96,2048]{1,0:T(8,128)(2,1)S(1)}, u32[]{:S(2)}, u32[]{:S(2)}) collective-permute-start(bf16[96,2048]{1,0:T(8,128)(2,1)} %get-tuple-element.74), channel_id=1, source_target_pairs={{0,96},{32,0},{64,32},{96,64},{1,97},{33,1},{65,33},{97,65},{2,98}... | collective-permute-start | bytes 1179656 | tf_op jit(solution)/shard_map/ppermute | solution.py:456
  150.5 0.0 collective-permute-start.14
  150.5 0.0 collective-permute-done.15.refs_2_
  150.5 0.0 collective-permute-done.16.refs_3_
  150.5 3.0 %add_up.2.refs_2_ = bf16[384,2048]{1,0:T(8,128)(2,1)} custom-call(bf16[384,2048]{1,0:T(8,128)(2,1)S(1)} %copy-done, bf16[96,2048]{1,0:T(8,128)(2,1)} %collective-permute-done.11.refs_0_, bf16[96,2048]{1,0:T(8,128)(2,1)} %collective-permute-done.12.refs_1_, bf16[192,2048]{1,0:T(8,128)(2,1)} %collective-permute-done.15.refs_2_, ...), custom_call_target="tpu_custom_call" | custom-call | flops 1 | bytes 1 | tf_op jit(solution)/shard_map/add_up/pallas_call | solution.py:429
  153.5 2.6 %collective-permute-done.13.refs_0_ = bf16[96,2048]{1,0:T(8,128)(2,1)S(1)} collective-permute-done((bf16[96,2048]{1,0:T(8,128)(2,1)}, bf16[96,2048]{1,0:T(8,128)(2,1)S(1)}, u32[]{:S(2)}, u32[]{:S(2)}) %collective-permute-start.13) | collective-permute-done | bytes 393248 | tf_op jit(solution)/shard_map/ppermute | solution.py:456
  156.1 3.6 %collective-permute-done.14.refs_1_ = bf16[96,2048]{1,0:T(8,128)(2,1)S(1)} collective-permute-done((bf16[96,2048]{1,0:T(8,128)(2,1)}, bf16[96,2048]{1,0:T(8,128)(2,1)S(1)}, u32[]{:S(2)}, u32[]{:S(2)}) %collective-permute-start.14) | collective-permute-done | bytes 393248 | tf_op jit(solution)/shard_map/ppermute | solution.py:456
  159.7 0.9 add_up.3
  160.6 7.3 %all-to-all-start.5 = ((bf16[16,24,2048]{2,1,0:T(8,128)(2,1)}), bf16[16,24,2048]{2,1,0:T(8,128)(2,1)S(1)}, u32[]{:S(2)}, u32[]{:S(2)}) async-start(bf16[16,24,2048]{2,1,0:T(8,128)(2,1)} %bitcast.29), calls=%async_computation.5 | async-start | bytes 3145728 | tf_op jit(solution)/shard_map/all_to_all | solution.py:459
  167.9 2.6 %combine_far.1 = (bf16[128,2048]{1,0:T(8,128)(2,1)S(1)}, f32[128,2048]{1,0:T(8,128)S(1)}) custom-call(f32[8,128]{1,0:T(8,128)S(1)} %copy-done.5, bf16[384,2048]{1,0:T(8,128)(2,1)} %bitcast.15.back_ref, f32[128,2048]{1,0:T(8,128)} %get-tuple-element.82.mid_hbm), custom_call_target="tpu_custom_call" | custom-call | tf_op jit(solution)/shard_map/combine_far/pallas_call | solution.py:334
  170.6 0.1 collective-permute-start.17
  170.7 10.7 %collective-permute-done.17.far_ref = bf16[128,2048]{1,0:T(8,128)(2,1)S(1)} collective-permute-done((bf16[128,2048]{1,0:T(8,128)(2,1)S(1)}, bf16[128,2048]{1,0:T(8,128)(2,1)S(1)}, u32[]{:S(2)}, u32[]{:S(2)}) %collective-permute-start.17) | collective-permute-done | bytes 524320 | tf_op jit(solution)/shard_map/ppermute | solution.py:456
  181.4 4.1 %all-to-all-done.5 = bf16[16,24,2048]{2,1,0:T(8,128)(2,1)S(1)} async-done(((bf16[16,24,2048]{2,1,0:T(8,128)(2,1)}), bf16[16,24,2048]{2,1,0:T(8,128)(2,1)S(1)}, u32[]{:S(2)}, u32[]{:S(2)}) %all-to-all-start.5) | async-done | bytes 1572896 | tf_op jit(solution)/shard_map/all_to_all | solution.py:459
  185.5 1.7 combine.1
  (19 shorter events, 0.1 us)
Async XLA Ops:
  0.0 35.1 %collective-permute-start.1 = (bf16[2048,512]{1,0:T(8,128)(2,1)}, bf16[2048,512]{1,0:T(8,128)(2,1)}, u32[]{:S(2)}, u32[]{:S(2)}) collective-permute-start(bf16[2048,512]{1,0:T(8,128)(2,1)} %bitcast.33), channel_id=1, source_target_pairs={{0,16},{16,0},{1,17},{17,1},{2,18},{18,2},{3,19},{19,3},{4,20},{20... | collective-permute-start | bytes 6291464 | tf_op jit(solution)/shard_map/ppermute | solution.py:453
  0.0 35.1 %collective-permute-start.2 = (bf16[2048,512]{1,0:T(8,128)(2,1)}, bf16[2048,512]{1,0:T(8,128)(2,1)}, u32[]{:S(2)}, u32[]{:S(2)}) collective-permute-start(bf16[2048,512]{1,0:T(8,128)(2,1)} %bitcast.37), channel_id=1, source_target_pairs={{0,16},{16,0},{1,17},{17,1},{2,18},{18,2},{3,19},{19,3},{4,20},{20... | collective-permute-start | bytes 6291464 | tf_op jit(solution)/shard_map/ppermute | solution.py:453
  0.5 34.6 %collective-permute-start.3 = (bf16[512,2048]{1,0:T(8,128)(2,1)}, bf16[512,2048]{1,0:T(8,128)(2,1)}, u32[]{:S(2)}, u32[]{:S(2)}) collective-permute-start(bf16[512,2048]{1,0:T(8,128)(2,1)} %bitcast.41), channel_id=1, source_target_pairs={{0,16},{16,0},{1,17},{17,1},{2,18},{18,2},{3,19},{19,3},{4,20},{20... | collective-permute-start | bytes 6291464 | tf_op jit(solution)/shard_map/ppermute | solution.py:453
  3.0 4.7 %copy-start.6 = (s32[1,128,2]{1,2,0:T(2,128)S(1)}, s32[1,128,2]{1,2,0:T(2,128)}, u32[]{:S(2)}) copy-start(s32[1,128,2]{1,2,0:T(2,128)} %param.10) | copy-start | bytes 3076
  3.0 4.7 %copy-start.7 = (f32[1,128,2]{1,2,0:T(2,128)S(1)}, f32[1,128,2]{1,2,0:T(2,128)}, u32[]{:S(2)}) copy-start(f32[1,128,2]{1,2,0:T(2,128)} %param.11) | copy-start | bytes 3076
  3.0 26.2 %all-to-all-start = ((bf16[8,3,128,256]{3,2,1,0:T(8,128)(2,1)}), bf16[8,3,128,256]{3,2,1,0:T(8,128)(2,1)S(1)}, u32[]{:S(2)}, u32[]{:S(2)}) async-start(bf16[8,3,128,256]{3,2,1,0:T(8,128)(2,1)} %spread.1), calls=%async_computation | async-start | bytes 3145728 | tf_op jit(solution)/shard_map/all_to_all | solution.py:469
  7.9 40.1 %copy-start.2 = (f32[8,128]{1,0:T(8,128)}, f32[8,128]{1,0:T(8,128)S(1)}, u32[]{:S(2)}) copy-start(f32[8,128]{1,0:T(8,128)S(1)} %plan.1.info_ref) | copy-start | bytes 12292
  7.9 40.1 %copy-start.1 = (bf16[1,128,2048]{2,1,0:T(8,128)(2,1)S(1)}, bf16[1,128,2048]{2,1,0:T(8,128)(2,1)}, u32[]{:S(2)}) copy-start(bf16[1,128,2048]{2,1,0:T(8,128)(2,1)} %param.8) | copy-start | bytes 1572868
  7.9 27.2 %collective-permute-start = (f32[8,128]{1,0:T(8,128)S(1)}, f32[8,128]{1,0:T(8,128)S(1)}, u32[]{:S(2)}, u32[]{:S(2)}) collective-permute-start(f32[8,128]{1,0:T(8,128)S(1)} %plan.1.info_ref), channel_id=1, source_target_pairs={{0,64},{32,96},{64,0},{96,32},{1,65},{33,97},{65,1},{97,33},{2,66}... | collective-permute-start | bytes 12296 | tf_op jit(solution)/shard_map/ppermute | solution.py:456
  35.1 39.1 %copy-start.4 = (f32[8,128]{1,0:T(8,128)}, f32[8,128]{1,0:T(8,128)S(1)}, u32[]{:S(2)}) copy-start(f32[8,128]{1,0:T(8,128)S(1)} %collective-permute-done.info_ref) | copy-start | bytes 12292
  51.6 29.5 %all-to-all-start.2 = ((bf16[16,24,2048]{2,1,0:T(8,128)(2,1)}), bf16[16,24,2048]{2,1,0:T(8,128)(2,1)S(1)}, u32[]{:S(2)}, u32[]{:S(2)}) async-start(bf16[16,24,2048]{2,1,0:T(8,128)(2,1)} %bitcast.10), calls=%async_computation.2 | async-start | bytes 3145728 | tf_op jit(solution)/shard_map/all_to_all | solution.py:459
  60.0 14.2 %collective-permute-start.4 = (bf16[128,2048]{1,0:T(8,128)(2,1)S(1)}, bf16[128,2048]{1,0:T(8,128)(2,1)S(1)}, u32[]{:S(2)}, u32[]{:S(2)}) collective-permute-start(bf16[128,2048]{1,0:T(8,128)(2,1)S(1)} %get-tuple-element.49), channel_id=1, source_target_pairs={{0,64},{32,96},{64,0},{96,32},{1,65},{33,97},{65,1},{97,33},{2,66}... | collective-permute-start | bytes 1572872 | tf_op jit(solution)/shard_map/ppermute | solution.py:456
  82.1 12.1 %collective-permute-start.8 = (bf16[96,2048]{1,0:T(8,128)(2,1)S(1)}, bf16[96,2048]{1,0:T(8,128)(2,1)S(1)}, u32[]{:S(2)}, u32[]{:S(2)}) collective-permute-start(bf16[96,2048]{1,0:T(8,128)(2,1)S(1)} %slice.9), channel_id=1, source_target_pairs={{0,96},{32,0},{64,32},{96,64},{1,97},{33,1},{65,33},{97,65},{2,98}... | collective-permute-start | bytes 1179656 | tf_op jit(solution)/shard_map/ppermute | solution.py:456
  83.3 13.3 %collective-permute-start.7 = (bf16[96,2048]{1,0:T(8,128)(2,1)S(1)}, bf16[96,2048]{1,0:T(8,128)(2,1)S(1)}, u32[]{:S(2)}, u32[]{:S(2)}) collective-permute-start(bf16[96,2048]{1,0:T(8,128)(2,1)S(1)} %slice.9), channel_id=1, source_target_pairs={{0,32},{32,64},{64,96},{96,0},{1,33},{33,65},{65,97},{97,1},{2,34}... | collective-permute-start | bytes 1179656 | tf_op jit(solution)/shard_map/ppermute | solution.py:456
  84.2 27.9 %collective-permute-start.6 = (bf16[192,2048]{1,0:T(8,128)(2,1)}, bf16[192,2048]{1,0:T(8,128)(2,1)}, u32[]{:S(2)}, u32[]{:S(2)}) collective-permute-start(bf16[192,2048]{1,0:T(8,128)(2,1)} %slice.10), channel_id=1, source_target_pairs={{0,96},{32,0},{64,32},{96,64},{1,97},{33,1},{65,33},{97,65},{2,98}... | collective-permute-start | bytes 2359304 | tf_op jit(solution)/shard_map/ppermute | solution.py:456
  86.5 27.0 %collective-permute-start.5 = (bf16[192,2048]{1,0:T(8,128)(2,1)}, bf16[192,2048]{1,0:T(8,128)(2,1)}, u32[]{:S(2)}, u32[]{:S(2)}) collective-permute-start(bf16[192,2048]{1,0:T(8,128)(2,1)} %slice.10), channel_id=1, source_target_pairs={{0,32},{32,64},{64,96},{96,0},{1,33},{33,65},{65,97},{97,1},{2,34}... | collective-permute-start | bytes 2359304 | tf_op jit(solution)/shard_map/ppermute | solution.py:456
  87.3 27.0 %all-to-all-start.3 = ((bf16[16,24,2048]{2,1,0:T(8,128)(2,1)}), bf16[16,24,2048]{2,1,0:T(8,128)(2,1)}, u32[]{:S(2)}, u32[]{:S(2)}) async-start(bf16[16,24,2048]{2,1,0:T(8,128)(2,1)} %bitcast.12), calls=%async_computation.3 | async-start | bytes 3145728 | tf_op jit(solution)/shard_map/all_to_all | solution.py:459
  96.6 33.2 %collective-permute-start.10 = (bf16[96,2048]{1,0:T(8,128)(2,1)}, bf16[96,2048]{1,0:T(8,128)(2,1)}, u32[]{:S(2)}, u32[]{:S(2)}) collective-permute-start(bf16[96,2048]{1,0:T(8,128)(2,1)} %slice.11), channel_id=1, source_target_pairs={{0,96},{32,0},{64,32},{96,64},{1,97},{33,1},{65,33},{97,65},{2,98}... | collective-permute-start | bytes 1179656 | tf_op jit(solution)/shard_map/ppermute | solution.py:456
  97.5 32.3 %collective-permute-start.9 = (bf16[96,2048]{1,0:T(8,128)(2,1)}, bf16[96,2048]{1,0:T(8,128)(2,1)}, u32[]{:S(2)}, u32[]{:S(2)}) collective-permute-start(bf16[96,2048]{1,0:T(8,128)(2,1)} %slice.11), channel_id=1, source_target_pairs={{0,32},{32,64},{64,96},{96,0},{1,33},{33,65},{65,97},{97,1},{2,34}... | collective-permute-start | bytes 1179656 | tf_op jit(solution)/shard_map/ppermute | solution.py:456
  109.9 19.9 %collective-permute-start.11 = (bf16[96,2048]{1,0:T(8,128)(2,1)}, bf16[96,2048]{1,0:T(8,128)(2,1)}, u32[]{:S(2)}, u32[]{:S(2)}) collective-permute-start(bf16[96,2048]{1,0:T(8,128)(2,1)} %get-tuple-element.70), channel_id=1, source_target_pairs={{0,96},{32,0},{64,32},{96,64},{1,97},{33,1},{65,33},{97,65},{2,98}... | collective-permute-start | bytes 1179656 | tf_op jit(solution)/shard_map/ppermute | solution.py:456
  112.1 17.6 %collective-permute-start.12 = (bf16[96,2048]{1,0:T(8,128)(2,1)}, bf16[96,2048]{1,0:T(8,128)(2,1)}, u32[]{:S(2)}, u32[]{:S(2)}) collective-permute-start(bf16[96,2048]{1,0:T(8,128)(2,1)} %get-tuple-element.71), channel_id=1, source_target_pairs={{0,32},{32,64},{64,96},{96,0},{1,33},{33,65},{65,97},{97,1},{2,34}... | collective-permute-start | bytes 1179656 | tf_op jit(solution)/shard_map/ppermute | solution.py:456
  129.8 20.7 %collective-permute-start.15 = (bf16[192,2048]{1,0:T(8,128)(2,1)}, bf16[192,2048]{1,0:T(8,128)(2,1)}, u32[]{:S(2)}, u32[]{:S(2)}) collective-permute-start(bf16[192,2048]{1,0:T(8,128)(2,1)} %get-tuple-element.78), channel_id=1, source_target_pairs={{0,96},{32,0},{64,32},{96,64},{1,97},{33,1},{65,33},{97,65},{2,98}... | collective-permute-start | bytes 2359304 | tf_op jit(solution)/shard_map/ppermute | solution.py:456
  133.1 17.4 %collective-permute-start.16 = (bf16[192,2048]{1,0:T(8,128)(2,1)}, bf16[192,2048]{1,0:T(8,128)(2,1)}, u32[]{:S(2)}, u32[]{:S(2)}) collective-permute-start(bf16[192,2048]{1,0:T(8,128)(2,1)} %get-tuple-element.79), channel_id=1, source_target_pairs={{0,32},{32,64},{64,96},{96,0},{1,33},{33,65},{65,97},{97,1},{2,34}... | collective-permute-start | bytes 2359304 | tf_op jit(solution)/shard_map/ppermute | solution.py:456
  133.1 27.5 %all-to-all-start.4 = ((bf16[16,24,2048]{2,1,0:T(8,128)(2,1)}), bf16[16,24,2048]{2,1,0:T(8,128)(2,1)}, u32[]{:S(2)}, u32[]{:S(2)}) async-start(bf16[16,24,2048]{2,1,0:T(8,128)(2,1)} %bitcast.31), calls=%async_computation.4 | async-start | bytes 3145728 | tf_op jit(solution)/shard_map/all_to_all | solution.py:459
  139.0 11.5 %copy-start = (bf16[384,2048]{1,0:T(8,128)(2,1)S(1)}, bf16[384,2048]{1,0:T(8,128)(2,1)}, u32[]{:S(2)}) copy-start(bf16[384,2048]{1,0:T(8,128)(2,1)} %get-tuple-element.64.own_ref) | copy-start | bytes 4718596
  146.9 9.2 %collective-permute-start.13 = (bf16[96,2048]{1,0:T(8,128)(2,1)}, bf16[96,2048]{1,0:T(8,128)(2,1)S(1)}, u32[]{:S(2)}, u32[]{:S(2)}) collective-permute-start(bf16[96,2048]{1,0:T(8,128)(2,1)} %get-tuple-element.74), channel_id=1, source_target_pairs={{0,96},{32,0},{64,32},{96,64},{1,97},{33,1},{65,33},{97,65},{2,98}... | collective-permute-start | bytes 1179656 | tf_op jit(solution)/shard_map/ppermute | solution.py:456
  150.5 9.2 %collective-permute-start.14 = (bf16[96,2048]{1,0:T(8,128)(2,1)}, bf16[96,2048]{1,0:T(8,128)(2,1)S(1)}, u32[]{:S(2)}, u32[]{:S(2)}) collective-permute-start(bf16[96,2048]{1,0:T(8,128)(2,1)} %get-tuple-element.75), channel_id=1, source_target_pairs={{0,32},{32,64},{64,96},{96,0},{1,33},{33,65},{65,97},{97,1},{2,34}... | collective-permute-start | bytes 1179656 | tf_op jit(solution)/shard_map/ppermute | solution.py:456
  160.6 7.3 %copy-start.5 = (f32[8,128]{1,0:T(8,128)S(1)}, f32[8,128]{1,0:T(8,128)}, u32[]{:S(2)}) copy-start(f32[8,128]{1,0:T(8,128)} %copy-done.4) | copy-start | bytes 12292
  160.6 24.9 %all-to-all-start.5 = ((bf16[16,24,2048]{2,1,0:T(8,128)(2,1)}), bf16[16,24,2048]{2,1,0:T(8,128)(2,1)S(1)}, u32[]{:S(2)}, u32[]{:S(2)}) async-start(bf16[16,24,2048]{2,1,0:T(8,128)(2,1)} %bitcast.29), calls=%async_computation.5 | async-start | bytes 3145728 | tf_op jit(solution)/shard_map/all_to_all | solution.py:459
  167.9 17.6 %copy-start.3 = (f32[8,128]{1,0:T(8,128)S(1)}, f32[8,128]{1,0:T(8,128)}, u32[]{:S(2)}) copy-start(f32[8,128]{1,0:T(8,128)} %copy-done.2) | copy-start | bytes 12292
  170.6 10.8 %collective-permute-start.17 = (bf16[128,2048]{1,0:T(8,128)(2,1)S(1)}, bf16[128,2048]{1,0:T(8,128)(2,1)S(1)}, u32[]{:S(2)}, u32[]{:S(2)}) collective-permute-start(bf16[128,2048]{1,0:T(8,128)(2,1)S(1)} %get-tuple-element.83), channel_id=1, source_target_pairs={{0,64},{32,96},{64,0},{96,32},{1,65},{33,97},{65,1},{97,33},{2,66}... | collective-permute-start | bytes 1572872 | tf_op jit(solution)/shard_map/ppermute | solution.py:456

commit v12 on v11

--- a/solution.py
+++ b/solution.py
@@ -478,10 +478,8 @@
     own, far_buffer = tie((exchange(buffer), far_buffer))
     eighth = own.shape[0] // 8
     first, second = own[: 2 * eighth], own[2 * eighth : 6 * eighth]
-    rest, first, second = tie((own, first, second))
-    third = rest[6 * eighth :]
-    third, far_buffer = tie((third, far_buffer))
-    far_rows = exchange(far_buffer)
+    first, second, far_buffer = tie((first, second, far_buffer))
+    far_rows = exchange(keep(far_buffer))
 
     def send(x):
         return shift(x, 1), shift(x, -1)
@@ -490,8 +488,8 @@
         return shift(pair[0], -1), shift(pair[1], 1)
 
     at_first, at_second = send(first), send(second)
-    third, at_first = tie((third, at_first))
-    at_third = send(third)
+    own_seen, at_first = tie((own, at_first))
+    at_third = send(own_seen[6 * eighth :])
     own_part, *back = experts([own, *at_first], mine, other)
     home = [give_back(back)]
     far_rows, at_second, own_part = tie((far_rows, at_second, own_part))

time: 190 us -> 189 us (level)
  transfers between devices with their start and end apart: 23 -> 23, of which waited for: 10 -> 11; matrix products, arithmetic and copies ran while one was open for 0% -> 0% of each run, Pallas kernels for 27% -> 27%
where the time goes in v12:
time: 189 us; the launch traced here: 186 us
  waiting for transfers between devices  61.7 us (33%)
  Pallas kernels  55.5 us (29%)
  starting transfers between devices  53 us (28%)
  blocking collectives  12.8 us (7%)
  local copies, waits for them, and re-layouts  3.04 us (2%)
    ppermute x15, waiting for transfers between devices, shift(): return lax.ppermute(x, 'y', [(i, (i + by) % n_y) for i in range(n_y)])  34.7 us
    pallas_call x3, Pallas kernels, experts(): pl.pallas_call(functools.partial(expert_kernel, n_in=len(arrays), block=b...  34.6 us
    all_to_all x4, starting transfers between devices, exchange(): return lax.all_to_all(x, exp, split_axis=0, concat_axis=0, tiled=True)  28.5 us
    ppermute x15, starting transfers between devices, shift(): return lax.ppermute(x, 'y', [(i, (i + by) % n_y) for i in range(n_y)])  19.4 us
    all_to_all x1, waiting for transfers between devices, per_device(): arrived = lax.all_to_all(qkv, seq, split_axis=0, concat_axis=0, tiled=True)  17.7 us
    all_to_all x1, blocking collectives, per_device(): lax.all_to_all(context, seq, split_axis=0, concat_axis=0, tiled=True)  12.8 us
    all_to_all x4, waiting for transfers between devices, exchange(): return lax.all_to_all(x, exp, split_axis=0, concat_axis=0, tiled=True)  9.29 us
    pallas_call x1, Pallas kernels, attention(): pl.pallas_call(functools.partial(attention_kernel, block=2 * rows), grid=...  5.89 us
  transfers between devices with their start and end apart: 23, of which 11 were waited for; matrix products, arithmetic and copies ran while one was open for 0% of the time, Pallas kernels for 27%

profile of v12, /device:TPU:2, one launch (start us, length us, event | category | flops | bytes accessed | tf_op | source)
XLA Modules:
  0.0 186.4 jit_solution(8119921499391208212)
XLA Ops:
  0.0 0.0 collective-permute-start.1
  0.0 0.5 collective-permute-start.2
  0.5 0.0 collective-permute-start.3
  0.5 2.5 %spread.1 = bf16[8,3,128,256]{3,2,1,0:T(8,128)(2,1)} custom-call(bf16[3,128,2048]{2,1,0:T(8,128)(2,1)} %bitcast.31), custom_call_target="tpu_custom_call" | custom-call | tf_op jit(solution)/shard_map/spread/pallas_call | solution.py:391
  3.0 0.0 copy-start.7
  3.0 0.0 copy-start.8
  3.0 4.6 %all-to-all-start = ((bf16[8,3,128,256]{3,2,1,0:T(8,128)(2,1)}), bf16[8,3,128,256]{3,2,1,0:T(8,128)(2,1)S(1)}, u32[]{:S(2)}, u32[]{:S(2)}) async-start(bf16[8,3,128,256]{3,2,1,0:T(8,128)(2,1)} %spread.1), calls=%async_computation | async-start | bytes 3145728 | tf_op jit(solution)/shard_map/all_to_all | solution.py:469
  7.6 0.1 pad.2.clone
  7.7 0.1 maximum_maximum_fusion.info_ref
  7.8 0.1 plan.1.info_ref
  7.9 3.6 %collective-permute-start = (f32[8,128]{1,0:T(8,128)S(1)}, f32[8,128]{1,0:T(8,128)S(1)}, u32[]{:S(2)}, u32[]{:S(2)}) collective-permute-start(f32[8,128]{1,0:T(8,128)S(1)} %plan.1.info_ref), channel_id=1, source_target_pairs={{0,64},{32,96},{64,0},{96,32},{1,65},{33,97},{65,1},{97,33},{2,66}... | collective-permute-start | bytes 12296 | tf_op jit(solution)/shard_map/ppermute | solution.py:456
  11.5 17.7 %all-to-all-done.x_ref = bf16[8,3,128,256]{3,2,1,0:T(8,128)(2,1)S(1)} async-done(((bf16[8,3,128,256]{3,2,1,0:T(8,128)(2,1)}), bf16[8,3,128,256]{3,2,1,0:T(8,128)(2,1)S(1)}, u32[]{:S(2)}, u32[]{:S(2)}) %all-to-all-start) | async-done | bytes 1572896 | tf_op jit(solution)/shard_map/all_to_all | solution.py:469
  29.2 5.9 %attention.1 = (bf16[8,128,256]{2,1,0:T(8,128)(2,1)S(1)}, bf16[2048,2048]{1,0:T(8,128)(2,1)S(1)}) custom-call(bf16[8,3,128,256]{3,2,1,0:T(8,128)(2,1)S(1)} %all-to-all-done.x_ref, bf16[2048,2048]{1,0:T(8,128)(2,1)} %w_hbm.1), custom_call_target="tpu_custom_call" | custom-call | tf_op jit(solution)/shard_map/attention/pallas_call | solution.py:77
  35.1 0.0 collective-permute-done.info_ref
  35.1 0.0 collective-permute-done.1.refs_6_.refs_5_
  35.2 0.0 collective-permute-done.2.refs_7_.refs_6_
  35.2 0.0 collective-permute-done.3.refs_8_.refs_7_
  35.2 12.8 %all_to_all.56.ctx_ref = bf16[8,128,256]{2,1,0:T(8,128)(2,1)S(1)} all-to-all(bf16[8,128,256]{2,1,0:T(8,128)(2,1)S(1)} %get-tuple-element.44), channel_id=1, replica_groups=mesh['y'=4,'core'=2,'z'=4,'x'=4] {'y','core'}, dimensions={0} | all-to-all | bytes 1048576 | tf_op jit(solution)/shard_map/all_to_all | solution.py:472
  48.0 3.7 %project.1 = (f32[128,2048]{1,0:T(8,128)}, bf16[128,2048]{1,0:T(8,128)(2,1)S(1)}, bf16[384,2048]{1,0:T(8,128)(2,1)}) custom-call(bf16[8,128,256]{2,1,0:T(8,128)(2,1)S(1)} %all_to_all.56.ctx_ref, bf16[2048,2048]{1,0:T(8,128)(2,1)S(1)} %get-tuple-element.45.w_ref, bf16[128,2048]{1,0:T(8,128)(2,1)S(1)} %bitcast.29, f32[8,128]{1,0:T(8,128)S(1)} %plan.1.info_ref), custom_call_target="tpu_custom_call" | custom-call | tf_op jit(solution)/shard_map/project/pallas_call | solution.py:155
  51.6 8.3 %all-to-all-start.2 = ((bf16[16,24,2048]{2,1,0:T(8,128)(2,1)}), bf16[16,24,2048]{2,1,0:T(8,128)(2,1)S(1)}, u32[]{:S(2)}, u32[]{:S(2)}) async-start(bf16[16,24,2048]{2,1,0:T(8,128)(2,1)} %bitcast.10), calls=%async_computation.2 | async-start | bytes 3145728 | tf_op jit(solution)/shard_map/all_to_all | solution.py:459
  60.0 0.3 collective-permute-start.4
  60.3 13.9 %collective-permute-done.4.normed_ref = bf16[128,2048]{1,0:T(8,128)(2,1)S(1)} collective-permute-done((bf16[128,2048]{1,0:T(8,128)(2,1)S(1)}, bf16[128,2048]{1,0:T(8,128)(2,1)S(1)}, u32[]{:S(2)}, u32[]{:S(2)}) %collective-permute-start.4) | collective-permute-done | bytes 524320 | tf_op jit(solution)/shard_map/ppermute | solution.py:456
  74.2 0.6 route.1.x_ref
  74.8 1.1 copy-done
  75.9 5.2 %all-to-all-done.2 = bf16[16,24,2048]{2,1,0:T(8,128)(2,1)S(1)} async-done(((bf16[16,24,2048]{2,1,0:T(8,128)(2,1)}), bf16[16,24,2048]{2,1,0:T(8,128)(2,1)S(1)}, u32[]{:S(2)}, u32[]{:S(2)}) %all-to-all-start.2) | async-done | bytes 1572896 | tf_op jit(solution)/shard_map/all_to_all | solution.py:459
  81.2 1.0 slice.10
  82.1 1.2 collective-permute-start.8
  83.3 0.9 collective-permute-start.7
  84.2 2.4 %collective-permute-start.6 = (bf16[192,2048]{1,0:T(8,128)(2,1)}, bf16[192,2048]{1,0:T(8,128)(2,1)}, u32[]{:S(2)}, u32[]{:S(2)}) collective-permute-start(bf16[192,2048]{1,0:T(8,128)(2,1)} %slice.10), channel_id=1, source_target_pairs={{0,96},{32,0},{64,32},{96,64},{1,97},{33,1},{65,33},{97,65},{2,98}... | collective-permute-start | bytes 2359304 | tf_op jit(solution)/shard_map/ppermute | solution.py:456
  86.6 0.0 collective-permute-start.5
  86.6 6.9 %all-to-all-start.3 = ((bf16[16,24,2048]{2,1,0:T(8,128)(2,1)}), bf16[16,24,2048]{2,1,0:T(8,128)(2,1)}, u32[]{:S(2)}, u32[]{:S(2)}) async-start(bf16[16,24,2048]{2,1,0:T(8,128)(2,1)} %bitcast.28), calls=%async_computation.3 | async-start | bytes 3145728 | tf_op jit(solution)/shard_map/all_to_all | solution.py:459
  93.5 0.7 collective-permute-done.8.refs_2_
  94.2 2.4 %collective-permute-done.7.refs_1_ = bf16[96,2048]{1,0:T(8,128)(2,1)S(1)} collective-permute-done((bf16[96,2048]{1,0:T(8,128)(2,1)S(1)}, bf16[96,2048]{1,0:T(8,128)(2,1)S(1)}, u32[]{:S(2)}, u32[]{:S(2)}) %collective-permute-start.7) | collective-permute-done | bytes 393248 | tf_op jit(solution)/shard_map/ppermute | solution.py:456
  96.6 0.8 slice.11
  97.4 0.1 collective-permute-start.10
  97.5 1.9 %collective-permute-start.9 = (bf16[96,2048]{1,0:T(8,128)(2,1)}, bf16[96,2048]{1,0:T(8,128)(2,1)}, u32[]{:S(2)}, u32[]{:S(2)}) collective-permute-start(bf16[96,2048]{1,0:T(8,128)(2,1)} %slice.11), channel_id=1, source_target_pairs={{0,32},{32,64},{64,96},{96,0},{1,33},{33,65},{65,97},{97,1},{2,34}... | collective-permute-start | bytes 1179656 | tf_op jit(solution)/shard_map/ppermute | solution.py:456
  99.4 11.3 %experts.3 = (bf16[384,2048]{1,0:T(8,128)(2,1)}, bf16[96,2048]{1,0:T(8,128)(2,1)}, bf16[96,2048]{1,0:T(8,128)(2,1)}) custom-call(bf16[384,2048]{1,0:T(8,128)(2,1)S(1)} %bitcast.26, bf16[96,2048]{1,0:T(8,128)(2,1)S(1)} %collective-permute-done.7.refs_1_, bf16[96,2048]{1,0:T(8,128)(2,1)S(1)} %collective-permute-done.8.refs_2_, bf16[2048,512]{1,0:T(8,128)(2,1)} %bitcast.35, ...), custom_call_target="tpu_custom_call" | custom-call | flops 724775731200 | bytes 17301504 | tf_op jit(solution)/shard_map/experts/pallas_call | solution.py:259
  110.7 1.4 collective-permute-start.11
  112.1 0.0 collective-permute-done.6.refs_2_
  112.1 0.7 collective-permute-start.12
  112.8 0.8 collective-permute-done.5.refs_1_
  113.5 0.1 all-to-all-done.3
  113.6 15.4 %experts.4 = (bf16[384,2048]{1,0:T(8,128)(2,1)}, bf16[192,2048]{1,0:T(8,128)(2,1)}, bf16[192,2048]{1,0:T(8,128)(2,1)}) custom-call(bf16[384,2048]{1,0:T(8,128)(2,1)} %bitcast.13.refs_0_, bf16[192,2048]{1,0:T(8,128)(2,1)} %collective-permute-done.5.refs_1_, bf16[192,2048]{1,0:T(8,128)(2,1)} %collective-permute-done.6.refs_2_, bf16[2048,512]{1,0:T(8,128)(2,1)} %bitcast.36, ...), custom_call_target="tpu_custom_call" | custom-call | flops 966367641600 | bytes 18874368 | tf_op jit(solution)/shard_map/experts/pallas_call | solution.py:259
  129.0 0.0 collective-permute-done.10.refs_1_
  129.0 0.0 collective-permute-done.11.refs_0_
  129.0 0.0 collective-permute-done.12.refs_1_
  129.1 3.3 %collective-permute-start.15 = (bf16[192,2048]{1,0:T(8,128)(2,1)}, bf16[192,2048]{1,0:T(8,128)(2,1)}, u32[]{:S(2)}, u32[]{:S(2)}) collective-permute-start(bf16[192,2048]{1,0:T(8,128)(2,1)} %get-tuple-element.74), channel_id=1, source_target_pairs={{0,96},{32,0},{64,32},{96,64},{1,97},{33,1},{65,33},{97,65},{2,98}... | collective-permute-start | bytes 2359304 | tf_op jit(solution)/shard_map/ppermute | solution.py:456
  132.3 0.0 collective-permute-start.16
  132.3 6.0 %all-to-all-start.4 = ((bf16[16,24,2048]{2,1,0:T(8,128)(2,1)}), bf16[16,24,2048]{2,1,0:T(8,128)(2,1)}, u32[]{:S(2)}, u32[]{:S(2)}) async-start(bf16[16,24,2048]{2,1,0:T(8,128)(2,1)} %bitcast.32), calls=%async_computation.4 | async-start | bytes 3145728 | tf_op jit(solution)/shard_map/all_to_all | solution.py:459
  138.3 7.9 %experts.5 = (bf16[96,2048]{1,0:T(8,128)(2,1)}, bf16[96,2048]{1,0:T(8,128)(2,1)}) custom-call(bf16[96,2048]{1,0:T(8,128)(2,1)} %collective-permute-done.9.refs_0_, bf16[96,2048]{1,0:T(8,128)(2,1)} %collective-permute-done.10.refs_1_, bf16[2048,512]{1,0:T(8,128)(2,1)} %bitcast.37, bf16[2048,512]{1,0:T(8,128)(2,1)} %bitcast.41, bf16[512,2048]{1,0:T(8,128)(2,1)} %bitcast.45, ...), custom_call_target="tpu_custom_call" | custom-call | flops 241591910400 | bytes 14155776 | tf_op jit(solution)/shard_map/experts/pallas_call | solution.py:259
  146.2 3.6 %collective-permute-start.13 = (bf16[96,2048]{1,0:T(8,128)(2,1)}, bf16[96,2048]{1,0:T(8,128)(2,1)S(1)}, u32[]{:S(2)}, u32[]{:S(2)}) collective-permute-start(bf16[96,2048]{1,0:T(8,128)(2,1)} %get-tuple-element.70), channel_id=1, source_target_pairs={{0,96},{32,0},{64,32},{96,64},{1,97},{33,1},{65,33},{97,65},{2,98}... | collective-permute-start | bytes 1179656 | tf_op jit(solution)/shard_map/ppermute | solution.py:456
  149.8 0.0 collective-permute-start.14
  149.8 0.0 collective-permute-done.15.refs_2_
  149.8 0.0 collective-permute-done.16.refs_3_
  149.8 3.0 %add_up.2.refs_2_ = bf16[384,2048]{1,0:T(8,128)(2,1)} custom-call(bf16[384,2048]{1,0:T(8,128)(2,1)S(1)} %copy-done.1, bf16[96,2048]{1,0:T(8,128)(2,1)} %collective-permute-done.11.refs_0_, bf16[96,2048]{1,0:T(8,128)(2,1)} %collective-permute-done.12.refs_1_, bf16[192,2048]{1,0:T(8,128)(2,1)} %collective-permute-done.15.refs_2_, ...), custom_call_target="tpu_custom_call" | custom-call | flops 1 | bytes 1 | tf_op jit(solution)/shard_map/add_up/pallas_call | solution.py:429
  152.8 2.6 %collective-permute-done.13.refs_0_ = bf16[96,2048]{1,0:T(8,128)(2,1)S(1)} collective-permute-done((bf16[96,2048]{1,0:T(8,128)(2,1)}, bf16[96,2048]{1,0:T(8,128)(2,1)S(1)}, u32[]{:S(2)}, u32[]{:S(2)}) %collective-permute-start.13) | collective-permute-done | bytes 393248 | tf_op jit(solution)/shard_map/ppermute | solution.py:456
  155.4 3.6 %collective-permute-done.14.refs_1_ = bf16[96,2048]{1,0:T(8,128)(2,1)S(1)} collective-permute-done((bf16[96,2048]{1,0:T(8,128)(2,1)}, bf16[96,2048]{1,0:T(8,128)(2,1)S(1)}, u32[]{:S(2)}, u32[]{:S(2)}) %collective-permute-start.14) | collective-permute-done | bytes 393248 | tf_op jit(solution)/shard_map/ppermute | solution.py:456
  159.0 0.9 add_up.3
  159.9 7.3 %all-to-all-start.5 = ((bf16[16,24,2048]{2,1,0:T(8,128)(2,1)}), bf16[16,24,2048]{2,1,0:T(8,128)(2,1)S(1)}, u32[]{:S(2)}, u32[]{:S(2)}) async-start(bf16[16,24,2048]{2,1,0:T(8,128)(2,1)} %bitcast.30), calls=%async_computation.5 | async-start | bytes 3145728 | tf_op jit(solution)/shard_map/all_to_all | solution.py:459
  167.2 2.6 %combine_far.1 = (bf16[128,2048]{1,0:T(8,128)(2,1)S(1)}, f32[128,2048]{1,0:T(8,128)S(1)}) custom-call(f32[8,128]{1,0:T(8,128)S(1)} %copy-done.6, bf16[384,2048]{1,0:T(8,128)(2,1)} %bitcast.15.back_ref, f32[128,2048]{1,0:T(8,128)} %get-tuple-element.78.mid_hbm), custom_call_target="tpu_custom_call" | custom-call | tf_op jit(solution)/shard_map/combine_far/pallas_call | solution.py:334
  169.9 0.1 collective-permute-start.17
  170.0 10.7 %collective-permute-done.17.far_ref = bf16[128,2048]{1,0:T(8,128)(2,1)S(1)} collective-permute-done((bf16[128,2048]{1,0:T(8,128)(2,1)S(1)}, bf16[128,2048]{1,0:T(8,128)(2,1)S(1)}, u32[]{:S(2)}, u32[]{:S(2)}) %collective-permute-start.17) | collective-permute-done | bytes 524320 | tf_op jit(solution)/shard_map/ppermute | solution.py:456
  180.7 4.0 %all-to-all-done.5 = bf16[16,24,2048]{2,1,0:T(8,128)(2,1)S(1)} async-done(((bf16[16,24,2048]{2,1,0:T(8,128)(2,1)}), bf16[16,24,2048]{2,1,0:T(8,128)(2,1)S(1)}, u32[]{:S(2)}, u32[]{:S(2)}) %all-to-all-start.5) | async-done | bytes 1572896 | tf_op jit(solution)/shard_map/all_to_all | solution.py:459
  184.7 1.7 combine.1
  (22 shorter events, 0.1 us)
Async XLA Ops:
  0.0 35.1 %collective-permute-start.1 = (bf16[2048,512]{1,0:T(8,128)(2,1)}, bf16[2048,512]{1,0:T(8,128)(2,1)}, u32[]{:S(2)}, u32[]{:S(2)}) collective-permute-start(bf16[2048,512]{1,0:T(8,128)(2,1)} %bitcast.34), channel_id=1, source_target_pairs={{0,16},{16,0},{1,17},{17,1},{2,18},{18,2},{3,19},{19,3},{4,20},{20... | collective-permute-start | bytes 6291464 | tf_op jit(solution)/shard_map/ppermute | solution.py:453
  0.0 35.1 %collective-permute-start.2 = (bf16[2048,512]{1,0:T(8,128)(2,1)}, bf16[2048,512]{1,0:T(8,128)(2,1)}, u32[]{:S(2)}, u32[]{:S(2)}) collective-permute-start(bf16[2048,512]{1,0:T(8,128)(2,1)} %bitcast.38), channel_id=1, source_target_pairs={{0,16},{16,0},{1,17},{17,1},{2,18},{18,2},{3,19},{19,3},{4,20},{20... | collective-permute-start | bytes 6291464 | tf_op jit(solution)/shard_map/ppermute | solution.py:453
  0.5 34.7 %collective-permute-start.3 = (bf16[512,2048]{1,0:T(8,128)(2,1)}, bf16[512,2048]{1,0:T(8,128)(2,1)}, u32[]{:S(2)}, u32[]{:S(2)}) collective-permute-start(bf16[512,2048]{1,0:T(8,128)(2,1)} %bitcast.42), channel_id=1, source_target_pairs={{0,16},{16,0},{1,17},{17,1},{2,18},{18,2},{3,19},{19,3},{4,20},{20... | collective-permute-start | bytes 6291464 | tf_op jit(solution)/shard_map/ppermute | solution.py:453
  3.0 4.7 %copy-start.7 = (s32[1,128,2]{1,2,0:T(2,128)S(1)}, s32[1,128,2]{1,2,0:T(2,128)}, u32[]{:S(2)}) copy-start(s32[1,128,2]{1,2,0:T(2,128)} %param.10) | copy-start | bytes 3076
  3.0 4.7 %copy-start.8 = (f32[1,128,2]{1,2,0:T(2,128)S(1)}, f32[1,128,2]{1,2,0:T(2,128)}, u32[]{:S(2)}) copy-start(f32[1,128,2]{1,2,0:T(2,128)} %param.11) | copy-start | bytes 3076
  3.0 26.2 %all-to-all-start = ((bf16[8,3,128,256]{3,2,1,0:T(8,128)(2,1)}), bf16[8,3,128,256]{3,2,1,0:T(8,128)(2,1)S(1)}, u32[]{:S(2)}, u32[]{:S(2)}) async-start(bf16[8,3,128,256]{3,2,1,0:T(8,128)(2,1)} %spread.1), calls=%async_computation | async-start | bytes 3145728 | tf_op jit(solution)/shard_map/all_to_all | solution.py:469
  7.9 40.1 %copy-start.3 = (f32[8,128]{1,0:T(8,128)}, f32[8,128]{1,0:T(8,128)S(1)}, u32[]{:S(2)}) copy-start(f32[8,128]{1,0:T(8,128)S(1)} %plan.1.info_ref) | copy-start | bytes 12292
  7.9 40.1 %copy-start.2 = (bf16[1,128,2048]{2,1,0:T(8,128)(2,1)S(1)}, bf16[1,128,2048]{2,1,0:T(8,128)(2,1)}, u32[]{:S(2)}) copy-start(bf16[1,128,2048]{2,1,0:T(8,128)(2,1)} %param.8) | copy-start | bytes 1572868
  7.9 27.2 %collective-permute-start = (f32[8,128]{1,0:T(8,128)S(1)}, f32[8,128]{1,0:T(8,128)S(1)}, u32[]{:S(2)}, u32[]{:S(2)}) collective-permute-start(f32[8,128]{1,0:T(8,128)S(1)} %plan.1.info_ref), channel_id=1, source_target_pairs={{0,64},{32,96},{64,0},{96,32},{1,65},{33,97},{65,1},{97,33},{2,66}... | collective-permute-start | bytes 12296 | tf_op jit(solution)/shard_map/ppermute | solution.py:456
  35.1 39.1 %copy-start.5 = (f32[8,128]{1,0:T(8,128)}, f32[8,128]{1,0:T(8,128)S(1)}, u32[]{:S(2)}) copy-start(f32[8,128]{1,0:T(8,128)S(1)} %collective-permute-done.info_ref) | copy-start | bytes 12292
  51.6 29.5 %all-to-all-start.2 = ((bf16[16,24,2048]{2,1,0:T(8,128)(2,1)}), bf16[16,24,2048]{2,1,0:T(8,128)(2,1)S(1)}, u32[]{:S(2)}, u32[]{:S(2)}) async-start(bf16[16,24,2048]{2,1,0:T(8,128)(2,1)} %bitcast.10), calls=%async_computation.2 | async-start | bytes 3145728 | tf_op jit(solution)/shard_map/all_to_all | solution.py:459
  60.0 14.2 %collective-permute-start.4 = (bf16[128,2048]{1,0:T(8,128)(2,1)S(1)}, bf16[128,2048]{1,0:T(8,128)(2,1)S(1)}, u32[]{:S(2)}, u32[]{:S(2)}) collective-permute-start(bf16[128,2048]{1,0:T(8,128)(2,1)S(1)} %get-tuple-element.47), channel_id=1, source_target_pairs={{0,64},{32,96},{64,0},{96,32},{1,65},{33,97},{65,1},{97,33},{2,66}... | collective-permute-start | bytes 1572872 | tf_op jit(solution)/shard_map/ppermute | solution.py:456
  74.8 1.1 copy-start
  82.1 12.1 %collective-permute-start.8 = (bf16[96,2048]{1,0:T(8,128)(2,1)S(1)}, bf16[96,2048]{1,0:T(8,128)(2,1)S(1)}, u32[]{:S(2)}, u32[]{:S(2)}) collective-permute-start(bf16[96,2048]{1,0:T(8,128)(2,1)S(1)} %slice.9), channel_id=1, source_target_pairs={{0,96},{32,0},{64,32},{96,64},{1,97},{33,1},{65,33},{97,65},{2,98}... | collective-permute-start | bytes 1179656 | tf_op jit(solution)/shard_map/ppermute | solution.py:456
  83.3 13.3 %collective-permute-start.7 = (bf16[96,2048]{1,0:T(8,128)(2,1)S(1)}, bf16[96,2048]{1,0:T(8,128)(2,1)S(1)}, u32[]{:S(2)}, u32[]{:S(2)}) collective-permute-start(bf16[96,2048]{1,0:T(8,128)(2,1)S(1)} %slice.9), channel_id=1, source_target_pairs={{0,32},{32,64},{64,96},{96,0},{1,33},{33,65},{65,97},{97,1},{2,34}... | collective-permute-start | bytes 1179656 | tf_op jit(solution)/shard_map/ppermute | solution.py:456
  84.2 27.9 %collective-permute-start.6 = (bf16[192,2048]{1,0:T(8,128)(2,1)}, bf16[192,2048]{1,0:T(8,128)(2,1)}, u32[]{:S(2)}, u32[]{:S(2)}) collective-permute-start(bf16[192,2048]{1,0:T(8,128)(2,1)} %slice.10), channel_id=1, source_target_pairs={{0,96},{32,0},{64,32},{96,64},{1,97},{33,1},{65,33},{97,65},{2,98}... | collective-permute-start | bytes 2359304 | tf_op jit(solution)/shard_map/ppermute | solution.py:456
  86.6 27.0 %collective-permute-start.5 = (bf16[192,2048]{1,0:T(8,128)(2,1)}, bf16[192,2048]{1,0:T(8,128)(2,1)}, u32[]{:S(2)}, u32[]{:S(2)}) collective-permute-start(bf16[192,2048]{1,0:T(8,128)(2,1)} %slice.10), channel_id=1, source_target_pairs={{0,32},{32,64},{64,96},{96,0},{1,33},{33,65},{65,97},{97,1},{2,34}... | collective-permute-start | bytes 2359304 | tf_op jit(solution)/shard_map/ppermute | solution.py:456
  86.6 27.1 %all-to-all-start.3 = ((bf16[16,24,2048]{2,1,0:T(8,128)(2,1)}), bf16[16,24,2048]{2,1,0:T(8,128)(2,1)}, u32[]{:S(2)}, u32[]{:S(2)}) async-start(bf16[16,24,2048]{2,1,0:T(8,128)(2,1)} %bitcast.28), calls=%async_computation.3 | async-start | bytes 3145728 | tf_op jit(solution)/shard_map/all_to_all | solution.py:459
  97.4 31.7 %collective-permute-start.10 = (bf16[96,2048]{1,0:T(8,128)(2,1)}, bf16[96,2048]{1,0:T(8,128)(2,1)}, u32[]{:S(2)}, u32[]{:S(2)}) collective-permute-start(bf16[96,2048]{1,0:T(8,128)(2,1)} %slice.11), channel_id=1, source_target_pairs={{0,96},{32,0},{64,32},{96,64},{1,97},{33,1},{65,33},{97,65},{2,98}... | collective-permute-start | bytes 1179656 | tf_op jit(solution)/shard_map/ppermute | solution.py:456
  97.5 31.5 %collective-permute-start.9 = (bf16[96,2048]{1,0:T(8,128)(2,1)}, bf16[96,2048]{1,0:T(8,128)(2,1)}, u32[]{:S(2)}, u32[]{:S(2)}) collective-permute-start(bf16[96,2048]{1,0:T(8,128)(2,1)} %slice.11), channel_id=1, source_target_pairs={{0,32},{32,64},{64,96},{96,0},{1,33},{33,65},{65,97},{97,1},{2,34}... | collective-permute-start | bytes 1179656 | tf_op jit(solution)/shard_map/ppermute | solution.py:456
  110.7 18.3 %collective-permute-start.11 = (bf16[96,2048]{1,0:T(8,128)(2,1)}, bf16[96,2048]{1,0:T(8,128)(2,1)}, u32[]{:S(2)}, u32[]{:S(2)}) collective-permute-start(bf16[96,2048]{1,0:T(8,128)(2,1)} %get-tuple-element.66), channel_id=1, source_target_pairs={{0,96},{32,0},{64,32},{96,64},{1,97},{33,1},{65,33},{97,65},{2,98}... | collective-permute-start | bytes 1179656 | tf_op jit(solution)/shard_map/ppermute | solution.py:456
  112.1 16.9 %collective-permute-start.12 = (bf16[96,2048]{1,0:T(8,128)(2,1)}, bf16[96,2048]{1,0:T(8,128)(2,1)}, u32[]{:S(2)}, u32[]{:S(2)}) collective-permute-start(bf16[96,2048]{1,0:T(8,128)(2,1)} %get-tuple-element.67), channel_id=1, source_target_pairs={{0,32},{32,64},{64,96},{96,0},{1,33},{33,65},{65,97},{97,1},{2,34}... | collective-permute-start | bytes 1179656 | tf_op jit(solution)/shard_map/ppermute | solution.py:456
  129.1 20.7 %collective-permute-start.15 = (bf16[192,2048]{1,0:T(8,128)(2,1)}, bf16[192,2048]{1,0:T(8,128)(2,1)}, u32[]{:S(2)}, u32[]{:S(2)}) collective-permute-start(bf16[192,2048]{1,0:T(8,128)(2,1)} %get-tuple-element.74), channel_id=1, source_target_pairs={{0,96},{32,0},{64,32},{96,64},{1,97},{33,1},{65,33},{97,65},{2,98}... | collective-permute-start | bytes 2359304 | tf_op jit(solution)/shard_map/ppermute | solution.py:456
  132.3 17.5 %collective-permute-start.16 = (bf16[192,2048]{1,0:T(8,128)(2,1)}, bf16[192,2048]{1,0:T(8,128)(2,1)}, u32[]{:S(2)}, u32[]{:S(2)}) collective-permute-start(bf16[192,2048]{1,0:T(8,128)(2,1)} %get-tuple-element.75), channel_id=1, source_target_pairs={{0,32},{32,64},{64,96},{96,0},{1,33},{33,65},{65,97},{97,1},{2,34}... | collective-permute-start | bytes 2359304 | tf_op jit(solution)/shard_map/ppermute | solution.py:456
  132.3 27.6 %all-to-all-start.4 = ((bf16[16,24,2048]{2,1,0:T(8,128)(2,1)}), bf16[16,24,2048]{2,1,0:T(8,128)(2,1)}, u32[]{:S(2)}, u32[]{:S(2)}) async-start(bf16[16,24,2048]{2,1,0:T(8,128)(2,1)} %bitcast.32), calls=%async_computation.4 | async-start | bytes 3145728 | tf_op jit(solution)/shard_map/all_to_all | solution.py:459
  138.3 11.5 %copy-start.1 = (bf16[384,2048]{1,0:T(8,128)(2,1)S(1)}, bf16[384,2048]{1,0:T(8,128)(2,1)}, u32[]{:S(2)}) copy-start(bf16[384,2048]{1,0:T(8,128)(2,1)} %get-tuple-element.60.own_ref) | copy-start | bytes 4718596
  146.2 9.2 %collective-permute-start.13 = (bf16[96,2048]{1,0:T(8,128)(2,1)}, bf16[96,2048]{1,0:T(8,128)(2,1)S(1)}, u32[]{:S(2)}, u32[]{:S(2)}) collective-permute-start(bf16[96,2048]{1,0:T(8,128)(2,1)} %get-tuple-element.70), channel_id=1, source_target_pairs={{0,96},{32,0},{64,32},{96,64},{1,97},{33,1},{65,33},{97,65},{2,98}... | collective-permute-start | bytes 1179656 | tf_op jit(solution)/shard_map/ppermute | solution.py:456
  149.8 9.2 %collective-permute-start.14 = (bf16[96,2048]{1,0:T(8,128)(2,1)}, bf16[96,2048]{1,0:T(8,128)(2,1)S(1)}, u32[]{:S(2)}, u32[]{:S(2)}) collective-permute-start(bf16[96,2048]{1,0:T(8,128)(2,1)} %get-tuple-element.71), channel_id=1, source_target_pairs={{0,32},{32,64},{64,96},{96,0},{1,33},{33,65},{65,97},{97,1},{2,34}... | collective-permute-start | bytes 1179656 | tf_op jit(solution)/shard_map/ppermute | solution.py:456
  159.9 7.3 %copy-start.6 = (f32[8,128]{1,0:T(8,128)S(1)}, f32[8,128]{1,0:T(8,128)}, u32[]{:S(2)}) copy-start(f32[8,128]{1,0:T(8,128)} %copy-done.5) | copy-start | bytes 12292
  159.9 24.7 %all-to-all-start.5 = ((bf16[16,24,2048]{2,1,0:T(8,128)(2,1)}), bf16[16,24,2048]{2,1,0:T(8,128)(2,1)S(1)}, u32[]{:S(2)}, u32[]{:S(2)}) async-start(bf16[16,24,2048]{2,1,0:T(8,128)(2,1)} %bitcast.30), calls=%async_computation.5 | async-start | bytes 3145728 | tf_op jit(solution)/shard_map/all_to_all | solution.py:459
  167.2 17.4 %copy-start.4 = (f32[8,128]{1,0:T(8,128)S(1)}, f32[8,128]{1,0:T(8,128)}, u32[]{:S(2)}) copy-start(f32[8,128]{1,0:T(8,128)} %copy-done.3) | copy-start | bytes 12292
  169.9 10.8 %collective-permute-start.17 = (bf16[128,2048]{1,0:T(8,128)(2,1)S(1)}, bf16[128,2048]{1,0:T(8,128)(2,1)S(1)}, u32[]{:S(2)}, u32[]{:S(2)}) collective-permute-start(bf16[128,2048]{1,0:T(8,128)(2,1)S(1)} %get-tuple-element.79), channel_id=1, source_target_pairs={{0,64},{32,96},{64,0},{96,32},{1,65},{33,97},{65,1},{97,33},{2,66}... | collective-permute-start | bytes 1572872 | tf_op jit(solution)/shard_map/ppermute | solution.py:456

commit v13 on v12

--- a/solution.py
+++ b/solution.py
@@ -255,7 +255,7 @@
     width = arrays[0].shape[1]
     hidden = 2 * mine[0].shape[1]
     total = sum(x.shape[0] for x in arrays)
-    block = 256
+    block = mine[0].shape[1] if total <= 256 else 256
     return pl.pallas_call(
         functools.partial(expert_kernel, n_in=len(arrays), block=block),
         grid=(1,),

time: 189 us -> 189 us (level)
  no operation moved by 1% of the time
where the time goes in v13:
time: 189 us; the launch traced here: 186 us
  waiting for transfers between devices  61.6 us (33%)
  Pallas kernels  55.8 us (30%)
  starting transfers between devices  52.8 us (28%)
  blocking collectives  12.8 us (7%)
  local copies, waits for them, and re-layouts  3.04 us (2%)
    pallas_call x3, Pallas kernels, experts(): pl.pallas_call(functools.partial(expert_kernel, n_in=len(arrays), block=b...  34.8 us
    ppermute x15, waiting for transfers between devices, shift(): return lax.ppermute(x, 'y', [(i, (i + by) % n_y) for i in range(n_y)])  34.7 us
    all_to_all x4, starting transfers between devices, exchange(): return lax.all_to_all(x, exp, split_axis=0, concat_axis=0, tiled=True)  28.5 us
    ppermute x15, starting transfers between devices, shift(): return lax.ppermute(x, 'y', [(i, (i + by) % n_y) for i in range(n_y)])  19.2 us
    all_to_all x1, waiting for transfers between devices, per_device(): arrived = lax.all_to_all(qkv, seq, split_axis=0, concat_axis=0, tiled=True)  17.7 us
    all_to_all x1, blocking collectives, per_device(): lax.all_to_all(context, seq, split_axis=0, concat_axis=0, tiled=True)  12.8 us
    all_to_all x4, waiting for transfers between devices, exchange(): return lax.all_to_all(x, exp, split_axis=0, concat_axis=0, tiled=True)  9.27 us
    pallas_call x1, Pallas kernels, attention(): pl.pallas_call(functools.partial(attention_kernel, block=2 * rows), grid=...  5.89 us
  transfers between devices with their start and end apart: 23, of which 11 were waited for; matrix products, arithmetic and copies ran while one was open for 0% of the time, Pallas kernels for 27%

profile of v13, /device:TPU:2, one launch (start us, length us, event | category | flops | bytes accessed | tf_op | source)
XLA Modules:
  0.0 186.3 jit_solution(1528850995321862805)
XLA Ops:
  0.0 0.0 collective-permute-start.1
  0.0 0.5 collective-permute-start.2
  0.5 0.0 collective-permute-start.3
  0.5 2.5 %spread.1 = bf16[8,3,128,256]{3,2,1,0:T(8,128)(2,1)} custom-call(bf16[3,128,2048]{2,1,0:T(8,128)(2,1)} %bitcast.31), custom_call_target="tpu_custom_call" | custom-call | tf_op jit(solution)/shard_map/spread/pallas_call | solution.py:391
  3.0 0.0 copy-start.7
  3.0 0.0 copy-start.8
  3.0 4.6 %all-to-all-start = ((bf16[8,3,128,256]{3,2,1,0:T(8,128)(2,1)}), bf16[8,3,128,256]{3,2,1,0:T(8,128)(2,1)S(1)}, u32[]{:S(2)}, u32[]{:S(2)}) async-start(bf16[8,3,128,256]{3,2,1,0:T(8,128)(2,1)} %spread.1), calls=%async_computation | async-start | bytes 3145728 | tf_op jit(solution)/shard_map/all_to_all | solution.py:469
  7.6 0.1 pad.2.clone
  7.7 0.1 maximum_maximum_fusion.info_ref
  7.8 0.1 plan.1.info_ref
  7.9 3.6 %collective-permute-start = (f32[8,128]{1,0:T(8,128)S(1)}, f32[8,128]{1,0:T(8,128)S(1)}, u32[]{:S(2)}, u32[]{:S(2)}) collective-permute-start(f32[8,128]{1,0:T(8,128)S(1)} %plan.1.info_ref), channel_id=1, source_target_pairs={{0,64},{32,96},{64,0},{96,32},{1,65},{33,97},{65,1},{97,33},{2,66}... | collective-permute-start | bytes 12296 | tf_op jit(solution)/shard_map/ppermute | solution.py:456
  11.5 17.7 %all-to-all-done.x_ref = bf16[8,3,128,256]{3,2,1,0:T(8,128)(2,1)S(1)} async-done(((bf16[8,3,128,256]{3,2,1,0:T(8,128)(2,1)}), bf16[8,3,128,256]{3,2,1,0:T(8,128)(2,1)S(1)}, u32[]{:S(2)}, u32[]{:S(2)}) %all-to-all-start) | async-done | bytes 1572896 | tf_op jit(solution)/shard_map/all_to_all | solution.py:469
  29.2 5.9 %attention.1 = (bf16[8,128,256]{2,1,0:T(8,128)(2,1)S(1)}, bf16[2048,2048]{1,0:T(8,128)(2,1)S(1)}) custom-call(bf16[8,3,128,256]{3,2,1,0:T(8,128)(2,1)S(1)} %all-to-all-done.x_ref, bf16[2048,2048]{1,0:T(8,128)(2,1)} %w_hbm.1), custom_call_target="tpu_custom_call" | custom-call | tf_op jit(solution)/shard_map/attention/pallas_call | solution.py:77
  35.1 0.0 collective-permute-done.info_ref
  35.1 0.0 collective-permute-done.1.refs_6_.refs_5_
  35.2 0.0 collective-permute-done.2.refs_7_.refs_6_
  35.2 0.0 collective-permute-done.3.refs_8_.refs_7_
  35.2 12.8 %all_to_all.56.ctx_ref = bf16[8,128,256]{2,1,0:T(8,128)(2,1)S(1)} all-to-all(bf16[8,128,256]{2,1,0:T(8,128)(2,1)S(1)} %get-tuple-element.44), channel_id=1, replica_groups=mesh['y'=4,'core'=2,'z'=4,'x'=4] {'y','core'}, dimensions={0} | all-to-all | bytes 1048576 | tf_op jit(solution)/shard_map/all_to_all | solution.py:472
  48.0 3.7 %project.1 = (f32[128,2048]{1,0:T(8,128)}, bf16[128,2048]{1,0:T(8,128)(2,1)S(1)}, bf16[384,2048]{1,0:T(8,128)(2,1)}) custom-call(bf16[8,128,256]{2,1,0:T(8,128)(2,1)S(1)} %all_to_all.56.ctx_ref, bf16[2048,2048]{1,0:T(8,128)(2,1)S(1)} %get-tuple-element.45.w_ref, bf16[128,2048]{1,0:T(8,128)(2,1)S(1)} %bitcast.29, f32[8,128]{1,0:T(8,128)S(1)} %plan.1.info_ref), custom_call_target="tpu_custom_call" | custom-call | tf_op jit(solution)/shard_map/project/pallas_call | solution.py:155
  51.6 8.3 %all-to-all-start.2 = ((bf16[16,24,2048]{2,1,0:T(8,128)(2,1)}), bf16[16,24,2048]{2,1,0:T(8,128)(2,1)S(1)}, u32[]{:S(2)}, u32[]{:S(2)}) async-start(bf16[16,24,2048]{2,1,0:T(8,128)(2,1)} %bitcast.10), calls=%async_computation.2 | async-start | bytes 3145728 | tf_op jit(solution)/shard_map/all_to_all | solution.py:459
  60.0 0.3 collective-permute-start.4
  60.3 13.9 %collective-permute-done.4.normed_ref = bf16[128,2048]{1,0:T(8,128)(2,1)S(1)} collective-permute-done((bf16[128,2048]{1,0:T(8,128)(2,1)S(1)}, bf16[128,2048]{1,0:T(8,128)(2,1)S(1)}, u32[]{:S(2)}, u32[]{:S(2)}) %collective-permute-start.4) | collective-permute-done | bytes 524320 | tf_op jit(solution)/shard_map/ppermute | solution.py:456
  74.2 0.6 route.1.x_ref
  74.8 1.1 copy-done
  75.9 5.2 %all-to-all-done.2 = bf16[16,24,2048]{2,1,0:T(8,128)(2,1)S(1)} async-done(((bf16[16,24,2048]{2,1,0:T(8,128)(2,1)}), bf16[16,24,2048]{2,1,0:T(8,128)(2,1)S(1)}, u32[]{:S(2)}, u32[]{:S(2)}) %all-to-all-start.2) | async-done | bytes 1572896 | tf_op jit(solution)/shard_map/all_to_all | solution.py:459
  81.2 1.0 slice.10
  82.1 1.2 collective-permute-start.8
  83.3 0.9 collective-permute-start.7
  84.2 2.4 %collective-permute-start.6 = (bf16[192,2048]{1,0:T(8,128)(2,1)}, bf16[192,2048]{1,0:T(8,128)(2,1)}, u32[]{:S(2)}, u32[]{:S(2)}) collective-permute-start(bf16[192,2048]{1,0:T(8,128)(2,1)} %slice.10), channel_id=1, source_target_pairs={{0,96},{32,0},{64,32},{96,64},{1,97},{33,1},{65,33},{97,65},{2,98}... | collective-permute-start | bytes 2359304 | tf_op jit(solution)/shard_map/ppermute | solution.py:456
  86.6 0.0 collective-permute-start.5
  86.6 6.9 %all-to-all-start.3 = ((bf16[16,24,2048]{2,1,0:T(8,128)(2,1)}), bf16[16,24,2048]{2,1,0:T(8,128)(2,1)}, u32[]{:S(2)}, u32[]{:S(2)}) async-start(bf16[16,24,2048]{2,1,0:T(8,128)(2,1)} %bitcast.28), calls=%async_computation.3 | async-start | bytes 3145728 | tf_op jit(solution)/shard_map/all_to_all | solution.py:459
  93.5 0.7 collective-permute-done.8.refs_2_
  94.2 2.4 %collective-permute-done.7.refs_1_ = bf16[96,2048]{1,0:T(8,128)(2,1)S(1)} collective-permute-done((bf16[96,2048]{1,0:T(8,128)(2,1)S(1)}, bf16[96,2048]{1,0:T(8,128)(2,1)S(1)}, u32[]{:S(2)}, u32[]{:S(2)}) %collective-permute-start.7) | collective-permute-done | bytes 393248 | tf_op jit(solution)/shard_map/ppermute | solution.py:456
  96.6 0.8 slice.11
  97.4 0.1 collective-permute-start.10
  97.5 1.9 %collective-permute-start.9 = (bf16[96,2048]{1,0:T(8,128)(2,1)}, bf16[96,2048]{1,0:T(8,128)(2,1)}, u32[]{:S(2)}, u32[]{:S(2)}) collective-permute-start(bf16[96,2048]{1,0:T(8,128)(2,1)} %slice.11), channel_id=1, source_target_pairs={{0,32},{32,64},{64,96},{96,0},{1,33},{33,65},{65,97},{97,1},{2,34}... | collective-permute-start | bytes 1179656 | tf_op jit(solution)/shard_map/ppermute | solution.py:456
  99.4 11.3 %experts.3 = (bf16[384,2048]{1,0:T(8,128)(2,1)}, bf16[96,2048]{1,0:T(8,128)(2,1)}, bf16[96,2048]{1,0:T(8,128)(2,1)}) custom-call(bf16[384,2048]{1,0:T(8,128)(2,1)S(1)} %bitcast.26, bf16[96,2048]{1,0:T(8,128)(2,1)S(1)} %collective-permute-done.7.refs_1_, bf16[96,2048]{1,0:T(8,128)(2,1)S(1)} %collective-permute-done.8.refs_2_, bf16[2048,512]{1,0:T(8,128)(2,1)} %bitcast.35, ...), custom_call_target="tpu_custom_call" | custom-call | flops 724775731200 | bytes 17301504 | tf_op jit(solution)/shard_map/experts/pallas_call | solution.py:259
  110.7 1.4 collective-permute-start.11
  112.1 0.0 collective-permute-done.6.refs_2_
  112.1 0.7 collective-permute-start.12
  112.8 0.8 collective-permute-done.5.refs_1_
  113.5 0.1 all-to-all-done.3
  113.6 15.4 %experts.4 = (bf16[384,2048]{1,0:T(8,128)(2,1)}, bf16[192,2048]{1,0:T(8,128)(2,1)}, bf16[192,2048]{1,0:T(8,128)(2,1)}) custom-call(bf16[384,2048]{1,0:T(8,128)(2,1)} %bitcast.13.refs_0_, bf16[192,2048]{1,0:T(8,128)(2,1)} %collective-permute-done.5.refs_1_, bf16[192,2048]{1,0:T(8,128)(2,1)} %collective-permute-done.6.refs_2_, bf16[2048,512]{1,0:T(8,128)(2,1)} %bitcast.36, ...), custom_call_target="tpu_custom_call" | custom-call | flops 966367641600 | bytes 18874368 | tf_op jit(solution)/shard_map/experts/pallas_call | solution.py:259
  129.0 0.0 collective-permute-done.10.refs_1_
  129.0 0.0 collective-permute-done.9.refs_0_
  129.0 0.0 collective-permute-done.11.refs_0_
  129.0 0.0 collective-permute-done.12.refs_1_
  129.1 3.3 %collective-permute-start.15 = (bf16[192,2048]{1,0:T(8,128)(2,1)}, bf16[192,2048]{1,0:T(8,128)(2,1)}, u32[]{:S(2)}, u32[]{:S(2)}) collective-permute-start(bf16[192,2048]{1,0:T(8,128)(2,1)} %get-tuple-element.74), channel_id=1, source_target_pairs={{0,96},{32,0},{64,32},{96,64},{1,97},{33,1},{65,33},{97,65},{2,98}... | collective-permute-start | bytes 2359304 | tf_op jit(solution)/shard_map/ppermute | solution.py:456
  132.3 6.0 %all-to-all-start.4 = ((bf16[16,24,2048]{2,1,0:T(8,128)(2,1)}), bf16[16,24,2048]{2,1,0:T(8,128)(2,1)}, u32[]{:S(2)}, u32[]{:S(2)}) async-start(bf16[16,24,2048]{2,1,0:T(8,128)(2,1)} %bitcast.32), calls=%async_computation.4 | async-start | bytes 3145728 | tf_op jit(solution)/shard_map/all_to_all | solution.py:459
  138.3 8.2 %experts.5 = (bf16[96,2048]{1,0:T(8,128)(2,1)}, bf16[96,2048]{1,0:T(8,128)(2,1)}) custom-call(bf16[96,2048]{1,0:T(8,128)(2,1)} %collective-permute-done.9.refs_0_, bf16[96,2048]{1,0:T(8,128)(2,1)} %collective-permute-done.10.refs_1_, bf16[2048,512]{1,0:T(8,128)(2,1)} %bitcast.37, bf16[2048,512]{1,0:T(8,128)(2,1)} %bitcast.41, bf16[512,2048]{1,0:T(8,128)(2,1)} %bitcast.45, ...), custom_call_target="tpu_custom_call" | custom-call | flops 241591910400 | bytes 14155776 | tf_op jit(solution)/shard_map/experts/pallas_call | solution.py:259
  146.5 3.3 %collective-permute-start.13 = (bf16[96,2048]{1,0:T(8,128)(2,1)}, bf16[96,2048]{1,0:T(8,128)(2,1)S(1)}, u32[]{:S(2)}, u32[]{:S(2)}) collective-permute-start(bf16[96,2048]{1,0:T(8,128)(2,1)} %get-tuple-element.70), channel_id=1, source_target_pairs={{0,96},{32,0},{64,32},{96,64},{1,97},{33,1},{65,33},{97,65},{2,98}... | collective-permute-start | bytes 1179656 | tf_op jit(solution)/shard_map/ppermute | solution.py:456
  149.8 0.0 collective-permute-start.14
  149.8 0.0 collective-permute-done.15.refs_2_
  149.8 3.0 %add_up.2.refs_2_ = bf16[384,2048]{1,0:T(8,128)(2,1)} custom-call(bf16[384,2048]{1,0:T(8,128)(2,1)S(1)} %copy-done.1, bf16[96,2048]{1,0:T(8,128)(2,1)} %collective-permute-done.11.refs_0_, bf16[96,2048]{1,0:T(8,128)(2,1)} %collective-permute-done.12.refs_1_, bf16[192,2048]{1,0:T(8,128)(2,1)} %collective-permute-done.15.refs_2_, ...), custom_call_target="tpu_custom_call" | custom-call | flops 1 | bytes 1 | tf_op jit(solution)/shard_map/add_up/pallas_call | solution.py:429
  152.8 2.6 %collective-permute-done.13.refs_0_ = bf16[96,2048]{1,0:T(8,128)(2,1)S(1)} collective-permute-done((bf16[96,2048]{1,0:T(8,128)(2,1)}, bf16[96,2048]{1,0:T(8,128)(2,1)S(1)}, u32[]{:S(2)}, u32[]{:S(2)}) %collective-permute-start.13) | collective-permute-done | bytes 393248 | tf_op jit(solution)/shard_map/ppermute | solution.py:456
  155.4 3.6 %collective-permute-done.14.refs_1_ = bf16[96,2048]{1,0:T(8,128)(2,1)S(1)} collective-permute-done((bf16[96,2048]{1,0:T(8,128)(2,1)}, bf16[96,2048]{1,0:T(8,128)(2,1)S(1)}, u32[]{:S(2)}, u32[]{:S(2)}) %collective-permute-start.14) | collective-permute-done | bytes 393248 | tf_op jit(solution)/shard_map/ppermute | solution.py:456
  159.0 0.9 add_up.3
  159.9 0.0 all-to-all-done.4
  159.9 7.3 %all-to-all-start.5 = ((bf16[16,24,2048]{2,1,0:T(8,128)(2,1)}), bf16[16,24,2048]{2,1,0:T(8,128)(2,1)S(1)}, u32[]{:S(2)}, u32[]{:S(2)}) async-start(bf16[16,24,2048]{2,1,0:T(8,128)(2,1)} %bitcast.30), calls=%async_computation.5 | async-start | bytes 3145728 | tf_op jit(solution)/shard_map/all_to_all | solution.py:459
  167.2 2.6 %combine_far.1 = (bf16[128,2048]{1,0:T(8,128)(2,1)S(1)}, f32[128,2048]{1,0:T(8,128)S(1)}) custom-call(f32[8,128]{1,0:T(8,128)S(1)} %copy-done.6, bf16[384,2048]{1,0:T(8,128)(2,1)} %bitcast.15.back_ref, f32[128,2048]{1,0:T(8,128)} %get-tuple-element.78.mid_hbm), custom_call_target="tpu_custom_call" | custom-call | tf_op jit(solution)/shard_map/combine_far/pallas_call | solution.py:334
  169.9 0.1 collective-permute-start.17
  170.0 10.7 %collective-permute-done.17.far_ref = bf16[128,2048]{1,0:T(8,128)(2,1)S(1)} collective-permute-done((bf16[128,2048]{1,0:T(8,128)(2,1)S(1)}, bf16[128,2048]{1,0:T(8,128)(2,1)S(1)}, u32[]{:S(2)}, u32[]{:S(2)}) %collective-permute-start.17) | collective-permute-done | bytes 524320 | tf_op jit(solution)/shard_map/ppermute | solution.py:456
  180.6 4.0 %all-to-all-done.5 = bf16[16,24,2048]{2,1,0:T(8,128)(2,1)S(1)} async-done(((bf16[16,24,2048]{2,1,0:T(8,128)(2,1)}), bf16[16,24,2048]{2,1,0:T(8,128)(2,1)S(1)}, u32[]{:S(2)}, u32[]{:S(2)}) %all-to-all-start.5) | async-done | bytes 1572896 | tf_op jit(solution)/shard_map/all_to_all | solution.py:459
  184.6 1.7 combine.1
  (22 shorter events, 0.1 us)
Async XLA Ops:
  0.0 35.1 %collective-permute-start.1 = (bf16[2048,512]{1,0:T(8,128)(2,1)}, bf16[2048,512]{1,0:T(8,128)(2,1)}, u32[]{:S(2)}, u32[]{:S(2)}) collective-permute-start(bf16[2048,512]{1,0:T(8,128)(2,1)} %bitcast.34), channel_id=1, source_target_pairs={{0,16},{16,0},{1,17},{17,1},{2,18},{18,2},{3,19},{19,3},{4,20},{20... | collective-permute-start | bytes 6291464 | tf_op jit(solution)/shard_map/ppermute | solution.py:453
  0.0 35.1 %collective-permute-start.2 = (bf16[2048,512]{1,0:T(8,128)(2,1)}, bf16[2048,512]{1,0:T(8,128)(2,1)}, u32[]{:S(2)}, u32[]{:S(2)}) collective-permute-start(bf16[2048,512]{1,0:T(8,128)(2,1)} %bitcast.38), channel_id=1, source_target_pairs={{0,16},{16,0},{1,17},{17,1},{2,18},{18,2},{3,19},{19,3},{4,20},{20... | collective-permute-start | bytes 6291464 | tf_op jit(solution)/shard_map/ppermute | solution.py:453
  0.5 34.7 %collective-permute-start.3 = (bf16[512,2048]{1,0:T(8,128)(2,1)}, bf16[512,2048]{1,0:T(8,128)(2,1)}, u32[]{:S(2)}, u32[]{:S(2)}) collective-permute-start(bf16[512,2048]{1,0:T(8,128)(2,1)} %bitcast.42), channel_id=1, source_target_pairs={{0,16},{16,0},{1,17},{17,1},{2,18},{18,2},{3,19},{19,3},{4,20},{20... | collective-permute-start | bytes 6291464 | tf_op jit(solution)/shard_map/ppermute | solution.py:453
  3.0 4.7 %copy-start.7 = (s32[1,128,2]{1,2,0:T(2,128)S(1)}, s32[1,128,2]{1,2,0:T(2,128)}, u32[]{:S(2)}) copy-start(s32[1,128,2]{1,2,0:T(2,128)} %param.10) | copy-start | bytes 3076
  3.0 4.7 %copy-start.8 = (f32[1,128,2]{1,2,0:T(2,128)S(1)}, f32[1,128,2]{1,2,0:T(2,128)}, u32[]{:S(2)}) copy-start(f32[1,128,2]{1,2,0:T(2,128)} %param.11) | copy-start | bytes 3076
  3.0 26.2 %all-to-all-start = ((bf16[8,3,128,256]{3,2,1,0:T(8,128)(2,1)}), bf16[8,3,128,256]{3,2,1,0:T(8,128)(2,1)S(1)}, u32[]{:S(2)}, u32[]{:S(2)}) async-start(bf16[8,3,128,256]{3,2,1,0:T(8,128)(2,1)} %spread.1), calls=%async_computation | async-start | bytes 3145728 | tf_op jit(solution)/shard_map/all_to_all | solution.py:469
  7.9 40.1 %copy-start.3 = (f32[8,128]{1,0:T(8,128)}, f32[8,128]{1,0:T(8,128)S(1)}, u32[]{:S(2)}) copy-start(f32[8,128]{1,0:T(8,128)S(1)} %plan.1.info_ref) | copy-start | bytes 12292
  7.9 40.1 %copy-start.2 = (bf16[1,128,2048]{2,1,0:T(8,128)(2,1)S(1)}, bf16[1,128,2048]{2,1,0:T(8,128)(2,1)}, u32[]{:S(2)}) copy-start(bf16[1,128,2048]{2,1,0:T(8,128)(2,1)} %param.8) | copy-start | bytes 1572868
  7.9 27.2 %collective-permute-start = (f32[8,128]{1,0:T(8,128)S(1)}, f32[8,128]{1,0:T(8,128)S(1)}, u32[]{:S(2)}, u32[]{:S(2)}) collective-permute-start(f32[8,128]{1,0:T(8,128)S(1)} %plan.1.info_ref), channel_id=1, source_target_pairs={{0,64},{32,96},{64,0},{96,32},{1,65},{33,97},{65,1},{97,33},{2,66}... | collective-permute-start | bytes 12296 | tf_op jit(solution)/shard_map/ppermute | solution.py:456
  35.1 39.1 %copy-start.5 = (f32[8,128]{1,0:T(8,128)}, f32[8,128]{1,0:T(8,128)S(1)}, u32[]{:S(2)}) copy-start(f32[8,128]{1,0:T(8,128)S(1)} %collective-permute-done.info_ref) | copy-start | bytes 12292
  51.6 29.5 %all-to-all-start.2 = ((bf16[16,24,2048]{2,1,0:T(8,128)(2,1)}), bf16[16,24,2048]{2,1,0:T(8,128)(2,1)S(1)}, u32[]{:S(2)}, u32[]{:S(2)}) async-start(bf16[16,24,2048]{2,1,0:T(8,128)(2,1)} %bitcast.10), calls=%async_computation.2 | async-start | bytes 3145728 | tf_op jit(solution)/shard_map/all_to_all | solution.py:459
  60.0 14.2 %collective-permute-start.4 = (bf16[128,2048]{1,0:T(8,128)(2,1)S(1)}, bf16[128,2048]{1,0:T(8,128)(2,1)S(1)}, u32[]{:S(2)}, u32[]{:S(2)}) collective-permute-start(bf16[128,2048]{1,0:T(8,128)(2,1)S(1)} %get-tuple-element.47), channel_id=1, source_target_pairs={{0,64},{32,96},{64,0},{96,32},{1,65},{33,97},{65,1},{97,33},{2,66}... | collective-permute-start | bytes 1572872 | tf_op jit(solution)/shard_map/ppermute | solution.py:456
  74.8 1.1 copy-start
  82.1 12.1 %collective-permute-start.8 = (bf16[96,2048]{1,0:T(8,128)(2,1)S(1)}, bf16[96,2048]{1,0:T(8,128)(2,1)S(1)}, u32[]{:S(2)}, u32[]{:S(2)}) collective-permute-start(bf16[96,2048]{1,0:T(8,128)(2,1)S(1)} %slice.9), channel_id=1, source_target_pairs={{0,96},{32,0},{64,32},{96,64},{1,97},{33,1},{65,33},{97,65},{2,98}... | collective-permute-start | bytes 1179656 | tf_op jit(solution)/shard_map/ppermute | solution.py:456
  83.3 13.3 %collective-permute-start.7 = (bf16[96,2048]{1,0:T(8,128)(2,1)S(1)}, bf16[96,2048]{1,0:T(8,128)(2,1)S(1)}, u32[]{:S(2)}, u32[]{:S(2)}) collective-permute-start(bf16[96,2048]{1,0:T(8,128)(2,1)S(1)} %slice.9), channel_id=1, source_target_pairs={{0,32},{32,64},{64,96},{96,0},{1,33},{33,65},{65,97},{97,1},{2,34}... | collective-permute-start | bytes 1179656 | tf_op jit(solution)/shard_map/ppermute | solution.py:456
  84.2 27.9 %collective-permute-start.6 = (bf16[192,2048]{1,0:T(8,128)(2,1)}, bf16[192,2048]{1,0:T(8,128)(2,1)}, u32[]{:S(2)}, u32[]{:S(2)}) collective-permute-start(bf16[192,2048]{1,0:T(8,128)(2,1)} %slice.10), channel_id=1, source_target_pairs={{0,96},{32,0},{64,32},{96,64},{1,97},{33,1},{65,33},{97,65},{2,98}... | collective-permute-start | bytes 2359304 | tf_op jit(solution)/shard_map/ppermute | solution.py:456
  86.6 27.0 %collective-permute-start.5 = (bf16[192,2048]{1,0:T(8,128)(2,1)}, bf16[192,2048]{1,0:T(8,128)(2,1)}, u32[]{:S(2)}, u32[]{:S(2)}) collective-permute-start(bf16[192,2048]{1,0:T(8,128)(2,1)} %slice.10), channel_id=1, source_target_pairs={{0,32},{32,64},{64,96},{96,0},{1,33},{33,65},{65,97},{97,1},{2,34}... | collective-permute-start | bytes 2359304 | tf_op jit(solution)/shard_map/ppermute | solution.py:456
  86.6 27.1 %all-to-all-start.3 = ((bf16[16,24,2048]{2,1,0:T(8,128)(2,1)}), bf16[16,24,2048]{2,1,0:T(8,128)(2,1)}, u32[]{:S(2)}, u32[]{:S(2)}) async-start(bf16[16,24,2048]{2,1,0:T(8,128)(2,1)} %bitcast.28), calls=%async_computation.3 | async-start | bytes 3145728 | tf_op jit(solution)/shard_map/all_to_all | solution.py:459
  97.4 31.7 %collective-permute-start.10 = (bf16[96,2048]{1,0:T(8,128)(2,1)}, bf16[96,2048]{1,0:T(8,128)(2,1)}, u32[]{:S(2)}, u32[]{:S(2)}) collective-permute-start(bf16[96,2048]{1,0:T(8,128)(2,1)} %slice.11), channel_id=1, source_target_pairs={{0,96},{32,0},{64,32},{96,64},{1,97},{33,1},{65,33},{97,65},{2,98}... | collective-permute-start | bytes 1179656 | tf_op jit(solution)/shard_map/ppermute | solution.py:456
  97.5 31.5 %collective-permute-start.9 = (bf16[96,2048]{1,0:T(8,128)(2,1)}, bf16[96,2048]{1,0:T(8,128)(2,1)}, u32[]{:S(2)}, u32[]{:S(2)}) collective-permute-start(bf16[96,2048]{1,0:T(8,128)(2,1)} %slice.11), channel_id=1, source_target_pairs={{0,32},{32,64},{64,96},{96,0},{1,33},{33,65},{65,97},{97,1},{2,34}... | collective-permute-start | bytes 1179656 | tf_op jit(solution)/shard_map/ppermute | solution.py:456
  110.7 18.3 %collective-permute-start.11 = (bf16[96,2048]{1,0:T(8,128)(2,1)}, bf16[96,2048]{1,0:T(8,128)(2,1)}, u32[]{:S(2)}, u32[]{:S(2)}) collective-permute-start(bf16[96,2048]{1,0:T(8,128)(2,1)} %get-tuple-element.66), channel_id=1, source_target_pairs={{0,96},{32,0},{64,32},{96,64},{1,97},{33,1},{65,33},{97,65},{2,98}... | collective-permute-start | bytes 1179656 | tf_op jit(solution)/shard_map/ppermute | solution.py:456
  112.1 16.9 %collective-permute-start.12 = (bf16[96,2048]{1,0:T(8,128)(2,1)}, bf16[96,2048]{1,0:T(8,128)(2,1)}, u32[]{:S(2)}, u32[]{:S(2)}) collective-permute-start(bf16[96,2048]{1,0:T(8,128)(2,1)} %get-tuple-element.67), channel_id=1, source_target_pairs={{0,32},{32,64},{64,96},{96,0},{1,33},{33,65},{65,97},{97,1},{2,34}... | collective-permute-start | bytes 1179656 | tf_op jit(solution)/shard_map/ppermute | solution.py:456
  129.1 20.7 %collective-permute-start.15 = (bf16[192,2048]{1,0:T(8,128)(2,1)}, bf16[192,2048]{1,0:T(8,128)(2,1)}, u32[]{:S(2)}, u32[]{:S(2)}) collective-permute-start(bf16[192,2048]{1,0:T(8,128)(2,1)} %get-tuple-element.74), channel_id=1, source_target_pairs={{0,96},{32,0},{64,32},{96,64},{1,97},{33,1},{65,33},{97,65},{2,98}... | collective-permute-start | bytes 2359304 | tf_op jit(solution)/shard_map/ppermute | solution.py:456
  132.3 17.4 %collective-permute-start.16 = (bf16[192,2048]{1,0:T(8,128)(2,1)}, bf16[192,2048]{1,0:T(8,128)(2,1)}, u32[]{:S(2)}, u32[]{:S(2)}) collective-permute-start(bf16[192,2048]{1,0:T(8,128)(2,1)} %get-tuple-element.75), channel_id=1, source_target_pairs={{0,32},{32,64},{64,96},{96,0},{1,33},{33,65},{65,97},{97,1},{2,34}... | collective-permute-start | bytes 2359304 | tf_op jit(solution)/shard_map/ppermute | solution.py:456
  132.3 27.5 %all-to-all-start.4 = ((bf16[16,24,2048]{2,1,0:T(8,128)(2,1)}), bf16[16,24,2048]{2,1,0:T(8,128)(2,1)}, u32[]{:S(2)}, u32[]{:S(2)}) async-start(bf16[16,24,2048]{2,1,0:T(8,128)(2,1)} %bitcast.32), calls=%async_computation.4 | async-start | bytes 3145728 | tf_op jit(solution)/shard_map/all_to_all | solution.py:459
  138.3 11.5 %copy-start.1 = (bf16[384,2048]{1,0:T(8,128)(2,1)S(1)}, bf16[384,2048]{1,0:T(8,128)(2,1)}, u32[]{:S(2)}) copy-start(bf16[384,2048]{1,0:T(8,128)(2,1)} %get-tuple-element.60.own_ref) | copy-start | bytes 4718596
  146.5 8.9 %collective-permute-start.13 = (bf16[96,2048]{1,0:T(8,128)(2,1)}, bf16[96,2048]{1,0:T(8,128)(2,1)S(1)}, u32[]{:S(2)}, u32[]{:S(2)}) collective-permute-start(bf16[96,2048]{1,0:T(8,128)(2,1)} %get-tuple-element.70), channel_id=1, source_target_pairs={{0,96},{32,0},{64,32},{96,64},{1,97},{33,1},{65,33},{97,65},{2,98}... | collective-permute-start | bytes 1179656 | tf_op jit(solution)/shard_map/ppermute | solution.py:456
  149.8 9.2 %collective-permute-start.14 = (bf16[96,2048]{1,0:T(8,128)(2,1)}, bf16[96,2048]{1,0:T(8,128)(2,1)S(1)}, u32[]{:S(2)}, u32[]{:S(2)}) collective-permute-start(bf16[96,2048]{1,0:T(8,128)(2,1)} %get-tuple-element.71), channel_id=1, source_target_pairs={{0,32},{32,64},{64,96},{96,0},{1,33},{33,65},{65,97},{97,1},{2,34}... | collective-permute-start | bytes 1179656 | tf_op jit(solution)/shard_map/ppermute | solution.py:456
  159.9 7.3 %copy-start.6 = (f32[8,128]{1,0:T(8,128)S(1)}, f32[8,128]{1,0:T(8,128)}, u32[]{:S(2)}) copy-start(f32[8,128]{1,0:T(8,128)} %copy-done.5) | copy-start | bytes 12292
  159.9 24.7 %all-to-all-start.5 = ((bf16[16,24,2048]{2,1,0:T(8,128)(2,1)}), bf16[16,24,2048]{2,1,0:T(8,128)(2,1)S(1)}, u32[]{:S(2)}, u32[]{:S(2)}) async-start(bf16[16,24,2048]{2,1,0:T(8,128)(2,1)} %bitcast.30), calls=%async_computation.5 | async-start | bytes 3145728 | tf_op jit(solution)/shard_map/all_to_all | solution.py:459
  167.2 17.4 %copy-start.4 = (f32[8,128]{1,0:T(8,128)S(1)}, f32[8,128]{1,0:T(8,128)}, u32[]{:S(2)}) copy-start(f32[8,128]{1,0:T(8,128)} %copy-done.3) | copy-start | bytes 12292
  169.9 10.8 %collective-permute-start.17 = (bf16[128,2048]{1,0:T(8,128)(2,1)S(1)}, bf16[128,2048]{1,0:T(8,128)(2,1)S(1)}, u32[]{:S(2)}, u32[]{:S(2)}) collective-permute-start(bf16[128,2048]{1,0:T(8,128)(2,1)S(1)} %get-tuple-element.79), channel_id=1, source_target_pairs={{0,64},{32,96},{64,0},{96,32},{1,65},{33,97},{65,1},{97,33},{2,66}... | collective-permute-start | bytes 1572872 | tf_op jit(solution)/shard_map/ppermute | solution.py:456
